TPU v7x, 32 devices: a whole 2x2x4 slice. The times are simulated.
32 devices in a mesh: parts: 2 (over y), dp: 4 (over z), tensor: 2 (over x), query: 2 (over core).
Axes of the slice: x: 2, y: 2, z: 4, core: 2. Of those that a mesh axis runs over, the one named last changes fastest.
Arguments:
- acts: bfloat16 [4, 2048, 4096], P('query', ('parts', 'dp'), 'tensor'), parts along dimension 1, may hold values from -6 to 6
- out_grads: bfloat16 [4, 2048, 4096], P('query', ('parts', 'dp', 'tensor')), parts along dimension 1, may hold values from -6 to 6
- lengths: int32 [16], P(('parts', 'dp', 'tensor')), parts along dimension 0, may hold values from 32 to 128, as said below
- proj_in: bfloat16 [4, 4096, 64], P('query', 'tensor'), may hold values from -0.09375 to 0.09375
- proj_out: bfloat16 [4, 4096, 64], P('query', 'tensor'), may hold values from -0.09375 to 0.09375
- query_grads: bfloat16 [4, 64, 4096], P('query', ('dp', 'tensor')), may hold values from -0.005859375 to 0.005859375
Outputs:
- scores: float32 [16, 64], P(('parts', 'query'), ('dp', 'tensor')), parts along dimension 0
There are 2 independent parts, one for each index of `parts`. A program takes and returns all parts, laid end to end along the dimension named above; an argument that names none is the same for every part. Nothing has to cross between parts.
Inputs may be any that keep to these rules, and one draw needn't show every extreme that they name: `lengths`: some example has exactly 128 tokens in every draw.
All inputs are finite; a program needn't handle non-finite values.
Results may differ from a plain program's by a relative error of at most 0.0054.
Values may be sent and summed in bfloat16 or wider, within the bound.
No kernel may reach another device: no remote copies, remote signals or barrier semaphores. Data moves between devices by JAX's collectives and lax.ppermute only.
A program may use at most 64 MiB of HBM per device.

v0:
```python
import jax
import jax.numpy as jnp
from jax import lax
from jax.sharding import PartitionSpec as P


def local(acts, out_grads, lengths, proj_in, proj_out, query_grads):
    slot_rows = out_grads.shape[1]
    live_rows = (jnp.arange(slot_rows, dtype=jnp.int32) < lengths[0])[:, None]
    owners = lax.axis_size(("dp", "tensor"))
    whole_out = lax.all_gather(proj_out, "tensor", axis=1, tiled=True)
    partial_value = jnp.zeros((owners, query_grads.shape[1]), jnp.float32)
    for layer_index in range(acts.shape[0]):
        layer_acts = acts[layer_index]
        in_factor = proj_in[layer_index]
        inputs = lax.psum_scatter(
            jnp.dot(layer_acts, in_factor, preferred_element_type=jnp.float32),
            "tensor",
            scatter_dimension=0,
            tiled=True,
        ).astype(jnp.bfloat16)
        outputs = jnp.dot(
            out_grads[layer_index], whole_out[layer_index], preferred_element_type=jnp.float32
        )
        outputs = jnp.where(live_rows, outputs, jnp.zeros_like(outputs)).astype(jnp.bfloat16)
        example_grad = lax.dot_general(
            inputs, outputs, (((0,), (0,)), ((), ())), preferred_element_type=jnp.float32
        )
        example_grad = example_grad.reshape(1, -1).astype(jnp.bfloat16)
        local_queries = query_grads[layer_index]
        scored = jnp.dot(
            lax.all_gather(example_grad, ("dp", "tensor"), axis=0, tiled=True),
            local_queries.T,
            preferred_element_type=jnp.float32,
        )
        partial_value = partial_value + scored
    return lax.psum_scatter(partial_value, "query", scatter_dimension=0, tiled=True)


def solution(mesh):
    placed = (
        P("query", ("parts", "dp"), "tensor"),
        P("query", ("parts", "dp", "tensor"), None),
        P(("parts", "dp", "tensor")),
        P("query", "tensor", None),
        P("query", "tensor", None),
        P("query", ("dp", "tensor"), None),
    )
    return jax.shard_map(
        local,
        mesh=mesh,
        in_specs=placed,
        out_specs=P(("parts", "query"), ("dp", "tensor")),
        check_vma=False,
    )
```

profile of v0, /device:TPU:0, one launch (start us, length us, event | category | flops | bytes accessed | tf_op | source)
XLA Modules:
  0.0 130.0 jit_solution(1584879012506689758)
XLA Ops:
  6.5 0.0 copy-start.3
  6.5 0.0 copy-start
  6.5 0.0 reduce-scatter.5.cloned.1.call-start
  6.5 2.5 %fusion.4 = f32[256,64]{0,1:T(8,128)} fusion(bf16[2,256,2048]{2,1,0:T(8,128)(2,1)} %param.6, bf16[2,2048,64]{1,2,0:T(8,128)(2,1)} %param.9), kind=kOutput, calls=%fused_computation.8 | convolution fusion | flops 67108864 | bytes 1376256 | tf_op jit(solution)/shard_map/dot_general | solution.py:17
  9.0 0.0 reduce-scatter.5.cloned.1.call-update
  9.1 0.0 all-gather.4.cloned.1.call-start
  9.1 0.7 all-gather.4.cloned.1.call-update
  9.8 0.0 reduce-scatter.3.cloned.1.call-start
  9.9 0.0 copy-done
  9.9 2.0 %fusion.8 = f32[256,64]{0,1:T(8,128)} fusion(bf16[2,256,2048]{2,1,0:T(8,128)(2,1)S(1)} %copy-done, bf16[2,2048,64]{1,2,0:T(8,128)(2,1)} %param.9), kind=kOutput, calls=%fused_computation.11 | convolution fusion | flops 67108864 | bytes 1376256 | tf_op jit(solution)/shard_map/dot_general | solution.py:17
  11.9 0.0 copy-start.1
  11.9 0.0 reduce-scatter.3.cloned.1.call-update
  12.7 0.0 copy-done.3
  12.7 0.6 dynamic-slice
  14.0 0.0 copy-start.2
  14.0 8.2 %reduce-scatter.5.cloned.1.call-done = f32[128,64]{0,1:T(8,128)} async-done(((f32[256,64]{0,1:T(8,128)}), f32[128,64]{0,1:T(8,128)}) %reduce-scatter.5.cloned.1.call-update) | async-done | bytes 32784 | tf_op jit(solution)/shard_map/reduce_scatter | solution.py:16
  22.2 22.9 %all-gather.4.cloned.1.call-done = bf16[2,4096,64]{1,2,0:T(8,128)(2,1)} async-done(((bf16[2,2048,64]{1,2,0:T(8,128)(2,1)}), bf16[2,4096,64]{1,2,0:T(8,128)(2,1)}) %all-gather.4.cloned.1.call-update) | async-done | bytes 1048592 | tf_op jit(solution)/shard_map/all_gather | solution.py:11
  45.1 2.0 %convolution_convert_fusion = bf16[64,64]{1,0:T(8,128)(2,1)S(1)} fusion(bf16[2,128,4096]{2,1,0:T(8,128)(2,1)} %param.7, bf16[2,4096,64]{1,2,0:T(8,128)(2,1)} %all-gather.4.cloned.1.call-done, f32[128,64]{0,1:T(8,128)} %reduce-scatter.5.cloned.1.call-done, pred[128]{0:T(512)(128)(4,1)S(1)} %iota_compare_fusion), kind=kOutput, calls=%fused_computation.4 | convolution fusion | flops 68186112 | bytes 1613952 | tf_op jit(solution)/shard_map/dot_general | solution.py:26
  47.0 0.1 reshape.34
  47.1 10.1 %reduce-scatter.3.cloned.1.call-done = f32[128,64]{0,1:T(8,128)} async-done(((f32[256,64]{0,1:T(8,128)}), f32[128,64]{0,1:T(8,128)}) %reduce-scatter.3.cloned.1.call-update) | async-done | bytes 32784 | tf_op jit(solution)/shard_map/reduce_scatter | solution.py:16
  57.2 0.0 copy-done.1
  57.2 1.7 %convolution_convert_fusion.1 = bf16[64,64]{1,0:T(8,128)(2,1)S(1)} fusion(bf16[2,128,4096]{2,1,0:T(8,128)(2,1)S(1)} %copy-done.1, bf16[2,4096,64]{1,2,0:T(8,128)(2,1)} %all-gather.4.cloned.1.call-done, f32[128,64]{0,1:T(8,128)} %reduce-scatter.3.cloned.1.call-done, pred[128]{0:T(512)(128)(4,1)S(1)} %iota_compare_fusion), kind=kOutput, calls=%fused_computation.5 | convolution fusion | flops 68186112 | bytes 1614336 | tf_op jit(solution)/shard_map/dot_general | solution.py:26
  58.8 0.1 reshape.32
  58.9 30.6 %all-gather = bf16[8,1,4096]{2,1,0:T(2,128)(2,1)S(1)} all-gather(bf16[1,1,4096]{2,1,0:T(2,128)(2,1)S(1)} %reshape.32), channel_id=1, replica_groups=mesh['parts'=2,'dp'=4,'tensor'=2,'query'=2] {'dp','tensor'}, dimensions={0}, use_global_device_ids=true | all-gather | bytes 73728 | tf_op jit(solution)/shard_map/all_gather | solution.py:32
  89.5 30.5 %all-gather.1 = bf16[8,1,4096]{2,1,0:T(2,128)(2,1)S(1)} all-gather(bf16[1,1,4096]{2,1,0:T(2,128)(2,1)S(1)} %reshape.34), channel_id=1, replica_groups=mesh['parts'=2,'dp'=4,'tensor'=2,'query'=2] {'dp','tensor'}, dimensions={0}, use_global_device_ids=true | all-gather | bytes 73728 | tf_op jit(solution)/shard_map/all_gather | solution.py:32
  120.1 0.0 copy-done.2
  120.1 0.2 fusion.22
  120.2 0.2 convolution_add_fusion
  120.4 2.5 %all-reduce = f32[8,8]{1,0:T(8,128)S(1)} all-reduce(f32[8,8]{1,0:T(8,128)S(1)} %convolution_add_fusion), channel_id=4, replica_groups=mesh['parts'=2,'dp'=4,'tensor'=2,'query'=2] {'query'}, use_global_device_ids=true, to_apply=%region_2.3.clone | all-reduce | flops 64 | bytes 512
  122.9 0.6 constant_dynamic-slice_fusion
  (1 shorter events, 0.0 us)
Async XLA Ops:
  6.5 6.2 %copy-start.3 = (u32[32]{0:T(128)S(1)}, u32[32]{0:T(128)}, u32[]{:S(2)}) copy-start(u32[32]{0:T(128)} %constant.5) | copy-start | bytes 388
  6.5 3.3 %copy-start = (bf16[2,256,2048]{2,1,0:T(8,128)(2,1)S(1)}, bf16[2,256,2048]{2,1,0:T(8,128)(2,1)}, u32[]{:S(2)}) copy-start(bf16[2,256,2048]{2,1,0:T(8,128)(2,1)} %param.6) | copy-start | bytes 6291460
  6.5 15.6 %reduce-scatter.5.cloned.1.call-start = ((), (), s32[]{:S(2)}) async-start(), calls=%async_computation.4 | async-start | bytes 98304 | tf_op jit(solution)/shard_map/reduce_scatter | solution.py:16
  9.1 36.0 %all-gather.4.cloned.1.call-start = ((), (), s32[]{:S(2)}) async-start(), calls=%async_computation.3 | async-start | bytes 1572864 | tf_op jit(solution)/shard_map/all_gather | solution.py:11
  9.8 47.4 %reduce-scatter.3.cloned.1.call-start = ((), (), s32[]{:S(2)}) async-start(), calls=%async_computation.2 | async-start | bytes 98304 | tf_op jit(solution)/shard_map/reduce_scatter | solution.py:16
  11.9 45.3 %copy-start.1 = (bf16[2,128,4096]{2,1,0:T(8,128)(2,1)S(1)}, bf16[2,128,4096]{2,1,0:T(8,128)(2,1)}, u32[]{:S(2)}) copy-start(bf16[2,128,4096]{2,1,0:T(8,128)(2,1)} %param.7) | copy-start | bytes 6291460
  14.0 106.1 %copy-start.2 = (bf16[2,8,4096]{2,1,0:T(8,128)(2,1)S(1)}, bf16[2,8,4096]{2,1,0:T(8,128)(2,1)}, u32[]{:S(2)}) copy-start(bf16[2,8,4096]{2,1,0:T(8,128)(2,1)} %param.11) | copy-start | bytes 393220
Sparse Core Ops, SparseCore 0:
  9.6 12.5 reduce-scatter.4
  23.7 21.3 all-gather.3
  47.2 9.8 reduce-scatter.2
where the time goes:
time: 130 us
  blocking collectives  63.6 us (49%)
  waiting for transfers between devices  41.9 us (32%)
  between operations  14.6 us (11%)
  matrix products  8.5 us (7%)
  local copies, waits for them, and re-layouts  1.37 us (1%)
    all_gather x2, blocking collectives, local(): lax.all_gather(example_grad, ('dp', 'tensor'), axis=0, tiled=True)  61.1 us
    all_gather x1, waiting for transfers between devices, local(): whole_out = lax.all_gather(proj_out, 'tensor', axis=1, tiled=True)  22.9 us
    reduce_scatter x2, waiting for transfers between devices, local(): lax.psum_scatter(jnp.dot(layer_acts, in_factor, preferred_element_type=jn...  18.2 us
    dot_general x2, matrix products, local(): jnp.dot(layer_acts, in_factor, preferred_element_type=jnp.float32)  4.51 us
    dot_general x2, matrix products, local(): lax.dot_general(inputs, outputs, (((0,), (0,)), ((), ())), preferred_elem...  3.62 us
  transfers between devices with their start and end apart: 3, of which 3 were waited for; matrix products, arithmetic and copies ran while one was open for 4% of the time, Pallas kernels for 0%

commit v1 on v0

v1 whole, which is shorter than its diff:
```python
import functools

import jax
import jax.numpy as jnp
from jax import lax
from jax.experimental import pallas as pl
from jax.experimental.pallas import tpu as pltpu
from jax.sharding import PartitionSpec as P

F32 = jnp.float32
BF16 = jnp.bfloat16
VMEM = pl.BlockSpec(memory_space=pltpu.VMEM)
SMEM = pl.BlockSpec(memory_space=pltpu.SMEM)
NT = (((1,), (1,)), ((), ()))
TN = (((0,), (0,)), ((), ()))


def dot(a, b, dims):
    return lax.dot_general(a, b, dims, preferred_element_type=F32)


def call(kernel, out_shape, *args):
    specs = [SMEM if a.dtype == jnp.int32 else VMEM for a in args]
    return pl.pallas_call(
        kernel,
        out_shape=out_shape,
        in_specs=specs,
        out_specs=jax.tree.map(lambda _: VMEM, out_shape),
        compiler_params=pltpu.CompilerParams(vmem_limit_bytes=48 * 2**20),
    )(*args)


def project_inputs(acts, factor, out):
    out[...] = jnp.concatenate(
        [dot(acts[l], factor[l], NT) for l in range(acts.shape[0])], axis=1
    )


def project_outputs(block, grads, factor, out):
    depth = factor.shape[2]
    columns = pl.ds(pl.multiple_of(block[0] * depth, 128), depth)
    out[...] = jnp.concatenate(
        [dot(grads[l, :, columns], factor[l], NT) for l in range(grads.shape[0])], axis=1
    )


def example_gradient(n, blocks, length, grads, outputs, *rest):
    factors, inputs, out = rest[: n - 1], rest[n - 1 : -1], rest[-1]
    layers, depth = factors[0].shape[0], factors[0].shape[2]
    total = outputs[...]
    for i, factor in enumerate(factors):
        columns = pl.ds(pl.multiple_of(blocks[i] * depth, 128), depth)
        total = total + jnp.concatenate(
            [dot(grads[l, :, columns], factor[l], NT) for l in range(layers)], axis=1
        )
    live = lax.broadcasted_iota(jnp.int32, total.shape, 0) < length[0]
    total = jnp.where(live, total, 0.0).astype(BF16)
    ins = inputs[0][...]
    for other in inputs[1:]:
        ins = ins + other[...]
    both = dot(ins.astype(BF16), total, TN)
    width = both.shape[1] // layers
    out[...] = jnp.concatenate(
        [both[l * width : (l + 1) * width, l * width : (l + 1) * width] for l in range(layers)],
        axis=1,
    ).astype(BF16)


def score(place, grads, queries, mine, theirs):
    n, nq = grads.shape[0], queries.shape[0]
    asked = queries[...].astype(F32)
    rows = []
    for s in range(n):
        product = asked * grads[s].astype(F32)[None]
        rows.append(jnp.sum(product, axis=1))
    table = jnp.sum(jnp.stack(rows), axis=2)
    bit = 1
    while bit < n:
        swapped = table.reshape(n // (2 * bit), 2, bit, nq)
        swapped = jnp.stack([swapped[:, 1], swapped[:, 0]], axis=1).reshape(n, nq)
        table = jnp.where((place[0] & bit) != 0, swapped, table)
        bit *= 2
    low, high = table[: n // 2], table[n // 2 :]
    first = place[1] == 0
    mine[...] = jnp.where(first, low, high)
    theirs[...] = jnp.where(first, high, low)


def shifted(x, axis, shift):
    n = lax.axis_size(axis)
    return lax.ppermute(x, axis, [(i, (i + shift) % n) for i in range(n)])


def flipped(x, axis, bit):
    n = lax.axis_size(axis)
    return lax.ppermute(x, axis, [(i, i ^ bit) for i in range(n)])


def local(acts, out_grads, lengths, proj_in, proj_out, query_grads):
    layers, rows, depth = acts.shape
    slots = out_grads.shape[1]
    width = proj_in.shape[2]
    nq = query_grads.shape[1]
    n = lax.axis_size("tensor")
    t = lax.axis_index("tensor")
    lanes = layers * width

    factor_out = proj_out.transpose(0, 2, 1)
    factors = [shifted(factor_out, "tensor", s) for s in range(1, n)]
    blocks = jnp.stack([(t - s + n) % n for s in range(1, n)]).astype(jnp.int32)

    partial = call(
        project_inputs,
        jax.ShapeDtypeStruct((rows, lanes), F32),
        acts,
        proj_in.transpose(0, 2, 1),
    ).reshape(n, slots, lanes)
    ins = [lax.dynamic_index_in_dim(partial, t, 0, keepdims=False)]
    for s in range(1, n):
        block = lax.dynamic_index_in_dim(partial, (t + s) % n, 0, keepdims=False)
        ins.append(shifted(block, "tensor", s))
    outs = call(
        project_outputs,
        jax.ShapeDtypeStruct((slots, lanes), F32),
        t.astype(jnp.int32).reshape(1),
        out_grads,
        factor_out,
    )
    grad = call(
        functools.partial(example_gradient, n),
        jax.ShapeDtypeStruct((width, lanes), BF16),
        blocks,
        lengths,
        out_grads,
        outs,
        *factors,
        *ins,
    )
    queries = query_grads.reshape(layers, nq, width, width).transpose(1, 2, 0, 3)
    queries = queries.reshape(nq, width, lanes)

    grads = grad[None]
    n_dp = lax.axis_size("dp")
    steps = [("tensor", 1 << b) for b in range(n.bit_length() - 1)]
    steps += [("dp", 1 << b) for b in range(n_dp.bit_length() - 1)]
    for axis, bit in steps:
        grads = jnp.concatenate([grads, flipped(grads, axis, bit)])
    place = jnp.stack([lax.axis_index("dp") * n + t, lax.axis_index("query")]).astype(jnp.int32)
    half = jax.ShapeDtypeStruct((grads.shape[0] // 2, nq), F32)
    mine, theirs = call(score, (half, half), place, grads, queries)
    return mine + flipped(theirs, "query", 1)


def solution(mesh):
    placed = (
        P("query", ("parts", "dp"), "tensor"),
        P("query", ("parts", "dp", "tensor"), None),
        P(("parts", "dp", "tensor")),
        P("query", "tensor", None),
        P("query", "tensor", None),
        P("query", ("dp", "tensor"), None),
    )
    return jax.shard_map(
        local,
        mesh=mesh,
        in_specs=placed,
        out_specs=P(("parts", "query"), ("dp", "tensor")),
        check_vma=False,
    )
```

time: 130 us -> 33.2 us (0.26)
  blocking collectives: 63.6 us -> 0 us
  waiting for transfers between devices: 41.9 us -> 15.4 us
  between operations: 14.6 us -> 0.76 us
  starting transfers between devices: 0.08 us -> 10 us
  matrix products: 8.5 us -> 0 us
  Pallas kernels: 0 us -> 2.79 us
  local copies, waits for them, and re-layouts: 1.37 us -> 3.32 us
    all_gather x2 -> x0, blocking collectives: 61.1 us -> none  [local(): lax.all_gather(example_grad, ('dp', 'tensor'), axis=0, tiled=True)]
    all_gather x1 -> x0, waiting for transfers between devices: 22.9 us -> none  [local(): whole_out = lax.all_gather(proj_out, 'tensor', axis=1, tiled=True)]
    reduce_scatter x2 -> x0, waiting for transfers between devices: 18.2 us -> none  [local(): lax.psum_scatter(jnp.dot(layer_acts, in_factor, preferred_element_type=jn...]
    ppermute x0 -> x6, waiting for transfers between devices: none -> 15.4 us  [the longest x2 8.72 us: shifted(): return lax.ppermute(x, axis, [(i, (i + shift) % n) for i in range(n)])]
    ppermute x0 -> x6, starting transfers between devices: none -> 10 us  [the longest x4 6.89 us: flipped(): return lax.ppermute(x, axis, [(i, i ^ bit) for i in range(n)])]
    dot_general x6 -> x0, matrix products: 8.5 us -> none  [the longest x2 4.51 us: local(): jnp.dot(layer_acts, in_factor, preferred_element_type=jnp.float32)]
    pallas_call x0 -> x4, Pallas kernels: none -> 2.79 us  [call(): pl.pallas_call(kernel, out_shape=out_shape, in_specs=specs, out_specs=jax...]
    unnamed x1 -> x0, blocking collectives: 2.46 us -> none
  transfers between devices with their start and end apart: 3 -> 6, of which waited for: 3 -> 5; matrix products, arithmetic and copies ran while one was open for 4% -> 2% of each run, Pallas kernels for 0% -> 4%
where the time goes in v1:
time: 33.2 us; the launch traced here: 33 us
  waiting for transfers between devices  15.4 us (46%)
  starting transfers between devices  10 us (30%)
  local copies, waits for them, and re-layouts  3.32 us (10%)
  Pallas kernels  2.79 us (8%)
  between operations  0.76 us (2%)
  other arithmetic  0.69 us (2%)
    ppermute x2, waiting for transfers between devices, shifted(): return lax.ppermute(x, axis, [(i, (i + shift) % n) for i in range(n)])  8.72 us
    ppermute x4, starting transfers between devices, flipped(): return lax.ppermute(x, axis, [(i, i ^ bit) for i in range(n)])  6.89 us
    ppermute x4, waiting for transfers between devices, flipped(): return lax.ppermute(x, axis, [(i, i ^ bit) for i in range(n)])  6.71 us
    ppermute x2, starting transfers between devices, shifted(): return lax.ppermute(x, axis, [(i, (i + shift) % n) for i in range(n)])  3.16 us
    pallas_call x4, Pallas kernels, call(): pl.pallas_call(kernel, out_shape=out_shape, in_specs=specs, out_specs=jax...  2.79 us
    unnamed x10, local copies, waits for them, and re-layouts  2.65 us
  transfers between devices with their start and end apart: 6, of which 5 were waited for; matrix products, arithmetic and copies ran while one was open for 2% of the time, Pallas kernels for 4%

profile of v1, /device:TPU:0, one launch (start us, length us, event | category | flops | bytes accessed | tf_op | source)
XLA Modules:
  0.0 33.0 jit_solution(10246826422769682320)
XLA Ops:
  0.0 0.0 copy-start
  0.0 2.9 %collective-permute-start = (bf16[2,64,2048]{2,1,0:T(8,128)(2,1)}, bf16[2,64,2048]{2,1,0:T(8,128)(2,1)S(1)}, u32[]{:S(2)}, u32[]{:S(2)}) collective-permute-start(bf16[2,64,2048]{2,1,0:T(8,128)(2,1)} %bitcast.16), channel_id=1, source_target_pairs={{0,2},{2,0},{1,3},{3,1},{4,6},{6,4},{5,7},{7,5},{8,10},{10,8},{9,1... | collective-permute-start | bytes 1572872 | tf_op jit(solution)/shard_map/ppermute | solution.py:91
  2.9 0.0 copy-start.1
  2.9 1.6 %copy-done.1 = bf16[2,256,2048]{2,1,0:T(8,128)(2,1)S(1)} copy-done((bf16[2,256,2048]{2,1,0:T(8,128)(2,1)S(1)}, bf16[2,256,2048]{2,1,0:T(8,128)(2,1)}, u32[]{:S(2)}) %copy-start.1) | copy-done | bytes 2097176
  4.5 0.0 copy-start.2
  4.5 1.0 %copy-done.2 = bf16[2,2048,64]{1,2,0:T(8,128)(2,1)S(1)} copy-done((bf16[2,2048,64]{1,2,0:T(8,128)(2,1)S(1)}, bf16[2,2048,64]{1,2,0:T(8,128)(2,1)}, u32[]{:S(2)}) %copy-start.2) | copy-done | bytes 524312
  5.6 0.0 copy-start.3
  5.6 0.8 %shard_map.65 = f32[256,128]{1,0:T(8,128)S(1)} custom-call(bf16[2,256,2048]{2,1,0:T(8,128)(2,1)S(1)} %copy-done.1, bf16[2,64,2048]{2,1,0:T(8,128)(2,1)S(1)} %bitcast.15), custom_call_target="tpu_custom_call" | custom-call | tf_op jit(solution)/shard_map/pallas_call | solution.py:24
  6.4 0.2 collective-permute-start.1
  7.2 0.0 copy-done
  7.2 0.0 copy-done.3
  7.3 0.5 %shard_map.64.outputs = f32[128,128]{1,0:T(8,128)S(1)} custom-call(s32[1]{0:T(128)} %bitcast.3.block, bf16[2,128,4096]{2,1,0:T(8,128)(2,1)S(1)} %copy-done, bf16[2,64,2048]{2,1,0:T(8,128)(2,1)S(1)} %bitcast.17), custom_call_target="tpu_custom_call" | custom-call | tf_op jit(solution)/shard_map/pallas_call | solution.py:24
  7.7 0.0 copy-start.4
  7.8 8.7 %collective-permute-done.1.rest_2_ = f32[128,128]{1,0:T(8,128)S(1)} collective-permute-done((f32[128,128]{1,0:T(8,128)S(1)}, f32[128,128]{1,0:T(8,128)S(1)}, u32[]{:S(2)}, u32[]{:S(2)}) %collective-permute-start.1) | collective-permute-done | bytes 65568 | tf_op jit(solution)/shard_map/ppermute | solution.py:91
  16.5 0.0 collective-permute-done.rest_0_
  16.5 0.6 %shard_map.66 = bf16[64,128]{1,0:T(8,128)(2,1)S(1)} custom-call(s32[1]{0:T(128)} %bitcast.2.blocks, s32[1]{0:T(128)S(6)} %copy.10.length, bf16[2,128,4096]{2,1,0:T(8,128)(2,1)S(1)} %copy-done, f32[128,128]{1,0:T(8,128)S(1)} %shard_map.64.outputs, bf16[2,64,2048]{2,1,0:T(8,128)(2,1)S(1)} %collective-permute-done.rest_0_, ...), custom_call_target="tpu_custom_call" | custom-call | tf_op jit(solution)/shard_map/pallas_call | solution.py:24
  17.1 1.8 %collective-permute-start.2 = (bf16[1,64,128]{2,1,0:T(8,128)(2,1)S(1)}, bf16[1,64,128]{2,1,0:T(8,128)(2,1)S(1)}, u32[]{:S(2)}, u32[]{:S(2)}) collective-permute-start(bf16[1,64,128]{2,1,0:T(8,128)(2,1)S(1)} %bitcast.19), channel_id=1, source_target_pairs={{0,2},{2,0},{1,3},{3,1},{4,6},{6,4},{5,7},{7,5},{8,10},{10,8},{9,1... | collective-permute-start | bytes 49160 | tf_op jit(solution)/shard_map/ppermute | solution.py:96
  18.9 2.0 %collective-permute-done.2 = bf16[1,64,128]{2,1,0:T(8,128)(2,1)S(1)} collective-permute-done((bf16[1,64,128]{2,1,0:T(8,128)(2,1)S(1)}, bf16[1,64,128]{2,1,0:T(8,128)(2,1)S(1)}, u32[]{:S(2)}, u32[]{:S(2)}) %collective-permute-start.2) | collective-permute-done | bytes 16416 | tf_op jit(solution)/shard_map/ppermute | solution.py:96
  20.9 1.8 %collective-permute-start.3 = (bf16[2,64,128]{2,1,0:T(8,128)(2,1)S(1)}, bf16[2,64,128]{2,1,0:T(8,128)(2,1)S(1)}, u32[]{:S(2)}, u32[]{:S(2)}) collective-permute-start(bf16[2,64,128]{2,1,0:T(8,128)(2,1)S(1)} %pad_maximum_fusion.2), channel_id=1, source_target_pairs={{0,4},{4,0},{8,12},{12,8},{1,5},{5,1},{9,13},{13,9},{2,6},{6,2},{1... | collective-permute-start | bytes 98312 | tf_op jit(solution)/shard_map/ppermute | solution.py:96
  22.7 0.0 copy-done.4
  22.7 0.2 reshape.14
  23.0 0.3 copy.9
  23.3 0.1 reshape.15.queries
  23.4 1.4 %collective-permute-done.3 = bf16[2,64,128]{2,1,0:T(8,128)(2,1)S(1)} collective-permute-done((bf16[2,64,128]{2,1,0:T(8,128)(2,1)S(1)}, bf16[2,64,128]{2,1,0:T(8,128)(2,1)S(1)}, u32[]{:S(2)}, u32[]{:S(2)}) %collective-permute-start.3) | collective-permute-done | bytes 32800 | tf_op jit(solution)/shard_map/ppermute | solution.py:96
  24.8 3.2 %collective-permute-start.4 = (bf16[4,64,128]{2,1,0:T(8,128)(2,1)S(1)}, bf16[4,64,128]{2,1,0:T(8,128)(2,1)S(1)}, u32[]{:S(2)}, u32[]{:S(2)}) collective-permute-start(bf16[4,64,128]{2,1,0:T(8,128)(2,1)S(1)} %pad_maximum_fusion.1), channel_id=1, source_target_pairs={{0,8},{4,12},{8,0},{12,4},{1,9},{5,13},{9,1},{13,5},{2,10},{6,14},... | collective-permute-start | bytes 196616 | tf_op jit(solution)/shard_map/ppermute | solution.py:96
  28.0 0.1 pad_add_fusion.place
  28.1 2.2 %collective-permute-done.4 = bf16[4,64,128]{2,1,0:T(8,128)(2,1)S(1)} collective-permute-done((bf16[4,64,128]{2,1,0:T(8,128)(2,1)S(1)}, bf16[4,64,128]{2,1,0:T(8,128)(2,1)S(1)}, u32[]{:S(2)}, u32[]{:S(2)}) %collective-permute-start.4) | collective-permute-done | bytes 65568 | tf_op jit(solution)/shard_map/ppermute | solution.py:96
  30.3 0.9 %shard_map.67 = (f32[4,8]{1,0:T(4,128)S(1)}, f32[4,8]{1,0:T(4,128)S(1)}) custom-call(s32[2]{0:T(128)S(1)} %pad_add_fusion.place, bf16[8,64,128]{2,1,0:T(8,128)(2,1)S(1)} %pad_maximum_fusion.grads, bf16[8,64,128]{2,1,0:T(8,128)(2,1)S(1)} %reshape.15.queries), custom_call_target="tpu_custom_call" | custom-call | tf_op jit(solution)/shard_map/pallas_call | solution.py:24
  31.2 0.1 collective-permute-start.5
  31.3 1.1 %collective-permute-done.5 = f32[4,8]{1,0:T(4,128)S(1)} collective-permute-done((f32[4,8]{1,0:T(4,128)S(1)}, f32[4,8]{1,0:T(4,128)S(1)}, u32[]{:S(2)}, u32[]{:S(2)}) %collective-permute-start.5) | collective-permute-done | bytes 160 | tf_op jit(solution)/shard_map/ppermute | solution.py:96
  32.5 0.6 %add.30 = f32[4,8]{1,0:T(4,128)} add(f32[4,8]{1,0:T(4,128)S(1)} %get-tuple-element.7, f32[4,8]{1,0:T(4,128)S(1)} %collective-permute-done.5) | non-fusion elementwise | flops 32 | bytes 384 | tf_op jit(solution)/shard_map/add | solution.py:151
  (4 shorter events, 0.0 us)
Async XLA Ops:
  0.0 7.2 %copy-start = (bf16[2,128,4096]{2,1,0:T(8,128)(2,1)S(1)}, bf16[2,128,4096]{2,1,0:T(8,128)(2,1)}, u32[]{:S(2)}) copy-start(bf16[2,128,4096]{2,1,0:T(8,128)(2,1)} %grads.3) | copy-start | bytes 6291460
  0.0 16.5 %collective-permute-start = (bf16[2,64,2048]{2,1,0:T(8,128)(2,1)}, bf16[2,64,2048]{2,1,0:T(8,128)(2,1)S(1)}, u32[]{:S(2)}, u32[]{:S(2)}) collective-permute-start(bf16[2,64,2048]{2,1,0:T(8,128)(2,1)} %bitcast.16), channel_id=1, source_target_pairs={{0,2},{2,0},{1,3},{3,1},{4,6},{6,4},{5,7},{7,5},{8,10},{10,8},{9,1... | collective-permute-start | bytes 1572872 | tf_op jit(solution)/shard_map/ppermute | solution.py:91
  2.9 1.6 %copy-start.1 = (bf16[2,256,2048]{2,1,0:T(8,128)(2,1)S(1)}, bf16[2,256,2048]{2,1,0:T(8,128)(2,1)}, u32[]{:S(2)}) copy-start(bf16[2,256,2048]{2,1,0:T(8,128)(2,1)} %acts.1) | copy-start | bytes 6291460
  4.5 1.0 %copy-start.2 = (bf16[2,2048,64]{1,2,0:T(8,128)(2,1)S(1)}, bf16[2,2048,64]{1,2,0:T(8,128)(2,1)}, u32[]{:S(2)}) copy-start(bf16[2,2048,64]{1,2,0:T(8,128)(2,1)} %param.9) | copy-start | bytes 1572868
  5.6 1.7 %copy-start.3 = (bf16[2,2048,64]{1,2,0:T(8,128)(2,1)S(1)}, bf16[2,2048,64]{1,2,0:T(8,128)(2,1)}, u32[]{:S(2)}) copy-start(bf16[2,2048,64]{1,2,0:T(8,128)(2,1)} %param.10) | copy-start | bytes 1572868
  6.4 10.1 %collective-permute-start.1 = (f32[128,128]{1,0:T(8,128)S(1)}, f32[128,128]{1,0:T(8,128)S(1)}, u32[]{:S(2)}, u32[]{:S(2)}) collective-permute-start(f32[128,128]{1,0:T(8,128)S(1)} %get-tuple-element.9), channel_id=1, source_target_pairs={{0,2},{2,0},{1,3},{3,1},{4,6},{6,4},{5,7},{7,5},{8,10},{10,8},{9,1... | collective-permute-start | bytes 196616 | tf_op jit(solution)/shard_map/ppermute | solution.py:91
  7.7 15.0 %copy-start.4 = (bf16[2,8,4096]{2,1,0:T(8,128)(2,1)S(1)}, bf16[2,8,4096]{2,1,0:T(8,128)(2,1)}, u32[]{:S(2)}) copy-start(bf16[2,8,4096]{2,1,0:T(8,128)(2,1)} %param.11) | copy-start | bytes 393220
  17.1 3.8 %collective-permute-start.2 = (bf16[1,64,128]{2,1,0:T(8,128)(2,1)S(1)}, bf16[1,64,128]{2,1,0:T(8,128)(2,1)S(1)}, u32[]{:S(2)}, u32[]{:S(2)}) collective-permute-start(bf16[1,64,128]{2,1,0:T(8,128)(2,1)S(1)} %bitcast.19), channel_id=1, source_target_pairs={{0,2},{2,0},{1,3},{3,1},{4,6},{6,4},{5,7},{7,5},{8,10},{10,8},{9,1... | collective-permute-start | bytes 49160 | tf_op jit(solution)/shard_map/ppermute | solution.py:96
  20.9 3.9 %collective-permute-start.3 = (bf16[2,64,128]{2,1,0:T(8,128)(2,1)S(1)}, bf16[2,64,128]{2,1,0:T(8,128)(2,1)S(1)}, u32[]{:S(2)}, u32[]{:S(2)}) collective-permute-start(bf16[2,64,128]{2,1,0:T(8,128)(2,1)S(1)} %pad_maximum_fusion.2), channel_id=1, source_target_pairs={{0,4},{4,0},{8,12},{12,8},{1,5},{5,1},{9,13},{13,9},{2,6},{6,2},{1... | collective-permute-start | bytes 98312 | tf_op jit(solution)/shard_map/ppermute | solution.py:96
  24.8 5.4 %collective-permute-start.4 = (bf16[4,64,128]{2,1,0:T(8,128)(2,1)S(1)}, bf16[4,64,128]{2,1,0:T(8,128)(2,1)S(1)}, u32[]{:S(2)}, u32[]{:S(2)}) collective-permute-start(bf16[4,64,128]{2,1,0:T(8,128)(2,1)S(1)} %pad_maximum_fusion.1), channel_id=1, source_target_pairs={{0,8},{4,12},{8,0},{12,4},{1,9},{5,13},{9,1},{13,5},{2,10},{6,14},... | collective-permute-start | bytes 196616 | tf_op jit(solution)/shard_map/ppermute | solution.py:96
  31.2 1.2 %collective-permute-start.5 = (f32[4,8]{1,0:T(4,128)S(1)}, f32[4,8]{1,0:T(4,128)S(1)}, u32[]{:S(2)}, u32[]{:S(2)}) collective-permute-start(f32[4,8]{1,0:T(4,128)S(1)} %get-tuple-element.8), channel_id=1, source_target_pairs={{0,1},{1,0},{2,3},{3,2},{4,5},{5,4},{6,7},{7,6},{8,9},{9,8},{10,11... | collective-permute-start | bytes 392 | tf_op jit(solution)/shard_map/ppermute | solution.py:96

commit v2 on v1

v2 whole, which is shorter than its diff:
```python
import functools

import jax
import jax.numpy as jnp
from jax import lax
from jax.experimental import pallas as pl
from jax.experimental.pallas import tpu as pltpu
from jax.sharding import PartitionSpec as P

F32 = jnp.float32
BF16 = jnp.bfloat16
VMEM = pl.BlockSpec(memory_space=pltpu.VMEM)
SMEM = pl.BlockSpec(memory_space=pltpu.SMEM)
NT = (((1,), (1,)), ((), ()))
TN = (((0,), (0,)), ((), ()))
FOLD = 16


def dot(a, b, dims):
    return lax.dot_general(a, b, dims, preferred_element_type=F32)


def call(kernel, out_shape, *args, after=()):
    specs = [SMEM if a.dtype == jnp.int32 else VMEM for a in args]
    specs += [pl.BlockSpec(memory_space=pl.ANY) for _ in after]

    def body(*refs):
        kernel(*refs[: len(args)], *refs[len(args) + len(after) :])

    return pl.pallas_call(
        body,
        out_shape=out_shape,
        in_specs=specs,
        out_specs=jax.tree.map(lambda _: VMEM, out_shape),
        compiler_params=pltpu.CompilerParams(vmem_limit_bytes=48 * 2**20),
    )(*args, *after)


def project_inputs(acts, factor, out):
    out[...] = jnp.concatenate(
        [dot(acts[l], factor[l], NT) for l in range(acts.shape[0])], axis=1
    )


def project_outputs(block, grads, factor, out):
    depth = factor.shape[2]
    columns = pl.ds(pl.multiple_of(block[0] * depth, 128), depth)
    out[...] = jnp.concatenate(
        [dot(grads[l, :, columns], factor[l], NT) for l in range(grads.shape[0])], axis=1
    )


def example_gradient(n, blocks, length, grads, outputs, *rest):
    factors, inputs, out = rest[: n - 1], rest[n - 1 : -1], rest[-1]
    layers, depth = factors[0].shape[0], factors[0].shape[2]
    total = outputs[...]
    for i, factor in enumerate(factors):
        columns = pl.ds(pl.multiple_of(blocks[i] * depth, 128), depth)
        total = total + jnp.concatenate(
            [dot(grads[l, :, columns], factor[l], NT) for l in range(layers)], axis=1
        )
    live = lax.broadcasted_iota(jnp.int32, total.shape, 0) < length[0]
    total = jnp.where(live, total, 0.0).astype(BF16)
    ins = inputs[0][...]
    for other in inputs[1:]:
        ins = ins + other[...].astype(F32)
    both = dot(ins.astype(BF16), total, TN)
    width = both.shape[1] // layers
    layer = lax.broadcasted_iota(jnp.int32, (width, both.shape[1]), 1) // width
    grad = both[:width]
    for l in range(1, layers):
        grad = jnp.where(layer == l, both[l * width : (l + 1) * width], grad)
    grad = grad.astype(BF16)
    out[...] = jnp.concatenate(
        [grad[g * FOLD : (g + 1) * FOLD] for g in range(width // FOLD)], axis=1
    )


def score(order, places, grads, own, other, near, near_other, mine, theirs):
    nq = mine.shape[1]

    def against(queries, chosen, place, out):
        lhs = jnp.concatenate([grads[s] for s in chosen], axis=0)
        products = dot(lhs, queries[...], NT)
        row = lax.broadcasted_iota(jnp.int32, products.shape, 0) % FOLD
        column = lax.broadcasted_iota(jnp.int32, products.shape, 1) % FOLD
        products = jnp.where(row == column, products, 0.0)
        sums = jnp.sum(products.reshape(len(chosen), FOLD, nq * FOLD), axis=1)
        fold = lax.broadcasted_iota(jnp.int32, (nq * FOLD, nq), 0) // FOLD
        fold = fold == lax.broadcasted_iota(jnp.int32, (nq * FOLD, nq), 1)
        table = lax.dot_general(
            sums,
            fold.astype(F32),
            (((1,), (0,)), ((), ())),
            precision=lax.Precision.HIGHEST,
            preferred_element_type=F32,
        )
        for i, s in enumerate(chosen):
            out[pl.ds(place ^ order[s], 1), :] = table[i : i + 1]

    even = [s for s in range(len(order)) if s.bit_count() % 2 == 0]
    odd = [s for s in range(len(order)) if s.bit_count() % 2 == 1]
    against(own, even, places[0], mine)
    against(other, odd, places[0], mine)
    against(near, even, places[1], theirs)
    against(near_other, odd, places[1], theirs)


def shifted(x, axis, shift):
    n = lax.axis_size(axis)
    return lax.ppermute(x, axis, [(i, (i + shift) % n) for i in range(n)])


def flipped(x, axis, bit):
    n = lax.axis_size(axis)
    return lax.ppermute(x, axis, [(i, i ^ bit) for i in range(n)])


def crossed(x, axis, bit):
    n = lax.axis_size(axis) * lax.axis_size("query")
    bits = bit * lax.axis_size("query") + 1
    return lax.ppermute(x, (axis, "query"), [(i, i ^ bits) for i in range(n)])


def local(acts, out_grads, lengths, proj_in, proj_out, query_grads):
    layers, rows, depth = acts.shape
    slots = out_grads.shape[1]
    width = proj_in.shape[2]
    nq = query_grads.shape[1]
    n = lax.axis_size("tensor")
    n_dp = lax.axis_size("dp")
    t = lax.axis_index("tensor")
    z = lax.axis_index("dp")
    lanes = layers * width

    factor_out = proj_out.transpose(0, 2, 1)
    factors = [shifted(factor_out, "tensor", s) for s in range(1, n)]
    blocks = jnp.stack([(t - s + n) % n for s in range(1, n)]).astype(jnp.int32)

    queries = query_grads.reshape(layers, nq, width // FOLD, FOLD, width)
    queries = queries.transpose(1, 3, 2, 0, 4).reshape(nq * FOLD, -1)
    near = flipped(queries, "dp", 1)
    queries_other = flipped(queries, "query", 1)
    near_other = flipped(near, "query", 1)

    partial = call(
        project_inputs,
        jax.ShapeDtypeStruct((rows, lanes), F32),
        acts,
        proj_in.transpose(0, 2, 1),
        after=(queries,),
    ).reshape(n, slots, lanes)
    ins = [lax.dynamic_index_in_dim(partial, t, 0, keepdims=False)]
    for s in range(1, n):
        block = lax.dynamic_index_in_dim(partial, (t + s) % n, 0, keepdims=False)
        ins.append(shifted(block.astype(BF16), "tensor", s))
    outs = call(
        project_outputs,
        jax.ShapeDtypeStruct((slots, lanes), F32),
        t.astype(jnp.int32).reshape(1),
        out_grads,
        factor_out,
    )

    grad = call(
        functools.partial(example_gradient, n),
        jax.ShapeDtypeStruct((FOLD, width // FOLD * lanes), BF16),
        blocks,
        lengths,
        out_grads,
        outs,
        *factors,
        *ins,
        after=(queries_other, near, near_other),
    )
    z_bits, t_bits = n_dp.bit_length() - 1, n.bit_length() - 1
    steps = [("dp", 1 << b) for b in reversed(range(1, z_bits))]
    steps += [("tensor", 1 << b) for b in range(t_bits)]
    grads = grad[None]
    order = [0]
    for axis, bit in steps:
        grads = jnp.concatenate([grads, crossed(grads, axis, bit)])
        order += [o ^ (bit if axis == "tensor" else bit * n // 2) for o in order]
    top = len(order) // 2
    core = lax.axis_index("query")
    place = z // 2 * n + t
    places = jnp.stack([place ^ (core * top), place ^ ((1 - core) * top)]).astype(jnp.int32)
    table = jax.ShapeDtypeStruct((len(order), nq), F32)
    mine, theirs = call(
        functools.partial(score, order),
        (table, table),
        places,
        grads,
        queries,
        queries_other,
        near,
        near_other,
    )
    got = crossed(theirs, "dp", 1)
    kept, sent = jnp.stack([mine[:top], got[:top]]), jnp.stack([mine[top:], got[top:]])
    kept = kept + flipped(sent, "query", 1)
    kept = jnp.where(z % 2 == 0, kept, kept[::-1]).reshape(2, -1, n, nq)
    return kept.transpose(1, 0, 2, 3).reshape(-1, nq)


def solution(mesh):
    placed = (
        P("query", ("parts", "dp"), "tensor"),
        P("query", ("parts", "dp", "tensor"), None),
        P(("parts", "dp", "tensor")),
        P("query", "tensor", None),
        P("query", "tensor", None),
        P("query", ("dp", "tensor"), None),
    )
    return jax.shard_map(
        local,
        mesh=mesh,
        in_specs=placed,
        out_specs=P(("parts", "query"), ("dp", "tensor")),
        check_vma=False,
    )
```

time: 33.2 us -> 31.4 us (0.946)
  waiting for transfers between devices: 15.4 us -> 10.4 us
  Pallas kernels: 2.79 us -> 4.21 us
  local copies, waits for them, and re-layouts: 3.32 us -> 4.32 us
  starting transfers between devices: 10 us -> 10.7 us
    ppermute x4, waiting for transfers between devices: 6.71 us -> 0.85 us  [flipped(): return lax.ppermute(x, axis, [(i, i ^ bit) for i in range(n)])]
    ppermute x0 -> x3, waiting for transfers between devices: none -> 5.77 us  [crossed(): return lax.ppermute(x, (axis, 'query'), [(i, i ^ bits) for i in range(n)])]
    ppermute x2, waiting for transfers between devices: 8.72 us -> 3.82 us  [shifted(): return lax.ppermute(x, axis, [(i, (i + shift) % n) for i in range(n)])]
    ppermute x0 -> x3, starting transfers between devices: none -> 4.64 us  [crossed(): return lax.ppermute(x, (axis, 'query'), [(i, i ^ bits) for i in range(n)])]
    ppermute x4, starting transfers between devices: 6.89 us -> 2.59 us  [flipped(): return lax.ppermute(x, axis, [(i, i ^ bit) for i in range(n)])]
    pallas_call x4, Pallas kernels: 2.79 us -> 4.21 us  [call(): pl.pallas_call(body, out_shape=out_shape, in_specs=specs, out_specs=jax.t...]
    reshape x3, local copies, waits for them, and re-layouts: 0.66 us -> 1.66 us  [the longest x2 1.45 us: local(): queries = query_grads.reshape(layers, nq, width // FOLD, FOLD, width)]
    select_n x0 -> x1, other arithmetic: none -> 0.58 us  [local(): kept = jnp.where(z % 2 == 0, kept, kept[::-1]).reshape(2, -1, n, nq)]
  transfers between devices with their start and end apart: 6 -> 9, of which waited for: 5 -> 5; matrix products, arithmetic and copies ran while one was open for 2% -> 6% of each run, Pallas kernels for 4% -> 4%
where the time goes in v2:
time: 31.4 us; the launch traced here: 31.1 us
  starting transfers between devices  10.7 us (34%)
  waiting for transfers between devices  10.4 us (33%)
  local copies, waits for them, and re-layouts  4.32 us (14%)
  Pallas kernels  4.21 us (13%)
  between operations  0.74 us (2%)
  other arithmetic  0.69 us (2%)
    ppermute x3, waiting for transfers between devices, crossed(): return lax.ppermute(x, (axis, 'query'), [(i, i ^ bits) for i in range(n)])  5.77 us
    ppermute x3, starting transfers between devices, crossed(): return lax.ppermute(x, (axis, 'query'), [(i, i ^ bits) for i in range(n)])  4.64 us
    pallas_call x4, Pallas kernels, call(): pl.pallas_call(body, out_shape=out_shape, in_specs=specs, out_specs=jax.t...  4.21 us
    ppermute x2, waiting for transfers between devices, shifted(): return lax.ppermute(x, axis, [(i, (i + shift) % n) for i in range(n)])  3.82 us
    ppermute x2, starting transfers between devices, shifted(): return lax.ppermute(x, axis, [(i, (i + shift) % n) for i in range(n)])  3.48 us
    unnamed x8, local copies, waits for them, and re-layouts  2.64 us
    ppermute x4, starting transfers between devices, flipped(): return lax.ppermute(x, axis, [(i, i ^ bit) for i in range(n)])  2.59 us
    reshape x2, local copies, waits for them, and re-layouts, local(): queries = query_grads.reshape(layers, nq, width // FOLD, FOLD, width)  1.45 us
  transfers between devices with their start and end apart: 9, of which 5 were waited for; matrix products, arithmetic and copies ran while one was open for 6% of the time, Pallas kernels for 4%

profile of v2, /device:TPU:0, one launch (start us, length us, event | category | flops | bytes accessed | tf_op | source)
XLA Modules:
  0.0 31.1 jit_solution(4794043103317295267)
XLA Ops:
  0.0 2.9 %collective-permute-start = (bf16[2,64,2048]{2,1,0:T(8,128)(2,1)}, bf16[2,64,2048]{2,1,0:T(8,128)(2,1)}, u32[]{:S(2)}, u32[]{:S(2)}) collective-permute-start(bf16[2,64,2048]{2,1,0:T(8,128)(2,1)} %bitcast.25), channel_id=1, source_target_pairs={{0,2},{2,0},{1,3},{3,1},{4,6},{6,4},{5,7},{7,5},{8,10},{10,8},{9,1... | collective-permute-start | bytes 1572872 | tf_op jit(solution)/shard_map/ppermute | solution.py:111
  2.9 1.2 %reshape.14 = bf16[2,8,4,16,64]{4,3,2,1,0:T(8,128)(2,1)S(1)} reshape(bf16[2,8,4096]{2,1,0:T(8,128)(2,1)} %param.11) | data formatting | bytes 262144 | tf_op jit(solution)/shard_map/reshape | solution.py:140
  4.1 0.0 copy-start
  4.1 0.3 copy.9
  4.4 0.2 reshape.15.refs_2_
  4.6 1.6 %collective-permute-start.3 = (bf16[128,512]{1,0:T(8,128)(2,1)S(1)}, bf16[128,512]{1,0:T(8,128)(2,1)S(1)}, u32[]{:S(2)}, u32[]{:S(2)}) collective-permute-start(bf16[128,512]{1,0:T(8,128)(2,1)S(1)} %reshape.15.refs_2_), channel_id=1, source_target_pairs={{0,4},{4,0},{8,12},{12,8},{1,5},{5,1},{9,13},{13,9},{2,6},{6,2},{1... | collective-permute-start | bytes 393224 | tf_op jit(solution)/shard_map/ppermute | solution.py:116
  6.3 0.0 collective-permute-start.2
  6.3 1.6 %copy-done.1 = bf16[2,256,2048]{2,1,0:T(8,128)(2,1)S(1)} copy-done((bf16[2,256,2048]{2,1,0:T(8,128)(2,1)S(1)}, bf16[2,256,2048]{2,1,0:T(8,128)(2,1)}, u32[]{:S(2)}) %copy-start.1) | copy-done | bytes 2097176
  7.9 1.0 %copy-done.2 = bf16[2,2048,64]{1,2,0:T(8,128)(2,1)S(1)} copy-done((bf16[2,2048,64]{1,2,0:T(8,128)(2,1)S(1)}, bf16[2,2048,64]{1,2,0:T(8,128)(2,1)}, u32[]{:S(2)}) %copy-start.2) | copy-done | bytes 524312
  8.9 0.8 %shard_map.65 = f32[256,128]{1,0:T(8,128)S(1)} custom-call(bf16[2,256,2048]{2,1,0:T(8,128)(2,1)S(1)} %copy-done.1, bf16[2,64,2048]{2,1,0:T(8,128)(2,1)S(1)} %bitcast.24, bf16[128,512]{1,0:T(8,128)(2,1)S(1)} %reshape.15.refs_2_), custom_call_target="tpu_custom_call" | custom-call | tf_op jit(solution)/shard_map/pallas_call | solution.py:30
  9.7 0.0 collective-permute-done.3.refs_8_.refs_4_
  9.7 0.6 %collective-permute-start.4 = (bf16[128,512]{1,0:T(8,128)(2,1)S(1)}, bf16[128,512]{1,0:T(8,128)(2,1)S(1)}, u32[]{:S(2)}, u32[]{:S(2)}) collective-permute-start(bf16[128,512]{1,0:T(8,128)(2,1)S(1)} %collective-permute-done.3.refs_8_.refs_4_), channel_id=1, source_target_pairs={{0,1},{1,0},{2,3},{3,2},{4,5},{5,4},{6,7},{7,6},{8,9},{9,8},{10,11... | collective-permute-start | bytes 393224 | tf_op jit(solution)/shard_map/ppermute | solution.py:116
  10.2 0.5 %collective-permute-start.1 = (bf16[128,128]{1,0:T(8,128)(2,1)S(1)}, bf16[128,128]{1,0:T(8,128)(2,1)S(1)}, u32[]{:S(2)}, u32[]{:S(2)}) collective-permute-start(bf16[128,128]{1,0:T(8,128)(2,1)S(1)} %fusion), channel_id=1, source_target_pairs={{0,2},{2,0},{1,3},{3,1},{4,6},{6,4},{5,7},{7,5},{8,10},{10,8},{9,1... | collective-permute-start | bytes 98312 | tf_op jit(solution)/shard_map/ppermute | solution.py:111
  11.4 0.0 copy-done
  11.5 0.0 copy-done.3
  11.5 0.5 %shard_map.64.refs_3_ = f32[128,128]{1,0:T(8,128)S(1)} custom-call(s32[1]{0:T(128)} %bitcast.3.refs_0_, bf16[2,128,4096]{2,1,0:T(8,128)(2,1)S(1)} %copy-done, bf16[2,64,2048]{2,1,0:T(8,128)(2,1)S(1)} %bitcast.26), custom_call_target="tpu_custom_call" | custom-call | tf_op jit(solution)/shard_map/pallas_call | solution.py:30
  12.0 3.8 %collective-permute-done.1.refs_6_ = bf16[128,128]{1,0:T(8,128)(2,1)S(1)} collective-permute-done((bf16[128,128]{1,0:T(8,128)(2,1)S(1)}, bf16[128,128]{1,0:T(8,128)(2,1)S(1)}, u32[]{:S(2)}, u32[]{:S(2)}) %collective-permute-start.1) | collective-permute-done | bytes 32800 | tf_op jit(solution)/shard_map/ppermute | solution.py:111
  15.8 0.0 collective-permute-done.2.refs_7_.refs_3_
  15.8 0.0 collective-permute-done.4.refs_9_.refs_5_
  15.8 0.0 collective-permute-done.refs_4_
  15.8 1.7 %shard_map.66 = bf16[16,512]{1,0:T(8,128)(2,1)S(1)} custom-call(s32[1]{0:T(128)} %bitcast.2.refs_0_, s32[1]{0:T(128)S(6)} %copy.10.refs_1_, bf16[2,128,4096]{2,1,0:T(8,128)(2,1)S(1)} %copy-done, f32[128,128]{1,0:T(8,128)S(1)} %shard_map.64.refs_3_, bf16[2,64,2048]{2,1,0:T(8,128)(2,1)} %collective-permute-done.refs_4_, ...), custom_call_target="tpu_custom_call" | custom-call | tf_op jit(solution)/shard_map/pallas_call | solution.py:30
  17.5 1.6 %collective-permute-start.5 = (bf16[1,16,512]{2,1,0:T(8,128)(2,1)S(1)}, bf16[1,16,512]{2,1,0:T(8,128)(2,1)S(1)}, u32[]{:S(2)}, u32[]{:S(2)}) collective-permute-start(bf16[1,16,512]{2,1,0:T(8,128)(2,1)S(1)} %bitcast.29), channel_id=1, source_target_pairs={{0,9},{1,8},{4,13},{5,12},{8,1},{9,0},{12,5},{13,4},{2,11},{3,10},... | collective-permute-start | bytes 49160 | tf_op jit(solution)/shard_map/ppermute | solution.py:122
  19.0 2.6 %collective-permute-done.5 = bf16[1,16,512]{2,1,0:T(8,128)(2,1)S(1)} collective-permute-done((bf16[1,16,512]{2,1,0:T(8,128)(2,1)S(1)}, bf16[1,16,512]{2,1,0:T(8,128)(2,1)S(1)}, u32[]{:S(2)}, u32[]{:S(2)}) %collective-permute-start.5) | collective-permute-done | bytes 16416 | tf_op jit(solution)/shard_map/ppermute | solution.py:122
  21.6 1.5 %collective-permute-start.6 = (bf16[2,16,512]{2,1,0:T(8,128)(2,1)S(1)}, bf16[2,16,512]{2,1,0:T(8,128)(2,1)S(1)}, u32[]{:S(2)}, u32[]{:S(2)}) collective-permute-start(bf16[2,16,512]{2,1,0:T(8,128)(2,1)S(1)} %pad_maximum_fusion.1), channel_id=1, source_target_pairs={{0,3},{1,2},{2,1},{3,0},{4,7},{5,6},{6,5},{7,4},{8,11},{9,10},{10,... | collective-permute-start | bytes 98312 | tf_op jit(solution)/shard_map/ppermute | solution.py:122
  23.0 0.1 pad_add_fusion.refs_0_
  23.1 1.8 %collective-permute-done.6 = bf16[2,16,512]{2,1,0:T(8,128)(2,1)S(1)} collective-permute-done((bf16[2,16,512]{2,1,0:T(8,128)(2,1)S(1)}, bf16[2,16,512]{2,1,0:T(8,128)(2,1)S(1)}, u32[]{:S(2)}, u32[]{:S(2)}) %collective-permute-start.6) | collective-permute-done | bytes 32800 | tf_op jit(solution)/shard_map/ppermute | solution.py:122
  24.9 1.3 %shard_map.67 = (f32[4,8]{1,0:T(4,128)S(1)}, f32[4,8]{1,0:T(4,128)S(1)}) custom-call(s32[2]{0:T(128)S(1)} %pad_add_fusion.refs_0_, bf16[4,16,512]{2,1,0:T(8,128)(2,1)S(1)} %pad_maximum_fusion.refs_1_, bf16[128,512]{1,0:T(8,128)(2,1)S(1)} %reshape.15.refs_2_, bf16[128,512]{1,0:T(8,128)(2,1)S(1)} %collective-permute-done.2.refs_7_.refs_3_, ...), custom_call_target="tpu_custom_call" | custom-call | tf_op jit(solution)/shard_map/pallas_call | solution.py:30
  26.3 1.6 %collective-permute-start.7 = (f32[4,8]{1,0:T(4,128)S(1)}, f32[4,8]{1,0:T(4,128)S(1)}, u32[]{:S(2)}, u32[]{:S(2)}) collective-permute-start(f32[4,8]{1,0:T(4,128)S(1)} %get-tuple-element.8), channel_id=1, source_target_pairs={{0,5},{1,4},{4,1},{5,0},{8,13},{9,12},{12,9},{13,8},{2,7},{3,6},{6... | collective-permute-start | bytes 392 | tf_op jit(solution)/shard_map/ppermute | solution.py:122
  27.9 1.4 %collective-permute-done.7 = f32[4,8]{1,0:T(4,128)S(1)} collective-permute-done((f32[4,8]{1,0:T(4,128)S(1)}, f32[4,8]{1,0:T(4,128)S(1)}, u32[]{:S(2)}, u32[]{:S(2)}) %collective-permute-start.7) | collective-permute-done | bytes 160 | tf_op jit(solution)/shard_map/ppermute | solution.py:122
  29.3 0.4 %collective-permute-start.8 = (f32[2,2,8]{2,1,0:T(2,128)S(1)}, f32[2,2,8]{2,1,0:T(2,128)S(1)}, u32[]{:S(2)}, u32[]{:S(2)}) collective-permute-start(f32[2,2,8]{2,1,0:T(2,128)S(1)} %pad_maximum_fusion.2), channel_id=1, source_target_pairs={{0,1},{1,0},{2,3},{3,2},{4,5},{5,4},{6,7},{7,6},{8,9},{9,8},{10,11... | collective-permute-start | bytes 392 | tf_op jit(solution)/shard_map/ppermute | solution.py:116
  29.7 0.8 %collective-permute-done.8 = f32[2,2,8]{2,1,0:T(2,128)S(1)} collective-permute-done((f32[2,2,8]{2,1,0:T(2,128)S(1)}, f32[2,2,8]{2,1,0:T(2,128)S(1)}, u32[]{:S(2)}, u32[]{:S(2)}) %collective-permute-start.8) | collective-permute-done | bytes 160 | tf_op jit(solution)/shard_map/ppermute | solution.py:116
  30.5 0.6 %reverse_select_fusion = f32[2,2,8]{2,1,0:T(2,128)} fusion(f32[2,2,8]{2,1,0:T(2,128)S(1)} %maximum_add_fusion, pred[]{:T(512)S(6)} %eq.7), kind=kLoop, calls=%fused_computation.6 | loop fusion | flops 32 | bytes 257 | tf_op jit(solution)/shard_map/jit(_where)/select_n | solution.py:202
  (11 shorter events, 0.0 us)
Async XLA Ops:
  0.0 15.8 %collective-permute-start = (bf16[2,64,2048]{2,1,0:T(8,128)(2,1)}, bf16[2,64,2048]{2,1,0:T(8,128)(2,1)}, u32[]{:S(2)}, u32[]{:S(2)}) collective-permute-start(bf16[2,64,2048]{2,1,0:T(8,128)(2,1)} %bitcast.25), channel_id=1, source_target_pairs={{0,2},{2,0},{1,3},{3,1},{4,6},{6,4},{5,7},{7,5},{8,10},{10,8},{9,1... | collective-permute-start | bytes 1572872 | tf_op jit(solution)/shard_map/ppermute | solution.py:111
  4.1 7.3 %copy-start = (bf16[2,128,4096]{2,1,0:T(8,128)(2,1)S(1)}, bf16[2,128,4096]{2,1,0:T(8,128)(2,1)}, u32[]{:S(2)}) copy-start(bf16[2,128,4096]{2,1,0:T(8,128)(2,1)} %refs_2_.1) | copy-start | bytes 6291460
  4.6 5.0 %collective-permute-start.3 = (bf16[128,512]{1,0:T(8,128)(2,1)S(1)}, bf16[128,512]{1,0:T(8,128)(2,1)S(1)}, u32[]{:S(2)}, u32[]{:S(2)}) collective-permute-start(bf16[128,512]{1,0:T(8,128)(2,1)S(1)} %reshape.15.refs_2_), channel_id=1, source_target_pairs={{0,4},{4,0},{8,12},{12,8},{1,5},{5,1},{9,13},{13,9},{2,6},{6,2},{1... | collective-permute-start | bytes 393224 | tf_op jit(solution)/shard_map/ppermute | solution.py:116
  6.3 9.5 %collective-permute-start.2 = (bf16[128,512]{1,0:T(8,128)(2,1)S(1)}, bf16[128,512]{1,0:T(8,128)(2,1)S(1)}, u32[]{:S(2)}, u32[]{:S(2)}) collective-permute-start(bf16[128,512]{1,0:T(8,128)(2,1)S(1)} %reshape.15.refs_2_), channel_id=1, source_target_pairs={{0,1},{1,0},{2,3},{3,2},{4,5},{5,4},{6,7},{7,6},{8,9},{9,8},{10,11... | collective-permute-start | bytes 393224 | tf_op jit(solution)/shard_map/ppermute | solution.py:116
  6.3 1.6 %copy-start.1 = (bf16[2,256,2048]{2,1,0:T(8,128)(2,1)S(1)}, bf16[2,256,2048]{2,1,0:T(8,128)(2,1)}, u32[]{:S(2)}) copy-start(bf16[2,256,2048]{2,1,0:T(8,128)(2,1)} %refs_0_.1) | copy-start | bytes 6291460
  7.9 1.0 %copy-start.2 = (bf16[2,2048,64]{1,2,0:T(8,128)(2,1)S(1)}, bf16[2,2048,64]{1,2,0:T(8,128)(2,1)}, u32[]{:S(2)}) copy-start(bf16[2,2048,64]{1,2,0:T(8,128)(2,1)} %param.9) | copy-start | bytes 1572868
  8.9 2.6 %copy-start.3 = (bf16[2,2048,64]{1,2,0:T(8,128)(2,1)S(1)}, bf16[2,2048,64]{1,2,0:T(8,128)(2,1)}, u32[]{:S(2)}) copy-start(bf16[2,2048,64]{1,2,0:T(8,128)(2,1)} %param.10) | copy-start | bytes 1572868
  9.7 6.1 %collective-permute-start.4 = (bf16[128,512]{1,0:T(8,128)(2,1)S(1)}, bf16[128,512]{1,0:T(8,128)(2,1)S(1)}, u32[]{:S(2)}, u32[]{:S(2)}) collective-permute-start(bf16[128,512]{1,0:T(8,128)(2,1)S(1)} %collective-permute-done.3.refs_8_.refs_4_), channel_id=1, source_target_pairs={{0,1},{1,0},{2,3},{3,2},{4,5},{5,4},{6,7},{7,6},{8,9},{9,8},{10,11... | collective-permute-start | bytes 393224 | tf_op jit(solution)/shard_map/ppermute | solution.py:116
  10.2 5.5 %collective-permute-start.1 = (bf16[128,128]{1,0:T(8,128)(2,1)S(1)}, bf16[128,128]{1,0:T(8,128)(2,1)S(1)}, u32[]{:S(2)}, u32[]{:S(2)}) collective-permute-start(bf16[128,128]{1,0:T(8,128)(2,1)S(1)} %fusion), channel_id=1, source_target_pairs={{0,2},{2,0},{1,3},{3,1},{4,6},{6,4},{5,7},{7,5},{8,10},{10,8},{9,1... | collective-permute-start | bytes 98312 | tf_op jit(solution)/shard_map/ppermute | solution.py:111
  17.5 4.1 %collective-permute-start.5 = (bf16[1,16,512]{2,1,0:T(8,128)(2,1)S(1)}, bf16[1,16,512]{2,1,0:T(8,128)(2,1)S(1)}, u32[]{:S(2)}, u32[]{:S(2)}) collective-permute-start(bf16[1,16,512]{2,1,0:T(8,128)(2,1)S(1)} %bitcast.29), channel_id=1, source_target_pairs={{0,9},{1,8},{4,13},{5,12},{8,1},{9,0},{12,5},{13,4},{2,11},{3,10},... | collective-permute-start | bytes 49160 | tf_op jit(solution)/shard_map/ppermute | solution.py:122
  21.6 3.3 %collective-permute-start.6 = (bf16[2,16,512]{2,1,0:T(8,128)(2,1)S(1)}, bf16[2,16,512]{2,1,0:T(8,128)(2,1)S(1)}, u32[]{:S(2)}, u32[]{:S(2)}) collective-permute-start(bf16[2,16,512]{2,1,0:T(8,128)(2,1)S(1)} %pad_maximum_fusion.1), channel_id=1, source_target_pairs={{0,3},{1,2},{2,1},{3,0},{4,7},{5,6},{6,5},{7,4},{8,11},{9,10},{10,... | collective-permute-start | bytes 98312 | tf_op jit(solution)/shard_map/ppermute | solution.py:122
  26.3 3.0 %collective-permute-start.7 = (f32[4,8]{1,0:T(4,128)S(1)}, f32[4,8]{1,0:T(4,128)S(1)}, u32[]{:S(2)}, u32[]{:S(2)}) collective-permute-start(f32[4,8]{1,0:T(4,128)S(1)} %get-tuple-element.8), channel_id=1, source_target_pairs={{0,5},{1,4},{4,1},{5,0},{8,13},{9,12},{12,9},{13,8},{2,7},{3,6},{6... | collective-permute-start | bytes 392 | tf_op jit(solution)/shard_map/ppermute | solution.py:122
  29.3 1.2 %collective-permute-start.8 = (f32[2,2,8]{2,1,0:T(2,128)S(1)}, f32[2,2,8]{2,1,0:T(2,128)S(1)}, u32[]{:S(2)}, u32[]{:S(2)}) collective-permute-start(f32[2,2,8]{2,1,0:T(2,128)S(1)} %pad_maximum_fusion.2), channel_id=1, source_target_pairs={{0,1},{1,0},{2,3},{3,2},{4,5},{5,4},{6,7},{7,6},{8,9},{9,8},{10,11... | collective-permute-start | bytes 392 | tf_op jit(solution)/shard_map/ppermute | solution.py:116

commit v3 on v2

--- a/solution.py
+++ b/solution.py
@@ -66,10 +66,10 @@
         ins = ins + other[...].astype(F32)
     both = dot(ins.astype(BF16), total, TN)
     width = both.shape[1] // layers
-    layer = lax.broadcasted_iota(jnp.int32, (width, both.shape[1]), 1) // width
+    lane = lax.broadcasted_iota(jnp.int32, (width, both.shape[1]), 1)
     grad = both[:width]
     for l in range(1, layers):
-        grad = jnp.where(layer == l, both[l * width : (l + 1) * width], grad)
+        grad = jnp.where(lane >= l * width, both[l * width : (l + 1) * width], grad)
     grad = grad.astype(BF16)
     out[...] = jnp.concatenate(
         [grad[g * FOLD : (g + 1) * FOLD] for g in range(width // FOLD)], axis=1
@@ -82,12 +82,13 @@
     def against(queries, chosen, place, out):
         lhs = jnp.concatenate([grads[s] for s in chosen], axis=0)
         products = dot(lhs, queries[...], NT)
-        row = lax.broadcasted_iota(jnp.int32, products.shape, 0) % FOLD
-        column = lax.broadcasted_iota(jnp.int32, products.shape, 1) % FOLD
-        products = jnp.where(row == column, products, 0.0)
+        row = lax.broadcasted_iota(jnp.int32, products.shape, 0)
+        column = lax.broadcasted_iota(jnp.int32, products.shape, 1)
+        products = jnp.where((row ^ column) & (FOLD - 1) == 0, products, 0.0)
         sums = jnp.sum(products.reshape(len(chosen), FOLD, nq * FOLD), axis=1)
-        fold = lax.broadcasted_iota(jnp.int32, (nq * FOLD, nq), 0) // FOLD
-        fold = fold == lax.broadcasted_iota(jnp.int32, (nq * FOLD, nq), 1)
+        fold = lax.broadcasted_iota(jnp.int32, (nq * FOLD, nq), 0)
+        fold = fold - FOLD * lax.broadcasted_iota(jnp.int32, (nq * FOLD, nq), 1)
+        fold = (fold >= 0) & (fold < FOLD)
         table = lax.dot_general(
             sums,
             fold.astype(F32),

time: 31.4 us -> 31.4 us (level)
  no operation moved by 1% of the time
where the time goes in v3:
time: 31.4 us; the launch traced here: 31.1 us
  starting transfers between devices  10.7 us (34%)
  waiting for transfers between devices  10.4 us (33%)
  local copies, waits for them, and re-layouts  4.32 us (14%)
  Pallas kernels  4.21 us (13%)
  between operations  0.74 us (2%)
  other arithmetic  0.69 us (2%)
    ppermute x3, waiting for transfers between devices, crossed(): return lax.ppermute(x, (axis, 'query'), [(i, i ^ bits) for i in range(n)])  5.77 us
    ppermute x3, starting transfers between devices, crossed(): return lax.ppermute(x, (axis, 'query'), [(i, i ^ bits) for i in range(n)])  4.64 us
    pallas_call x4, Pallas kernels, call(): pl.pallas_call(body, out_shape=out_shape, in_specs=specs, out_specs=jax.t...  4.21 us
    ppermute x2, waiting for transfers between devices, shifted(): return lax.ppermute(x, axis, [(i, (i + shift) % n) for i in range(n)])  3.82 us
    ppermute x2, starting transfers between devices, shifted(): return lax.ppermute(x, axis, [(i, (i + shift) % n) for i in range(n)])  3.48 us
    unnamed x8, local copies, waits for them, and re-layouts  2.64 us
    ppermute x4, starting transfers between devices, flipped(): return lax.ppermute(x, axis, [(i, i ^ bit) for i in range(n)])  2.59 us
    reshape x2, local copies, waits for them, and re-layouts, local(): queries = query_grads.reshape(layers, nq, width // FOLD, FOLD, width)  1.45 us
  transfers between devices with their start and end apart: 9, of which 5 were waited for; matrix products, arithmetic and copies ran while one was open for 6% of the time, Pallas kernels for 4%

profile of v3, /device:TPU:0, one launch (start us, length us, event | category | flops | bytes accessed | tf_op | source)
XLA Modules:
  0.0 31.1 jit_solution(12845764499234358879)
XLA Ops:
  0.0 2.9 %collective-permute-start = (bf16[2,64,2048]{2,1,0:T(8,128)(2,1)}, bf16[2,64,2048]{2,1,0:T(8,128)(2,1)}, u32[]{:S(2)}, u32[]{:S(2)}) collective-permute-start(bf16[2,64,2048]{2,1,0:T(8,128)(2,1)} %bitcast.25), channel_id=1, source_target_pairs={{0,2},{2,0},{1,3},{3,1},{4,6},{6,4},{5,7},{7,5},{8,10},{10,8},{9,1... | collective-permute-start | bytes 1572872 | tf_op jit(solution)/shard_map/ppermute | solution.py:112
  2.9 1.2 %reshape.14 = bf16[2,8,4,16,64]{4,3,2,1,0:T(8,128)(2,1)S(1)} reshape(bf16[2,8,4096]{2,1,0:T(8,128)(2,1)} %param.11) | data formatting | bytes 262144 | tf_op jit(solution)/shard_map/reshape | solution.py:141
  4.1 0.0 copy-start
  4.1 0.3 copy.9
  4.4 0.2 reshape.15.refs_2_
  4.6 1.6 %collective-permute-start.3 = (bf16[128,512]{1,0:T(8,128)(2,1)S(1)}, bf16[128,512]{1,0:T(8,128)(2,1)S(1)}, u32[]{:S(2)}, u32[]{:S(2)}) collective-permute-start(bf16[128,512]{1,0:T(8,128)(2,1)S(1)} %reshape.15.refs_2_), channel_id=1, source_target_pairs={{0,4},{4,0},{8,12},{12,8},{1,5},{5,1},{9,13},{13,9},{2,6},{6,2},{1... | collective-permute-start | bytes 393224 | tf_op jit(solution)/shard_map/ppermute | solution.py:117
  6.3 0.0 collective-permute-start.2
  6.3 1.6 %copy-done.1 = bf16[2,256,2048]{2,1,0:T(8,128)(2,1)S(1)} copy-done((bf16[2,256,2048]{2,1,0:T(8,128)(2,1)S(1)}, bf16[2,256,2048]{2,1,0:T(8,128)(2,1)}, u32[]{:S(2)}) %copy-start.1) | copy-done | bytes 2097176
  7.9 1.0 %copy-done.2 = bf16[2,2048,64]{1,2,0:T(8,128)(2,1)S(1)} copy-done((bf16[2,2048,64]{1,2,0:T(8,128)(2,1)S(1)}, bf16[2,2048,64]{1,2,0:T(8,128)(2,1)}, u32[]{:S(2)}) %copy-start.2) | copy-done | bytes 524312
  8.9 0.8 %shard_map.65 = f32[256,128]{1,0:T(8,128)S(1)} custom-call(bf16[2,256,2048]{2,1,0:T(8,128)(2,1)S(1)} %copy-done.1, bf16[2,64,2048]{2,1,0:T(8,128)(2,1)S(1)} %bitcast.24, bf16[128,512]{1,0:T(8,128)(2,1)S(1)} %reshape.15.refs_2_), custom_call_target="tpu_custom_call" | custom-call | tf_op jit(solution)/shard_map/pallas_call | solution.py:30
  9.7 0.0 collective-permute-done.3.refs_8_.refs_4_
  9.7 0.6 %collective-permute-start.4 = (bf16[128,512]{1,0:T(8,128)(2,1)S(1)}, bf16[128,512]{1,0:T(8,128)(2,1)S(1)}, u32[]{:S(2)}, u32[]{:S(2)}) collective-permute-start(bf16[128,512]{1,0:T(8,128)(2,1)S(1)} %collective-permute-done.3.refs_8_.refs_4_), channel_id=1, source_target_pairs={{0,1},{1,0},{2,3},{3,2},{4,5},{5,4},{6,7},{7,6},{8,9},{9,8},{10,11... | collective-permute-start | bytes 393224 | tf_op jit(solution)/shard_map/ppermute | solution.py:117
  10.2 0.5 %collective-permute-start.1 = (bf16[128,128]{1,0:T(8,128)(2,1)S(1)}, bf16[128,128]{1,0:T(8,128)(2,1)S(1)}, u32[]{:S(2)}, u32[]{:S(2)}) collective-permute-start(bf16[128,128]{1,0:T(8,128)(2,1)S(1)} %fusion), channel_id=1, source_target_pairs={{0,2},{2,0},{1,3},{3,1},{4,6},{6,4},{5,7},{7,5},{8,10},{10,8},{9,1... | collective-permute-start | bytes 98312 | tf_op jit(solution)/shard_map/ppermute | solution.py:112
  11.4 0.0 copy-done
  11.5 0.0 copy-done.3
  11.5 0.5 %shard_map.64.refs_3_ = f32[128,128]{1,0:T(8,128)S(1)} custom-call(s32[1]{0:T(128)} %bitcast.3.refs_0_, bf16[2,128,4096]{2,1,0:T(8,128)(2,1)S(1)} %copy-done, bf16[2,64,2048]{2,1,0:T(8,128)(2,1)S(1)} %bitcast.26), custom_call_target="tpu_custom_call" | custom-call | tf_op jit(solution)/shard_map/pallas_call | solution.py:30
  12.0 3.8 %collective-permute-done.1.refs_6_ = bf16[128,128]{1,0:T(8,128)(2,1)S(1)} collective-permute-done((bf16[128,128]{1,0:T(8,128)(2,1)S(1)}, bf16[128,128]{1,0:T(8,128)(2,1)S(1)}, u32[]{:S(2)}, u32[]{:S(2)}) %collective-permute-start.1) | collective-permute-done | bytes 32800 | tf_op jit(solution)/shard_map/ppermute | solution.py:112
  15.8 0.0 collective-permute-done.2.refs_7_.refs_3_
  15.8 0.0 collective-permute-done.4.refs_9_.refs_5_
  15.8 0.0 collective-permute-done.refs_4_
  15.8 1.7 %shard_map.66 = bf16[16,512]{1,0:T(8,128)(2,1)S(1)} custom-call(s32[1]{0:T(128)} %bitcast.2.refs_0_, s32[1]{0:T(128)S(6)} %copy.10.refs_1_, bf16[2,128,4096]{2,1,0:T(8,128)(2,1)S(1)} %copy-done, f32[128,128]{1,0:T(8,128)S(1)} %shard_map.64.refs_3_, bf16[2,64,2048]{2,1,0:T(8,128)(2,1)} %collective-permute-done.refs_4_, ...), custom_call_target="tpu_custom_call" | custom-call | tf_op jit(solution)/shard_map/pallas_call | solution.py:30
  17.5 1.6 %collective-permute-start.5 = (bf16[1,16,512]{2,1,0:T(8,128)(2,1)S(1)}, bf16[1,16,512]{2,1,0:T(8,128)(2,1)S(1)}, u32[]{:S(2)}, u32[]{:S(2)}) collective-permute-start(bf16[1,16,512]{2,1,0:T(8,128)(2,1)S(1)} %bitcast.29), channel_id=1, source_target_pairs={{0,9},{1,8},{4,13},{5,12},{8,1},{9,0},{12,5},{13,4},{2,11},{3,10},... | collective-permute-start | bytes 49160 | tf_op jit(solution)/shard_map/ppermute | solution.py:123
  19.0 2.6 %collective-permute-done.5 = bf16[1,16,512]{2,1,0:T(8,128)(2,1)S(1)} collective-permute-done((bf16[1,16,512]{2,1,0:T(8,128)(2,1)S(1)}, bf16[1,16,512]{2,1,0:T(8,128)(2,1)S(1)}, u32[]{:S(2)}, u32[]{:S(2)}) %collective-permute-start.5) | collective-permute-done | bytes 16416 | tf_op jit(solution)/shard_map/ppermute | solution.py:123
  21.6 1.5 %collective-permute-start.6 = (bf16[2,16,512]{2,1,0:T(8,128)(2,1)S(1)}, bf16[2,16,512]{2,1,0:T(8,128)(2,1)S(1)}, u32[]{:S(2)}, u32[]{:S(2)}) collective-permute-start(bf16[2,16,512]{2,1,0:T(8,128)(2,1)S(1)} %pad_maximum_fusion.1), channel_id=1, source_target_pairs={{0,3},{1,2},{2,1},{3,0},{4,7},{5,6},{6,5},{7,4},{8,11},{9,10},{10,... | collective-permute-start | bytes 98312 | tf_op jit(solution)/shard_map/ppermute | solution.py:123
  23.0 0.1 pad_add_fusion.refs_0_
  23.1 1.8 %collective-permute-done.6 = bf16[2,16,512]{2,1,0:T(8,128)(2,1)S(1)} collective-permute-done((bf16[2,16,512]{2,1,0:T(8,128)(2,1)S(1)}, bf16[2,16,512]{2,1,0:T(8,128)(2,1)S(1)}, u32[]{:S(2)}, u32[]{:S(2)}) %collective-permute-start.6) | collective-permute-done | bytes 32800 | tf_op jit(solution)/shard_map/ppermute | solution.py:123
  24.9 1.3 %shard_map.67 = (f32[4,8]{1,0:T(4,128)S(1)}, f32[4,8]{1,0:T(4,128)S(1)}) custom-call(s32[2]{0:T(128)S(1)} %pad_add_fusion.refs_0_, bf16[4,16,512]{2,1,0:T(8,128)(2,1)S(1)} %pad_maximum_fusion.refs_1_, bf16[128,512]{1,0:T(8,128)(2,1)S(1)} %reshape.15.refs_2_, bf16[128,512]{1,0:T(8,128)(2,1)S(1)} %collective-permute-done.2.refs_7_.refs_3_, ...), custom_call_target="tpu_custom_call" | custom-call | tf_op jit(solution)/shard_map/pallas_call | solution.py:30
  26.3 1.6 %collective-permute-start.7 = (f32[4,8]{1,0:T(4,128)S(1)}, f32[4,8]{1,0:T(4,128)S(1)}, u32[]{:S(2)}, u32[]{:S(2)}) collective-permute-start(f32[4,8]{1,0:T(4,128)S(1)} %get-tuple-element.8), channel_id=1, source_target_pairs={{0,5},{1,4},{4,1},{5,0},{8,13},{9,12},{12,9},{13,8},{2,7},{3,6},{6... | collective-permute-start | bytes 392 | tf_op jit(solution)/shard_map/ppermute | solution.py:123
  27.9 1.4 %collective-permute-done.7 = f32[4,8]{1,0:T(4,128)S(1)} collective-permute-done((f32[4,8]{1,0:T(4,128)S(1)}, f32[4,8]{1,0:T(4,128)S(1)}, u32[]{:S(2)}, u32[]{:S(2)}) %collective-permute-start.7) | collective-permute-done | bytes 160 | tf_op jit(solution)/shard_map/ppermute | solution.py:123
  29.3 0.4 %collective-permute-start.8 = (f32[2,2,8]{2,1,0:T(2,128)S(1)}, f32[2,2,8]{2,1,0:T(2,128)S(1)}, u32[]{:S(2)}, u32[]{:S(2)}) collective-permute-start(f32[2,2,8]{2,1,0:T(2,128)S(1)} %pad_maximum_fusion.2), channel_id=1, source_target_pairs={{0,1},{1,0},{2,3},{3,2},{4,5},{5,4},{6,7},{7,6},{8,9},{9,8},{10,11... | collective-permute-start | bytes 392 | tf_op jit(solution)/shard_map/ppermute | solution.py:117
  29.7 0.8 %collective-permute-done.8 = f32[2,2,8]{2,1,0:T(2,128)S(1)} collective-permute-done((f32[2,2,8]{2,1,0:T(2,128)S(1)}, f32[2,2,8]{2,1,0:T(2,128)S(1)}, u32[]{:S(2)}, u32[]{:S(2)}) %collective-permute-start.8) | collective-permute-done | bytes 160 | tf_op jit(solution)/shard_map/ppermute | solution.py:117
  30.5 0.6 %reverse_select_fusion = f32[2,2,8]{2,1,0:T(2,128)} fusion(f32[2,2,8]{2,1,0:T(2,128)S(1)} %maximum_add_fusion, pred[]{:T(512)S(6)} %eq.7), kind=kLoop, calls=%fused_computation.6 | loop fusion | flops 32 | bytes 257 | tf_op jit(solution)/shard_map/jit(_where)/select_n | solution.py:203
  (11 shorter events, 0.0 us)
Async XLA Ops:
  0.0 15.8 %collective-permute-start = (bf16[2,64,2048]{2,1,0:T(8,128)(2,1)}, bf16[2,64,2048]{2,1,0:T(8,128)(2,1)}, u32[]{:S(2)}, u32[]{:S(2)}) collective-permute-start(bf16[2,64,2048]{2,1,0:T(8,128)(2,1)} %bitcast.25), channel_id=1, source_target_pairs={{0,2},{2,0},{1,3},{3,1},{4,6},{6,4},{5,7},{7,5},{8,10},{10,8},{9,1... | collective-permute-start | bytes 1572872 | tf_op jit(solution)/shard_map/ppermute | solution.py:112
  4.1 7.3 %copy-start = (bf16[2,128,4096]{2,1,0:T(8,128)(2,1)S(1)}, bf16[2,128,4096]{2,1,0:T(8,128)(2,1)}, u32[]{:S(2)}) copy-start(bf16[2,128,4096]{2,1,0:T(8,128)(2,1)} %refs_2_.1) | copy-start | bytes 6291460
  4.6 5.0 %collective-permute-start.3 = (bf16[128,512]{1,0:T(8,128)(2,1)S(1)}, bf16[128,512]{1,0:T(8,128)(2,1)S(1)}, u32[]{:S(2)}, u32[]{:S(2)}) collective-permute-start(bf16[128,512]{1,0:T(8,128)(2,1)S(1)} %reshape.15.refs_2_), channel_id=1, source_target_pairs={{0,4},{4,0},{8,12},{12,8},{1,5},{5,1},{9,13},{13,9},{2,6},{6,2},{1... | collective-permute-start | bytes 393224 | tf_op jit(solution)/shard_map/ppermute | solution.py:117
  6.3 9.5 %collective-permute-start.2 = (bf16[128,512]{1,0:T(8,128)(2,1)S(1)}, bf16[128,512]{1,0:T(8,128)(2,1)S(1)}, u32[]{:S(2)}, u32[]{:S(2)}) collective-permute-start(bf16[128,512]{1,0:T(8,128)(2,1)S(1)} %reshape.15.refs_2_), channel_id=1, source_target_pairs={{0,1},{1,0},{2,3},{3,2},{4,5},{5,4},{6,7},{7,6},{8,9},{9,8},{10,11... | collective-permute-start | bytes 393224 | tf_op jit(solution)/shard_map/ppermute | solution.py:117
  6.3 1.6 %copy-start.1 = (bf16[2,256,2048]{2,1,0:T(8,128)(2,1)S(1)}, bf16[2,256,2048]{2,1,0:T(8,128)(2,1)}, u32[]{:S(2)}) copy-start(bf16[2,256,2048]{2,1,0:T(8,128)(2,1)} %refs_0_.1) | copy-start | bytes 6291460
  7.9 1.0 %copy-start.2 = (bf16[2,2048,64]{1,2,0:T(8,128)(2,1)S(1)}, bf16[2,2048,64]{1,2,0:T(8,128)(2,1)}, u32[]{:S(2)}) copy-start(bf16[2,2048,64]{1,2,0:T(8,128)(2,1)} %param.9) | copy-start | bytes 1572868
  8.9 2.6 %copy-start.3 = (bf16[2,2048,64]{1,2,0:T(8,128)(2,1)S(1)}, bf16[2,2048,64]{1,2,0:T(8,128)(2,1)}, u32[]{:S(2)}) copy-start(bf16[2,2048,64]{1,2,0:T(8,128)(2,1)} %param.10) | copy-start | bytes 1572868
  9.7 6.1 %collective-permute-start.4 = (bf16[128,512]{1,0:T(8,128)(2,1)S(1)}, bf16[128,512]{1,0:T(8,128)(2,1)S(1)}, u32[]{:S(2)}, u32[]{:S(2)}) collective-permute-start(bf16[128,512]{1,0:T(8,128)(2,1)S(1)} %collective-permute-done.3.refs_8_.refs_4_), channel_id=1, source_target_pairs={{0,1},{1,0},{2,3},{3,2},{4,5},{5,4},{6,7},{7,6},{8,9},{9,8},{10,11... | collective-permute-start | bytes 393224 | tf_op jit(solution)/shard_map/ppermute | solution.py:117
  10.2 5.5 %collective-permute-start.1 = (bf16[128,128]{1,0:T(8,128)(2,1)S(1)}, bf16[128,128]{1,0:T(8,128)(2,1)S(1)}, u32[]{:S(2)}, u32[]{:S(2)}) collective-permute-start(bf16[128,128]{1,0:T(8,128)(2,1)S(1)} %fusion), channel_id=1, source_target_pairs={{0,2},{2,0},{1,3},{3,1},{4,6},{6,4},{5,7},{7,5},{8,10},{10,8},{9,1... | collective-permute-start | bytes 98312 | tf_op jit(solution)/shard_map/ppermute | solution.py:112
  17.5 4.1 %collective-permute-start.5 = (bf16[1,16,512]{2,1,0:T(8,128)(2,1)S(1)}, bf16[1,16,512]{2,1,0:T(8,128)(2,1)S(1)}, u32[]{:S(2)}, u32[]{:S(2)}) collective-permute-start(bf16[1,16,512]{2,1,0:T(8,128)(2,1)S(1)} %bitcast.29), channel_id=1, source_target_pairs={{0,9},{1,8},{4,13},{5,12},{8,1},{9,0},{12,5},{13,4},{2,11},{3,10},... | collective-permute-start | bytes 49160 | tf_op jit(solution)/shard_map/ppermute | solution.py:123
  21.6 3.3 %collective-permute-start.6 = (bf16[2,16,512]{2,1,0:T(8,128)(2,1)S(1)}, bf16[2,16,512]{2,1,0:T(8,128)(2,1)S(1)}, u32[]{:S(2)}, u32[]{:S(2)}) collective-permute-start(bf16[2,16,512]{2,1,0:T(8,128)(2,1)S(1)} %pad_maximum_fusion.1), channel_id=1, source_target_pairs={{0,3},{1,2},{2,1},{3,0},{4,7},{5,6},{6,5},{7,4},{8,11},{9,10},{10,... | collective-permute-start | bytes 98312 | tf_op jit(solution)/shard_map/ppermute | solution.py:123
  26.3 3.0 %collective-permute-start.7 = (f32[4,8]{1,0:T(4,128)S(1)}, f32[4,8]{1,0:T(4,128)S(1)}, u32[]{:S(2)}, u32[]{:S(2)}) collective-permute-start(f32[4,8]{1,0:T(4,128)S(1)} %get-tuple-element.8), channel_id=1, source_target_pairs={{0,5},{1,4},{4,1},{5,0},{8,13},{9,12},{12,9},{13,8},{2,7},{3,6},{6... | collective-permute-start | bytes 392 | tf_op jit(solution)/shard_map/ppermute | solution.py:123
  29.3 1.2 %collective-permute-start.8 = (f32[2,2,8]{2,1,0:T(2,128)S(1)}, f32[2,2,8]{2,1,0:T(2,128)S(1)}, u32[]{:S(2)}, u32[]{:S(2)}) collective-permute-start(f32[2,2,8]{2,1,0:T(2,128)S(1)} %pad_maximum_fusion.2), channel_id=1, source_target_pairs={{0,1},{1,0},{2,3},{3,2},{4,5},{5,4},{6,7},{7,6},{8,9},{9,8},{10,11... | collective-permute-start | bytes 392 | tf_op jit(solution)/shard_map/ppermute | solution.py:117

commit v4 on v0

v4 whole, which is shorter than its diff:
```python
import functools

import jax
import jax.numpy as jnp
from jax import lax
from jax.experimental import pallas as pl
from jax.experimental.pallas import tpu as pltpu
from jax.sharding import PartitionSpec as P

F32 = jnp.float32
BF16 = jnp.bfloat16
VMEM = pl.BlockSpec(memory_space=pltpu.VMEM)
SMEM = pl.BlockSpec(memory_space=pltpu.SMEM)
ANY = pl.BlockSpec(memory_space=pl.ANY)
NT = (((1,), (1,)), ((), ()))
TN = (((0,), (0,)), ((), ()))
FOLD = 16
EARLY = 1


def dot(a, b, dims):
    return lax.dot_general(a, b, dims, preferred_element_type=F32)


def call(kernel, out_shape, *args, after=(), specs=None, scratch=(), weight=1):
    specs = specs or [SMEM if a.dtype == jnp.int32 else VMEM for a in args]

    def body(*refs):
        kernel(*refs[: len(args)], *refs[len(args) + len(after) :])

    return pl.pallas_call(
        body,
        out_shape=out_shape,
        in_specs=specs + [ANY] * len(after),
        out_specs=jax.tree.map(lambda _: VMEM, out_shape),
        scratch_shapes=scratch,
        compiler_params=pltpu.CompilerParams(vmem_limit_bytes=16 * 2**20),
        cost_estimate=pl.CostEstimate(
            flops=1, bytes_accessed=weight, transcendentals=0
        ),
    )(*args, *after)


def in_vmem(x):
    return pltpu.with_memory_space_constraint(x, pltpu.VMEM)


def in_hbm(x):
    return pltpu.with_memory_space_constraint(x, pltpu.HBM)


def block_of(t, shift, n):
    return lax.rem(t + n - shift, n)


def side():
    return jnp.where(lax.axis_index("query") == 0, lax.axis_index("parts"), lax.axis_index("dp") & 1)


def cut(factor, piece, rest, sems):
    width = piece.shape[2]
    start = pl.multiple_of(side() * width, 128)
    copies = [
        pltpu.make_async_copy(factor.at[:, :, pl.ds(start, width)], piece, sems.at[0]),
        pltpu.make_async_copy(factor.at[:, :, pl.ds(2 * width, rest.shape[2])], rest, sems.at[1]),
    ]
    for copy in copies:
        copy.start()
    for copy in copies:
        copy.wait()


def project_inputs(n, acts, factor, mine, *theirs):
    slots = mine.shape[0]
    t = lax.axis_index("tensor")
    total = jnp.concatenate(
        [dot(acts[l], factor[l], NT) for l in range(acts.shape[0])], axis=1
    )
    for s, out in enumerate((mine, *theirs)):
        block = total[:slots]
        for i in range(1, n):
            block = jnp.where(lax.rem(t + s, n) == i, total[i * slots : (i + 1) * slots], block)
        out[...] = block.astype(out.dtype)


def fold_queries(width, own, near, out, rows):
    layers, nq, _ = own.shape
    wide = [
        jnp.concatenate([own[l].astype(F32), near[l].astype(F32)], axis=0) for l in range(layers)
    ]
    lanes = layers * width
    for g in range(width // FOLD):
        for r in range(FOLD):
            start = (g * FOLD + r) * width
            rows[g, pl.ds(r, 2 * nq, stride=FOLD), :] = jnp.concatenate(
                [w[:, start : start + width] for w in wide], axis=1
            )
        out[:, g * lanes : (g + 1) * lanes] = rows[g].astype(BF16)


def product(grads, start, factor):
    columns = pl.ds(pl.multiple_of(start, 128), factor.shape[2])
    return jnp.concatenate(
        [dot(grads[l, :, columns], factor[l], NT) for l in range(grads.shape[0])], axis=1
    )


def early(n, length, grads, factor, mine, *rest):
    pieces, others, outputs, inputs = rest[: n - 1], rest[n - 1 : -2], rest[-2], rest[-1]
    depth = factor.shape[2]
    t = lax.axis_index("tensor")
    total = product(grads, t * depth, factor)
    for s, piece in enumerate(pieces, 1):
        start = block_of(t, s, n) * depth + side() * piece.shape[2]
        total = total + product(grads, start, piece)
    outputs[...] = total
    ins = mine[...]
    for other in others:
        ins = ins + other[...].astype(F32)
    live = lax.broadcasted_iota(jnp.int32, ins.shape, 0) < length[0]
    inputs[...] = jnp.where(live, ins, 0.0).astype(BF16)


def example_gradient(n, depth, grads, outputs, inputs, *rest):
    pieces, wholes, out = rest[: n - 1], rest[n - 1 : -1], rest[-1]
    t = lax.axis_index("tensor")
    total = outputs[...]
    for s in range(1, n):
        start = block_of(t, s, n) * depth
        piece, whole = pieces[s - 1], wholes[s - 1]
        total = total + product(grads, start + 2 * piece.shape[2], whole)
        total = total + product(grads, start + (1 - side()) * piece.shape[2], piece)
    both = dot(inputs[...], total.astype(BF16), TN)
    layers = grads.shape[0]
    width = both.shape[1] // layers
    lane = lax.broadcasted_iota(jnp.int32, (width, both.shape[1]), 1)
    grad = both[:width]
    for l in range(1, layers):
        grad = jnp.where(lane >= l * width, both[l * width : (l + 1) * width], grad)
    grad = grad.astype(BF16)
    out[...] = jnp.concatenate(
        [grad[g * FOLD : (g + 1) * FOLD] for g in range(width // FOLD)], axis=1
    )


def score(n, order, grads, queries, queries_other, mine, theirs, odd_place):
    slots, nq = mine.shape
    even = [s for s in range(slots) if s.bit_count() % 2 == 0]
    odd = [s for s in range(slots) if s.bit_count() % 2 == 1]
    products = []
    for rows in (slice(0, nq * FOLD), slice(nq * FOLD, 2 * nq * FOLD)):
        for asked, chosen in ((queries, even), (queries_other, odd)):
            lhs = jnp.concatenate([grads[s] for s in chosen], axis=0)
            products.append(dot(lhs, asked[rows], NT))
    products = jnp.concatenate(products, axis=0)
    row = lax.broadcasted_iota(jnp.int32, products.shape, 0)
    column = lax.broadcasted_iota(jnp.int32, products.shape, 1)
    products = jnp.where((row ^ column) & (FOLD - 1) == 0, products, 0.0)
    sums = jnp.sum(products.reshape(2 * slots, FOLD, nq * FOLD), axis=1)
    fold = lax.broadcasted_iota(jnp.int32, (nq * FOLD, nq), 0)
    fold = fold - FOLD * lax.broadcasted_iota(jnp.int32, (nq * FOLD, nq), 1)
    fold = ((fold >= 0) & (fold < FOLD)).astype(F32)
    table = lax.dot_general(
        sums,
        fold,
        (((1,), (0,)), ((), ())),
        precision=lax.Precision.HIGHEST,
        preferred_element_type=F32,
    )
    odd_place[...] = jnp.full(odd_place.shape, lax.axis_index("dp") & 1, jnp.int32)
    core = lax.axis_index("query")
    place = lax.axis_index("dp") // 2 * n + lax.axis_index("tensor")
    kept, sent = place ^ (core * (slots // 2)), place ^ ((1 - core) * (slots // 2))
    for i, s in enumerate(even + odd):
        mine[pl.ds(kept ^ order[s], 1), :] = table[i : i + 1]
        theirs[pl.ds(sent ^ order[s], 1), :] = table[slots + i : slots + i + 1]


def shifted(x, axis, shift):
    n = lax.axis_size(axis)
    return lax.ppermute(x, axis, [(i, (i + shift) % n) for i in range(n)])


def flipped(x, axis, bit):
    n = lax.axis_size(axis)
    return lax.ppermute(x, axis, [(i, i ^ bit) for i in range(n)])


def crossed(x, axis, bit):
    cores = lax.axis_size("query")
    n = lax.axis_size(axis) * cores
    return lax.ppermute(x, (axis, "query"), [(i, i ^ (bit * cores + 1)) for i in range(n)])


def forwarded(x):
    n, cores = lax.axis_size("dp"), lax.axis_size("query")
    size = lax.axis_size("parts") * n * cores
    pairs = [(i, i ^ (n * cores if i % cores == 0 else cores)) for i in range(size)]
    return lax.ppermute(x, ("parts", "dp", "query"), pairs)


def local(acts, out_grads, lengths, proj_in, proj_out, query_grads):
    layers, rows, depth = acts.shape
    slots = out_grads.shape[1]
    width = proj_in.shape[2]
    nq = query_grads.shape[1]
    n = lax.axis_size("tensor")
    n_dp = lax.axis_size("dp")
    lanes = layers * width
    step = depth // 4

    factor = proj_out.transpose(0, 2, 1)
    piece, rest = call(
        cut,
        (
            jax.ShapeDtypeStruct((layers, width, step), BF16),
            jax.ShapeDtypeStruct((layers, width, depth - 2 * step), BF16),
        ),
        in_hbm(factor),
        specs=[ANY],
        scratch=[pltpu.SemaphoreType.DMA((2,))],
    )
    asked, piece = lax.optimization_barrier((query_grads, piece))
    firsts = [shifted(piece, "tensor", s) for s in range(1, n)]
    wholes = [shifted(rest, "tensor", s) for s in range(1, n)]
    seconds = [forwarded(first) for first in firsts]

    mine, *theirs = call(
        functools.partial(project_inputs, n),
        (
            jax.ShapeDtypeStruct((slots, lanes), F32),
            *[jax.ShapeDtypeStruct((slots, lanes), BF16)] * (n - 1),
        ),
        acts,
        proj_in.transpose(0, 2, 1),
        after=(rest,),
    )
    others = [shifted(block, "tensor", s) for s, block in enumerate(theirs, 1)]
    near = flipped(asked, "dp", 1)
    queries = call(
        functools.partial(fold_queries, width),
        jax.ShapeDtypeStruct((2 * nq * FOLD, width // FOLD * lanes), BF16),
        query_grads,
        near,
        after=(mine, firsts[0]),
        scratch=[pltpu.VMEM((width // FOLD, 2 * nq * FOLD, lanes), F32)],
    )
    queries_other = flipped(queries, "query", 1)

    outputs, inputs = call(
        functools.partial(early, n),
        (
            jax.ShapeDtypeStruct((slots, lanes), F32),
            jax.ShapeDtypeStruct((slots, lanes), BF16),
        ),
        lengths,
        out_grads,
        factor,
        mine,
        *firsts,
        *others,
        weight=EARLY,
    )
    grad = call(
        functools.partial(example_gradient, n, depth),
        jax.ShapeDtypeStruct((FOLD, width // FOLD * lanes), BF16),
        out_grads,
        outputs,
        inputs,
        *[in_vmem(x) for x in seconds],
        *[in_vmem(x) for x in wholes],
        after=(queries_other,),
    )
    steps = [("dp", 1 << b) for b in reversed(range(1, n_dp.bit_length() - 1))]
    steps += [("tensor", 1 << b) for b in range(n.bit_length() - 1)]
    grads = grad[None]
    order = [0]
    for axis, bit in steps:
        grads = jnp.concatenate([grads, crossed(grads, axis, bit)])
        order += [o ^ (bit if axis == "tensor" else bit * n // 2) for o in order]
    table = jax.ShapeDtypeStruct((len(order), nq), F32)
    top = len(order) // 2
    flag = jax.ShapeDtypeStruct((2, top, nq), jnp.int32)
    mine, theirs, odd_place = call(
        functools.partial(score, n, order), (table, table, flag), grads, queries, queries_other
    )
    got = crossed(theirs, "dp", 1)
    kept, sent = jnp.stack([mine[:top], got[:top]]), jnp.stack([mine[top:], got[top:]])
    kept = kept + flipped(sent, "query", 1)
    kept = jnp.where(odd_place == 0, kept, kept[::-1]).reshape(2, -1, n, nq)
    return kept.transpose(1, 0, 2, 3).reshape(-1, nq)


def solution(mesh):
    placed = (
        P("query", ("parts", "dp"), "tensor"),
        P("query", ("parts", "dp", "tensor"), None),
        P(("parts", "dp", "tensor")),
        P("query", "tensor", None),
        P("query", "tensor", None),
        P("query", ("dp", "tensor"), None),
    )
    return jax.shard_map(
        local,
        mesh=mesh,
        in_specs=placed,
        out_specs=P(("parts", "query"), ("dp", "tensor")),
        check_vma=False,
    )
```

time: 130 us -> 30 us (0.23)
  blocking collectives: 63.6 us -> 0 us
  waiting for transfers between devices: 41.9 us -> 9.86 us
  between operations: 14.6 us -> 0.75 us
  starting transfers between devices: 0.08 us -> 12 us
  matrix products: 8.5 us -> 0 us
  Pallas kernels: 0 us -> 3.77 us
  local copies, waits for them, and re-layouts: 1.37 us -> 2.77 us
    all_gather x2 -> x0, blocking collectives: 61.1 us -> none  [local(): lax.all_gather(example_grad, ('dp', 'tensor'), axis=0, tiled=True)]
    all_gather x1 -> x0, waiting for transfers between devices: 22.9 us -> none  [local(): whole_out = lax.all_gather(proj_out, 'tensor', axis=1, tiled=True)]
    reduce_scatter x2 -> x0, waiting for transfers between devices: 18.2 us -> none  [local(): lax.psum_scatter(jnp.dot(layer_acts, in_factor, preferred_element_type=jn...]
    ppermute x0 -> x10, starting transfers between devices: none -> 12 us  [the longest x3 5.03 us: shifted(): return lax.ppermute(x, axis, [(i, (i + shift) % n) for i in range(n)])]
    ppermute x0 -> x10, waiting for transfers between devices: none -> 9.86 us  [the longest x3 7.04 us: crossed(): lax.ppermute(x, (axis, 'query'), [(i, i ^ bit * cores + 1) for i in range...]
    dot_general x6 -> x0, matrix products: 8.5 us -> none  [the longest x2 4.51 us: local(): jnp.dot(layer_acts, in_factor, preferred_element_type=jnp.float32)]
    pallas_call x0 -> x6, Pallas kernels: none -> 3.77 us  [call(): pl.pallas_call(body, out_shape=out_shape, in_specs=specs + [ANY] * len(af...]
    unnamed x1 -> x0, blocking collectives: 2.46 us -> none
  transfers between devices with their start and end apart: 3 -> 10, of which waited for: 3 -> 5; matrix products, arithmetic and copies ran while one was open for 4% -> 0% of each run, Pallas kernels for 0% -> 5%
where the time goes in v4:
time: 30 us; the launch traced here: 29.8 us
  starting transfers between devices  12 us (40%)
  waiting for transfers between devices  9.86 us (33%)
  Pallas kernels  3.77 us (13%)
  local copies, waits for them, and re-layouts  2.77 us (9%)
  between operations  0.75 us (2%)
  other arithmetic  0.61 us (2%)
    ppermute x3, waiting for transfers between devices, crossed(): lax.ppermute(x, (axis, 'query'), [(i, i ^ bit * cores + 1) for i in range...  7.04 us
    ppermute x3, starting transfers between devices, shifted(): return lax.ppermute(x, axis, [(i, (i + shift) % n) for i in range(n)])  5.03 us
    pallas_call x6, Pallas kernels, call(): pl.pallas_call(body, out_shape=out_shape, in_specs=specs + [ANY] * len(af...  3.77 us
    ppermute x3, starting transfers between devices, crossed(): lax.ppermute(x, (axis, 'query'), [(i, i ^ bit * cores + 1) for i in range...  3.55 us
    unnamed x10, local copies, waits for them, and re-layouts  2.76 us
    ppermute x3, starting transfers between devices, flipped(): return lax.ppermute(x, axis, [(i, i ^ bit) for i in range(n)])  1.83 us
    ppermute x3, waiting for transfers between devices, shifted(): return lax.ppermute(x, axis, [(i, (i + shift) % n) for i in range(n)])  1.78 us
    ppermute x1, starting transfers between devices, forwarded(): return lax.ppermute(x, ('parts', 'dp', 'query'), pairs)  1.58 us
  transfers between devices with their start and end apart: 10, of which 5 were waited for; matrix products, arithmetic and copies ran while one was open for 0% of the time, Pallas kernels for 5%

profile of v4, /device:TPU:0, one launch (start us, length us, event | category | flops | bytes accessed | tf_op | source)
XLA Modules:
  0.0 29.8 jit_solution(14727557951033062640)
XLA Ops:
  0.0 1.2 %shard_map.64 = (bf16[2,64,512]{2,1,0:T(8,128)(2,1)S(1)}, bf16[2,64,1024]{2,1,0:T(8,128)(2,1)S(1)}) custom-call(bf16[2,64,2048]{2,1,0:T(8,128)(2,1)} %bitcast.12), custom_call_target="tpu_custom_call" | custom-call | flops 1 | bytes 1 | tf_op jit(solution)/shard_map/pallas_call | solution.py:31
  1.2 3.0 %collective-permute-start = (bf16[2,64,512]{2,1,0:T(8,128)(2,1)S(1)}, bf16[2,64,512]{2,1,0:T(8,128)(2,1)S(1)}, u32[]{:S(2)}, u32[]{:S(2)}) collective-permute-start(bf16[2,64,512]{2,1,0:T(8,128)(2,1)S(1)} %get-tuple-element.19), channel_id=1, source_target_pairs={{0,2},{2,0},{1,3},{3,1},{4,6},{6,4},{5,7},{7,5},{8,10},{10,8},{9,1... | collective-permute-start | bytes 393224 | tf_op jit(solution)/shard_map/ppermute | solution.py:181
  4.2 1.6 %collective-permute-start.4 = (bf16[2,8,4096]{2,1,0:T(8,128)(2,1)}, bf16[2,8,4096]{2,1,0:T(8,128)(2,1)S(1)}, u32[]{:S(2)}, u32[]{:S(2)}) collective-permute-start(bf16[2,8,4096]{2,1,0:T(8,128)(2,1)} %refs_0_.5), channel_id=1, source_target_pairs={{0,4},{4,0},{8,12},{12,8},{1,5},{5,1},{9,13},{13,9},{2,6},{6,2},{1... | collective-permute-start | bytes 393224 | tf_op jit(solution)/shard_map/ppermute | solution.py:186
  5.8 0.5 %collective-permute-start.3 = (bf16[2,64,1024]{2,1,0:T(8,128)(2,1)S(1)}, bf16[2,64,1024]{2,1,0:T(8,128)(2,1)S(1)}, u32[]{:S(2)}, u32[]{:S(2)}) collective-permute-start(bf16[2,64,1024]{2,1,0:T(8,128)(2,1)S(1)} %get-tuple-element.16.refs_2_), channel_id=1, source_target_pairs={{0,2},{2,0},{1,3},{3,1},{4,6},{6,4},{5,7},{7,5},{8,10},{10,8},{9,1... | collective-permute-start | bytes 786440 | tf_op jit(solution)/shard_map/ppermute | solution.py:181
  6.3 1.6 %copy-done.1 = bf16[2,256,2048]{2,1,0:T(8,128)(2,1)S(1)} copy-done((bf16[2,256,2048]{2,1,0:T(8,128)(2,1)S(1)}, bf16[2,256,2048]{2,1,0:T(8,128)(2,1)}, u32[]{:S(2)}) %copy-start.1) | copy-done | bytes 2097176
  7.9 1.0 %copy-done.3 = bf16[2,2048,64]{1,2,0:T(8,128)(2,1)S(1)} copy-done((bf16[2,2048,64]{1,2,0:T(8,128)(2,1)S(1)}, bf16[2,2048,64]{1,2,0:T(8,128)(2,1)}, u32[]{:S(2)}) %copy-start.3) | copy-done | bytes 524312
  8.9 0.8 %shard_map.65 = (f32[128,128]{1,0:T(8,128)S(1)}, bf16[128,128]{1,0:T(8,128)(2,1)S(1)}) custom-call(bf16[2,256,2048]{2,1,0:T(8,128)(2,1)S(1)} %copy-done.1, bf16[2,64,2048]{2,1,0:T(8,128)(2,1)S(1)} %bitcast.14, bf16[2,64,1024]{2,1,0:T(8,128)(2,1)S(1)} %get-tuple-element.16.refs_2_), custom_call_target="tpu_custom_call" | custom-call | flops 1 | bytes 1 | tf_op jit(solution)/shard_map/pallas_call | solution.py:31
  9.7 0.0 collective-permute-done.refs_4_.refs_3_
  9.7 0.0 collective-permute-done.4.refs_1_
  9.7 0.1 copy-done.4
  9.8 0.3 shard_map.67.refs_1_
  10.1 0.1 collective-permute-start.5
  10.2 1.6 %collective-permute-start.2 = (bf16[2,64,512]{2,1,0:T(8,128)(2,1)S(1)}, bf16[2,64,512]{2,1,0:T(8,128)(2,1)S(1)}, u32[]{:S(2)}, u32[]{:S(2)}) collective-permute-start(bf16[2,64,512]{2,1,0:T(8,128)(2,1)S(1)} %collective-permute-done.refs_4_.refs_3_), channel_id=1, source_target_pairs={{0,16},{1,5},{4,20},{5,1},{8,24},{9,13},{12,28},{13,9},{16,0},{17,... | collective-permute-start | bytes 393224 | tf_op jit(solution)/shard_map/ppermute | solution.py:199
  11.8 1.5 %collective-permute-start.1 = (bf16[128,128]{1,0:T(8,128)(2,1)S(1)}, bf16[128,128]{1,0:T(8,128)(2,1)S(1)}, u32[]{:S(2)}, u32[]{:S(2)}) collective-permute-start(bf16[128,128]{1,0:T(8,128)(2,1)S(1)} %get-tuple-element.20), channel_id=1, source_target_pairs={{0,2},{2,0},{1,3},{3,1},{4,6},{6,4},{5,7},{7,5},{8,10},{10,8},{9,1... | collective-permute-start | bytes 98312 | tf_op jit(solution)/shard_map/ppermute | solution.py:181
  13.9 1.8 %collective-permute-done.1.refs_5_ = bf16[128,128]{1,0:T(8,128)(2,1)S(1)} collective-permute-done((bf16[128,128]{1,0:T(8,128)(2,1)S(1)}, bf16[128,128]{1,0:T(8,128)(2,1)S(1)}, u32[]{:S(2)}, u32[]{:S(2)}) %collective-permute-start.1) | collective-permute-done | bytes 32800 | tf_op jit(solution)/shard_map/ppermute | solution.py:181
  15.7 0.0 copy-done
  15.7 0.0 copy-done.2
  15.7 0.6 %shard_map.66 = (f32[128,128]{1,0:T(8,128)S(1)}, bf16[128,128]{1,0:T(8,128)(2,1)S(1)}) custom-call(s32[1]{0:T(128)S(6)} %copy.7.refs_0_, bf16[2,128,4096]{2,1,0:T(8,128)(2,1)S(1)} %copy-done, bf16[2,64,2048]{2,1,0:T(8,128)(2,1)S(1)} %bitcast.13, f32[128,128]{1,0:T(8,128)S(1)} %get-tuple-element.17.refs_3_.refs_2_, ...), custom_call_target="tpu_custom_call" | custom-call | flops 1 | bytes 1 | tf_op jit(solution)/shard_map/pallas_call | solution.py:31
  16.3 0.0 collective-permute-done.2.refs_3_
  16.3 0.0 collective-permute-done.3.refs_4_
  16.3 0.0 collective-permute-done.5.refs_5_.refs_2_
  16.3 0.5 %shard_map.68 = bf16[16,512]{1,0:T(8,128)(2,1)S(1)} custom-call(bf16[2,128,4096]{2,1,0:T(8,128)(2,1)S(1)} %copy-done, f32[128,128]{1,0:T(8,128)S(1)} %get-tuple-element.21.refs_1_, bf16[128,128]{1,0:T(8,128)(2,1)S(1)} %get-tuple-element.22.refs_2_, bf16[2,64,512]{2,1,0:T(8,128)(2,1)S(1)} %collective-permute-done.2.refs_3_, ...), custom_call_target="tpu_custom_call" | custom-call | flops 1 | bytes 1 | tf_op jit(solution)/shard_map/pallas_call | solution.py:31
  16.9 1.1 %collective-permute-start.6 = (bf16[1,16,512]{2,1,0:T(8,128)(2,1)S(1)}, bf16[1,16,512]{2,1,0:T(8,128)(2,1)S(1)}, u32[]{:S(2)}, u32[]{:S(2)}) collective-permute-start(bf16[1,16,512]{2,1,0:T(8,128)(2,1)S(1)} %bitcast.15), channel_id=1, source_target_pairs={{0,9},{1,8},{4,13},{5,12},{8,1},{9,0},{12,5},{13,4},{2,11},{3,10},... | collective-permute-start | bytes 49160 | tf_op jit(solution)/shard_map/ppermute | solution.py:192
  18.0 3.0 %collective-permute-done.6 = bf16[1,16,512]{2,1,0:T(8,128)(2,1)S(1)} collective-permute-done((bf16[1,16,512]{2,1,0:T(8,128)(2,1)S(1)}, bf16[1,16,512]{2,1,0:T(8,128)(2,1)S(1)}, u32[]{:S(2)}, u32[]{:S(2)}) %collective-permute-start.6) | collective-permute-done | bytes 16416 | tf_op jit(solution)/shard_map/ppermute | solution.py:192
  21.0 1.5 %collective-permute-start.7 = (bf16[2,16,512]{2,1,0:T(8,128)(2,1)S(1)}, bf16[2,16,512]{2,1,0:T(8,128)(2,1)S(1)}, u32[]{:S(2)}, u32[]{:S(2)}) collective-permute-start(bf16[2,16,512]{2,1,0:T(8,128)(2,1)S(1)} %pad_maximum_fusion.1), channel_id=1, source_target_pairs={{0,3},{1,2},{2,1},{3,0},{4,7},{5,6},{6,5},{7,4},{8,11},{9,10},{10,... | collective-permute-start | bytes 98312 | tf_op jit(solution)/shard_map/ppermute | solution.py:192
  22.5 1.9 %collective-permute-done.7 = bf16[2,16,512]{2,1,0:T(8,128)(2,1)S(1)} collective-permute-done((bf16[2,16,512]{2,1,0:T(8,128)(2,1)S(1)}, bf16[2,16,512]{2,1,0:T(8,128)(2,1)S(1)}, u32[]{:S(2)}, u32[]{:S(2)}) %collective-permute-start.7) | collective-permute-done | bytes 32800 | tf_op jit(solution)/shard_map/ppermute | solution.py:192
  24.4 0.4 %shard_map.69 = (f32[4,8]{1,0:T(4,128)S(1)}, f32[4,8]{1,0:T(4,128)S(1)}, s32[2,2,8]{2,1,0:T(2,128)S(1)}) custom-call(bf16[4,16,512]{2,1,0:T(8,128)(2,1)S(1)} %pad_maximum_fusion.refs_0_, bf16[256,512]{1,0:T(8,128)(2,1)S(1)} %shard_map.67.refs_1_, bf16[256,512]{1,0:T(8,128)(2,1)S(1)} %collective-permute-done.5.refs_5_.refs_2_), custom_call_target="tpu_custom_call" | custom-call | flops 1 | bytes 1 | tf_op jit(solution)/shard_map/pallas_call | solution.py:31
  24.9 0.9 %collective-permute-start.8 = (f32[4,8]{1,0:T(4,128)S(1)}, f32[4,8]{1,0:T(4,128)S(1)}, u32[]{:S(2)}, u32[]{:S(2)}) collective-permute-start(f32[4,8]{1,0:T(4,128)S(1)} %get-tuple-element.26), channel_id=1, source_target_pairs={{0,5},{1,4},{4,1},{5,0},{8,13},{9,12},{12,9},{13,8},{2,7},{3,6},{6... | collective-permute-start | bytes 392 | tf_op jit(solution)/shard_map/ppermute | solution.py:192
  25.7 2.2 %collective-permute-done.8 = f32[4,8]{1,0:T(4,128)S(1)} collective-permute-done((f32[4,8]{1,0:T(4,128)S(1)}, f32[4,8]{1,0:T(4,128)S(1)}, u32[]{:S(2)}, u32[]{:S(2)}) %collective-permute-start.8) | collective-permute-done | bytes 160 | tf_op jit(solution)/shard_map/ppermute | solution.py:192
  27.9 0.2 collective-permute-start.9
  28.1 1.0 %collective-permute-done.9 = f32[2,2,8]{2,1,0:T(2,128)S(1)} collective-permute-done((f32[2,2,8]{2,1,0:T(2,128)S(1)}, f32[2,2,8]{2,1,0:T(2,128)S(1)}, u32[]{:S(2)}, u32[]{:S(2)}) %collective-permute-start.9) | collective-permute-done | bytes 160 | tf_op jit(solution)/shard_map/ppermute | solution.py:186
  29.2 0.6 %compare_select_fusion = f32[2,2,8]{2,1,0:T(2,128)} fusion(f32[2,2,8]{2,1,0:T(2,128)S(1)} %maximum_add_fusion, s32[2,2,8]{2,1,0:T(2,128)S(1)} %get-tuple-element.24), kind=kLoop, calls=%fused_computation.2 | loop fusion | flops 64 | bytes 384 | tf_op jit(solution)/shard_map/jit(_where)/select_n | solution.py:290
  (11 shorter events, 0.0 us)
Async XLA Ops:
  0.0 15.7 %copy-start = (bf16[2,128,4096]{2,1,0:T(8,128)(2,1)S(1)}, bf16[2,128,4096]{2,1,0:T(8,128)(2,1)}, u32[]{:S(2)}) copy-start(bf16[2,128,4096]{2,1,0:T(8,128)(2,1)} %refs_0_.6) | copy-start | bytes 6291460
  1.2 8.5 %collective-permute-start = (bf16[2,64,512]{2,1,0:T(8,128)(2,1)S(1)}, bf16[2,64,512]{2,1,0:T(8,128)(2,1)S(1)}, u32[]{:S(2)}, u32[]{:S(2)}) collective-permute-start(bf16[2,64,512]{2,1,0:T(8,128)(2,1)S(1)} %get-tuple-element.19), channel_id=1, source_target_pairs={{0,2},{2,0},{1,3},{3,1},{4,6},{6,4},{5,7},{7,5},{8,10},{10,8},{9,1... | collective-permute-start | bytes 393224 | tf_op jit(solution)/shard_map/ppermute | solution.py:181
  4.2 5.5 %collective-permute-start.4 = (bf16[2,8,4096]{2,1,0:T(8,128)(2,1)}, bf16[2,8,4096]{2,1,0:T(8,128)(2,1)S(1)}, u32[]{:S(2)}, u32[]{:S(2)}) collective-permute-start(bf16[2,8,4096]{2,1,0:T(8,128)(2,1)} %refs_0_.5), channel_id=1, source_target_pairs={{0,4},{4,0},{8,12},{12,8},{1,5},{5,1},{9,13},{13,9},{2,6},{6,2},{1... | collective-permute-start | bytes 393224 | tf_op jit(solution)/shard_map/ppermute | solution.py:186
  5.8 10.5 %collective-permute-start.3 = (bf16[2,64,1024]{2,1,0:T(8,128)(2,1)S(1)}, bf16[2,64,1024]{2,1,0:T(8,128)(2,1)S(1)}, u32[]{:S(2)}, u32[]{:S(2)}) collective-permute-start(bf16[2,64,1024]{2,1,0:T(8,128)(2,1)S(1)} %get-tuple-element.16.refs_2_), channel_id=1, source_target_pairs={{0,2},{2,0},{1,3},{3,1},{4,6},{6,4},{5,7},{7,5},{8,10},{10,8},{9,1... | collective-permute-start | bytes 786440 | tf_op jit(solution)/shard_map/ppermute | solution.py:181
  6.3 1.6 %copy-start.1 = (bf16[2,256,2048]{2,1,0:T(8,128)(2,1)S(1)}, bf16[2,256,2048]{2,1,0:T(8,128)(2,1)}, u32[]{:S(2)}) copy-start(bf16[2,256,2048]{2,1,0:T(8,128)(2,1)} %refs_0_.4) | copy-start | bytes 6291460
  7.9 1.0 %copy-start.3 = (bf16[2,2048,64]{1,2,0:T(8,128)(2,1)S(1)}, bf16[2,2048,64]{1,2,0:T(8,128)(2,1)}, u32[]{:S(2)}) copy-start(bf16[2,2048,64]{1,2,0:T(8,128)(2,1)} %param.9) | copy-start | bytes 1572868
  8.9 0.9 %copy-start.4 = (bf16[2,8,4096]{2,1,0:T(8,128)(2,1)S(1)}, bf16[2,8,4096]{2,1,0:T(8,128)(2,1)}, u32[]{:S(2)}) copy-start(bf16[2,8,4096]{2,1,0:T(8,128)(2,1)} %refs_0_.5) | copy-start | bytes 393220
  8.9 6.8 %copy-start.2 = (bf16[2,2048,64]{1,2,0:T(8,128)(2,1)S(1)}, bf16[2,2048,64]{1,2,0:T(8,128)(2,1)}, u32[]{:S(2)}) copy-start(bf16[2,2048,64]{1,2,0:T(8,128)(2,1)} %param.10) | copy-start | bytes 1572868
  10.1 6.2 %collective-permute-start.5 = (bf16[256,512]{1,0:T(8,128)(2,1)S(1)}, bf16[256,512]{1,0:T(8,128)(2,1)S(1)}, u32[]{:S(2)}, u32[]{:S(2)}) collective-permute-start(bf16[256,512]{1,0:T(8,128)(2,1)S(1)} %shard_map.67.refs_1_), channel_id=1, source_target_pairs={{0,1},{1,0},{2,3},{3,2},{4,5},{5,4},{6,7},{7,6},{8,9},{9,8},{10,11... | collective-permute-start | bytes 786440 | tf_op jit(solution)/shard_map/ppermute | solution.py:186
  10.2 6.1 %collective-permute-start.2 = (bf16[2,64,512]{2,1,0:T(8,128)(2,1)S(1)}, bf16[2,64,512]{2,1,0:T(8,128)(2,1)S(1)}, u32[]{:S(2)}, u32[]{:S(2)}) collective-permute-start(bf16[2,64,512]{2,1,0:T(8,128)(2,1)S(1)} %collective-permute-done.refs_4_.refs_3_), channel_id=1, source_target_pairs={{0,16},{1,5},{4,20},{5,1},{8,24},{9,13},{12,28},{13,9},{16,0},{17,... | collective-permute-start | bytes 393224 | tf_op jit(solution)/shard_map/ppermute | solution.py:199
  11.8 3.9 %collective-permute-start.1 = (bf16[128,128]{1,0:T(8,128)(2,1)S(1)}, bf16[128,128]{1,0:T(8,128)(2,1)S(1)}, u32[]{:S(2)}, u32[]{:S(2)}) collective-permute-start(bf16[128,128]{1,0:T(8,128)(2,1)S(1)} %get-tuple-element.20), channel_id=1, source_target_pairs={{0,2},{2,0},{1,3},{3,1},{4,6},{6,4},{5,7},{7,5},{8,10},{10,8},{9,1... | collective-permute-start | bytes 98312 | tf_op jit(solution)/shard_map/ppermute | solution.py:181
  16.9 4.1 %collective-permute-start.6 = (bf16[1,16,512]{2,1,0:T(8,128)(2,1)S(1)}, bf16[1,16,512]{2,1,0:T(8,128)(2,1)S(1)}, u32[]{:S(2)}, u32[]{:S(2)}) collective-permute-start(bf16[1,16,512]{2,1,0:T(8,128)(2,1)S(1)} %bitcast.15), channel_id=1, source_target_pairs={{0,9},{1,8},{4,13},{5,12},{8,1},{9,0},{12,5},{13,4},{2,11},{3,10},... | collective-permute-start | bytes 49160 | tf_op jit(solution)/shard_map/ppermute | solution.py:192
  21.0 3.4 %collective-permute-start.7 = (bf16[2,16,512]{2,1,0:T(8,128)(2,1)S(1)}, bf16[2,16,512]{2,1,0:T(8,128)(2,1)S(1)}, u32[]{:S(2)}, u32[]{:S(2)}) collective-permute-start(bf16[2,16,512]{2,1,0:T(8,128)(2,1)S(1)} %pad_maximum_fusion.1), channel_id=1, source_target_pairs={{0,3},{1,2},{2,1},{3,0},{4,7},{5,6},{6,5},{7,4},{8,11},{9,10},{10,... | collective-permute-start | bytes 98312 | tf_op jit(solution)/shard_map/ppermute | solution.py:192
  24.9 3.1 %collective-permute-start.8 = (f32[4,8]{1,0:T(4,128)S(1)}, f32[4,8]{1,0:T(4,128)S(1)}, u32[]{:S(2)}, u32[]{:S(2)}) collective-permute-start(f32[4,8]{1,0:T(4,128)S(1)} %get-tuple-element.26), channel_id=1, source_target_pairs={{0,5},{1,4},{4,1},{5,0},{8,13},{9,12},{12,9},{13,8},{2,7},{3,6},{6... | collective-permute-start | bytes 392 | tf_op jit(solution)/shard_map/ppermute | solution.py:192
  27.9 1.2 %collective-permute-start.9 = (f32[2,2,8]{2,1,0:T(2,128)S(1)}, f32[2,2,8]{2,1,0:T(2,128)S(1)}, u32[]{:S(2)}, u32[]{:S(2)}) collective-permute-start(f32[2,2,8]{2,1,0:T(2,128)S(1)} %pad_maximum_fusion.2), channel_id=1, source_target_pairs={{0,1},{1,0},{2,3},{3,2},{4,5},{5,4},{6,7},{7,6},{8,9},{9,8},{10,11... | collective-permute-start | bytes 392 | tf_op jit(solution)/shard_map/ppermute | solution.py:186

commit v5 on v4

--- a/solution.py
+++ b/solution.py
@@ -57,30 +57,41 @@
     return jnp.where(lax.axis_index("query") == 0, lax.axis_index("parts"), lax.axis_index("dp") & 1)
 
 
-def cut(factor, piece, rest, sems):
+def clear(out):
+    out[...] = jnp.zeros(out.shape, out.dtype)
+
+
+def cut(factor, piece, sem):
     width = piece.shape[2]
     start = pl.multiple_of(side() * width, 128)
+    copy = pltpu.make_async_copy(factor.at[:, :, pl.ds(start, width)], piece, sem)
+    copy.start()
+    copy.wait()
+
+
+def project_inputs(n, acts, factor, factor_out, mine, *rest):
+    parcels, sems = rest[:-1], rest[-1]
+    slots, lanes = mine.shape
+    layers, width, size = parcels[0].shape
+    tail = pl.ds(factor_out.shape[2] - (size - lanes), size - lanes)
     copies = [
-        pltpu.make_async_copy(factor.at[:, :, pl.ds(start, width)], piece, sems.at[0]),
-        pltpu.make_async_copy(factor.at[:, :, pl.ds(2 * width, rest.shape[2])], rest, sems.at[1]),
+        pltpu.make_async_copy(factor_out.at[:, :, tail], out.at[:, :, : size - lanes], sems.at[s])
+        for s, out in enumerate(parcels)
     ]
     for copy in copies:
         copy.start()
-    for copy in copies:
-        copy.wait()
-
-
-def project_inputs(n, acts, factor, mine, *theirs):
-    slots = mine.shape[0]
     t = lax.axis_index("tensor")
-    total = jnp.concatenate(
-        [dot(acts[l], factor[l], NT) for l in range(acts.shape[0])], axis=1
-    )
-    for s, out in enumerate((mine, *theirs)):
+    total = jnp.concatenate([dot(acts[l], factor[l], NT) for l in range(layers)], axis=1)
+    for s in range(n):
         block = total[:slots]
         for i in range(1, n):
             block = jnp.where(lax.rem(t + s, n) == i, total[i * slots : (i + 1) * slots], block)
-        out[...] = block.astype(out.dtype)
+        if s == 0:
+            mine[...] = block
+        else:
+            parcels[s - 1][:, :, size - lanes :] = block.astype(BF16).reshape(layers, width, lanes)
+    for copy in copies:
+        copy.wait()
 
 
 def fold_queries(width, own, near, out, rows):
@@ -105,32 +116,33 @@
     )
 
 
-def early(n, length, grads, factor, mine, *rest):
-    pieces, others, outputs, inputs = rest[: n - 1], rest[n - 1 : -2], rest[-2], rest[-1]
+def early(n, grads, factor, *rest):
+    pieces, out = rest[:-1], rest[-1]
     depth = factor.shape[2]
     t = lax.axis_index("tensor")
     total = product(grads, t * depth, factor)
     for s, piece in enumerate(pieces, 1):
         start = block_of(t, s, n) * depth + side() * piece.shape[2]
         total = total + product(grads, start, piece)
-    outputs[...] = total
-    ins = mine[...]
-    for other in others:
-        ins = ins + other[...].astype(F32)
-    live = lax.broadcasted_iota(jnp.int32, ins.shape, 0) < length[0]
-    inputs[...] = jnp.where(live, ins, 0.0).astype(BF16)
-
-
-def example_gradient(n, depth, grads, outputs, inputs, *rest):
-    pieces, wholes, out = rest[: n - 1], rest[n - 1 : -1], rest[-1]
+    out[...] = total
+
+
+def example_gradient(n, depth, length, grads, outputs, inputs, *rest):
+    pieces, parcels, out = rest[: n - 1], rest[n - 1 : -1], rest[-1]
+    slots, lanes = inputs.shape
     t = lax.axis_index("tensor")
     total = outputs[...]
-    for s in range(1, n):
+    ins = inputs[...]
+    for s, (piece, parcel) in enumerate(zip(pieces, parcels), 1):
         start = block_of(t, s, n) * depth
-        piece, whole = pieces[s - 1], wholes[s - 1]
-        total = total + product(grads, start + 2 * piece.shape[2], whole)
-        total = total + product(grads, start + (1 - side()) * piece.shape[2], piece)
-    both = dot(inputs[...], total.astype(BF16), TN)
+        width = piece.shape[2]
+        whole = parcel.at[:, :, : parcel.shape[2] - lanes]
+        total = total + product(grads, start + 2 * width, whole)
+        total = total + product(grads, start + (1 - side()) * width, piece)
+        ins = ins + parcel[:, :, parcel.shape[2] - lanes :].reshape(slots, lanes).astype(F32)
+    live = lax.broadcasted_iota(jnp.int32, ins.shape, 0) < length[0]
+    ins = jnp.where(live, ins, 0.0).astype(BF16)
+    both = dot(ins, total.astype(BF16), TN)
     layers = grads.shape[0]
     width = both.shape[1] // layers
     lane = lax.broadcasted_iota(jnp.int32, (width, both.shape[1]), 1)
@@ -207,70 +219,68 @@
     n = lax.axis_size("tensor")
     n_dp = lax.axis_size("dp")
     lanes = layers * width
-    step = depth // 4
+    step = depth * 5 // 16 // 128 * 128
 
     factor = proj_out.transpose(0, 2, 1)
-    piece, rest = call(
+    piece = call(
         cut,
-        (
-            jax.ShapeDtypeStruct((layers, width, step), BF16),
-            jax.ShapeDtypeStruct((layers, width, depth - 2 * step), BF16),
-        ),
+        jax.ShapeDtypeStruct((layers, width, step), BF16),
         in_hbm(factor),
         specs=[ANY],
-        scratch=[pltpu.SemaphoreType.DMA((2,))],
-    )
-    asked, piece = lax.optimization_barrier((query_grads, piece))
+        scratch=[pltpu.SemaphoreType.DMA],
+    )
     firsts = [shifted(piece, "tensor", s) for s in range(1, n)]
-    wholes = [shifted(rest, "tensor", s) for s in range(1, n)]
-    seconds = [forwarded(first) for first in firsts]
-
-    mine, *theirs = call(
+
+    token = call(
+        clear, jax.ShapeDtypeStruct((8, 128), F32), after=(piece, *[in_hbm(x) for x in (acts, out_grads)])
+    )
+    asked, token = lax.optimization_barrier((query_grads, token))
+    firsts = [shifted(piece, "tensor", s) for s in range(1, n)]
+
+    near = flipped(asked, "dp", 1)
+    mine, *parcels = call(
         functools.partial(project_inputs, n),
         (
             jax.ShapeDtypeStruct((slots, lanes), F32),
-            *[jax.ShapeDtypeStruct((slots, lanes), BF16)] * (n - 1),
+            *[jax.ShapeDtypeStruct((layers, width, depth - 2 * step + lanes), BF16)] * (n - 1),
         ),
         acts,
         proj_in.transpose(0, 2, 1),
-        after=(rest,),
-    )
-    others = [shifted(block, "tensor", s) for s, block in enumerate(theirs, 1)]
-    near = flipped(asked, "dp", 1)
+        in_hbm(factor),
+        after=(token,),
+        specs=[VMEM, VMEM, ANY],
+        scratch=[pltpu.SemaphoreType.DMA((n - 1,))],
+    )
+    parcels = [shifted(parcel, "tensor", s) for s, parcel in enumerate(parcels, 1)]
+    firsts, mine, near = lax.optimization_barrier((firsts, mine, near))
+    seconds = [forwarded(first) for first in firsts]
+    outputs = call(
+        functools.partial(early, n),
+        jax.ShapeDtypeStruct((slots, lanes), F32),
+        out_grads,
+        factor,
+        *firsts,
+        after=(near,),
+    )
+    grad = call(
+        functools.partial(example_gradient, n, depth),
+        jax.ShapeDtypeStruct((FOLD, width // FOLD * lanes), BF16),
+        lengths,
+        out_grads,
+        outputs,
+        mine,
+        *[in_vmem(x) for x in seconds],
+        *[in_vmem(x) for x in parcels],
+    )
     queries = call(
         functools.partial(fold_queries, width),
         jax.ShapeDtypeStruct((2 * nq * FOLD, width // FOLD * lanes), BF16),
         query_grads,
         near,
-        after=(mine, firsts[0]),
+        after=(grad,),
         scratch=[pltpu.VMEM((width // FOLD, 2 * nq * FOLD, lanes), F32)],
     )
     queries_other = flipped(queries, "query", 1)
-
-    outputs, inputs = call(
-        functools.partial(early, n),
-        (
-            jax.ShapeDtypeStruct((slots, lanes), F32),
-            jax.ShapeDtypeStruct((slots, lanes), BF16),
-        ),
-        lengths,
-        out_grads,
-        factor,
-        mine,
-        *firsts,
-        *others,
-        weight=EARLY,
-    )
-    grad = call(
-        functools.partial(example_gradient, n, depth),
-        jax.ShapeDtypeStruct((FOLD, width // FOLD * lanes), BF16),
-        out_grads,
-        outputs,
-        inputs,
-        *[in_vmem(x) for x in seconds],
-        *[in_vmem(x) for x in wholes],
-        after=(queries_other,),
-    )
     steps = [("dp", 1 << b) for b in reversed(range(1, n_dp.bit_length() - 1))]
     steps += [("tensor", 1 << b) for b in range(n.bit_length() - 1)]
     grads = grad[None]

time: 30 us -> 27.9 us (0.930)
  local copies, waits for them, and re-layouts: 2.77 us -> 0.03 us
  waiting for transfers between devices: 9.86 us -> 10.4 us
    unnamed x10, local copies, waits for them, and re-layouts: 2.76 us -> 0.03 us
    ppermute x3, starting transfers between devices: 1.83 us -> 4.55 us  [flipped(): return lax.ppermute(x, axis, [(i, i ^ bit) for i in range(n)])]
    ppermute x3, waiting for transfers between devices: 7.04 us -> 5.24 us  [crossed(): lax.ppermute(x, (axis, 'query'), [(i, i ^ bit * cores + 1) for i in range...]
    ppermute x3, waiting for transfers between devices: 1.05 us -> 2.63 us  [flipped(): return lax.ppermute(x, axis, [(i, i ^ bit) for i in range(n)])]
    ppermute x3 -> x2, starting transfers between devices: 5.03 us -> 3.8 us  [shifted(): return lax.ppermute(x, axis, [(i, (i + shift) % n) for i in range(n)])]
    ppermute x3, starting transfers between devices: 3.55 us -> 2.33 us  [crossed(): lax.ppermute(x, (axis, 'query'), [(i, i ^ bit * cores + 1) for i in range...]
    ppermute x1, waiting for transfers between devices: 0.01 us -> 0.86 us  [forwarded(): return lax.ppermute(x, ('parts', 'dp', 'query'), pairs)]
    ppermute x3 -> x2, waiting for transfers between devices: 1.78 us -> 1.69 us  [shifted(): return lax.ppermute(x, axis, [(i, (i + shift) % n) for i in range(n)])]
  transfers between devices with their start and end apart: 10 -> 9, of which waited for: 5 -> 7; matrix products, arithmetic and copies ran while one was open for 0% -> 0% of each run, Pallas kernels for 5% -> 7%
where the time goes in v5:
time: 27.9 us; the launch traced here: 27.8 us
  starting transfers between devices  12.2 us (44%)
  waiting for transfers between devices  10.4 us (37%)
  Pallas kernels  3.75 us (13%)
  between operations  0.75 us (3%)
  other arithmetic  0.61 us (2%)
    ppermute x3, waiting for transfers between devices, crossed(): lax.ppermute(x, (axis, 'query'), [(i, i ^ bit * cores + 1) for i in range...  5.24 us
    ppermute x3, starting transfers between devices, flipped(): return lax.ppermute(x, axis, [(i, i ^ bit) for i in range(n)])  4.55 us
    ppermute x2, starting transfers between devices, shifted(): return lax.ppermute(x, axis, [(i, (i + shift) % n) for i in range(n)])  3.8 us
    pallas_call x7, Pallas kernels, call(): pl.pallas_call(body, out_shape=out_shape, in_specs=specs + [ANY] * len(af...  3.75 us
    ppermute x3, waiting for transfers between devices, flipped(): return lax.ppermute(x, axis, [(i, i ^ bit) for i in range(n)])  2.63 us
    ppermute x3, starting transfers between devices, crossed(): lax.ppermute(x, (axis, 'query'), [(i, i ^ bit * cores + 1) for i in range...  2.33 us
    ppermute x2, waiting for transfers between devices, shifted(): return lax.ppermute(x, axis, [(i, (i + shift) % n) for i in range(n)])  1.69 us
    ppermute x1, starting transfers between devices, forwarded(): return lax.ppermute(x, ('parts', 'dp', 'query'), pairs)  1.52 us
  transfers between devices with their start and end apart: 9, of which 7 were waited for; matrix products, arithmetic and copies ran while one was open for 0% of the time, Pallas kernels for 7%

profile of v5, /device:TPU:0, one launch (start us, length us, event | category | flops | bytes accessed | tf_op | source)
XLA Modules:
  0.0 27.8 jit_solution(11699997434863372402)
XLA Ops:
  0.0 0.9 %shard_map.64.refs_0_ = bf16[2,64,640]{2,1,0:T(8,128)(2,1)S(1)} custom-call(bf16[2,64,2048]{2,1,0:T(8,128)(2,1)} %bitcast.12), custom_call_target="tpu_custom_call" | custom-call | flops 1 | bytes 1 | tf_op jit(solution)/shard_map/pallas_call | solution.py:31
  0.9 0.0 copy-start.4
  0.9 0.0 copy-start.1
  1.0 0.0 copy-start.3
  1.0 3.0 %collective-permute-start = (bf16[2,64,640]{2,1,0:T(8,128)(2,1)S(1)}, bf16[2,64,640]{2,1,0:T(8,128)(2,1)S(1)}, u32[]{:S(2)}, u32[]{:S(2)}) collective-permute-start(bf16[2,64,640]{2,1,0:T(8,128)(2,1)S(1)} %shard_map.64.refs_0_), channel_id=1, source_target_pairs={{0,2},{2,0},{1,3},{3,1},{4,6},{6,4},{5,7},{7,5},{8,10},{10,8},{9,1... | collective-permute-start | bytes 491528 | tf_op jit(solution)/shard_map/ppermute | solution.py:193
  4.0 0.0 copy-done.4
  4.0 1.6 %collective-permute-start.1 = (bf16[2,8,4096]{2,1,0:T(8,128)(2,1)S(1)}, bf16[2,8,4096]{2,1,0:T(8,128)(2,1)S(1)}, u32[]{:S(2)}, u32[]{:S(2)}) collective-permute-start(bf16[2,8,4096]{2,1,0:T(8,128)(2,1)S(1)} %copy-done.4), channel_id=1, source_target_pairs={{0,4},{4,0},{8,12},{12,8},{1,5},{5,1},{9,13},{13,9},{2,6},{6,2},{1... | collective-permute-start | bytes 393224 | tf_op jit(solution)/shard_map/ppermute | solution.py:198
  5.6 0.0 copy-done.1
  5.6 0.0 copy-done.3
  5.6 1.0 %shard_map.66 = (f32[128,128]{1,0:T(8,128)S(1)}, bf16[2,64,896]{2,1,0:T(8,128)(2,1)S(1)}) custom-call(bf16[2,256,2048]{2,1,0:T(8,128)(2,1)S(1)} %copy-done.1, bf16[2,64,2048]{2,1,0:T(8,128)(2,1)S(1)} %bitcast.15, bf16[2,64,2048]{2,1,0:T(8,128)(2,1)} %bitcast.13, f32[8,128]{1,0:T(8,128)S(1)} %shard_map.65.refs_3_), custom_call_target="tpu_custom_call" | custom-call | flops 1 | bytes 1 | tf_op jit(solution)/shard_map/pallas_call | solution.py:31
  6.6 0.8 %collective-permute-start.3 = (bf16[2,64,896]{2,1,0:T(8,128)(2,1)S(1)}, bf16[2,64,896]{2,1,0:T(8,128)(2,1)S(1)}, u32[]{:S(2)}, u32[]{:S(2)}) collective-permute-start(bf16[2,64,896]{2,1,0:T(8,128)(2,1)S(1)} %get-tuple-element.21), channel_id=1, source_target_pairs={{0,2},{2,0},{1,3},{3,1},{4,6},{6,4},{5,7},{7,5},{8,10},{10,8},{9,1... | collective-permute-start | bytes 688136 | tf_op jit(solution)/shard_map/ppermute | solution.py:193
  7.4 1.6 %collective-permute-done.1.refs_3_.refs_1_ = bf16[2,8,4096]{2,1,0:T(8,128)(2,1)S(1)} collective-permute-done((bf16[2,8,4096]{2,1,0:T(8,128)(2,1)S(1)}, bf16[2,8,4096]{2,1,0:T(8,128)(2,1)S(1)}, u32[]{:S(2)}, u32[]{:S(2)}) %collective-permute-start.1) | collective-permute-done | bytes 131104 | tf_op jit(solution)/shard_map/ppermute | solution.py:198
  9.0 0.0 collective-permute-done.refs_2_
  9.0 1.5 %collective-permute-start.2 = (bf16[2,64,640]{2,1,0:T(8,128)(2,1)S(1)}, bf16[2,64,640]{2,1,0:T(8,128)(2,1)S(1)}, u32[]{:S(2)}, u32[]{:S(2)}) collective-permute-start(bf16[2,64,640]{2,1,0:T(8,128)(2,1)S(1)} %collective-permute-done.refs_2_), channel_id=1, source_target_pairs={{0,16},{1,5},{4,20},{5,1},{8,24},{9,13},{12,28},{13,9},{16,0},{17,... | collective-permute-start | bytes 491528 | tf_op jit(solution)/shard_map/ppermute | solution.py:211
  11.2 0.0 copy-done
  11.2 0.6 %shard_map.67.refs_2_ = f32[128,128]{1,0:T(8,128)S(1)} custom-call(bf16[2,128,4096]{2,1,0:T(8,128)(2,1)S(1)} %copy-done, bf16[2,64,2048]{2,1,0:T(8,128)(2,1)S(1)} %bitcast.14, bf16[2,64,640]{2,1,0:T(8,128)(2,1)S(1)} %collective-permute-done.refs_2_, bf16[2,8,4096]{2,1,0:T(8,128)(2,1)S(1)} %collective-permute-done.1.refs_3_.refs_1_), custom_call_target="tpu_custom_call" | custom-call | flops 1 | bytes 1 | tf_op jit(solution)/shard_map/pallas_call | solution.py:31
  11.8 1.7 %collective-permute-done.3.refs_5_ = bf16[2,64,896]{2,1,0:T(8,128)(2,1)S(1)} collective-permute-done((bf16[2,64,896]{2,1,0:T(8,128)(2,1)S(1)}, bf16[2,64,896]{2,1,0:T(8,128)(2,1)S(1)}, u32[]{:S(2)}, u32[]{:S(2)}) %collective-permute-start.3) | collective-permute-done | bytes 229408 | tf_op jit(solution)/shard_map/ppermute | solution.py:193
  13.5 0.9 %collective-permute-done.2.refs_4_ = bf16[2,64,640]{2,1,0:T(8,128)(2,1)S(1)} collective-permute-done((bf16[2,64,640]{2,1,0:T(8,128)(2,1)S(1)}, bf16[2,64,640]{2,1,0:T(8,128)(2,1)S(1)}, u32[]{:S(2)}, u32[]{:S(2)}) %collective-permute-start.2) | collective-permute-done | bytes 163872 | tf_op jit(solution)/shard_map/ppermute | solution.py:211
  14.3 0.5 %shard_map.68.refs_2_ = bf16[16,512]{1,0:T(8,128)(2,1)S(1)} custom-call(s32[1]{0:T(128)S(6)} %copy.7.refs_0_, bf16[2,128,4096]{2,1,0:T(8,128)(2,1)S(1)} %copy-done, f32[128,128]{1,0:T(8,128)S(1)} %shard_map.67.refs_2_, f32[128,128]{1,0:T(8,128)S(1)} %get-tuple-element.20.refs_3_, bf16[2,64,640]{2,1,0:T(8,128)(2,1)S(1)} %collective-permute-done.2.refs_4_, ...), custom_call_target="tpu_custom_call" | custom-call | flops 1 | bytes 1 | tf_op jit(solution)/shard_map/pallas_call | solution.py:31
  14.9 0.1 collective-permute-start.4
  15.0 0.3 %shard_map.69.refs_1_ = bf16[256,512]{1,0:T(8,128)(2,1)S(1)} custom-call(bf16[2,8,4096]{2,1,0:T(8,128)(2,1)S(1)} %copy-done.4, bf16[2,8,4096]{2,1,0:T(8,128)(2,1)S(1)} %collective-permute-done.1.refs_3_.refs_1_, bf16[16,512]{1,0:T(8,128)(2,1)S(1)} %shard_map.68.refs_2_), custom_call_target="tpu_custom_call" | custom-call | flops 1 | bytes 1 | tf_op jit(solution)/shard_map/pallas_call | solution.py:31
  15.3 2.7 %collective-permute-start.6 = (bf16[256,512]{1,0:T(8,128)(2,1)S(1)}, bf16[256,512]{1,0:T(8,128)(2,1)S(1)}, u32[]{:S(2)}, u32[]{:S(2)}) collective-permute-start(bf16[256,512]{1,0:T(8,128)(2,1)S(1)} %shard_map.69.refs_1_), channel_id=1, source_target_pairs={{0,1},{1,0},{2,3},{3,2},{4,5},{5,4},{6,7},{7,6},{8,9},{9,8},{10,11... | collective-permute-start | bytes 786440 | tf_op jit(solution)/shard_map/ppermute | solution.py:198
  18.0 1.0 %collective-permute-done.4 = bf16[1,16,512]{2,1,0:T(8,128)(2,1)S(1)} collective-permute-done((bf16[1,16,512]{2,1,0:T(8,128)(2,1)S(1)}, bf16[1,16,512]{2,1,0:T(8,128)(2,1)S(1)}, u32[]{:S(2)}, u32[]{:S(2)}) %collective-permute-start.4) | collective-permute-done | bytes 16416 | tf_op jit(solution)/shard_map/ppermute | solution.py:204
  19.0 0.9 %collective-permute-start.5 = (bf16[2,16,512]{2,1,0:T(8,128)(2,1)S(1)}, bf16[2,16,512]{2,1,0:T(8,128)(2,1)S(1)}, u32[]{:S(2)}, u32[]{:S(2)}) collective-permute-start(bf16[2,16,512]{2,1,0:T(8,128)(2,1)S(1)} %pad_maximum_fusion.1), channel_id=1, source_target_pairs={{0,3},{1,2},{2,1},{3,0},{4,7},{5,6},{6,5},{7,4},{8,11},{9,10},{10,... | collective-permute-start | bytes 98312 | tf_op jit(solution)/shard_map/ppermute | solution.py:204
  19.9 2.5 %collective-permute-done.5 = bf16[2,16,512]{2,1,0:T(8,128)(2,1)S(1)} collective-permute-done((bf16[2,16,512]{2,1,0:T(8,128)(2,1)S(1)}, bf16[2,16,512]{2,1,0:T(8,128)(2,1)S(1)}, u32[]{:S(2)}, u32[]{:S(2)}) %collective-permute-start.5) | collective-permute-done | bytes 32800 | tf_op jit(solution)/shard_map/ppermute | solution.py:204
  22.4 0.0 collective-permute-done.6.refs_2_
  22.4 0.4 %shard_map.70 = (f32[4,8]{1,0:T(4,128)S(1)}, f32[4,8]{1,0:T(4,128)S(1)}, s32[2,2,8]{2,1,0:T(2,128)S(1)}) custom-call(bf16[4,16,512]{2,1,0:T(8,128)(2,1)S(1)} %pad_maximum_fusion.refs_0_, bf16[256,512]{1,0:T(8,128)(2,1)S(1)} %shard_map.69.refs_1_, bf16[256,512]{1,0:T(8,128)(2,1)S(1)} %collective-permute-done.6.refs_2_), custom_call_target="tpu_custom_call" | custom-call | flops 1 | bytes 1 | tf_op jit(solution)/shard_map/pallas_call | solution.py:31
  22.9 1.4 %collective-permute-start.7 = (f32[4,8]{1,0:T(4,128)S(1)}, f32[4,8]{1,0:T(4,128)S(1)}, u32[]{:S(2)}, u32[]{:S(2)}) collective-permute-start(f32[4,8]{1,0:T(4,128)S(1)} %get-tuple-element.24), channel_id=1, source_target_pairs={{0,5},{1,4},{4,1},{5,0},{8,13},{9,12},{12,9},{13,8},{2,7},{3,6},{6... | collective-permute-start | bytes 392 | tf_op jit(solution)/shard_map/ppermute | solution.py:204
  24.2 1.7 %collective-permute-done.7 = f32[4,8]{1,0:T(4,128)S(1)} collective-permute-done((f32[4,8]{1,0:T(4,128)S(1)}, f32[4,8]{1,0:T(4,128)S(1)}, u32[]{:S(2)}, u32[]{:S(2)}) %collective-permute-start.7) | collective-permute-done | bytes 160 | tf_op jit(solution)/shard_map/ppermute | solution.py:204
  26.0 0.2 collective-permute-start.8
  26.1 1.0 %collective-permute-done.8 = f32[2,2,8]{2,1,0:T(2,128)S(1)} collective-permute-done((f32[2,2,8]{2,1,0:T(2,128)S(1)}, f32[2,2,8]{2,1,0:T(2,128)S(1)}, u32[]{:S(2)}, u32[]{:S(2)}) %collective-permute-start.8) | collective-permute-done | bytes 160 | tf_op jit(solution)/shard_map/ppermute | solution.py:198
  27.2 0.6 %compare_select_fusion = f32[2,2,8]{2,1,0:T(2,128)} fusion(f32[2,2,8]{2,1,0:T(2,128)S(1)} %maximum_add_fusion, s32[2,2,8]{2,1,0:T(2,128)S(1)} %get-tuple-element.22), kind=kLoop, calls=%fused_computation.2 | loop fusion | flops 64 | bytes 384 | tf_op jit(solution)/shard_map/jit(_where)/select_n | solution.py:300
  (10 shorter events, 0.0 us)
Async XLA Ops:
  0.9 3.0 %copy-start.4 = (bf16[2,8,4096]{2,1,0:T(8,128)(2,1)S(1)}, bf16[2,8,4096]{2,1,0:T(8,128)(2,1)}, u32[]{:S(2)}) copy-start(bf16[2,8,4096]{2,1,0:T(8,128)(2,1)} %refs_0_.6) | copy-start | bytes 393220
  0.9 4.7 %copy-start.1 = (bf16[2,256,2048]{2,1,0:T(8,128)(2,1)S(1)}, bf16[2,256,2048]{2,1,0:T(8,128)(2,1)}, u32[]{:S(2)}) copy-start(bf16[2,256,2048]{2,1,0:T(8,128)(2,1)} %refs_0_.4) | copy-start | bytes 6291460
  1.0 4.7 %copy-start.3 = (bf16[2,2048,64]{1,2,0:T(8,128)(2,1)S(1)}, bf16[2,2048,64]{1,2,0:T(8,128)(2,1)}, u32[]{:S(2)}) copy-start(bf16[2,2048,64]{1,2,0:T(8,128)(2,1)} %param.9) | copy-start | bytes 1572868
  1.0 8.1 %collective-permute-start = (bf16[2,64,640]{2,1,0:T(8,128)(2,1)S(1)}, bf16[2,64,640]{2,1,0:T(8,128)(2,1)S(1)}, u32[]{:S(2)}, u32[]{:S(2)}) collective-permute-start(bf16[2,64,640]{2,1,0:T(8,128)(2,1)S(1)} %shard_map.64.refs_0_), channel_id=1, source_target_pairs={{0,2},{2,0},{1,3},{3,1},{4,6},{6,4},{5,7},{7,5},{8,10},{10,8},{9,1... | collective-permute-start | bytes 491528 | tf_op jit(solution)/shard_map/ppermute | solution.py:193
  4.0 7.2 %copy-start = (bf16[2,128,4096]{2,1,0:T(8,128)(2,1)S(1)}, bf16[2,128,4096]{2,1,0:T(8,128)(2,1)}, u32[]{:S(2)}) copy-start(bf16[2,128,4096]{2,1,0:T(8,128)(2,1)} %refs_1_.3) | copy-start | bytes 6291460
  4.0 7.2 %copy-start.2 = (bf16[2,2048,64]{1,2,0:T(8,128)(2,1)S(1)}, bf16[2,2048,64]{1,2,0:T(8,128)(2,1)}, u32[]{:S(2)}) copy-start(bf16[2,2048,64]{1,2,0:T(8,128)(2,1)} %param.10) | copy-start | bytes 1572868
  4.0 5.0 %collective-permute-start.1 = (bf16[2,8,4096]{2,1,0:T(8,128)(2,1)S(1)}, bf16[2,8,4096]{2,1,0:T(8,128)(2,1)S(1)}, u32[]{:S(2)}, u32[]{:S(2)}) collective-permute-start(bf16[2,8,4096]{2,1,0:T(8,128)(2,1)S(1)} %copy-done.4), channel_id=1, source_target_pairs={{0,4},{4,0},{8,12},{12,8},{1,5},{5,1},{9,13},{13,9},{2,6},{6,2},{1... | collective-permute-start | bytes 393224 | tf_op jit(solution)/shard_map/ppermute | solution.py:198
  6.6 6.8 %collective-permute-start.3 = (bf16[2,64,896]{2,1,0:T(8,128)(2,1)S(1)}, bf16[2,64,896]{2,1,0:T(8,128)(2,1)S(1)}, u32[]{:S(2)}, u32[]{:S(2)}) collective-permute-start(bf16[2,64,896]{2,1,0:T(8,128)(2,1)S(1)} %get-tuple-element.21), channel_id=1, source_target_pairs={{0,2},{2,0},{1,3},{3,1},{4,6},{6,4},{5,7},{7,5},{8,10},{10,8},{9,1... | collective-permute-start | bytes 688136 | tf_op jit(solution)/shard_map/ppermute | solution.py:193
  9.0 5.3 %collective-permute-start.2 = (bf16[2,64,640]{2,1,0:T(8,128)(2,1)S(1)}, bf16[2,64,640]{2,1,0:T(8,128)(2,1)S(1)}, u32[]{:S(2)}, u32[]{:S(2)}) collective-permute-start(bf16[2,64,640]{2,1,0:T(8,128)(2,1)S(1)} %collective-permute-done.refs_2_), channel_id=1, source_target_pairs={{0,16},{1,5},{4,20},{5,1},{8,24},{9,13},{12,28},{13,9},{16,0},{17,... | collective-permute-start | bytes 491528 | tf_op jit(solution)/shard_map/ppermute | solution.py:211
  14.9 4.1 %collective-permute-start.4 = (bf16[1,16,512]{2,1,0:T(8,128)(2,1)S(1)}, bf16[1,16,512]{2,1,0:T(8,128)(2,1)S(1)}, u32[]{:S(2)}, u32[]{:S(2)}) collective-permute-start(bf16[1,16,512]{2,1,0:T(8,128)(2,1)S(1)} %bitcast.16), channel_id=1, source_target_pairs={{0,9},{1,8},{4,13},{5,12},{8,1},{9,0},{12,5},{13,4},{2,11},{3,10},... | collective-permute-start | bytes 49160 | tf_op jit(solution)/shard_map/ppermute | solution.py:204
  15.3 7.2 %collective-permute-start.6 = (bf16[256,512]{1,0:T(8,128)(2,1)S(1)}, bf16[256,512]{1,0:T(8,128)(2,1)S(1)}, u32[]{:S(2)}, u32[]{:S(2)}) collective-permute-start(bf16[256,512]{1,0:T(8,128)(2,1)S(1)} %shard_map.69.refs_1_), channel_id=1, source_target_pairs={{0,1},{1,0},{2,3},{3,2},{4,5},{5,4},{6,7},{7,6},{8,9},{9,8},{10,11... | collective-permute-start | bytes 786440 | tf_op jit(solution)/shard_map/ppermute | solution.py:198
  19.0 3.4 %collective-permute-start.5 = (bf16[2,16,512]{2,1,0:T(8,128)(2,1)S(1)}, bf16[2,16,512]{2,1,0:T(8,128)(2,1)S(1)}, u32[]{:S(2)}, u32[]{:S(2)}) collective-permute-start(bf16[2,16,512]{2,1,0:T(8,128)(2,1)S(1)} %pad_maximum_fusion.1), channel_id=1, source_target_pairs={{0,3},{1,2},{2,1},{3,0},{4,7},{5,6},{6,5},{7,4},{8,11},{9,10},{10,... | collective-permute-start | bytes 98312 | tf_op jit(solution)/shard_map/ppermute | solution.py:204
  22.9 3.1 %collective-permute-start.7 = (f32[4,8]{1,0:T(4,128)S(1)}, f32[4,8]{1,0:T(4,128)S(1)}, u32[]{:S(2)}, u32[]{:S(2)}) collective-permute-start(f32[4,8]{1,0:T(4,128)S(1)} %get-tuple-element.24), channel_id=1, source_target_pairs={{0,5},{1,4},{4,1},{5,0},{8,13},{9,12},{12,9},{13,8},{2,7},{3,6},{6... | collective-permute-start | bytes 392 | tf_op jit(solution)/shard_map/ppermute | solution.py:204
  26.0 1.2 %collective-permute-start.8 = (f32[2,2,8]{2,1,0:T(2,128)S(1)}, f32[2,2,8]{2,1,0:T(2,128)S(1)}, u32[]{:S(2)}, u32[]{:S(2)}) collective-permute-start(f32[2,2,8]{2,1,0:T(2,128)S(1)} %pad_maximum_fusion.2), channel_id=1, source_target_pairs={{0,1},{1,0},{2,3},{3,2},{4,5},{5,4},{6,7},{7,6},{8,9},{9,8},{10,11... | collective-permute-start | bytes 392 | tf_op jit(solution)/shard_map/ppermute | solution.py:198

commit v6 on v5

--- a/solution.py
+++ b/solution.py
@@ -234,10 +234,8 @@
     token = call(
         clear, jax.ShapeDtypeStruct((8, 128), F32), after=(piece, *[in_hbm(x) for x in (acts, out_grads)])
     )
-    asked, token = lax.optimization_barrier((query_grads, token))
     firsts = [shifted(piece, "tensor", s) for s in range(1, n)]
 
-    near = flipped(asked, "dp", 1)
     mine, *parcels = call(
         functools.partial(project_inputs, n),
         (
@@ -252,7 +250,7 @@
         scratch=[pltpu.SemaphoreType.DMA((n - 1,))],
     )
     parcels = [shifted(parcel, "tensor", s) for s, parcel in enumerate(parcels, 1)]
-    firsts, mine, near = lax.optimization_barrier((firsts, mine, near))
+    firsts, mine = lax.optimization_barrier((firsts, mine))
     seconds = [forwarded(first) for first in firsts]
     outputs = call(
         functools.partial(early, n),
@@ -260,8 +258,9 @@
         out_grads,
         factor,
         *firsts,
-        after=(near,),
-    )
+    )
+    asked, outputs = lax.optimization_barrier((query_grads, outputs))
+    near = flipped(asked, "dp", 1)
     grad = call(
         functools.partial(example_gradient, n, depth),
         jax.ShapeDtypeStruct((FOLD, width // FOLD * lanes), BF16),

time: 27.9 us -> 27.8 us (level)
  waiting for transfers between devices: 10.4 us -> 8.88 us
  starting transfers between devices: 12.2 us -> 13.4 us
    ppermute x3, starting transfers between devices: 2.33 us -> 3.91 us  [crossed(): lax.ppermute(x, (axis, 'query'), [(i, i ^ bit * cores + 1) for i in range...]
    ppermute x3, waiting for transfers between devices: 2.63 us -> 1.48 us  [flipped(): return lax.ppermute(x, axis, [(i, i ^ bit) for i in range(n)])]
    ppermute x3, starting transfers between devices: 4.55 us -> 3.41 us  [flipped(): return lax.ppermute(x, axis, [(i, i ^ bit) for i in range(n)])]
    ppermute x3, waiting for transfers between devices: 5.24 us -> 4.33 us  [crossed(): lax.ppermute(x, (axis, 'query'), [(i, i ^ bit * cores + 1) for i in range...]
    ppermute x2, starting transfers between devices: 3.8 us -> 4.48 us  [shifted(): return lax.ppermute(x, axis, [(i, (i + shift) % n) for i in range(n)])]
    ppermute x2, waiting for transfers between devices: 1.69 us -> 2.27 us  [shifted(): return lax.ppermute(x, axis, [(i, (i + shift) % n) for i in range(n)])]
  transfers between devices with their start and end apart: 9 -> 9, of which waited for: 7 -> 7; matrix products, arithmetic and copies ran while one was open for 0% -> 0% of each run, Pallas kernels for 7% -> 9%
where the time goes in v6:
time: 27.8 us; the launch traced here: 27.6 us
  starting transfers between devices  13.4 us (48%)
  waiting for transfers between devices  8.88 us (32%)
  Pallas kernels  3.9 us (14%)
  between operations  0.76 us (3%)
  other arithmetic  0.61 us (2%)
    ppermute x2, starting transfers between devices, shifted(): return lax.ppermute(x, axis, [(i, (i + shift) % n) for i in range(n)])  4.48 us
    ppermute x3, waiting for transfers between devices, crossed(): lax.ppermute(x, (axis, 'query'), [(i, i ^ bit * cores + 1) for i in range...  4.33 us
    ppermute x3, starting transfers between devices, crossed(): lax.ppermute(x, (axis, 'query'), [(i, i ^ bit * cores + 1) for i in range...  3.91 us
    pallas_call x7, Pallas kernels, call(): pl.pallas_call(body, out_shape=out_shape, in_specs=specs + [ANY] * len(af...  3.9 us
    ppermute x3, starting transfers between devices, flipped(): return lax.ppermute(x, axis, [(i, i ^ bit) for i in range(n)])  3.41 us
    ppermute x2, waiting for transfers between devices, shifted(): return lax.ppermute(x, axis, [(i, (i + shift) % n) for i in range(n)])  2.27 us
    ppermute x1, starting transfers between devices, forwarded(): return lax.ppermute(x, ('parts', 'dp', 'query'), pairs)  1.61 us
    ppermute x3, waiting for transfers between devices, flipped(): return lax.ppermute(x, axis, [(i, i ^ bit) for i in range(n)])  1.48 us
  transfers between devices with their start and end apart: 9, of which 7 were waited for; matrix products, arithmetic and copies ran while one was open for 0% of the time, Pallas kernels for 9%

profile of v6, /device:TPU:0, one launch (start us, length us, event | category | flops | bytes accessed | tf_op | source)
XLA Modules:
  0.0 27.6 jit_solution(7581435477768709357)
XLA Ops:
  0.0 0.9 %shard_map.64.refs_0_ = bf16[2,64,640]{2,1,0:T(8,128)(2,1)S(1)} custom-call(bf16[2,64,2048]{2,1,0:T(8,128)(2,1)} %bitcast.12), custom_call_target="tpu_custom_call" | custom-call | flops 1 | bytes 1 | tf_op jit(solution)/shard_map/pallas_call | solution.py:31
  0.9 0.0 copy-start.1
  0.9 0.0 copy-start.3
  1.0 3.0 %collective-permute-start = (bf16[2,64,640]{2,1,0:T(8,128)(2,1)S(1)}, bf16[2,64,640]{2,1,0:T(8,128)(2,1)S(1)}, u32[]{:S(2)}, u32[]{:S(2)}) collective-permute-start(bf16[2,64,640]{2,1,0:T(8,128)(2,1)S(1)} %shard_map.64.refs_0_), channel_id=1, source_target_pairs={{0,2},{2,0},{1,3},{3,1},{4,6},{6,4},{5,7},{7,5},{8,10},{10,8},{9,1... | collective-permute-start | bytes 491528 | tf_op jit(solution)/shard_map/ppermute | solution.py:193
  4.0 0.0 copy-done.1
  4.0 0.0 copy-done.3
  4.0 1.1 %shard_map.66 = (f32[128,128]{1,0:T(8,128)S(1)}, bf16[2,64,896]{2,1,0:T(8,128)(2,1)S(1)}) custom-call(bf16[2,256,2048]{2,1,0:T(8,128)(2,1)S(1)} %copy-done.1, bf16[2,64,2048]{2,1,0:T(8,128)(2,1)S(1)} %bitcast.15, bf16[2,64,2048]{2,1,0:T(8,128)(2,1)} %bitcast.13, f32[8,128]{1,0:T(8,128)S(1)} %shard_map.65.refs_3_), custom_call_target="tpu_custom_call" | custom-call | flops 1 | bytes 1 | tf_op jit(solution)/shard_map/pallas_call | solution.py:31
  5.1 0.0 copy-start.4
  5.1 1.5 %collective-permute-start.2 = (bf16[2,64,896]{2,1,0:T(8,128)(2,1)S(1)}, bf16[2,64,896]{2,1,0:T(8,128)(2,1)S(1)}, u32[]{:S(2)}, u32[]{:S(2)}) collective-permute-start(bf16[2,64,896]{2,1,0:T(8,128)(2,1)S(1)} %get-tuple-element.18), channel_id=1, source_target_pairs={{0,2},{2,0},{1,3},{3,1},{4,6},{6,4},{5,7},{7,5},{8,10},{10,8},{9,1... | collective-permute-start | bytes 688136 | tf_op jit(solution)/shard_map/ppermute | solution.py:193
  6.6 2.3 %collective-permute-done.refs_2_ = bf16[2,64,640]{2,1,0:T(8,128)(2,1)S(1)} collective-permute-done((bf16[2,64,640]{2,1,0:T(8,128)(2,1)S(1)}, bf16[2,64,640]{2,1,0:T(8,128)(2,1)S(1)}, u32[]{:S(2)}, u32[]{:S(2)}) %collective-permute-start) | collective-permute-done | bytes 163872 | tf_op jit(solution)/shard_map/ppermute | solution.py:193
  8.9 1.6 %collective-permute-start.1 = (bf16[2,64,640]{2,1,0:T(8,128)(2,1)S(1)}, bf16[2,64,640]{2,1,0:T(8,128)(2,1)S(1)}, u32[]{:S(2)}, u32[]{:S(2)}) collective-permute-start(bf16[2,64,640]{2,1,0:T(8,128)(2,1)S(1)} %collective-permute-done.refs_2_), channel_id=1, source_target_pairs={{0,16},{1,5},{4,20},{5,1},{8,24},{9,13},{12,28},{13,9},{16,0},{17,... | collective-permute-start | bytes 491528 | tf_op jit(solution)/shard_map/ppermute | solution.py:211
  10.5 0.0 copy-done
  10.5 0.0 copy-done.2
  10.5 0.6 %shard_map.67.refs_2_ = f32[128,128]{1,0:T(8,128)S(1)} custom-call(bf16[2,128,4096]{2,1,0:T(8,128)(2,1)S(1)} %copy-done, bf16[2,64,2048]{2,1,0:T(8,128)(2,1)S(1)} %bitcast.14, bf16[2,64,640]{2,1,0:T(8,128)(2,1)S(1)} %collective-permute-done.refs_2_), custom_call_target="tpu_custom_call" | custom-call | flops 1 | bytes 1 | tf_op jit(solution)/shard_map/pallas_call | solution.py:31
  11.1 1.6 %collective-permute-start.5 = (bf16[2,8,4096]{2,1,0:T(8,128)(2,1)S(1)}, bf16[2,8,4096]{2,1,0:T(8,128)(2,1)S(1)}, u32[]{:S(2)}, u32[]{:S(2)}) collective-permute-start(bf16[2,8,4096]{2,1,0:T(8,128)(2,1)S(1)} %copy-done.4), channel_id=1, source_target_pairs={{0,4},{4,0},{8,12},{12,8},{1,5},{5,1},{9,13},{13,9},{2,6},{6,2},{1... | collective-permute-start | bytes 393224 | tf_op jit(solution)/shard_map/ppermute | solution.py:198
  13.4 0.0 collective-permute-done.2.refs_5_
  13.4 0.8 %collective-permute-done.1.refs_4_ = bf16[2,64,640]{2,1,0:T(8,128)(2,1)S(1)} collective-permute-done((bf16[2,64,640]{2,1,0:T(8,128)(2,1)S(1)}, bf16[2,64,640]{2,1,0:T(8,128)(2,1)S(1)}, u32[]{:S(2)}, u32[]{:S(2)}) %collective-permute-start.1) | collective-permute-done | bytes 163872 | tf_op jit(solution)/shard_map/ppermute | solution.py:211
  14.2 0.5 %shard_map.68.refs_2_ = bf16[16,512]{1,0:T(8,128)(2,1)S(1)} custom-call(s32[1]{0:T(128)S(6)} %copy.7.refs_0_, bf16[2,128,4096]{2,1,0:T(8,128)(2,1)S(1)} %copy-done, f32[128,128]{1,0:T(8,128)S(1)} %shard_map.67.refs_2_, f32[128,128]{1,0:T(8,128)S(1)} %get-tuple-element.17.refs_3_, bf16[2,64,640]{2,1,0:T(8,128)(2,1)S(1)} %collective-permute-done.1.refs_4_, ...), custom_call_target="tpu_custom_call" | custom-call | flops 1 | bytes 1 | tf_op jit(solution)/shard_map/pallas_call | solution.py:31
  14.7 0.9 %collective-permute-start.3 = (bf16[1,16,512]{2,1,0:T(8,128)(2,1)S(1)}, bf16[1,16,512]{2,1,0:T(8,128)(2,1)S(1)}, u32[]{:S(2)}, u32[]{:S(2)}) collective-permute-start(bf16[1,16,512]{2,1,0:T(8,128)(2,1)S(1)} %bitcast.16), channel_id=1, source_target_pairs={{0,9},{1,8},{4,13},{5,12},{8,1},{9,0},{12,5},{13,4},{2,11},{3,10},... | collective-permute-start | bytes 49160 | tf_op jit(solution)/shard_map/ppermute | solution.py:204
  15.7 0.5 %collective-permute-done.5.refs_1_ = bf16[2,8,4096]{2,1,0:T(8,128)(2,1)S(1)} collective-permute-done((bf16[2,8,4096]{2,1,0:T(8,128)(2,1)S(1)}, bf16[2,8,4096]{2,1,0:T(8,128)(2,1)S(1)}, u32[]{:S(2)}, u32[]{:S(2)}) %collective-permute-start.5) | collective-permute-done | bytes 131104 | tf_op jit(solution)/shard_map/ppermute | solution.py:198
  16.1 0.3 %shard_map.69.refs_1_ = bf16[256,512]{1,0:T(8,128)(2,1)S(1)} custom-call(bf16[2,8,4096]{2,1,0:T(8,128)(2,1)S(1)} %copy-done.4, bf16[2,8,4096]{2,1,0:T(8,128)(2,1)S(1)} %collective-permute-done.5.refs_1_, bf16[16,512]{1,0:T(8,128)(2,1)S(1)} %shard_map.68.refs_2_), custom_call_target="tpu_custom_call" | custom-call | flops 1 | bytes 1 | tf_op jit(solution)/shard_map/pallas_call | solution.py:31
  16.4 1.5 %collective-permute-start.6 = (bf16[256,512]{1,0:T(8,128)(2,1)S(1)}, bf16[256,512]{1,0:T(8,128)(2,1)S(1)}, u32[]{:S(2)}, u32[]{:S(2)}) collective-permute-start(bf16[256,512]{1,0:T(8,128)(2,1)S(1)} %shard_map.69.refs_1_), channel_id=1, source_target_pairs={{0,1},{1,0},{2,3},{3,2},{4,5},{5,4},{6,7},{7,6},{8,9},{9,8},{10,11... | collective-permute-start | bytes 786440 | tf_op jit(solution)/shard_map/ppermute | solution.py:198
  18.0 0.9 %collective-permute-done.3 = bf16[1,16,512]{2,1,0:T(8,128)(2,1)S(1)} collective-permute-done((bf16[1,16,512]{2,1,0:T(8,128)(2,1)S(1)}, bf16[1,16,512]{2,1,0:T(8,128)(2,1)S(1)}, u32[]{:S(2)}, u32[]{:S(2)}) %collective-permute-start.3) | collective-permute-done | bytes 16416 | tf_op jit(solution)/shard_map/ppermute | solution.py:204
  18.9 1.5 %collective-permute-start.4 = (bf16[2,16,512]{2,1,0:T(8,128)(2,1)S(1)}, bf16[2,16,512]{2,1,0:T(8,128)(2,1)S(1)}, u32[]{:S(2)}, u32[]{:S(2)}) collective-permute-start(bf16[2,16,512]{2,1,0:T(8,128)(2,1)S(1)} %pad_maximum_fusion.1), channel_id=1, source_target_pairs={{0,3},{1,2},{2,1},{3,0},{4,7},{5,6},{6,5},{7,4},{8,11},{9,10},{10,... | collective-permute-start | bytes 98312 | tf_op jit(solution)/shard_map/ppermute | solution.py:204
  20.4 1.8 %collective-permute-done.4 = bf16[2,16,512]{2,1,0:T(8,128)(2,1)S(1)} collective-permute-done((bf16[2,16,512]{2,1,0:T(8,128)(2,1)S(1)}, bf16[2,16,512]{2,1,0:T(8,128)(2,1)S(1)}, u32[]{:S(2)}, u32[]{:S(2)}) %collective-permute-start.4) | collective-permute-done | bytes 32800 | tf_op jit(solution)/shard_map/ppermute | solution.py:204
  22.2 0.0 collective-permute-done.6.refs_2_
  22.3 0.4 %shard_map.70 = (f32[4,8]{1,0:T(4,128)S(1)}, f32[4,8]{1,0:T(4,128)S(1)}, s32[2,2,8]{2,1,0:T(2,128)S(1)}) custom-call(bf16[4,16,512]{2,1,0:T(8,128)(2,1)S(1)} %pad_maximum_fusion.refs_0_, bf16[256,512]{1,0:T(8,128)(2,1)S(1)} %shard_map.69.refs_1_, bf16[256,512]{1,0:T(8,128)(2,1)S(1)} %collective-permute-done.6.refs_2_), custom_call_target="tpu_custom_call" | custom-call | flops 1 | bytes 1 | tf_op jit(solution)/shard_map/pallas_call | solution.py:31
  22.7 1.5 %collective-permute-start.7 = (f32[4,8]{1,0:T(4,128)S(1)}, f32[4,8]{1,0:T(4,128)S(1)}, u32[]{:S(2)}, u32[]{:S(2)}) collective-permute-start(f32[4,8]{1,0:T(4,128)S(1)} %get-tuple-element.22), channel_id=1, source_target_pairs={{0,5},{1,4},{4,1},{5,0},{8,13},{9,12},{12,9},{13,8},{2,7},{3,6},{6... | collective-permute-start | bytes 392 | tf_op jit(solution)/shard_map/ppermute | solution.py:204
  24.2 1.6 %collective-permute-done.7 = f32[4,8]{1,0:T(4,128)S(1)} collective-permute-done((f32[4,8]{1,0:T(4,128)S(1)}, f32[4,8]{1,0:T(4,128)S(1)}, u32[]{:S(2)}, u32[]{:S(2)}) %collective-permute-start.7) | collective-permute-done | bytes 160 | tf_op jit(solution)/shard_map/ppermute | solution.py:204
  25.8 0.2 collective-permute-start.8
  26.0 1.0 %collective-permute-done.8 = f32[2,2,8]{2,1,0:T(2,128)S(1)} collective-permute-done((f32[2,2,8]{2,1,0:T(2,128)S(1)}, f32[2,2,8]{2,1,0:T(2,128)S(1)}, u32[]{:S(2)}, u32[]{:S(2)}) %collective-permute-start.8) | collective-permute-done | bytes 160 | tf_op jit(solution)/shard_map/ppermute | solution.py:198
  27.0 0.6 %compare_select_fusion = f32[2,2,8]{2,1,0:T(2,128)} fusion(f32[2,2,8]{2,1,0:T(2,128)S(1)} %maximum_add_fusion, s32[2,2,8]{2,1,0:T(2,128)S(1)} %get-tuple-element.20), kind=kLoop, calls=%fused_computation.2 | loop fusion | flops 64 | bytes 384 | tf_op jit(solution)/shard_map/jit(_where)/select_n | solution.py:299
  (10 shorter events, 0.0 us)
Async XLA Ops:
  0.9 3.0 %copy-start.1 = (bf16[2,256,2048]{2,1,0:T(8,128)(2,1)S(1)}, bf16[2,256,2048]{2,1,0:T(8,128)(2,1)}, u32[]{:S(2)}) copy-start(bf16[2,256,2048]{2,1,0:T(8,128)(2,1)} %refs_0_.4) | copy-start | bytes 6291460
  0.9 3.0 %copy-start.3 = (bf16[2,2048,64]{1,2,0:T(8,128)(2,1)S(1)}, bf16[2,2048,64]{1,2,0:T(8,128)(2,1)}, u32[]{:S(2)}) copy-start(bf16[2,2048,64]{1,2,0:T(8,128)(2,1)} %param.9) | copy-start | bytes 1572868
  1.0 7.9 %collective-permute-start = (bf16[2,64,640]{2,1,0:T(8,128)(2,1)S(1)}, bf16[2,64,640]{2,1,0:T(8,128)(2,1)S(1)}, u32[]{:S(2)}, u32[]{:S(2)}) collective-permute-start(bf16[2,64,640]{2,1,0:T(8,128)(2,1)S(1)} %shard_map.64.refs_0_), channel_id=1, source_target_pairs={{0,2},{2,0},{1,3},{3,1},{4,6},{6,4},{5,7},{7,5},{8,10},{10,8},{9,1... | collective-permute-start | bytes 491528 | tf_op jit(solution)/shard_map/ppermute | solution.py:193
  4.0 6.5 %copy-start = (bf16[2,128,4096]{2,1,0:T(8,128)(2,1)S(1)}, bf16[2,128,4096]{2,1,0:T(8,128)(2,1)}, u32[]{:S(2)}) copy-start(bf16[2,128,4096]{2,1,0:T(8,128)(2,1)} %refs_1_.3) | copy-start | bytes 6291460
  4.0 6.5 %copy-start.2 = (bf16[2,2048,64]{1,2,0:T(8,128)(2,1)S(1)}, bf16[2,2048,64]{1,2,0:T(8,128)(2,1)}, u32[]{:S(2)}) copy-start(bf16[2,2048,64]{1,2,0:T(8,128)(2,1)} %param.10) | copy-start | bytes 1572868
  5.1 6.0 %copy-start.4 = (bf16[2,8,4096]{2,1,0:T(8,128)(2,1)S(1)}, bf16[2,8,4096]{2,1,0:T(8,128)(2,1)}, u32[]{:S(2)}) copy-start(bf16[2,8,4096]{2,1,0:T(8,128)(2,1)} %refs_0_.6) | copy-start | bytes 393220
  5.1 8.3 %collective-permute-start.2 = (bf16[2,64,896]{2,1,0:T(8,128)(2,1)S(1)}, bf16[2,64,896]{2,1,0:T(8,128)(2,1)S(1)}, u32[]{:S(2)}, u32[]{:S(2)}) collective-permute-start(bf16[2,64,896]{2,1,0:T(8,128)(2,1)S(1)} %get-tuple-element.18), channel_id=1, source_target_pairs={{0,2},{2,0},{1,3},{3,1},{4,6},{6,4},{5,7},{7,5},{8,10},{10,8},{9,1... | collective-permute-start | bytes 688136 | tf_op jit(solution)/shard_map/ppermute | solution.py:193
  8.9 5.3 %collective-permute-start.1 = (bf16[2,64,640]{2,1,0:T(8,128)(2,1)S(1)}, bf16[2,64,640]{2,1,0:T(8,128)(2,1)S(1)}, u32[]{:S(2)}, u32[]{:S(2)}) collective-permute-start(bf16[2,64,640]{2,1,0:T(8,128)(2,1)S(1)} %collective-permute-done.refs_2_), channel_id=1, source_target_pairs={{0,16},{1,5},{4,20},{5,1},{8,24},{9,13},{12,28},{13,9},{16,0},{17,... | collective-permute-start | bytes 491528 | tf_op jit(solution)/shard_map/ppermute | solution.py:211
  11.1 5.0 %collective-permute-start.5 = (bf16[2,8,4096]{2,1,0:T(8,128)(2,1)S(1)}, bf16[2,8,4096]{2,1,0:T(8,128)(2,1)S(1)}, u32[]{:S(2)}, u32[]{:S(2)}) collective-permute-start(bf16[2,8,4096]{2,1,0:T(8,128)(2,1)S(1)} %copy-done.4), channel_id=1, source_target_pairs={{0,4},{4,0},{8,12},{12,8},{1,5},{5,1},{9,13},{13,9},{2,6},{6,2},{1... | collective-permute-start | bytes 393224 | tf_op jit(solution)/shard_map/ppermute | solution.py:198
  14.7 4.1 %collective-permute-start.3 = (bf16[1,16,512]{2,1,0:T(8,128)(2,1)S(1)}, bf16[1,16,512]{2,1,0:T(8,128)(2,1)S(1)}, u32[]{:S(2)}, u32[]{:S(2)}) collective-permute-start(bf16[1,16,512]{2,1,0:T(8,128)(2,1)S(1)} %bitcast.16), channel_id=1, source_target_pairs={{0,9},{1,8},{4,13},{5,12},{8,1},{9,0},{12,5},{13,4},{2,11},{3,10},... | collective-permute-start | bytes 49160 | tf_op jit(solution)/shard_map/ppermute | solution.py:204
  16.4 5.8 %collective-permute-start.6 = (bf16[256,512]{1,0:T(8,128)(2,1)S(1)}, bf16[256,512]{1,0:T(8,128)(2,1)S(1)}, u32[]{:S(2)}, u32[]{:S(2)}) collective-permute-start(bf16[256,512]{1,0:T(8,128)(2,1)S(1)} %shard_map.69.refs_1_), channel_id=1, source_target_pairs={{0,1},{1,0},{2,3},{3,2},{4,5},{5,4},{6,7},{7,6},{8,9},{9,8},{10,11... | collective-permute-start | bytes 786440 | tf_op jit(solution)/shard_map/ppermute | solution.py:198
  18.9 3.4 %collective-permute-start.4 = (bf16[2,16,512]{2,1,0:T(8,128)(2,1)S(1)}, bf16[2,16,512]{2,1,0:T(8,128)(2,1)S(1)}, u32[]{:S(2)}, u32[]{:S(2)}) collective-permute-start(bf16[2,16,512]{2,1,0:T(8,128)(2,1)S(1)} %pad_maximum_fusion.1), channel_id=1, source_target_pairs={{0,3},{1,2},{2,1},{3,0},{4,7},{5,6},{6,5},{7,4},{8,11},{9,10},{10,... | collective-permute-start | bytes 98312 | tf_op jit(solution)/shard_map/ppermute | solution.py:204
  22.7 3.1 %collective-permute-start.7 = (f32[4,8]{1,0:T(4,128)S(1)}, f32[4,8]{1,0:T(4,128)S(1)}, u32[]{:S(2)}, u32[]{:S(2)}) collective-permute-start(f32[4,8]{1,0:T(4,128)S(1)} %get-tuple-element.22), channel_id=1, source_target_pairs={{0,5},{1,4},{4,1},{5,0},{8,13},{9,12},{12,9},{13,8},{2,7},{3,6},{6... | collective-permute-start | bytes 392 | tf_op jit(solution)/shard_map/ppermute | solution.py:204
  25.8 1.2 %collective-permute-start.8 = (f32[2,2,8]{2,1,0:T(2,128)S(1)}, f32[2,2,8]{2,1,0:T(2,128)S(1)}, u32[]{:S(2)}, u32[]{:S(2)}) collective-permute-start(f32[2,2,8]{2,1,0:T(2,128)S(1)} %pad_maximum_fusion.2), channel_id=1, source_target_pairs={{0,1},{1,0},{2,3},{3,2},{4,5},{5,4},{6,7},{7,6},{8,9},{9,8},{10,11... | collective-permute-start | bytes 392 | tf_op jit(solution)/shard_map/ppermute | solution.py:198

commit v7 on v6

--- a/solution.py
+++ b/solution.py
@@ -53,20 +53,29 @@
     return lax.rem(t + n - shift, n)
 
 
-def side():
-    return jnp.where(lax.axis_index("query") == 0, lax.axis_index("parts"), lax.axis_index("dp") & 1)
+def side(parts=0, dp=0):
+    return 2 * (lax.axis_index("parts") ^ parts) + ((lax.axis_index("dp") & 1) ^ dp)
+
+
+def swapped(core_first):
+    by_parts = (lax.axis_index("query") == 1) == core_first
+    return jnp.where(by_parts, side(parts=1), side(dp=1))
 
 
 def clear(out):
     out[...] = jnp.zeros(out.shape, out.dtype)
 
 
-def cut(factor, piece, sem):
-    width = piece.shape[2]
-    start = pl.multiple_of(side() * width, 128)
-    copy = pltpu.make_async_copy(factor.at[:, :, pl.ds(start, width)], piece, sem)
-    copy.start()
-    copy.wait()
+def cut(factor, piece, other, sems):
+    step = piece.shape[2]
+    copies = []
+    for i, (out, place) in enumerate(((piece, side()), (other, side(1, 1)))):
+        columns = pl.ds(pl.multiple_of(place * step, 128), step)
+        copies.append(pltpu.make_async_copy(factor.at[:, :, columns], out, sems.at[i]))
+    for copy in copies:
+        copy.start()
+    for copy in copies:
+        copy.wait()
 
 
 def project_inputs(n, acts, factor, factor_out, mine, *rest):
@@ -94,16 +103,14 @@
         copy.wait()
 
 
-def fold_queries(width, own, near, out, rows):
-    layers, nq, _ = own.shape
-    wide = [
-        jnp.concatenate([own[l].astype(F32), near[l].astype(F32)], axis=0) for l in range(layers)
-    ]
+def fold_queries(width, queries, out, rows):
+    layers, nq, _ = queries.shape
+    wide = [queries[l].astype(F32) for l in range(layers)]
     lanes = layers * width
     for g in range(width // FOLD):
         for r in range(FOLD):
             start = (g * FOLD + r) * width
-            rows[g, pl.ds(r, 2 * nq, stride=FOLD), :] = jnp.concatenate(
+            rows[g, pl.ds(r, nq, stride=FOLD), :] = jnp.concatenate(
                 [w[:, start : start + width] for w in wide], axis=1
             )
         out[:, g * lanes : (g + 1) * lanes] = rows[g].astype(BF16)
@@ -128,18 +135,21 @@
 
 
 def example_gradient(n, depth, length, grads, outputs, inputs, *rest):
-    pieces, parcels, out = rest[: n - 1], rest[n - 1 : -1], rest[-1]
+    out = rest[-1]
+    seconds, thirds, fourths, parcels = (rest[i * (n - 1) : (i + 1) * (n - 1)] for i in range(4))
     slots, lanes = inputs.shape
     t = lax.axis_index("tensor")
     total = outputs[...]
     ins = inputs[...]
-    for s, (piece, parcel) in enumerate(zip(pieces, parcels), 1):
+    for s in range(1, n):
+        second, third, fourth, parcel = (x[s - 1] for x in (seconds, thirds, fourths, parcels))
         start = block_of(t, s, n) * depth
-        width = piece.shape[2]
-        whole = parcel.at[:, :, : parcel.shape[2] - lanes]
-        total = total + product(grads, start + 2 * width, whole)
-        total = total + product(grads, start + (1 - side()) * width, piece)
-        ins = ins + parcel[:, :, parcel.shape[2] - lanes :].reshape(slots, lanes).astype(F32)
+        step, size = second.shape[2], parcel.shape[2] - lanes
+        total = total + product(grads, start + side(1, 1) * step, fourth)
+        total = total + product(grads, start + 4 * step, parcel.at[:, :, :size])
+        total = total + product(grads, start + swapped(True) * step, second)
+        total = total + product(grads, start + swapped(False) * step, third)
+        ins = ins + parcel[:, :, size:].reshape(slots, lanes).astype(F32)
     live = lax.broadcasted_iota(jnp.int32, ins.shape, 0) < length[0]
     ins = jnp.where(live, ins, 0.0).astype(BF16)
     both = dot(ins, total.astype(BF16), TN)
@@ -155,15 +165,14 @@
     )
 
 
-def score(n, order, grads, queries, queries_other, mine, theirs, odd_place):
+def score(n, order, grads, own, own_other, near, near_other, mine, theirs, odd_place):
     slots, nq = mine.shape
     even = [s for s in range(slots) if s.bit_count() % 2 == 0]
     odd = [s for s in range(slots) if s.bit_count() % 2 == 1]
     products = []
-    for rows in (slice(0, nq * FOLD), slice(nq * FOLD, 2 * nq * FOLD)):
-        for asked, chosen in ((queries, even), (queries_other, odd)):
-            lhs = jnp.concatenate([grads[s] for s in chosen], axis=0)
-            products.append(dot(lhs, asked[rows], NT))
+    for asked, chosen in ((own, even), (own_other, odd), (near, even), (near_other, odd)):
+        lhs = jnp.concatenate([grads[s] for s in chosen], axis=0)
+        products.append(dot(lhs, asked[...], NT))
     products = jnp.concatenate(products, axis=0)
     row = lax.broadcasted_iota(jnp.int32, products.shape, 0)
     column = lax.broadcasted_iota(jnp.int32, products.shape, 1)
@@ -204,10 +213,10 @@
     return lax.ppermute(x, (axis, "query"), [(i, i ^ (bit * cores + 1)) for i in range(n)])
 
 
-def forwarded(x):
+def forwarded(x, core_first):
     n, cores = lax.axis_size("dp"), lax.axis_size("query")
     size = lax.axis_size("parts") * n * cores
-    pairs = [(i, i ^ (n * cores if i % cores == 0 else cores)) for i in range(size)]
+    pairs = [(i, i ^ (n * cores if (i % cores == 1) == core_first else cores)) for i in range(size)]
     return lax.ppermute(x, ("parts", "dp", "query"), pairs)
 
 
@@ -219,17 +228,18 @@
     n = lax.axis_size("tensor")
     n_dp = lax.axis_size("dp")
     lanes = layers * width
-    step = depth * 5 // 16 // 128 * 128
+    step = depth * 3 // 16 // 128 * 128
 
     factor = proj_out.transpose(0, 2, 1)
-    piece = call(
+    piece, other = call(
         cut,
-        jax.ShapeDtypeStruct((layers, width, step), BF16),
+        (jax.ShapeDtypeStruct((layers, width, step), BF16),) * 2,
         in_hbm(factor),
         specs=[ANY],
-        scratch=[pltpu.SemaphoreType.DMA],
+        scratch=[pltpu.SemaphoreType.DMA((2,))],
     )
     firsts = [shifted(piece, "tensor", s) for s in range(1, n)]
+    fourths = [shifted(other, "tensor", s) for s in range(1, n)]
 
     token = call(
         clear, jax.ShapeDtypeStruct((8, 128), F32), after=(piece, *[in_hbm(x) for x in (acts, out_grads)])
@@ -240,7 +250,7 @@
         functools.partial(project_inputs, n),
         (
             jax.ShapeDtypeStruct((slots, lanes), F32),
-            *[jax.ShapeDtypeStruct((layers, width, depth - 2 * step + lanes), BF16)] * (n - 1),
+            *[jax.ShapeDtypeStruct((layers, width, depth - 4 * step + lanes), BF16)] * (n - 1),
         ),
         acts,
         proj_in.transpose(0, 2, 1),
@@ -251,7 +261,8 @@
     )
     parcels = [shifted(parcel, "tensor", s) for s, parcel in enumerate(parcels, 1)]
     firsts, mine = lax.optimization_barrier((firsts, mine))
-    seconds = [forwarded(first) for first in firsts]
+    seconds = [forwarded(first, True) for first in firsts]
+    thirds = [forwarded(first, False) for first in firsts]
     outputs = call(
         functools.partial(early, n),
         jax.ShapeDtypeStruct((slots, lanes), F32),
@@ -261,6 +272,16 @@
     )
     asked, outputs = lax.optimization_barrier((query_grads, outputs))
     near = flipped(asked, "dp", 1)
+    fold = functools.partial(
+        call,
+        functools.partial(fold_queries, width),
+        jax.ShapeDtypeStruct((nq * FOLD, width // FOLD * lanes), BF16),
+        scratch=[pltpu.VMEM((width // FOLD, nq * FOLD, lanes), F32)],
+    )
+    own = fold(asked)
+    own_other = flipped(own, "query", 1)
+    near = fold(near)
+    near_other = flipped(near, "query", 1)
     grad = call(
         functools.partial(example_gradient, n, depth),
         jax.ShapeDtypeStruct((FOLD, width // FOLD * lanes), BF16),
@@ -269,29 +290,24 @@
         outputs,
         mine,
         *[in_vmem(x) for x in seconds],
+        *[in_vmem(x) for x in thirds],
+        *[in_vmem(x) for x in fourths],
         *[in_vmem(x) for x in parcels],
     )
-    queries = call(
-        functools.partial(fold_queries, width),
-        jax.ShapeDtypeStruct((2 * nq * FOLD, width // FOLD * lanes), BF16),
-        query_grads,
-        near,
-        after=(grad,),
-        scratch=[pltpu.VMEM((width // FOLD, 2 * nq * FOLD, lanes), F32)],
-    )
-    queries_other = flipped(queries, "query", 1)
     steps = [("dp", 1 << b) for b in reversed(range(1, n_dp.bit_length() - 1))]
     steps += [("tensor", 1 << b) for b in range(n.bit_length() - 1)]
     grads = grad[None]
     order = [0]
     for axis, bit in steps:
+        if len(order) == 2:
+            grads, near = lax.optimization_barrier((grads, near))
         grads = jnp.concatenate([grads, crossed(grads, axis, bit)])
         order += [o ^ (bit if axis == "tensor" else bit * n // 2) for o in order]
     table = jax.ShapeDtypeStruct((len(order), nq), F32)
     top = len(order) // 2
     flag = jax.ShapeDtypeStruct((2, top, nq), jnp.int32)
     mine, theirs, odd_place = call(
-        functools.partial(score, n, order), (table, table, flag), grads, queries, queries_other
+        functools.partial(score, n, order), (table, table, flag), grads, own, own_other, near, near_other
     )
     got = crossed(theirs, "dp", 1)
     kept, sent = jnp.stack([mine[:top], got[:top]]), jnp.stack([mine[top:], got[top:]])

time: 27.8 us -> 27.4 us (0.986)
  starting transfers between devices: 13.4 us -> 13.1 us
    ppermute x3 -> x4, starting transfers between devices: 3.41 us -> 1.27 us  [flipped(): return lax.ppermute(x, axis, [(i, i ^ bit) for i in range(n)])]
    ppermute x3, waiting for transfers between devices: 4.33 us -> 6.32 us  [crossed(): lax.ppermute(x, (axis, 'query'), [(i, i ^ bit * cores + 1) for i in range...]
    ppermute x1 -> x2, starting transfers between devices: 1.61 us -> 3.17 us  [forwarded(): return lax.ppermute(x, ('parts', 'dp', 'query'), pairs)]
    ppermute x2 -> x3, waiting for transfers between devices: 2.27 us -> 0.84 us  [shifted(): return lax.ppermute(x, axis, [(i, (i + shift) % n) for i in range(n)])]
    ppermute x2 -> x3, starting transfers between devices: 4.48 us -> 5.09 us  [shifted(): return lax.ppermute(x, axis, [(i, (i + shift) % n) for i in range(n)])]
    ppermute x3 -> x4, waiting for transfers between devices: 1.48 us -> 1.05 us  [flipped(): return lax.ppermute(x, axis, [(i, i ^ bit) for i in range(n)])]
    ppermute x3, starting transfers between devices: 3.91 us -> 3.59 us  [crossed(): lax.ppermute(x, (axis, 'query'), [(i, i ^ bit * cores + 1) for i in range...]
    ppermute x1 -> x2, waiting for transfers between devices: 0.8 us -> 0.52 us  [forwarded(): return lax.ppermute(x, ('parts', 'dp', 'query'), pairs)]
  transfers between devices with their start and end apart: 9 -> 12, of which waited for: 7 -> 6; matrix products, arithmetic and copies ran while one was open for 0% -> 0% of each run, Pallas kernels for 9% -> 9%
where the time goes in v7:
time: 27.4 us; the launch traced here: 27.2 us
  starting transfers between devices  13.1 us (48%)
  waiting for transfers between devices  8.73 us (32%)
  Pallas kernels  3.98 us (15%)
  between operations  0.78 us (3%)
  other arithmetic  0.61 us (2%)
    ppermute x3, waiting for transfers between devices, crossed(): lax.ppermute(x, (axis, 'query'), [(i, i ^ bit * cores + 1) for i in range...  6.32 us
    ppermute x3, starting transfers between devices, shifted(): return lax.ppermute(x, axis, [(i, (i + shift) % n) for i in range(n)])  5.09 us
    pallas_call x8, Pallas kernels, call(): pl.pallas_call(body, out_shape=out_shape, in_specs=specs + [ANY] * len(af...  3.98 us
    ppermute x3, starting transfers between devices, crossed(): lax.ppermute(x, (axis, 'query'), [(i, i ^ bit * cores + 1) for i in range...  3.59 us
    ppermute x2, starting transfers between devices, forwarded(): return lax.ppermute(x, ('parts', 'dp', 'query'), pairs)  3.17 us
    ppermute x4, starting transfers between devices, flipped(): return lax.ppermute(x, axis, [(i, i ^ bit) for i in range(n)])  1.27 us
    ppermute x4, waiting for transfers between devices, flipped(): return lax.ppermute(x, axis, [(i, i ^ bit) for i in range(n)])  1.05 us
    ppermute x3, waiting for transfers between devices, shifted(): return lax.ppermute(x, axis, [(i, (i + shift) % n) for i in range(n)])  0.84 us
  transfers between devices with their start and end apart: 12, of which 6 were waited for; matrix products, arithmetic and copies ran while one was open for 0% of the time, Pallas kernels for 9%

profile of v7, /device:TPU:0, one launch (start us, length us, event | category | flops | bytes accessed | tf_op | source)
XLA Modules:
  0.0 27.2 jit_solution(10430086167260835080)
XLA Ops:
  0.0 1.0 %shard_map.64 = (bf16[2,64,384]{2,1,0:T(8,128)(2,1)S(1)}, bf16[2,64,384]{2,1,0:T(8,128)(2,1)S(1)}) custom-call(bf16[2,64,2048]{2,1,0:T(8,128)(2,1)} %bitcast.12), custom_call_target="tpu_custom_call" | custom-call | flops 1 | bytes 1 | tf_op jit(solution)/shard_map/pallas_call | solution.py:31
  1.0 0.0 copy-start.1
  1.0 0.0 copy-start.3
  1.0 3.0 %collective-permute-start = (bf16[2,64,384]{2,1,0:T(8,128)(2,1)S(1)}, bf16[2,64,384]{2,1,0:T(8,128)(2,1)S(1)}, u32[]{:S(2)}, u32[]{:S(2)}) collective-permute-start(bf16[2,64,384]{2,1,0:T(8,128)(2,1)S(1)} %get-tuple-element.18.refs_0_), channel_id=1, source_target_pairs={{0,2},{2,0},{1,3},{3,1},{4,6},{6,4},{5,7},{7,5},{8,10},{10,8},{9,1... | collective-permute-start | bytes 294920 | tf_op jit(solution)/shard_map/ppermute | solution.py:202
  4.0 1.1 %shard_map.66 = (f32[128,128]{1,0:T(8,128)S(1)}, bf16[2,64,640]{2,1,0:T(8,128)(2,1)S(1)}) custom-call(bf16[2,256,2048]{2,1,0:T(8,128)(2,1)S(1)} %copy-done.1, bf16[2,64,2048]{2,1,0:T(8,128)(2,1)S(1)} %bitcast.15, bf16[2,64,2048]{2,1,0:T(8,128)(2,1)} %bitcast.13, f32[8,128]{1,0:T(8,128)S(1)} %shard_map.65.refs_3_), custom_call_target="tpu_custom_call" | custom-call | flops 1 | bytes 1 | tf_op jit(solution)/shard_map/pallas_call | solution.py:31
  5.1 0.0 copy-start.4
  5.2 1.5 %collective-permute-start.4 = (bf16[2,64,640]{2,1,0:T(8,128)(2,1)S(1)}, bf16[2,64,640]{2,1,0:T(8,128)(2,1)S(1)}, u32[]{:S(2)}, u32[]{:S(2)}) collective-permute-start(bf16[2,64,640]{2,1,0:T(8,128)(2,1)S(1)} %get-tuple-element.24), channel_id=1, source_target_pairs={{0,2},{2,0},{1,3},{3,1},{4,6},{6,4},{5,7},{7,5},{8,10},{10,8},{9,1... | collective-permute-start | bytes 491528 | tf_op jit(solution)/shard_map/ppermute | solution.py:202
  6.6 0.6 %collective-permute-start.3 = (bf16[2,64,384]{2,1,0:T(8,128)(2,1)S(1)}, bf16[2,64,384]{2,1,0:T(8,128)(2,1)S(1)}, u32[]{:S(2)}, u32[]{:S(2)}) collective-permute-start(bf16[2,64,384]{2,1,0:T(8,128)(2,1)S(1)} %get-tuple-element.23), channel_id=1, source_target_pairs={{0,2},{2,0},{1,3},{3,1},{4,6},{6,4},{5,7},{7,5},{8,10},{10,8},{9,1... | collective-permute-start | bytes 294920 | tf_op jit(solution)/shard_map/ppermute | solution.py:202
  7.2 0.0 collective-permute-done.refs_2_
  7.2 1.6 %collective-permute-start.1 = (bf16[2,64,384]{2,1,0:T(8,128)(2,1)S(1)}, bf16[2,64,384]{2,1,0:T(8,128)(2,1)S(1)}, u32[]{:S(2)}, u32[]{:S(2)}) collective-permute-start(bf16[2,64,384]{2,1,0:T(8,128)(2,1)S(1)} %collective-permute-done.refs_2_), channel_id=1, source_target_pairs={{0,4},{1,17},{4,0},{5,21},{8,12},{9,25},{12,8},{13,29},{16,20},{17... | collective-permute-start | bytes 294920 | tf_op jit(solution)/shard_map/ppermute | solution.py:220
  8.9 1.5 %collective-permute-start.2 = (bf16[2,64,384]{2,1,0:T(8,128)(2,1)S(1)}, bf16[2,64,384]{2,1,0:T(8,128)(2,1)S(1)}, u32[]{:S(2)}, u32[]{:S(2)}) collective-permute-start(bf16[2,64,384]{2,1,0:T(8,128)(2,1)S(1)} %collective-permute-done.refs_2_), channel_id=1, source_target_pairs={{0,16},{1,5},{4,20},{5,1},{8,24},{9,13},{12,28},{13,9},{16,0},{17,... | collective-permute-start | bytes 294920 | tf_op jit(solution)/shard_map/ppermute | solution.py:220
  10.4 0.5 %shard_map.67.refs_2_ = f32[128,128]{1,0:T(8,128)S(1)} custom-call(bf16[2,128,4096]{2,1,0:T(8,128)(2,1)S(1)} %copy-done, bf16[2,64,2048]{2,1,0:T(8,128)(2,1)S(1)} %bitcast.14, bf16[2,64,384]{2,1,0:T(8,128)(2,1)S(1)} %collective-permute-done.refs_2_), custom_call_target="tpu_custom_call" | custom-call | flops 1 | bytes 1 | tf_op jit(solution)/shard_map/pallas_call | solution.py:31
  11.0 0.5 %collective-permute-start.6 = (bf16[2,8,4096]{2,1,0:T(8,128)(2,1)S(1)}, bf16[2,8,4096]{2,1,0:T(8,128)(2,1)S(1)}, u32[]{:S(2)}, u32[]{:S(2)}) collective-permute-start(bf16[2,8,4096]{2,1,0:T(8,128)(2,1)S(1)} %copy-done.4), channel_id=1, source_target_pairs={{0,4},{4,0},{8,12},{12,8},{1,5},{5,1},{9,13},{13,9},{2,6},{6,2},{1... | collective-permute-start | bytes 393224 | tf_op jit(solution)/shard_map/ppermute | solution.py:207
  12.2 0.8 %collective-permute-done.3.refs_6_ = bf16[2,64,384]{2,1,0:T(8,128)(2,1)S(1)} collective-permute-done((bf16[2,64,384]{2,1,0:T(8,128)(2,1)S(1)}, bf16[2,64,384]{2,1,0:T(8,128)(2,1)S(1)}, u32[]{:S(2)}, u32[]{:S(2)}) %collective-permute-start.3) | collective-permute-done | bytes 98336 | tf_op jit(solution)/shard_map/ppermute | solution.py:202
  13.0 0.0 collective-permute-done.4.refs_7_
  13.0 0.5 %collective-permute-done.2.refs_5_ = bf16[2,64,384]{2,1,0:T(8,128)(2,1)S(1)} collective-permute-done((bf16[2,64,384]{2,1,0:T(8,128)(2,1)S(1)}, bf16[2,64,384]{2,1,0:T(8,128)(2,1)S(1)}, u32[]{:S(2)}, u32[]{:S(2)}) %collective-permute-start.2) | collective-permute-done | bytes 98336 | tf_op jit(solution)/shard_map/ppermute | solution.py:220
  13.5 0.6 %shard_map.68 = bf16[16,512]{1,0:T(8,128)(2,1)S(1)} custom-call(s32[1]{0:T(128)S(6)} %copy.7.refs_0_, bf16[2,128,4096]{2,1,0:T(8,128)(2,1)S(1)} %copy-done, f32[128,128]{1,0:T(8,128)S(1)} %shard_map.67.refs_2_, f32[128,128]{1,0:T(8,128)S(1)} %get-tuple-element.22.refs_3_, bf16[2,64,384]{2,1,0:T(8,128)(2,1)S(1)} %collective-permute-done.1.refs_4_, ...), custom_call_target="tpu_custom_call" | custom-call | flops 1 | bytes 1 | tf_op jit(solution)/shard_map/pallas_call | solution.py:31
  14.1 1.2 %collective-permute-start.5 = (bf16[1,16,512]{2,1,0:T(8,128)(2,1)S(1)}, bf16[1,16,512]{2,1,0:T(8,128)(2,1)S(1)}, u32[]{:S(2)}, u32[]{:S(2)}) collective-permute-start(bf16[1,16,512]{2,1,0:T(8,128)(2,1)S(1)} %bitcast.16), channel_id=1, source_target_pairs={{0,9},{1,8},{4,13},{5,12},{8,1},{9,0},{12,5},{13,4},{2,11},{3,10},... | collective-permute-start | bytes 49160 | tf_op jit(solution)/shard_map/ppermute | solution.py:213
  15.3 2.9 %collective-permute-done.5 = bf16[1,16,512]{2,1,0:T(8,128)(2,1)S(1)} collective-permute-done((bf16[1,16,512]{2,1,0:T(8,128)(2,1)S(1)}, bf16[1,16,512]{2,1,0:T(8,128)(2,1)S(1)}, u32[]{:S(2)}, u32[]{:S(2)}) %collective-permute-start.5) | collective-permute-done | bytes 16416 | tf_op jit(solution)/shard_map/ppermute | solution.py:213
  18.2 0.0 collective-permute-done.6.refs_0_
  18.2 0.2 shard_map.69.refs_3_
  18.4 1.1 %collective-permute-start.7 = (bf16[2,16,512]{2,1,0:T(8,128)(2,1)S(1)}, bf16[2,16,512]{2,1,0:T(8,128)(2,1)S(1)}, u32[]{:S(2)}, u32[]{:S(2)}) collective-permute-start(bf16[2,16,512]{2,1,0:T(8,128)(2,1)S(1)} %pad_maximum_fusion.1), channel_id=1, source_target_pairs={{0,3},{1,2},{2,1},{3,0},{4,7},{5,6},{6,5},{7,4},{8,11},{9,10},{10,... | collective-permute-start | bytes 98312 | tf_op jit(solution)/shard_map/ppermute | solution.py:213
  19.5 0.2 shard_map.70.refs_1_
  19.7 0.5 %collective-permute-start.8 = (bf16[128,512]{1,0:T(8,128)(2,1)S(1)}, bf16[128,512]{1,0:T(8,128)(2,1)S(1)}, u32[]{:S(2)}, u32[]{:S(2)}) collective-permute-start(bf16[128,512]{1,0:T(8,128)(2,1)S(1)} %shard_map.70.refs_1_), channel_id=1, source_target_pairs={{0,1},{1,0},{2,3},{3,2},{4,5},{5,4},{6,7},{7,6},{8,9},{9,8},{10,11... | collective-permute-start | bytes 393224 | tf_op jit(solution)/shard_map/ppermute | solution.py:207
  20.2 0.1 collective-permute-start.9
  20.3 1.6 %collective-permute-done.7 = bf16[2,16,512]{2,1,0:T(8,128)(2,1)S(1)} collective-permute-done((bf16[2,16,512]{2,1,0:T(8,128)(2,1)S(1)}, bf16[2,16,512]{2,1,0:T(8,128)(2,1)S(1)}, u32[]{:S(2)}, u32[]{:S(2)}) %collective-permute-start.7) | collective-permute-done | bytes 32800 | tf_op jit(solution)/shard_map/ppermute | solution.py:213
  21.9 0.4 %shard_map.71 = (f32[4,8]{1,0:T(4,128)S(1)}, f32[4,8]{1,0:T(4,128)S(1)}, s32[2,2,8]{2,1,0:T(2,128)S(1)}) custom-call(bf16[4,16,512]{2,1,0:T(8,128)(2,1)S(1)} %pad_maximum_fusion.refs_0_, bf16[128,512]{1,0:T(8,128)(2,1)S(1)} %shard_map.70.refs_1_, bf16[128,512]{1,0:T(8,128)(2,1)S(1)} %collective-permute-done.8.refs_2_, ...), custom_call_target="tpu_custom_call" | custom-call | flops 1 | bytes 1 | tf_op jit(solution)/shard_map/pallas_call | solution.py:31
  22.3 1.3 %collective-permute-start.10 = (f32[4,8]{1,0:T(4,128)S(1)}, f32[4,8]{1,0:T(4,128)S(1)}, u32[]{:S(2)}, u32[]{:S(2)}) collective-permute-start(f32[4,8]{1,0:T(4,128)S(1)} %get-tuple-element.30), channel_id=1, source_target_pairs={{0,5},{1,4},{4,1},{5,0},{8,13},{9,12},{12,9},{13,8},{2,7},{3,6},{6... | collective-permute-start | bytes 392 | tf_op jit(solution)/shard_map/ppermute | solution.py:213
  23.6 1.8 %collective-permute-done.10 = f32[4,8]{1,0:T(4,128)S(1)} collective-permute-done((f32[4,8]{1,0:T(4,128)S(1)}, f32[4,8]{1,0:T(4,128)S(1)}, u32[]{:S(2)}, u32[]{:S(2)}) %collective-permute-start.10) | collective-permute-done | bytes 160 | tf_op jit(solution)/shard_map/ppermute | solution.py:213
  25.4 0.2 collective-permute-start.11
  25.6 1.0 %collective-permute-done.11 = f32[2,2,8]{2,1,0:T(2,128)S(1)} collective-permute-done((f32[2,2,8]{2,1,0:T(2,128)S(1)}, f32[2,2,8]{2,1,0:T(2,128)S(1)}, u32[]{:S(2)}, u32[]{:S(2)}) %collective-permute-start.11) | collective-permute-done | bytes 160 | tf_op jit(solution)/shard_map/ppermute | solution.py:207
  26.7 0.6 %compare_select_fusion = f32[2,2,8]{2,1,0:T(2,128)} fusion(f32[2,2,8]{2,1,0:T(2,128)S(1)} %maximum_add_fusion, s32[2,2,8]{2,1,0:T(2,128)S(1)} %get-tuple-element.28), kind=kLoop, calls=%fused_computation.2 | loop fusion | flops 64 | bytes 384 | tf_op jit(solution)/shard_map/jit(_where)/select_n | solution.py:315
  (17 shorter events, 0.1 us)
Async XLA Ops:
  1.0 3.0 %copy-start.1 = (bf16[2,256,2048]{2,1,0:T(8,128)(2,1)S(1)}, bf16[2,256,2048]{2,1,0:T(8,128)(2,1)}, u32[]{:S(2)}) copy-start(bf16[2,256,2048]{2,1,0:T(8,128)(2,1)} %refs_0_.3) | copy-start | bytes 6291460
  1.0 3.0 %copy-start.3 = (bf16[2,2048,64]{1,2,0:T(8,128)(2,1)S(1)}, bf16[2,2048,64]{1,2,0:T(8,128)(2,1)}, u32[]{:S(2)}) copy-start(bf16[2,2048,64]{1,2,0:T(8,128)(2,1)} %param.9) | copy-start | bytes 1572868
  1.0 6.3 %collective-permute-start = (bf16[2,64,384]{2,1,0:T(8,128)(2,1)S(1)}, bf16[2,64,384]{2,1,0:T(8,128)(2,1)S(1)}, u32[]{:S(2)}, u32[]{:S(2)}) collective-permute-start(bf16[2,64,384]{2,1,0:T(8,128)(2,1)S(1)} %get-tuple-element.18.refs_0_), channel_id=1, source_target_pairs={{0,2},{2,0},{1,3},{3,1},{4,6},{6,4},{5,7},{7,5},{8,10},{10,8},{9,1... | collective-permute-start | bytes 294920 | tf_op jit(solution)/shard_map/ppermute | solution.py:202
  4.0 6.4 %copy-start = (bf16[2,128,4096]{2,1,0:T(8,128)(2,1)S(1)}, bf16[2,128,4096]{2,1,0:T(8,128)(2,1)}, u32[]{:S(2)}) copy-start(bf16[2,128,4096]{2,1,0:T(8,128)(2,1)} %refs_1_.3) | copy-start | bytes 6291460
  4.0 6.4 %copy-start.2 = (bf16[2,2048,64]{1,2,0:T(8,128)(2,1)S(1)}, bf16[2,2048,64]{1,2,0:T(8,128)(2,1)}, u32[]{:S(2)}) copy-start(bf16[2,2048,64]{1,2,0:T(8,128)(2,1)} %param.10) | copy-start | bytes 1572868
  5.1 5.8 %copy-start.4 = (bf16[2,8,4096]{2,1,0:T(8,128)(2,1)S(1)}, bf16[2,8,4096]{2,1,0:T(8,128)(2,1)}, u32[]{:S(2)}) copy-start(bf16[2,8,4096]{2,1,0:T(8,128)(2,1)} %refs_0_.5) | copy-start | bytes 393220
  5.2 7.8 %collective-permute-start.4 = (bf16[2,64,640]{2,1,0:T(8,128)(2,1)S(1)}, bf16[2,64,640]{2,1,0:T(8,128)(2,1)S(1)}, u32[]{:S(2)}, u32[]{:S(2)}) collective-permute-start(bf16[2,64,640]{2,1,0:T(8,128)(2,1)S(1)} %get-tuple-element.24), channel_id=1, source_target_pairs={{0,2},{2,0},{1,3},{3,1},{4,6},{6,4},{5,7},{7,5},{8,10},{10,8},{9,1... | collective-permute-start | bytes 491528 | tf_op jit(solution)/shard_map/ppermute | solution.py:202
  6.6 6.4 %collective-permute-start.3 = (bf16[2,64,384]{2,1,0:T(8,128)(2,1)S(1)}, bf16[2,64,384]{2,1,0:T(8,128)(2,1)S(1)}, u32[]{:S(2)}, u32[]{:S(2)}) collective-permute-start(bf16[2,64,384]{2,1,0:T(8,128)(2,1)S(1)} %get-tuple-element.23), channel_id=1, source_target_pairs={{0,2},{2,0},{1,3},{3,1},{4,6},{6,4},{5,7},{7,5},{8,10},{10,8},{9,1... | collective-permute-start | bytes 294920 | tf_op jit(solution)/shard_map/ppermute | solution.py:202
  7.2 5.7 %collective-permute-start.1 = (bf16[2,64,384]{2,1,0:T(8,128)(2,1)S(1)}, bf16[2,64,384]{2,1,0:T(8,128)(2,1)S(1)}, u32[]{:S(2)}, u32[]{:S(2)}) collective-permute-start(bf16[2,64,384]{2,1,0:T(8,128)(2,1)S(1)} %collective-permute-done.refs_2_), channel_id=1, source_target_pairs={{0,4},{1,17},{4,0},{5,21},{8,12},{9,25},{12,8},{13,29},{16,20},{17... | collective-permute-start | bytes 294920 | tf_op jit(solution)/shard_map/ppermute | solution.py:220
  8.9 4.6 %collective-permute-start.2 = (bf16[2,64,384]{2,1,0:T(8,128)(2,1)S(1)}, bf16[2,64,384]{2,1,0:T(8,128)(2,1)S(1)}, u32[]{:S(2)}, u32[]{:S(2)}) collective-permute-start(bf16[2,64,384]{2,1,0:T(8,128)(2,1)S(1)} %collective-permute-done.refs_2_), channel_id=1, source_target_pairs={{0,16},{1,5},{4,20},{5,1},{8,24},{9,13},{12,28},{13,9},{16,0},{17,... | collective-permute-start | bytes 294920 | tf_op jit(solution)/shard_map/ppermute | solution.py:220
  11.0 7.2 %collective-permute-start.6 = (bf16[2,8,4096]{2,1,0:T(8,128)(2,1)S(1)}, bf16[2,8,4096]{2,1,0:T(8,128)(2,1)S(1)}, u32[]{:S(2)}, u32[]{:S(2)}) collective-permute-start(bf16[2,8,4096]{2,1,0:T(8,128)(2,1)S(1)} %copy-done.4), channel_id=1, source_target_pairs={{0,4},{4,0},{8,12},{12,8},{1,5},{5,1},{9,13},{13,9},{2,6},{6,2},{1... | collective-permute-start | bytes 393224 | tf_op jit(solution)/shard_map/ppermute | solution.py:207
  14.1 4.1 %collective-permute-start.5 = (bf16[1,16,512]{2,1,0:T(8,128)(2,1)S(1)}, bf16[1,16,512]{2,1,0:T(8,128)(2,1)S(1)}, u32[]{:S(2)}, u32[]{:S(2)}) collective-permute-start(bf16[1,16,512]{2,1,0:T(8,128)(2,1)S(1)} %bitcast.16), channel_id=1, source_target_pairs={{0,9},{1,8},{4,13},{5,12},{8,1},{9,0},{12,5},{13,4},{2,11},{3,10},... | collective-permute-start | bytes 49160 | tf_op jit(solution)/shard_map/ppermute | solution.py:213
  18.4 3.5 %collective-permute-start.7 = (bf16[2,16,512]{2,1,0:T(8,128)(2,1)S(1)}, bf16[2,16,512]{2,1,0:T(8,128)(2,1)S(1)}, u32[]{:S(2)}, u32[]{:S(2)}) collective-permute-start(bf16[2,16,512]{2,1,0:T(8,128)(2,1)S(1)} %pad_maximum_fusion.1), channel_id=1, source_target_pairs={{0,3},{1,2},{2,1},{3,0},{4,7},{5,6},{6,5},{7,4},{8,11},{9,10},{10,... | collective-permute-start | bytes 98312 | tf_op jit(solution)/shard_map/ppermute | solution.py:213
  19.7 2.2 %collective-permute-start.8 = (bf16[128,512]{1,0:T(8,128)(2,1)S(1)}, bf16[128,512]{1,0:T(8,128)(2,1)S(1)}, u32[]{:S(2)}, u32[]{:S(2)}) collective-permute-start(bf16[128,512]{1,0:T(8,128)(2,1)S(1)} %shard_map.70.refs_1_), channel_id=1, source_target_pairs={{0,1},{1,0},{2,3},{3,2},{4,5},{5,4},{6,7},{7,6},{8,9},{9,8},{10,11... | collective-permute-start | bytes 393224 | tf_op jit(solution)/shard_map/ppermute | solution.py:207
  20.2 1.7 %collective-permute-start.9 = (bf16[128,512]{1,0:T(8,128)(2,1)S(1)}, bf16[128,512]{1,0:T(8,128)(2,1)S(1)}, u32[]{:S(2)}, u32[]{:S(2)}) collective-permute-start(bf16[128,512]{1,0:T(8,128)(2,1)S(1)} %shard_map.69.refs_3_), channel_id=1, source_target_pairs={{0,1},{1,0},{2,3},{3,2},{4,5},{5,4},{6,7},{7,6},{8,9},{9,8},{10,11... | collective-permute-start | bytes 393224 | tf_op jit(solution)/shard_map/ppermute | solution.py:207
  22.3 3.1 %collective-permute-start.10 = (f32[4,8]{1,0:T(4,128)S(1)}, f32[4,8]{1,0:T(4,128)S(1)}, u32[]{:S(2)}, u32[]{:S(2)}) collective-permute-start(f32[4,8]{1,0:T(4,128)S(1)} %get-tuple-element.30), channel_id=1, source_target_pairs={{0,5},{1,4},{4,1},{5,0},{8,13},{9,12},{12,9},{13,8},{2,7},{3,6},{6... | collective-permute-start | bytes 392 | tf_op jit(solution)/shard_map/ppermute | solution.py:213
  25.4 1.2 %collective-permute-start.11 = (f32[2,2,8]{2,1,0:T(2,128)S(1)}, f32[2,2,8]{2,1,0:T(2,128)S(1)}, u32[]{:S(2)}, u32[]{:S(2)}) collective-permute-start(f32[2,2,8]{2,1,0:T(2,128)S(1)} %pad_maximum_fusion.2), channel_id=1, source_target_pairs={{0,1},{1,0},{2,3},{3,2},{4,5},{5,4},{6,7},{7,6},{8,9},{9,8},{10,11... | collective-permute-start | bytes 392 | tf_op jit(solution)/shard_map/ppermute | solution.py:207

commit v8 on v7

--- a/solution.py
+++ b/solution.py
@@ -134,25 +134,34 @@
     out[...] = total
 
 
-def example_gradient(n, depth, length, grads, outputs, inputs, *rest):
-    out = rest[-1]
-    seconds, thirds, fourths, parcels = (rest[i * (n - 1) : (i + 1) * (n - 1)] for i in range(4))
+def middle(n, depth, length, grads, outputs, inputs, *rest):
+    seconds, fourths, parcels = (rest[i * (n - 1) : (i + 1) * (n - 1)] for i in range(3))
+    total_out, ins_out = rest[-2:]
     slots, lanes = inputs.shape
     t = lax.axis_index("tensor")
     total = outputs[...]
     ins = inputs[...]
     for s in range(1, n):
-        second, third, fourth, parcel = (x[s - 1] for x in (seconds, thirds, fourths, parcels))
+        second, fourth, parcel = (x[s - 1] for x in (seconds, fourths, parcels))
         start = block_of(t, s, n) * depth
         step, size = second.shape[2], parcel.shape[2] - lanes
         total = total + product(grads, start + side(1, 1) * step, fourth)
         total = total + product(grads, start + 4 * step, parcel.at[:, :, :size])
         total = total + product(grads, start + swapped(True) * step, second)
-        total = total + product(grads, start + swapped(False) * step, third)
         ins = ins + parcel[:, :, size:].reshape(slots, lanes).astype(F32)
+    total_out[...] = total
     live = lax.broadcasted_iota(jnp.int32, ins.shape, 0) < length[0]
-    ins = jnp.where(live, ins, 0.0).astype(BF16)
-    both = dot(ins, total.astype(BF16), TN)
+    ins_out[...] = jnp.where(live, ins, 0.0).astype(BF16)
+
+
+def example_gradient(n, depth, grads, outputs, inputs, *rest):
+    thirds, out = rest[:-1], rest[-1]
+    t = lax.axis_index("tensor")
+    total = outputs[...]
+    for s, third in enumerate(thirds, 1):
+        start = block_of(t, s, n) * depth + swapped(False) * third.shape[2]
+        total = total + product(grads, start, third)
+    both = dot(inputs[...], total.astype(BF16), TN)
     layers = grads.shape[0]
     width = both.shape[1] // layers
     lane = lax.broadcasted_iota(jnp.int32, (width, both.shape[1]), 1)
@@ -282,17 +291,27 @@
     own_other = flipped(own, "query", 1)
     near = fold(near)
     near_other = flipped(near, "query", 1)
-    grad = call(
-        functools.partial(example_gradient, n, depth),
-        jax.ShapeDtypeStruct((FOLD, width // FOLD * lanes), BF16),
+    outputs, inputs = call(
+        functools.partial(middle, n, depth),
+        (
+            jax.ShapeDtypeStruct((slots, lanes), F32),
+            jax.ShapeDtypeStruct((slots, lanes), BF16),
+        ),
         lengths,
         out_grads,
         outputs,
         mine,
         *[in_vmem(x) for x in seconds],
-        *[in_vmem(x) for x in thirds],
         *[in_vmem(x) for x in fourths],
         *[in_vmem(x) for x in parcels],
+    )
+    grad = call(
+        functools.partial(example_gradient, n, depth),
+        jax.ShapeDtypeStruct((FOLD, width // FOLD * lanes), BF16),
+        out_grads,
+        outputs,
+        inputs,
+        *[in_vmem(x) for x in thirds],
     )
     steps = [("dp", 1 << b) for b in reversed(range(1, n_dp.bit_length() - 1))]
     steps += [("tensor", 1 << b) for b in range(n.bit_length() - 1)]

time: 27.4 us -> 27.2 us (level)
  waiting for transfers between devices: 8.73 us -> 6.99 us
  starting transfers between devices: 13.1 us -> 14.4 us
    ppermute x3, waiting for transfers between devices: 6.32 us -> 5.2 us  [crossed(): lax.ppermute(x, (axis, 'query'), [(i, i ^ bit * cores + 1) for i in range...]
    ppermute x3, starting transfers between devices: 3.59 us -> 4.66 us  [crossed(): lax.ppermute(x, (axis, 'query'), [(i, i ^ bit * cores + 1) for i in range...]
    ppermute x2, waiting for transfers between devices: 0.52 us -> 0.12 us  [forwarded(): return lax.ppermute(x, ('parts', 'dp', 'query'), pairs)]
    pallas_call x8 -> x9, Pallas kernels: 3.98 us -> 4.2 us  [call(): pl.pallas_call(body, out_shape=out_shape, in_specs=specs + [ANY] * len(af...]
  transfers between devices with their start and end apart: 12 -> 12, of which waited for: 6 -> 6; matrix products, arithmetic and copies ran while one was open for 0% -> 0% of each run, Pallas kernels for 9% -> 10%
where the time goes in v8:
time: 27.2 us; the launch traced here: 27 us
  starting transfers between devices  14.4 us (53%)
  waiting for transfers between devices  6.99 us (26%)
  Pallas kernels  4.2 us (15%)
  between operations  0.79 us (3%)
  other arithmetic  0.61 us (2%)
    ppermute x3, waiting for transfers between devices, crossed(): lax.ppermute(x, (axis, 'query'), [(i, i ^ bit * cores + 1) for i in range...  5.2 us
    ppermute x3, starting transfers between devices, shifted(): return lax.ppermute(x, axis, [(i, (i + shift) % n) for i in range(n)])  5.09 us
    ppermute x3, starting transfers between devices, crossed(): lax.ppermute(x, (axis, 'query'), [(i, i ^ bit * cores + 1) for i in range...  4.66 us
    pallas_call x9, Pallas kernels, call(): pl.pallas_call(body, out_shape=out_shape, in_specs=specs + [ANY] * len(af...  4.2 us
    ppermute x2, starting transfers between devices, forwarded(): return lax.ppermute(x, ('parts', 'dp', 'query'), pairs)  3.17 us
    ppermute x4, starting transfers between devices, flipped(): return lax.ppermute(x, axis, [(i, i ^ bit) for i in range(n)])  1.51 us
    ppermute x3, waiting for transfers between devices, shifted(): return lax.ppermute(x, axis, [(i, (i + shift) % n) for i in range(n)])  0.84 us
    ppermute x4, waiting for transfers between devices, flipped(): return lax.ppermute(x, axis, [(i, i ^ bit) for i in range(n)])  0.83 us
  transfers between devices with their start and end apart: 12, of which 6 were waited for; matrix products, arithmetic and copies ran while one was open for 0% of the time, Pallas kernels for 10%

profile of v8, /device:TPU:0, one launch (start us, length us, event | category | flops | bytes accessed | tf_op | source)
XLA Modules:
  0.0 27.0 jit_solution(16189758098639477532)
XLA Ops:
  0.0 1.0 %shard_map.64 = (bf16[2,64,384]{2,1,0:T(8,128)(2,1)S(1)}, bf16[2,64,384]{2,1,0:T(8,128)(2,1)S(1)}) custom-call(bf16[2,64,2048]{2,1,0:T(8,128)(2,1)} %bitcast.12), custom_call_target="tpu_custom_call" | custom-call | flops 1 | bytes 1 | tf_op jit(solution)/shard_map/pallas_call | solution.py:31
  1.0 0.0 copy-start.1
  1.0 0.0 copy-start.3
  1.0 3.0 %collective-permute-start = (bf16[2,64,384]{2,1,0:T(8,128)(2,1)S(1)}, bf16[2,64,384]{2,1,0:T(8,128)(2,1)S(1)}, u32[]{:S(2)}, u32[]{:S(2)}) collective-permute-start(bf16[2,64,384]{2,1,0:T(8,128)(2,1)S(1)} %get-tuple-element.20.refs_0_), channel_id=1, source_target_pairs={{0,2},{2,0},{1,3},{3,1},{4,6},{6,4},{5,7},{7,5},{8,10},{10,8},{9,1... | collective-permute-start | bytes 294920 | tf_op jit(solution)/shard_map/ppermute | solution.py:211
  4.0 1.1 %shard_map.66 = (f32[128,128]{1,0:T(8,128)S(1)}, bf16[2,64,640]{2,1,0:T(8,128)(2,1)S(1)}) custom-call(bf16[2,256,2048]{2,1,0:T(8,128)(2,1)S(1)} %copy-done.1, bf16[2,64,2048]{2,1,0:T(8,128)(2,1)S(1)} %bitcast.15, bf16[2,64,2048]{2,1,0:T(8,128)(2,1)} %bitcast.13, f32[8,128]{1,0:T(8,128)S(1)} %shard_map.65.refs_3_), custom_call_target="tpu_custom_call" | custom-call | flops 1 | bytes 1 | tf_op jit(solution)/shard_map/pallas_call | solution.py:31
  5.1 0.0 copy-start.4
  5.2 1.5 %collective-permute-start.3 = (bf16[2,64,640]{2,1,0:T(8,128)(2,1)S(1)}, bf16[2,64,640]{2,1,0:T(8,128)(2,1)S(1)}, u32[]{:S(2)}, u32[]{:S(2)}) collective-permute-start(bf16[2,64,640]{2,1,0:T(8,128)(2,1)S(1)} %get-tuple-element.26), channel_id=1, source_target_pairs={{0,2},{2,0},{1,3},{3,1},{4,6},{6,4},{5,7},{7,5},{8,10},{10,8},{9,1... | collective-permute-start | bytes 491528 | tf_op jit(solution)/shard_map/ppermute | solution.py:211
  6.6 0.6 %collective-permute-start.2 = (bf16[2,64,384]{2,1,0:T(8,128)(2,1)S(1)}, bf16[2,64,384]{2,1,0:T(8,128)(2,1)S(1)}, u32[]{:S(2)}, u32[]{:S(2)}) collective-permute-start(bf16[2,64,384]{2,1,0:T(8,128)(2,1)S(1)} %get-tuple-element.25), channel_id=1, source_target_pairs={{0,2},{2,0},{1,3},{3,1},{4,6},{6,4},{5,7},{7,5},{8,10},{10,8},{9,1... | collective-permute-start | bytes 294920 | tf_op jit(solution)/shard_map/ppermute | solution.py:211
  7.2 0.0 collective-permute-done.refs_2_
  7.2 1.6 %collective-permute-start.1 = (bf16[2,64,384]{2,1,0:T(8,128)(2,1)S(1)}, bf16[2,64,384]{2,1,0:T(8,128)(2,1)S(1)}, u32[]{:S(2)}, u32[]{:S(2)}) collective-permute-start(bf16[2,64,384]{2,1,0:T(8,128)(2,1)S(1)} %collective-permute-done.refs_2_), channel_id=1, source_target_pairs={{0,4},{1,17},{4,0},{5,21},{8,12},{9,25},{12,8},{13,29},{16,20},{17... | collective-permute-start | bytes 294920 | tf_op jit(solution)/shard_map/ppermute | solution.py:229
  8.9 1.5 %collective-permute-start.4 = (bf16[2,64,384]{2,1,0:T(8,128)(2,1)S(1)}, bf16[2,64,384]{2,1,0:T(8,128)(2,1)S(1)}, u32[]{:S(2)}, u32[]{:S(2)}) collective-permute-start(bf16[2,64,384]{2,1,0:T(8,128)(2,1)S(1)} %collective-permute-done.refs_2_), channel_id=1, source_target_pairs={{0,16},{1,5},{4,20},{5,1},{8,24},{9,13},{12,28},{13,9},{16,0},{17,... | collective-permute-start | bytes 294920 | tf_op jit(solution)/shard_map/ppermute | solution.py:229
  10.4 0.5 %shard_map.67.refs_2_ = f32[128,128]{1,0:T(8,128)S(1)} custom-call(bf16[2,128,4096]{2,1,0:T(8,128)(2,1)S(1)} %copy-done, bf16[2,64,2048]{2,1,0:T(8,128)(2,1)S(1)} %bitcast.14, bf16[2,64,384]{2,1,0:T(8,128)(2,1)S(1)} %collective-permute-done.refs_2_), custom_call_target="tpu_custom_call" | custom-call | flops 1 | bytes 1 | tf_op jit(solution)/shard_map/pallas_call | solution.py:31
  11.0 0.5 %collective-permute-start.6 = (bf16[2,8,4096]{2,1,0:T(8,128)(2,1)S(1)}, bf16[2,8,4096]{2,1,0:T(8,128)(2,1)S(1)}, u32[]{:S(2)}, u32[]{:S(2)}) collective-permute-start(bf16[2,8,4096]{2,1,0:T(8,128)(2,1)S(1)} %copy-done.4), channel_id=1, source_target_pairs={{0,4},{4,0},{8,12},{12,8},{1,5},{5,1},{9,13},{13,9},{2,6},{6,2},{1... | collective-permute-start | bytes 393224 | tf_op jit(solution)/shard_map/ppermute | solution.py:216
  12.1 0.8 %collective-permute-done.2.refs_5_ = bf16[2,64,384]{2,1,0:T(8,128)(2,1)S(1)} collective-permute-done((bf16[2,64,384]{2,1,0:T(8,128)(2,1)S(1)}, bf16[2,64,384]{2,1,0:T(8,128)(2,1)S(1)}, u32[]{:S(2)}, u32[]{:S(2)}) %collective-permute-start.2) | collective-permute-done | bytes 98336 | tf_op jit(solution)/shard_map/ppermute | solution.py:211
  13.0 0.0 collective-permute-done.3.refs_6_
  13.0 0.4 %shard_map.68 = (f32[128,128]{1,0:T(8,128)S(1)}, bf16[128,128]{1,0:T(8,128)(2,1)S(1)}) custom-call(s32[1]{0:T(128)S(6)} %copy.7.refs_0_, bf16[2,128,4096]{2,1,0:T(8,128)(2,1)S(1)} %copy-done, f32[128,128]{1,0:T(8,128)S(1)} %shard_map.67.refs_2_, f32[128,128]{1,0:T(8,128)S(1)} %get-tuple-element.24.refs_3_, ...), custom_call_target="tpu_custom_call" | custom-call | flops 1 | bytes 1 | tf_op jit(solution)/shard_map/pallas_call | solution.py:31
  13.4 0.1 collective-permute-done.4.refs_3_
  13.5 0.4 %shard_map.69 = bf16[16,512]{1,0:T(8,128)(2,1)S(1)} custom-call(bf16[2,128,4096]{2,1,0:T(8,128)(2,1)S(1)} %copy-done, f32[128,128]{1,0:T(8,128)S(1)} %get-tuple-element.27.refs_1_, bf16[128,128]{1,0:T(8,128)(2,1)S(1)} %get-tuple-element.28.refs_2_, bf16[2,64,384]{2,1,0:T(8,128)(2,1)S(1)} %collective-permute-done.4.refs_3_), custom_call_target="tpu_custom_call" | custom-call | flops 1 | bytes 1 | tf_op jit(solution)/shard_map/pallas_call | solution.py:31
  13.9 1.6 %collective-permute-start.5 = (bf16[1,16,512]{2,1,0:T(8,128)(2,1)S(1)}, bf16[1,16,512]{2,1,0:T(8,128)(2,1)S(1)}, u32[]{:S(2)}, u32[]{:S(2)}) collective-permute-start(bf16[1,16,512]{2,1,0:T(8,128)(2,1)S(1)} %bitcast.16), channel_id=1, source_target_pairs={{0,9},{1,8},{4,13},{5,12},{8,1},{9,0},{12,5},{13,4},{2,11},{3,10},... | collective-permute-start | bytes 49160 | tf_op jit(solution)/shard_map/ppermute | solution.py:222
  15.5 2.5 %collective-permute-done.5 = bf16[1,16,512]{2,1,0:T(8,128)(2,1)S(1)} collective-permute-done((bf16[1,16,512]{2,1,0:T(8,128)(2,1)S(1)}, bf16[1,16,512]{2,1,0:T(8,128)(2,1)S(1)}, u32[]{:S(2)}, u32[]{:S(2)}) %collective-permute-start.5) | collective-permute-done | bytes 16416 | tf_op jit(solution)/shard_map/ppermute | solution.py:222
  18.1 0.2 shard_map.70.refs_3_
  18.2 1.4 %collective-permute-start.7 = (bf16[2,16,512]{2,1,0:T(8,128)(2,1)S(1)}, bf16[2,16,512]{2,1,0:T(8,128)(2,1)S(1)}, u32[]{:S(2)}, u32[]{:S(2)}) collective-permute-start(bf16[2,16,512]{2,1,0:T(8,128)(2,1)S(1)} %pad_maximum_fusion.1), channel_id=1, source_target_pairs={{0,3},{1,2},{2,1},{3,0},{4,7},{5,6},{6,5},{7,4},{8,11},{9,10},{10,... | collective-permute-start | bytes 98312 | tf_op jit(solution)/shard_map/ppermute | solution.py:222
  19.6 0.2 shard_map.71.refs_1_
  19.8 0.5 %collective-permute-start.8 = (bf16[128,512]{1,0:T(8,128)(2,1)S(1)}, bf16[128,512]{1,0:T(8,128)(2,1)S(1)}, u32[]{:S(2)}, u32[]{:S(2)}) collective-permute-start(bf16[128,512]{1,0:T(8,128)(2,1)S(1)} %shard_map.71.refs_1_), channel_id=1, source_target_pairs={{0,1},{1,0},{2,3},{3,2},{4,5},{5,4},{6,7},{7,6},{8,9},{9,8},{10,11... | collective-permute-start | bytes 393224 | tf_op jit(solution)/shard_map/ppermute | solution.py:216
  20.2 0.1 collective-permute-start.9
  20.4 1.3 %collective-permute-done.7 = bf16[2,16,512]{2,1,0:T(8,128)(2,1)S(1)} collective-permute-done((bf16[2,16,512]{2,1,0:T(8,128)(2,1)S(1)}, bf16[2,16,512]{2,1,0:T(8,128)(2,1)S(1)}, u32[]{:S(2)}, u32[]{:S(2)}) %collective-permute-start.7) | collective-permute-done | bytes 32800 | tf_op jit(solution)/shard_map/ppermute | solution.py:222
  21.7 0.4 %shard_map.72 = (f32[4,8]{1,0:T(4,128)S(1)}, f32[4,8]{1,0:T(4,128)S(1)}, s32[2,2,8]{2,1,0:T(2,128)S(1)}) custom-call(bf16[4,16,512]{2,1,0:T(8,128)(2,1)S(1)} %pad_maximum_fusion.refs_0_, bf16[128,512]{1,0:T(8,128)(2,1)S(1)} %shard_map.71.refs_1_, bf16[128,512]{1,0:T(8,128)(2,1)S(1)} %collective-permute-done.8.refs_2_, ...), custom_call_target="tpu_custom_call" | custom-call | flops 1 | bytes 1 | tf_op jit(solution)/shard_map/pallas_call | solution.py:31
  22.1 1.7 %collective-permute-start.10 = (f32[4,8]{1,0:T(4,128)S(1)}, f32[4,8]{1,0:T(4,128)S(1)}, u32[]{:S(2)}, u32[]{:S(2)}) collective-permute-start(f32[4,8]{1,0:T(4,128)S(1)} %get-tuple-element.34), channel_id=1, source_target_pairs={{0,5},{1,4},{4,1},{5,0},{8,13},{9,12},{12,9},{13,8},{2,7},{3,6},{6... | collective-permute-start | bytes 392 | tf_op jit(solution)/shard_map/ppermute | solution.py:222
  23.8 1.4 %collective-permute-done.10 = f32[4,8]{1,0:T(4,128)S(1)} collective-permute-done((f32[4,8]{1,0:T(4,128)S(1)}, f32[4,8]{1,0:T(4,128)S(1)}, u32[]{:S(2)}, u32[]{:S(2)}) %collective-permute-start.10) | collective-permute-done | bytes 160 | tf_op jit(solution)/shard_map/ppermute | solution.py:222
  25.2 0.4 %collective-permute-start.11 = (f32[2,2,8]{2,1,0:T(2,128)S(1)}, f32[2,2,8]{2,1,0:T(2,128)S(1)}, u32[]{:S(2)}, u32[]{:S(2)}) collective-permute-start(f32[2,2,8]{2,1,0:T(2,128)S(1)} %pad_maximum_fusion.2), channel_id=1, source_target_pairs={{0,1},{1,0},{2,3},{3,2},{4,5},{5,4},{6,7},{7,6},{8,9},{9,8},{10,11... | collective-permute-start | bytes 392 | tf_op jit(solution)/shard_map/ppermute | solution.py:216
  25.6 0.8 %collective-permute-done.11 = f32[2,2,8]{2,1,0:T(2,128)S(1)} collective-permute-done((f32[2,2,8]{2,1,0:T(2,128)S(1)}, f32[2,2,8]{2,1,0:T(2,128)S(1)}, u32[]{:S(2)}, u32[]{:S(2)}) %collective-permute-start.11) | collective-permute-done | bytes 160 | tf_op jit(solution)/shard_map/ppermute | solution.py:216
  26.5 0.6 %compare_select_fusion = f32[2,2,8]{2,1,0:T(2,128)} fusion(f32[2,2,8]{2,1,0:T(2,128)S(1)} %maximum_add_fusion, s32[2,2,8]{2,1,0:T(2,128)S(1)} %get-tuple-element.32), kind=kLoop, calls=%fused_computation.2 | loop fusion | flops 64 | bytes 384 | tf_op jit(solution)/shard_map/jit(_where)/select_n | solution.py:334
  (18 shorter events, 0.1 us)
Async XLA Ops:
  1.0 3.0 %copy-start.1 = (bf16[2,256,2048]{2,1,0:T(8,128)(2,1)S(1)}, bf16[2,256,2048]{2,1,0:T(8,128)(2,1)}, u32[]{:S(2)}) copy-start(bf16[2,256,2048]{2,1,0:T(8,128)(2,1)} %refs_0_.4) | copy-start | bytes 6291460
  1.0 3.0 %copy-start.3 = (bf16[2,2048,64]{1,2,0:T(8,128)(2,1)S(1)}, bf16[2,2048,64]{1,2,0:T(8,128)(2,1)}, u32[]{:S(2)}) copy-start(bf16[2,2048,64]{1,2,0:T(8,128)(2,1)} %param.9) | copy-start | bytes 1572868
  1.0 6.3 %collective-permute-start = (bf16[2,64,384]{2,1,0:T(8,128)(2,1)S(1)}, bf16[2,64,384]{2,1,0:T(8,128)(2,1)S(1)}, u32[]{:S(2)}, u32[]{:S(2)}) collective-permute-start(bf16[2,64,384]{2,1,0:T(8,128)(2,1)S(1)} %get-tuple-element.20.refs_0_), channel_id=1, source_target_pairs={{0,2},{2,0},{1,3},{3,1},{4,6},{6,4},{5,7},{7,5},{8,10},{10,8},{9,1... | collective-permute-start | bytes 294920 | tf_op jit(solution)/shard_map/ppermute | solution.py:211
  4.0 6.4 %copy-start = (bf16[2,128,4096]{2,1,0:T(8,128)(2,1)S(1)}, bf16[2,128,4096]{2,1,0:T(8,128)(2,1)}, u32[]{:S(2)}) copy-start(bf16[2,128,4096]{2,1,0:T(8,128)(2,1)} %refs_0_.6) | copy-start | bytes 6291460
  4.0 6.4 %copy-start.2 = (bf16[2,2048,64]{1,2,0:T(8,128)(2,1)S(1)}, bf16[2,2048,64]{1,2,0:T(8,128)(2,1)}, u32[]{:S(2)}) copy-start(bf16[2,2048,64]{1,2,0:T(8,128)(2,1)} %param.10) | copy-start | bytes 1572868
  5.1 5.8 %copy-start.4 = (bf16[2,8,4096]{2,1,0:T(8,128)(2,1)S(1)}, bf16[2,8,4096]{2,1,0:T(8,128)(2,1)}, u32[]{:S(2)}) copy-start(bf16[2,8,4096]{2,1,0:T(8,128)(2,1)} %refs_0_.7) | copy-start | bytes 393220
  5.2 7.8 %collective-permute-start.3 = (bf16[2,64,640]{2,1,0:T(8,128)(2,1)S(1)}, bf16[2,64,640]{2,1,0:T(8,128)(2,1)S(1)}, u32[]{:S(2)}, u32[]{:S(2)}) collective-permute-start(bf16[2,64,640]{2,1,0:T(8,128)(2,1)S(1)} %get-tuple-element.26), channel_id=1, source_target_pairs={{0,2},{2,0},{1,3},{3,1},{4,6},{6,4},{5,7},{7,5},{8,10},{10,8},{9,1... | collective-permute-start | bytes 491528 | tf_op jit(solution)/shard_map/ppermute | solution.py:211
  6.6 6.4 %collective-permute-start.2 = (bf16[2,64,384]{2,1,0:T(8,128)(2,1)S(1)}, bf16[2,64,384]{2,1,0:T(8,128)(2,1)S(1)}, u32[]{:S(2)}, u32[]{:S(2)}) collective-permute-start(bf16[2,64,384]{2,1,0:T(8,128)(2,1)S(1)} %get-tuple-element.25), channel_id=1, source_target_pairs={{0,2},{2,0},{1,3},{3,1},{4,6},{6,4},{5,7},{7,5},{8,10},{10,8},{9,1... | collective-permute-start | bytes 294920 | tf_op jit(solution)/shard_map/ppermute | solution.py:211
  7.2 5.7 %collective-permute-start.1 = (bf16[2,64,384]{2,1,0:T(8,128)(2,1)S(1)}, bf16[2,64,384]{2,1,0:T(8,128)(2,1)S(1)}, u32[]{:S(2)}, u32[]{:S(2)}) collective-permute-start(bf16[2,64,384]{2,1,0:T(8,128)(2,1)S(1)} %collective-permute-done.refs_2_), channel_id=1, source_target_pairs={{0,4},{1,17},{4,0},{5,21},{8,12},{9,25},{12,8},{13,29},{16,20},{17... | collective-permute-start | bytes 294920 | tf_op jit(solution)/shard_map/ppermute | solution.py:229
  8.9 4.6 %collective-permute-start.4 = (bf16[2,64,384]{2,1,0:T(8,128)(2,1)S(1)}, bf16[2,64,384]{2,1,0:T(8,128)(2,1)S(1)}, u32[]{:S(2)}, u32[]{:S(2)}) collective-permute-start(bf16[2,64,384]{2,1,0:T(8,128)(2,1)S(1)} %collective-permute-done.refs_2_), channel_id=1, source_target_pairs={{0,16},{1,5},{4,20},{5,1},{8,24},{9,13},{12,28},{13,9},{16,0},{17,... | collective-permute-start | bytes 294920 | tf_op jit(solution)/shard_map/ppermute | solution.py:229
  11.0 7.1 %collective-permute-start.6 = (bf16[2,8,4096]{2,1,0:T(8,128)(2,1)S(1)}, bf16[2,8,4096]{2,1,0:T(8,128)(2,1)S(1)}, u32[]{:S(2)}, u32[]{:S(2)}) collective-permute-start(bf16[2,8,4096]{2,1,0:T(8,128)(2,1)S(1)} %copy-done.4), channel_id=1, source_target_pairs={{0,4},{4,0},{8,12},{12,8},{1,5},{5,1},{9,13},{13,9},{2,6},{6,2},{1... | collective-permute-start | bytes 393224 | tf_op jit(solution)/shard_map/ppermute | solution.py:216
  13.9 4.1 %collective-permute-start.5 = (bf16[1,16,512]{2,1,0:T(8,128)(2,1)S(1)}, bf16[1,16,512]{2,1,0:T(8,128)(2,1)S(1)}, u32[]{:S(2)}, u32[]{:S(2)}) collective-permute-start(bf16[1,16,512]{2,1,0:T(8,128)(2,1)S(1)} %bitcast.16), channel_id=1, source_target_pairs={{0,9},{1,8},{4,13},{5,12},{8,1},{9,0},{12,5},{13,4},{2,11},{3,10},... | collective-permute-start | bytes 49160 | tf_op jit(solution)/shard_map/ppermute | solution.py:222
  18.2 3.4 %collective-permute-start.7 = (bf16[2,16,512]{2,1,0:T(8,128)(2,1)S(1)}, bf16[2,16,512]{2,1,0:T(8,128)(2,1)S(1)}, u32[]{:S(2)}, u32[]{:S(2)}) collective-permute-start(bf16[2,16,512]{2,1,0:T(8,128)(2,1)S(1)} %pad_maximum_fusion.1), channel_id=1, source_target_pairs={{0,3},{1,2},{2,1},{3,0},{4,7},{5,6},{6,5},{7,4},{8,11},{9,10},{10,... | collective-permute-start | bytes 98312 | tf_op jit(solution)/shard_map/ppermute | solution.py:222
  19.8 1.9 %collective-permute-start.8 = (bf16[128,512]{1,0:T(8,128)(2,1)S(1)}, bf16[128,512]{1,0:T(8,128)(2,1)S(1)}, u32[]{:S(2)}, u32[]{:S(2)}) collective-permute-start(bf16[128,512]{1,0:T(8,128)(2,1)S(1)} %shard_map.71.refs_1_), channel_id=1, source_target_pairs={{0,1},{1,0},{2,3},{3,2},{4,5},{5,4},{6,7},{7,6},{8,9},{9,8},{10,11... | collective-permute-start | bytes 393224 | tf_op jit(solution)/shard_map/ppermute | solution.py:216
  20.2 1.4 %collective-permute-start.9 = (bf16[128,512]{1,0:T(8,128)(2,1)S(1)}, bf16[128,512]{1,0:T(8,128)(2,1)S(1)}, u32[]{:S(2)}, u32[]{:S(2)}) collective-permute-start(bf16[128,512]{1,0:T(8,128)(2,1)S(1)} %shard_map.70.refs_3_), channel_id=1, source_target_pairs={{0,1},{1,0},{2,3},{3,2},{4,5},{5,4},{6,7},{7,6},{8,9},{9,8},{10,11... | collective-permute-start | bytes 393224 | tf_op jit(solution)/shard_map/ppermute | solution.py:216
  22.1 3.1 %collective-permute-start.10 = (f32[4,8]{1,0:T(4,128)S(1)}, f32[4,8]{1,0:T(4,128)S(1)}, u32[]{:S(2)}, u32[]{:S(2)}) collective-permute-start(f32[4,8]{1,0:T(4,128)S(1)} %get-tuple-element.34), channel_id=1, source_target_pairs={{0,5},{1,4},{4,1},{5,0},{8,13},{9,12},{12,9},{13,8},{2,7},{3,6},{6... | collective-permute-start | bytes 392 | tf_op jit(solution)/shard_map/ppermute | solution.py:222
  25.2 1.2 %collective-permute-start.11 = (f32[2,2,8]{2,1,0:T(2,128)S(1)}, f32[2,2,8]{2,1,0:T(2,128)S(1)}, u32[]{:S(2)}, u32[]{:S(2)}) collective-permute-start(f32[2,2,8]{2,1,0:T(2,128)S(1)} %pad_maximum_fusion.2), channel_id=1, source_target_pairs={{0,1},{1,0},{2,3},{3,2},{4,5},{5,4},{6,7},{7,6},{8,9},{9,8},{10,11... | collective-permute-start | bytes 392 | tf_op jit(solution)/shard_map/ppermute | solution.py:216

commit v9 on v8

--- a/solution.py
+++ b/solution.py
@@ -66,11 +66,11 @@
     out[...] = jnp.zeros(out.shape, out.dtype)
 
 
-def cut(factor, piece, other, sems):
+def cut(factor, piece, other, tail, sems):
     step = piece.shape[2]
     copies = []
-    for i, (out, place) in enumerate(((piece, side()), (other, side(1, 1)))):
-        columns = pl.ds(pl.multiple_of(place * step, 128), step)
+    for i, (out, start) in enumerate(((piece, side() * step), (other, side(1, 1) * step), (tail, 4 * step))):
+        columns = pl.ds(pl.multiple_of(start, 128), out.shape[2])
         copies.append(pltpu.make_async_copy(factor.at[:, :, columns], out, sems.at[i]))
     for copy in copies:
         copy.start()
@@ -78,29 +78,20 @@
         copy.wait()
 
 
-def project_inputs(n, acts, factor, factor_out, mine, *rest):
-    parcels, sems = rest[:-1], rest[-1]
-    slots, lanes = mine.shape
-    layers, width, size = parcels[0].shape
-    tail = pl.ds(factor_out.shape[2] - (size - lanes), size - lanes)
-    copies = [
-        pltpu.make_async_copy(factor_out.at[:, :, tail], out.at[:, :, : size - lanes], sems.at[s])
-        for s, out in enumerate(parcels)
-    ]
-    for copy in copies:
-        copy.start()
-    t = lax.axis_index("tensor")
-    total = jnp.concatenate([dot(acts[l], factor[l], NT) for l in range(layers)], axis=1)
-    for s in range(n):
-        block = total[:slots]
-        for i in range(1, n):
-            block = jnp.where(lax.rem(t + s, n) == i, total[i * slots : (i + 1) * slots], block)
-        if s == 0:
-            mine[...] = block
-        else:
-            parcels[s - 1][:, :, size - lanes :] = block.astype(BF16).reshape(layers, width, lanes)
-    for copy in copies:
-        copy.wait()
+def project(acts, block, slots, factor):
+    rows = pl.ds(pl.multiple_of(block * slots, slots), slots)
+    return jnp.concatenate(
+        [dot(acts[l, rows, :], factor[l], NT) for l in range(acts.shape[0])], axis=1
+    )
+
+
+def project_inputs(n, acts, factor, tail, *parcels):
+    layers, width, size = tail.shape
+    slots = acts.shape[1] // n
+    for s, out in enumerate(parcels, 1):
+        out[:, :, :size] = tail[...]
+        block = project(acts, lax.rem(lax.axis_index("tensor") + s, n), slots, factor)
+        out[:, :, size:] = block.astype(BF16).reshape(layers, width, layers * width)
 
 
 def fold_queries(width, queries, out, rows):
@@ -123,8 +114,8 @@
     )
 
 
-def early(n, grads, factor, *rest):
-    pieces, out = rest[:-1], rest[-1]
+def early(n, grads, factor, acts, factor_in, *rest):
+    pieces, out, inputs = rest[:-2], rest[-2], rest[-1]
     depth = factor.shape[2]
     t = lax.axis_index("tensor")
     total = product(grads, t * depth, factor)
@@ -132,6 +123,7 @@
         start = block_of(t, s, n) * depth + side() * piece.shape[2]
         total = total + product(grads, start, piece)
     out[...] = total
+    inputs[...] = project(acts, t, inputs.shape[0], factor_in)
 
 
 def middle(n, depth, length, grads, outputs, inputs, *rest):
@@ -240,12 +232,15 @@
     step = depth * 3 // 16 // 128 * 128
 
     factor = proj_out.transpose(0, 2, 1)
-    piece, other = call(
+    piece, other, tail = call(
         cut,
-        (jax.ShapeDtypeStruct((layers, width, step), BF16),) * 2,
+        (
+            *[jax.ShapeDtypeStruct((layers, width, step), BF16)] * 2,
+            jax.ShapeDtypeStruct((layers, width, depth - 4 * step), BF16),
+        ),
         in_hbm(factor),
         specs=[ANY],
-        scratch=[pltpu.SemaphoreType.DMA((2,))],
+        scratch=[pltpu.SemaphoreType.DMA((3,))],
     )
     firsts = [shifted(piece, "tensor", s) for s in range(1, n)]
     fourths = [shifted(other, "tensor", s) for s in range(1, n)]
@@ -255,28 +250,26 @@
     )
     firsts = [shifted(piece, "tensor", s) for s in range(1, n)]
 
-    mine, *parcels = call(
+    factor_in = proj_in.transpose(0, 2, 1)
+    parcels = call(
         functools.partial(project_inputs, n),
-        (
-            jax.ShapeDtypeStruct((slots, lanes), F32),
-            *[jax.ShapeDtypeStruct((layers, width, depth - 4 * step + lanes), BF16)] * (n - 1),
-        ),
+        [jax.ShapeDtypeStruct((layers, width, depth - 4 * step + lanes), BF16)] * (n - 1),
         acts,
-        proj_in.transpose(0, 2, 1),
-        in_hbm(factor),
+        factor_in,
+        tail,
         after=(token,),
-        specs=[VMEM, VMEM, ANY],
-        scratch=[pltpu.SemaphoreType.DMA((n - 1,))],
-    )
+    )
+    firsts, _ = lax.optimization_barrier((firsts, parcels))
     parcels = [shifted(parcel, "tensor", s) for s, parcel in enumerate(parcels, 1)]
-    firsts, mine = lax.optimization_barrier((firsts, mine))
     seconds = [forwarded(first, True) for first in firsts]
     thirds = [forwarded(first, False) for first in firsts]
-    outputs = call(
+    outputs, mine = call(
         functools.partial(early, n),
-        jax.ShapeDtypeStruct((slots, lanes), F32),
+        (jax.ShapeDtypeStruct((slots, lanes), F32),) * 2,
         out_grads,
         factor,
+        acts,
+        factor_in,
         *firsts,
     )
     asked, outputs = lax.optimization_barrier((query_grads, outputs))

time: 27.2 us -> 27.1 us (level)
  waiting for transfers between devices: 6.99 us -> 8.23 us
  starting transfers between devices: 14.4 us -> 13.4 us
  Pallas kernels: 4.2 us -> 3.91 us
    ppermute x3, waiting for transfers between devices: 5.2 us -> 6.3 us  [crossed(): lax.ppermute(x, (axis, 'query'), [(i, i ^ bit * cores + 1) for i in range...]
    ppermute x3, starting transfers between devices: 4.66 us -> 3.6 us  [crossed(): lax.ppermute(x, (axis, 'query'), [(i, i ^ bit * cores + 1) for i in range...]
    ppermute x3, waiting for transfers between devices: 0.84 us -> 0.38 us  [shifted(): return lax.ppermute(x, axis, [(i, (i + shift) % n) for i in range(n)])]
    ppermute x2, waiting for transfers between devices: 0.12 us -> 0.5 us  [forwarded(): return lax.ppermute(x, ('parts', 'dp', 'query'), pairs)]
    ppermute x2, starting transfers between devices: 3.17 us -> 3.47 us  [forwarded(): return lax.ppermute(x, ('parts', 'dp', 'query'), pairs)]
    pallas_call x9, Pallas kernels: 4.2 us -> 3.91 us  [call(): pl.pallas_call(body, out_shape=out_shape, in_specs=specs + [ANY] * len(af...]
  transfers between devices with their start and end apart: 12 -> 12, of which waited for: 6 -> 7; matrix products, arithmetic and copies ran while one was open for 0% -> 0% of each run, Pallas kernels for 10% -> 8%
where the time goes in v9:
time: 27.1 us; the launch traced here: 27 us
  starting transfers between devices  13.4 us (49%)
  waiting for transfers between devices  8.23 us (30%)
  Pallas kernels  3.91 us (14%)
  between operations  0.77 us (3%)
  other arithmetic  0.61 us (2%)
    ppermute x3, waiting for transfers between devices, crossed(): lax.ppermute(x, (axis, 'query'), [(i, i ^ bit * cores + 1) for i in range...  6.3 us
    ppermute x3, starting transfers between devices, shifted(): return lax.ppermute(x, axis, [(i, (i + shift) % n) for i in range(n)])  5.09 us
    pallas_call x9, Pallas kernels, call(): pl.pallas_call(body, out_shape=out_shape, in_specs=specs + [ANY] * len(af...  3.91 us
    ppermute x3, starting transfers between devices, crossed(): lax.ppermute(x, (axis, 'query'), [(i, i ^ bit * cores + 1) for i in range...  3.6 us
    ppermute x2, starting transfers between devices, forwarded(): return lax.ppermute(x, ('parts', 'dp', 'query'), pairs)  3.47 us
    ppermute x4, starting transfers between devices, flipped(): return lax.ppermute(x, axis, [(i, i ^ bit) for i in range(n)])  1.27 us
    ppermute x4, waiting for transfers between devices, flipped(): return lax.ppermute(x, axis, [(i, i ^ bit) for i in range(n)])  1.05 us
    select_n x1, other arithmetic, local(): kept = jnp.where(odd_place == 0, kept, kept[::-1]).reshape(2, -1, n, nq)  0.58 us
  transfers between devices with their start and end apart: 12, of which 7 were waited for; matrix products, arithmetic and copies ran while one was open for 0% of the time, Pallas kernels for 8%

profile of v9, /device:TPU:0, one launch (start us, length us, event | category | flops | bytes accessed | tf_op | source)
XLA Modules:
  0.0 27.0 jit_solution(10473316538046428310)
XLA Ops:
  0.0 1.0 %shard_map.64 = (bf16[2,64,384]{2,1,0:T(8,128)(2,1)S(1)}, bf16[2,64,384]{2,1,0:T(8,128)(2,1)S(1)}, bf16[2,64,512]{2,1,0:T(8,128)(2,1)S(1)}) custom-call(bf16[2,64,2048]{2,1,0:T(8,128)(2,1)} %bitcast.12), custom_call_target="tpu_custom_call" | custom-call | flops 1 | bytes 1 | tf_op jit(solution)/shard_map/pallas_call | solution.py:31
  1.0 0.0 copy-start.1
  1.0 0.0 copy-start.3
  1.1 3.0 %collective-permute-start = (bf16[2,64,384]{2,1,0:T(8,128)(2,1)S(1)}, bf16[2,64,384]{2,1,0:T(8,128)(2,1)S(1)}, u32[]{:S(2)}, u32[]{:S(2)}) collective-permute-start(bf16[2,64,384]{2,1,0:T(8,128)(2,1)S(1)} %get-tuple-element.20.refs_0_), channel_id=1, source_target_pairs={{0,2},{2,0},{1,3},{3,1},{4,6},{6,4},{5,7},{7,5},{8,10},{10,8},{9,1... | collective-permute-start | bytes 294920 | tf_op jit(solution)/shard_map/ppermute | solution.py:203
  4.1 0.5 %shard_map.66 = bf16[2,64,640]{2,1,0:T(8,128)(2,1)S(1)} custom-call(bf16[2,256,2048]{2,1,0:T(8,128)(2,1)S(1)} %copy-done.1, bf16[2,64,2048]{2,1,0:T(8,128)(2,1)S(1)} %bitcast.14, bf16[2,64,512]{2,1,0:T(8,128)(2,1)S(1)} %get-tuple-element.21.refs_2_, f32[8,128]{1,0:T(8,128)S(1)} %shard_map.65.refs_3_), custom_call_target="tpu_custom_call" | custom-call | flops 1 | bytes 1 | tf_op jit(solution)/shard_map/pallas_call | solution.py:31
  4.6 1.6 %collective-permute-start.3 = (bf16[2,64,640]{2,1,0:T(8,128)(2,1)S(1)}, bf16[2,64,640]{2,1,0:T(8,128)(2,1)S(1)}, u32[]{:S(2)}, u32[]{:S(2)}) collective-permute-start(bf16[2,64,640]{2,1,0:T(8,128)(2,1)S(1)} %shard_map.66), channel_id=1, source_target_pairs={{0,2},{2,0},{1,3},{3,1},{4,6},{6,4},{5,7},{7,5},{8,10},{10,8},{9,1... | collective-permute-start | bytes 491528 | tf_op jit(solution)/shard_map/ppermute | solution.py:203
  6.2 0.5 %collective-permute-start.2 = (bf16[2,64,384]{2,1,0:T(8,128)(2,1)S(1)}, bf16[2,64,384]{2,1,0:T(8,128)(2,1)S(1)}, u32[]{:S(2)}, u32[]{:S(2)}) collective-permute-start(bf16[2,64,384]{2,1,0:T(8,128)(2,1)S(1)} %get-tuple-element.26), channel_id=1, source_target_pairs={{0,2},{2,0},{1,3},{3,1},{4,6},{6,4},{5,7},{7,5},{8,10},{10,8},{9,1... | collective-permute-start | bytes 294920 | tf_op jit(solution)/shard_map/ppermute | solution.py:203
  6.7 0.2 collective-permute-done.refs_4_
  6.9 2.0 %collective-permute-start.1 = (bf16[2,64,384]{2,1,0:T(8,128)(2,1)S(1)}, bf16[2,64,384]{2,1,0:T(8,128)(2,1)S(1)}, u32[]{:S(2)}, u32[]{:S(2)}) collective-permute-start(bf16[2,64,384]{2,1,0:T(8,128)(2,1)S(1)} %collective-permute-done.refs_4_), channel_id=1, source_target_pairs={{0,4},{1,17},{4,0},{5,21},{8,12},{9,25},{12,8},{13,29},{16,20},{17... | collective-permute-start | bytes 294920 | tf_op jit(solution)/shard_map/ppermute | solution.py:221
  8.8 1.5 %collective-permute-start.4 = (bf16[2,64,384]{2,1,0:T(8,128)(2,1)S(1)}, bf16[2,64,384]{2,1,0:T(8,128)(2,1)S(1)}, u32[]{:S(2)}, u32[]{:S(2)}) collective-permute-start(bf16[2,64,384]{2,1,0:T(8,128)(2,1)S(1)} %collective-permute-done.refs_4_), channel_id=1, source_target_pairs={{0,16},{1,5},{4,20},{5,1},{8,24},{9,13},{12,28},{13,9},{16,0},{17,... | collective-permute-start | bytes 294920 | tf_op jit(solution)/shard_map/ppermute | solution.py:221
  10.3 0.8 %shard_map.67 = (f32[128,128]{1,0:T(8,128)S(1)}, f32[128,128]{1,0:T(8,128)S(1)}) custom-call(bf16[2,128,4096]{2,1,0:T(8,128)(2,1)S(1)} %copy-done, bf16[2,64,2048]{2,1,0:T(8,128)(2,1)S(1)} %bitcast.13, bf16[2,256,2048]{2,1,0:T(8,128)(2,1)S(1)} %copy-done.1, bf16[2,64,2048]{2,1,0:T(8,128)(2,1)S(1)} %bitcast.15, ...), custom_call_target="tpu_custom_call" | custom-call | flops 1 | bytes 1 | tf_op jit(solution)/shard_map/pallas_call | solution.py:31
  11.2 0.5 %collective-permute-start.6 = (bf16[2,8,4096]{2,1,0:T(8,128)(2,1)S(1)}, bf16[2,8,4096]{2,1,0:T(8,128)(2,1)S(1)}, u32[]{:S(2)}, u32[]{:S(2)}) collective-permute-start(bf16[2,8,4096]{2,1,0:T(8,128)(2,1)S(1)} %copy-done.4), channel_id=1, source_target_pairs={{0,4},{4,0},{8,12},{12,8},{1,5},{5,1},{9,13},{13,9},{2,6},{6,2},{1... | collective-permute-start | bytes 393224 | tf_op jit(solution)/shard_map/ppermute | solution.py:208
  12.3 0.2 collective-permute-done.2.refs_5_
  12.5 0.0 collective-permute-done.3.refs_6_
  12.5 0.0 collective-permute-done.1.refs_4_
  12.5 0.4 %shard_map.68 = (f32[128,128]{1,0:T(8,128)S(1)}, bf16[128,128]{1,0:T(8,128)(2,1)S(1)}) custom-call(s32[1]{0:T(128)S(6)} %copy.7.refs_0_, bf16[2,128,4096]{2,1,0:T(8,128)(2,1)S(1)} %copy-done, f32[128,128]{1,0:T(8,128)S(1)} %get-tuple-element.24.refs_2_, f32[128,128]{1,0:T(8,128)S(1)} %get-tuple-element.25.refs_3_, ...), custom_call_target="tpu_custom_call" | custom-call | flops 1 | bytes 1 | tf_op jit(solution)/shard_map/pallas_call | solution.py:31
  12.9 0.5 %collective-permute-done.4.refs_3_ = bf16[2,64,384]{2,1,0:T(8,128)(2,1)S(1)} collective-permute-done((bf16[2,64,384]{2,1,0:T(8,128)(2,1)S(1)}, bf16[2,64,384]{2,1,0:T(8,128)(2,1)S(1)}, u32[]{:S(2)}, u32[]{:S(2)}) %collective-permute-start.4) | collective-permute-done | bytes 98336 | tf_op jit(solution)/shard_map/ppermute | solution.py:221
  13.4 0.4 %shard_map.69 = bf16[16,512]{1,0:T(8,128)(2,1)S(1)} custom-call(bf16[2,128,4096]{2,1,0:T(8,128)(2,1)S(1)} %copy-done, f32[128,128]{1,0:T(8,128)S(1)} %get-tuple-element.27.refs_1_, bf16[128,128]{1,0:T(8,128)(2,1)S(1)} %get-tuple-element.28.refs_2_, bf16[2,64,384]{2,1,0:T(8,128)(2,1)S(1)} %collective-permute-done.4.refs_3_), custom_call_target="tpu_custom_call" | custom-call | flops 1 | bytes 1 | tf_op jit(solution)/shard_map/pallas_call | solution.py:31
  13.8 1.1 %collective-permute-start.5 = (bf16[1,16,512]{2,1,0:T(8,128)(2,1)S(1)}, bf16[1,16,512]{2,1,0:T(8,128)(2,1)S(1)}, u32[]{:S(2)}, u32[]{:S(2)}) collective-permute-start(bf16[1,16,512]{2,1,0:T(8,128)(2,1)S(1)} %bitcast.16), channel_id=1, source_target_pairs={{0,9},{1,8},{4,13},{5,12},{8,1},{9,0},{12,5},{13,4},{2,11},{3,10},... | collective-permute-start | bytes 49160 | tf_op jit(solution)/shard_map/ppermute | solution.py:214
  14.9 3.0 %collective-permute-done.5 = bf16[1,16,512]{2,1,0:T(8,128)(2,1)S(1)} collective-permute-done((bf16[1,16,512]{2,1,0:T(8,128)(2,1)S(1)}, bf16[1,16,512]{2,1,0:T(8,128)(2,1)S(1)}, u32[]{:S(2)}, u32[]{:S(2)}) %collective-permute-start.5) | collective-permute-done | bytes 16416 | tf_op jit(solution)/shard_map/ppermute | solution.py:214
  18.0 0.2 shard_map.70.refs_3_
  18.1 1.3 %collective-permute-start.7 = (bf16[2,16,512]{2,1,0:T(8,128)(2,1)S(1)}, bf16[2,16,512]{2,1,0:T(8,128)(2,1)S(1)}, u32[]{:S(2)}, u32[]{:S(2)}) collective-permute-start(bf16[2,16,512]{2,1,0:T(8,128)(2,1)S(1)} %pad_maximum_fusion.1), channel_id=1, source_target_pairs={{0,3},{1,2},{2,1},{3,0},{4,7},{5,6},{6,5},{7,4},{8,11},{9,10},{10,... | collective-permute-start | bytes 98312 | tf_op jit(solution)/shard_map/ppermute | solution.py:214
  19.4 0.2 shard_map.71.refs_1_
  19.6 0.5 %collective-permute-start.8 = (bf16[128,512]{1,0:T(8,128)(2,1)S(1)}, bf16[128,512]{1,0:T(8,128)(2,1)S(1)}, u32[]{:S(2)}, u32[]{:S(2)}) collective-permute-start(bf16[128,512]{1,0:T(8,128)(2,1)S(1)} %shard_map.71.refs_1_), channel_id=1, source_target_pairs={{0,1},{1,0},{2,3},{3,2},{4,5},{5,4},{6,7},{7,6},{8,9},{9,8},{10,11... | collective-permute-start | bytes 393224 | tf_op jit(solution)/shard_map/ppermute | solution.py:208
  20.1 0.1 collective-permute-start.9
  20.2 1.4 %collective-permute-done.7 = bf16[2,16,512]{2,1,0:T(8,128)(2,1)S(1)} collective-permute-done((bf16[2,16,512]{2,1,0:T(8,128)(2,1)S(1)}, bf16[2,16,512]{2,1,0:T(8,128)(2,1)S(1)}, u32[]{:S(2)}, u32[]{:S(2)}) %collective-permute-start.7) | collective-permute-done | bytes 32800 | tf_op jit(solution)/shard_map/ppermute | solution.py:214
  21.6 0.4 %shard_map.72 = (f32[4,8]{1,0:T(4,128)S(1)}, f32[4,8]{1,0:T(4,128)S(1)}, s32[2,2,8]{2,1,0:T(2,128)S(1)}) custom-call(bf16[4,16,512]{2,1,0:T(8,128)(2,1)S(1)} %pad_maximum_fusion.refs_0_, bf16[128,512]{1,0:T(8,128)(2,1)S(1)} %shard_map.71.refs_1_, bf16[128,512]{1,0:T(8,128)(2,1)S(1)} %collective-permute-done.8.refs_2_, ...), custom_call_target="tpu_custom_call" | custom-call | flops 1 | bytes 1 | tf_op jit(solution)/shard_map/pallas_call | solution.py:31
  22.1 1.2 %collective-permute-start.10 = (f32[4,8]{1,0:T(4,128)S(1)}, f32[4,8]{1,0:T(4,128)S(1)}, u32[]{:S(2)}, u32[]{:S(2)}) collective-permute-start(f32[4,8]{1,0:T(4,128)S(1)} %get-tuple-element.34), channel_id=1, source_target_pairs={{0,5},{1,4},{4,1},{5,0},{8,13},{9,12},{12,9},{13,8},{2,7},{3,6},{6... | collective-permute-start | bytes 392 | tf_op jit(solution)/shard_map/ppermute | solution.py:214
  23.3 1.8 %collective-permute-done.10 = f32[4,8]{1,0:T(4,128)S(1)} collective-permute-done((f32[4,8]{1,0:T(4,128)S(1)}, f32[4,8]{1,0:T(4,128)S(1)}, u32[]{:S(2)}, u32[]{:S(2)}) %collective-permute-start.10) | collective-permute-done | bytes 160 | tf_op jit(solution)/shard_map/ppermute | solution.py:214
  25.2 0.2 collective-permute-start.11
  25.4 1.0 %collective-permute-done.11 = f32[2,2,8]{2,1,0:T(2,128)S(1)} collective-permute-done((f32[2,2,8]{2,1,0:T(2,128)S(1)}, f32[2,2,8]{2,1,0:T(2,128)S(1)}, u32[]{:S(2)}, u32[]{:S(2)}) %collective-permute-start.11) | collective-permute-done | bytes 160 | tf_op jit(solution)/shard_map/ppermute | solution.py:208
  26.4 0.6 %compare_select_fusion = f32[2,2,8]{2,1,0:T(2,128)} fusion(f32[2,2,8]{2,1,0:T(2,128)S(1)} %maximum_add_fusion, s32[2,2,8]{2,1,0:T(2,128)S(1)} %get-tuple-element.32), kind=kLoop, calls=%fused_computation.2 | loop fusion | flops 64 | bytes 384 | tf_op jit(solution)/shard_map/jit(_where)/select_n | solution.py:327
  (18 shorter events, 0.1 us)
Async XLA Ops:
  1.0 3.0 %copy-start.1 = (bf16[2,256,2048]{2,1,0:T(8,128)(2,1)S(1)}, bf16[2,256,2048]{2,1,0:T(8,128)(2,1)}, u32[]{:S(2)}) copy-start(bf16[2,256,2048]{2,1,0:T(8,128)(2,1)} %refs_2_.3) | copy-start | bytes 6291460
  1.0 3.0 %copy-start.3 = (bf16[2,2048,64]{1,2,0:T(8,128)(2,1)S(1)}, bf16[2,2048,64]{1,2,0:T(8,128)(2,1)}, u32[]{:S(2)}) copy-start(bf16[2,2048,64]{1,2,0:T(8,128)(2,1)} %param.9) | copy-start | bytes 1572868
  1.1 5.8 %collective-permute-start = (bf16[2,64,384]{2,1,0:T(8,128)(2,1)S(1)}, bf16[2,64,384]{2,1,0:T(8,128)(2,1)S(1)}, u32[]{:S(2)}, u32[]{:S(2)}) collective-permute-start(bf16[2,64,384]{2,1,0:T(8,128)(2,1)S(1)} %get-tuple-element.20.refs_0_), channel_id=1, source_target_pairs={{0,2},{2,0},{1,3},{3,1},{4,6},{6,4},{5,7},{7,5},{8,10},{10,8},{9,1... | collective-permute-start | bytes 294920 | tf_op jit(solution)/shard_map/ppermute | solution.py:203
  4.1 6.3 %copy-start = (bf16[2,128,4096]{2,1,0:T(8,128)(2,1)S(1)}, bf16[2,128,4096]{2,1,0:T(8,128)(2,1)}, u32[]{:S(2)}) copy-start(bf16[2,128,4096]{2,1,0:T(8,128)(2,1)} %refs_0_.6) | copy-start | bytes 6291460
  4.1 6.3 %copy-start.2 = (bf16[2,2048,64]{1,2,0:T(8,128)(2,1)S(1)}, bf16[2,2048,64]{1,2,0:T(8,128)(2,1)}, u32[]{:S(2)}) copy-start(bf16[2,2048,64]{1,2,0:T(8,128)(2,1)} %param.10) | copy-start | bytes 1572868
  4.6 7.9 %collective-permute-start.3 = (bf16[2,64,640]{2,1,0:T(8,128)(2,1)S(1)}, bf16[2,64,640]{2,1,0:T(8,128)(2,1)S(1)}, u32[]{:S(2)}, u32[]{:S(2)}) collective-permute-start(bf16[2,64,640]{2,1,0:T(8,128)(2,1)S(1)} %shard_map.66), channel_id=1, source_target_pairs={{0,2},{2,0},{1,3},{3,1},{4,6},{6,4},{5,7},{7,5},{8,10},{10,8},{9,1... | collective-permute-start | bytes 491528 | tf_op jit(solution)/shard_map/ppermute | solution.py:203
  6.2 4.9 %copy-start.4 = (bf16[2,8,4096]{2,1,0:T(8,128)(2,1)S(1)}, bf16[2,8,4096]{2,1,0:T(8,128)(2,1)}, u32[]{:S(2)}) copy-start(bf16[2,8,4096]{2,1,0:T(8,128)(2,1)} %refs_0_.7) | copy-start | bytes 393220
  6.2 6.3 %collective-permute-start.2 = (bf16[2,64,384]{2,1,0:T(8,128)(2,1)S(1)}, bf16[2,64,384]{2,1,0:T(8,128)(2,1)S(1)}, u32[]{:S(2)}, u32[]{:S(2)}) collective-permute-start(bf16[2,64,384]{2,1,0:T(8,128)(2,1)S(1)} %get-tuple-element.26), channel_id=1, source_target_pairs={{0,2},{2,0},{1,3},{3,1},{4,6},{6,4},{5,7},{7,5},{8,10},{10,8},{9,1... | collective-permute-start | bytes 294920 | tf_op jit(solution)/shard_map/ppermute | solution.py:203
  6.9 5.7 %collective-permute-start.1 = (bf16[2,64,384]{2,1,0:T(8,128)(2,1)S(1)}, bf16[2,64,384]{2,1,0:T(8,128)(2,1)S(1)}, u32[]{:S(2)}, u32[]{:S(2)}) collective-permute-start(bf16[2,64,384]{2,1,0:T(8,128)(2,1)S(1)} %collective-permute-done.refs_4_), channel_id=1, source_target_pairs={{0,4},{1,17},{4,0},{5,21},{8,12},{9,25},{12,8},{13,29},{16,20},{17... | collective-permute-start | bytes 294920 | tf_op jit(solution)/shard_map/ppermute | solution.py:221
  8.8 4.6 %collective-permute-start.4 = (bf16[2,64,384]{2,1,0:T(8,128)(2,1)S(1)}, bf16[2,64,384]{2,1,0:T(8,128)(2,1)S(1)}, u32[]{:S(2)}, u32[]{:S(2)}) collective-permute-start(bf16[2,64,384]{2,1,0:T(8,128)(2,1)S(1)} %collective-permute-done.refs_4_), channel_id=1, source_target_pairs={{0,16},{1,5},{4,20},{5,1},{8,24},{9,13},{12,28},{13,9},{16,0},{17,... | collective-permute-start | bytes 294920 | tf_op jit(solution)/shard_map/ppermute | solution.py:221
  11.2 6.8 %collective-permute-start.6 = (bf16[2,8,4096]{2,1,0:T(8,128)(2,1)S(1)}, bf16[2,8,4096]{2,1,0:T(8,128)(2,1)S(1)}, u32[]{:S(2)}, u32[]{:S(2)}) collective-permute-start(bf16[2,8,4096]{2,1,0:T(8,128)(2,1)S(1)} %copy-done.4), channel_id=1, source_target_pairs={{0,4},{4,0},{8,12},{12,8},{1,5},{5,1},{9,13},{13,9},{2,6},{6,2},{1... | collective-permute-start | bytes 393224 | tf_op jit(solution)/shard_map/ppermute | solution.py:208
  13.8 4.1 %collective-permute-start.5 = (bf16[1,16,512]{2,1,0:T(8,128)(2,1)S(1)}, bf16[1,16,512]{2,1,0:T(8,128)(2,1)S(1)}, u32[]{:S(2)}, u32[]{:S(2)}) collective-permute-start(bf16[1,16,512]{2,1,0:T(8,128)(2,1)S(1)} %bitcast.16), channel_id=1, source_target_pairs={{0,9},{1,8},{4,13},{5,12},{8,1},{9,0},{12,5},{13,4},{2,11},{3,10},... | collective-permute-start | bytes 49160 | tf_op jit(solution)/shard_map/ppermute | solution.py:214
  18.1 3.5 %collective-permute-start.7 = (bf16[2,16,512]{2,1,0:T(8,128)(2,1)S(1)}, bf16[2,16,512]{2,1,0:T(8,128)(2,1)S(1)}, u32[]{:S(2)}, u32[]{:S(2)}) collective-permute-start(bf16[2,16,512]{2,1,0:T(8,128)(2,1)S(1)} %pad_maximum_fusion.1), channel_id=1, source_target_pairs={{0,3},{1,2},{2,1},{3,0},{4,7},{5,6},{6,5},{7,4},{8,11},{9,10},{10,... | collective-permute-start | bytes 98312 | tf_op jit(solution)/shard_map/ppermute | solution.py:214
  19.6 2.0 %collective-permute-start.8 = (bf16[128,512]{1,0:T(8,128)(2,1)S(1)}, bf16[128,512]{1,0:T(8,128)(2,1)S(1)}, u32[]{:S(2)}, u32[]{:S(2)}) collective-permute-start(bf16[128,512]{1,0:T(8,128)(2,1)S(1)} %shard_map.71.refs_1_), channel_id=1, source_target_pairs={{0,1},{1,0},{2,3},{3,2},{4,5},{5,4},{6,7},{7,6},{8,9},{9,8},{10,11... | collective-permute-start | bytes 393224 | tf_op jit(solution)/shard_map/ppermute | solution.py:208
  20.1 1.6 %collective-permute-start.9 = (bf16[128,512]{1,0:T(8,128)(2,1)S(1)}, bf16[128,512]{1,0:T(8,128)(2,1)S(1)}, u32[]{:S(2)}, u32[]{:S(2)}) collective-permute-start(bf16[128,512]{1,0:T(8,128)(2,1)S(1)} %shard_map.70.refs_3_), channel_id=1, source_target_pairs={{0,1},{1,0},{2,3},{3,2},{4,5},{5,4},{6,7},{7,6},{8,9},{9,8},{10,11... | collective-permute-start | bytes 393224 | tf_op jit(solution)/shard_map/ppermute | solution.py:208
  22.1 3.1 %collective-permute-start.10 = (f32[4,8]{1,0:T(4,128)S(1)}, f32[4,8]{1,0:T(4,128)S(1)}, u32[]{:S(2)}, u32[]{:S(2)}) collective-permute-start(f32[4,8]{1,0:T(4,128)S(1)} %get-tuple-element.34), channel_id=1, source_target_pairs={{0,5},{1,4},{4,1},{5,0},{8,13},{9,12},{12,9},{13,8},{2,7},{3,6},{6... | collective-permute-start | bytes 392 | tf_op jit(solution)/shard_map/ppermute | solution.py:214
  25.2 1.2 %collective-permute-start.11 = (f32[2,2,8]{2,1,0:T(2,128)S(1)}, f32[2,2,8]{2,1,0:T(2,128)S(1)}, u32[]{:S(2)}, u32[]{:S(2)}) collective-permute-start(f32[2,2,8]{2,1,0:T(2,128)S(1)} %pad_maximum_fusion.2), channel_id=1, source_target_pairs={{0,1},{1,0},{2,3},{3,2},{4,5},{5,4},{6,7},{7,6},{8,9},{9,8},{10,11... | collective-permute-start | bytes 392 | tf_op jit(solution)/shard_map/ppermute | solution.py:208

commit v10 on v9

--- a/solution.py
+++ b/solution.py
@@ -91,7 +91,11 @@
     for s, out in enumerate(parcels, 1):
         out[:, :, :size] = tail[...]
         block = project(acts, lax.rem(lax.axis_index("tensor") + s, n), slots, factor)
-        out[:, :, size:] = block.astype(BF16).reshape(layers, width, layers * width)
+        high = block.astype(BF16)
+        low = (block - high.astype(F32)).astype(BF16)
+        lanes = layers * width
+        out[:, :, size : size + lanes] = high.reshape(layers, width, lanes)
+        out[:, :, size + lanes :] = low.reshape(layers, width, lanes)
 
 
 def fold_queries(width, queries, out, rows):
@@ -136,11 +140,13 @@
     for s in range(1, n):
         second, fourth, parcel = (x[s - 1] for x in (seconds, fourths, parcels))
         start = block_of(t, s, n) * depth
-        step, size = second.shape[2], parcel.shape[2] - lanes
+        step, size = second.shape[2], parcel.shape[2] - 2 * lanes
         total = total + product(grads, start + side(1, 1) * step, fourth)
         total = total + product(grads, start + 4 * step, parcel.at[:, :, :size])
         total = total + product(grads, start + swapped(True) * step, second)
-        ins = ins + parcel[:, :, size:].reshape(slots, lanes).astype(F32)
+        high, low = parcel[:, :, size : size + lanes], parcel[:, :, size + lanes :]
+        ins = ins + high.reshape(slots, lanes).astype(F32)
+        ins = ins + low.reshape(slots, lanes).astype(F32)
     total_out[...] = total
     live = lax.broadcasted_iota(jnp.int32, ins.shape, 0) < length[0]
     ins_out[...] = jnp.where(live, ins, 0.0).astype(BF16)
@@ -253,7 +259,7 @@
     factor_in = proj_in.transpose(0, 2, 1)
     parcels = call(
         functools.partial(project_inputs, n),
-        [jax.ShapeDtypeStruct((layers, width, depth - 4 * step + lanes), BF16)] * (n - 1),
+        [jax.ShapeDtypeStruct((layers, width, depth - 4 * step + 2 * lanes), BF16)] * (n - 1),
         acts,
         factor_in,
         tail,
@@ -273,7 +279,6 @@
         *firsts,
     )
     asked, outputs = lax.optimization_barrier((query_grads, outputs))
-    near = flipped(asked, "dp", 1)
     fold = functools.partial(
         call,
         functools.partial(fold_queries, width),
@@ -282,7 +287,7 @@
     )
     own = fold(asked)
     own_other = flipped(own, "query", 1)
-    near = fold(near)
+    near = flipped(own, "dp", 1)
     near_other = flipped(near, "query", 1)
     outputs, inputs = call(
         functools.partial(middle, n, depth),

time: 27.1 us -> 27.1 us (level)
  starting transfers between devices: 13.4 us -> 14.8 us
  waiting for transfers between devices: 8.23 us -> 7.01 us
    ppermute x3, starting transfers between devices: 3.6 us -> 4.82 us  [crossed(): lax.ppermute(x, (axis, 'query'), [(i, i ^ bit * cores + 1) for i in range...]
    ppermute x3, waiting for transfers between devices: 6.3 us -> 5.27 us  [crossed(): lax.ppermute(x, (axis, 'query'), [(i, i ^ bit * cores + 1) for i in range...]
    ppermute x3, waiting for transfers between devices: 0.38 us -> 0.9 us  [shifted(): return lax.ppermute(x, axis, [(i, (i + shift) % n) for i in range(n)])]
    ppermute x2, waiting for transfers between devices: 0.5 us -> 0.01 us  [forwarded(): return lax.ppermute(x, ('parts', 'dp', 'query'), pairs)]
    pallas_call x9 -> x8, Pallas kernels: 3.91 us -> 3.74 us  [call(): pl.pallas_call(body, out_shape=out_shape, in_specs=specs + [ANY] * len(af...]
  transfers between devices with their start and end apart: 12 -> 12, of which waited for: 7 -> 6; matrix products, arithmetic and copies ran while one was open for 0% -> 0% of each run, Pallas kernels for 8% -> 8%
where the time goes in v10:
time: 27.1 us; the launch traced here: 27 us
  starting transfers between devices  14.8 us (55%)
  waiting for transfers between devices  7.01 us (26%)
  Pallas kernels  3.74 us (14%)
  between operations  0.78 us (3%)
  other arithmetic  0.61 us (2%)
    ppermute x3, waiting for transfers between devices, crossed(): lax.ppermute(x, (axis, 'query'), [(i, i ^ bit * cores + 1) for i in range...  5.27 us
    ppermute x3, starting transfers between devices, shifted(): return lax.ppermute(x, axis, [(i, (i + shift) % n) for i in range(n)])  5.09 us
    ppermute x3, starting transfers between devices, crossed(): lax.ppermute(x, (axis, 'query'), [(i, i ^ bit * cores + 1) for i in range...  4.82 us
    pallas_call x8, Pallas kernels, call(): pl.pallas_call(body, out_shape=out_shape, in_specs=specs + [ANY] * len(af...  3.74 us
    ppermute x2, starting transfers between devices, forwarded(): return lax.ppermute(x, ('parts', 'dp', 'query'), pairs)  3.49 us
    ppermute x4, starting transfers between devices, flipped(): return lax.ppermute(x, axis, [(i, i ^ bit) for i in range(n)])  1.42 us
    ppermute x3, waiting for transfers between devices, shifted(): return lax.ppermute(x, axis, [(i, (i + shift) % n) for i in range(n)])  0.9 us
    ppermute x4, waiting for transfers between devices, flipped(): return lax.ppermute(x, axis, [(i, i ^ bit) for i in range(n)])  0.83 us
  transfers between devices with their start and end apart: 12, of which 6 were waited for; matrix products, arithmetic and copies ran while one was open for 0% of the time, Pallas kernels for 8%

profile of v10, /device:TPU:0, one launch (start us, length us, event | category | flops | bytes accessed | tf_op | source)
XLA Modules:
  0.0 27.0 jit_solution(7594237060273429720)
XLA Ops:
  0.0 1.0 %shard_map.64 = (bf16[2,64,384]{2,1,0:T(8,128)(2,1)S(1)}, bf16[2,64,384]{2,1,0:T(8,128)(2,1)S(1)}, bf16[2,64,512]{2,1,0:T(8,128)(2,1)S(1)}) custom-call(bf16[2,64,2048]{2,1,0:T(8,128)(2,1)} %bitcast.12), custom_call_target="tpu_custom_call" | custom-call | flops 1 | bytes 1 | tf_op jit(solution)/shard_map/pallas_call | solution.py:31
  1.0 0.0 copy-start.1
  1.0 0.0 copy-start.3
  1.1 3.0 %collective-permute-start = (bf16[2,64,384]{2,1,0:T(8,128)(2,1)S(1)}, bf16[2,64,384]{2,1,0:T(8,128)(2,1)S(1)}, u32[]{:S(2)}, u32[]{:S(2)}) collective-permute-start(bf16[2,64,384]{2,1,0:T(8,128)(2,1)S(1)} %get-tuple-element.20.refs_0_), channel_id=1, source_target_pairs={{0,2},{2,0},{1,3},{3,1},{4,6},{6,4},{5,7},{7,5},{8,10},{10,8},{9,1... | collective-permute-start | bytes 294920 | tf_op jit(solution)/shard_map/ppermute | solution.py:209
  4.1 0.5 %shard_map.66 = bf16[2,64,768]{2,1,0:T(8,128)(2,1)S(1)} custom-call(bf16[2,256,2048]{2,1,0:T(8,128)(2,1)S(1)} %copy-done.1, bf16[2,64,2048]{2,1,0:T(8,128)(2,1)S(1)} %bitcast.14, bf16[2,64,512]{2,1,0:T(8,128)(2,1)S(1)} %get-tuple-element.21.refs_2_, f32[8,128]{1,0:T(8,128)S(1)} %shard_map.65.refs_3_), custom_call_target="tpu_custom_call" | custom-call | flops 1 | bytes 1 | tf_op jit(solution)/shard_map/pallas_call | solution.py:31
  4.6 1.6 %collective-permute-start.3 = (bf16[2,64,768]{2,1,0:T(8,128)(2,1)S(1)}, bf16[2,64,768]{2,1,0:T(8,128)(2,1)S(1)}, u32[]{:S(2)}, u32[]{:S(2)}) collective-permute-start(bf16[2,64,768]{2,1,0:T(8,128)(2,1)S(1)} %shard_map.66), channel_id=1, source_target_pairs={{0,2},{2,0},{1,3},{3,1},{4,6},{6,4},{5,7},{7,5},{8,10},{10,8},{9,1... | collective-permute-start | bytes 589832 | tf_op jit(solution)/shard_map/ppermute | solution.py:209
  6.2 0.5 %collective-permute-start.2 = (bf16[2,64,384]{2,1,0:T(8,128)(2,1)S(1)}, bf16[2,64,384]{2,1,0:T(8,128)(2,1)S(1)}, u32[]{:S(2)}, u32[]{:S(2)}) collective-permute-start(bf16[2,64,384]{2,1,0:T(8,128)(2,1)S(1)} %get-tuple-element.26), channel_id=1, source_target_pairs={{0,2},{2,0},{1,3},{3,1},{4,6},{6,4},{5,7},{7,5},{8,10},{10,8},{9,1... | collective-permute-start | bytes 294920 | tf_op jit(solution)/shard_map/ppermute | solution.py:209
  6.7 0.2 collective-permute-done.refs_4_
  6.9 1.9 %collective-permute-start.1 = (bf16[2,64,384]{2,1,0:T(8,128)(2,1)S(1)}, bf16[2,64,384]{2,1,0:T(8,128)(2,1)S(1)}, u32[]{:S(2)}, u32[]{:S(2)}) collective-permute-start(bf16[2,64,384]{2,1,0:T(8,128)(2,1)S(1)} %collective-permute-done.refs_4_), channel_id=1, source_target_pairs={{0,4},{1,17},{4,0},{5,21},{8,12},{9,25},{12,8},{13,29},{16,20},{17... | collective-permute-start | bytes 294920 | tf_op jit(solution)/shard_map/ppermute | solution.py:227
  8.8 1.5 %collective-permute-start.4 = (bf16[2,64,384]{2,1,0:T(8,128)(2,1)S(1)}, bf16[2,64,384]{2,1,0:T(8,128)(2,1)S(1)}, u32[]{:S(2)}, u32[]{:S(2)}) collective-permute-start(bf16[2,64,384]{2,1,0:T(8,128)(2,1)S(1)} %collective-permute-done.refs_4_), channel_id=1, source_target_pairs={{0,16},{1,5},{4,20},{5,1},{8,24},{9,13},{12,28},{13,9},{16,0},{17,... | collective-permute-start | bytes 294920 | tf_op jit(solution)/shard_map/ppermute | solution.py:227
  10.3 0.8 %shard_map.67 = (f32[128,128]{1,0:T(8,128)S(1)}, f32[128,128]{1,0:T(8,128)S(1)}) custom-call(bf16[2,128,4096]{2,1,0:T(8,128)(2,1)S(1)} %copy-done, bf16[2,64,2048]{2,1,0:T(8,128)(2,1)S(1)} %bitcast.13, bf16[2,256,2048]{2,1,0:T(8,128)(2,1)S(1)} %copy-done.1, bf16[2,64,2048]{2,1,0:T(8,128)(2,1)S(1)} %bitcast.15, ...), custom_call_target="tpu_custom_call" | custom-call | flops 1 | bytes 1 | tf_op jit(solution)/shard_map/pallas_call | solution.py:31
  11.2 0.2 shard_map.70.refs_1_
  11.4 0.5 %collective-permute-start.6 = (bf16[128,512]{1,0:T(8,128)(2,1)S(1)}, bf16[128,512]{1,0:T(8,128)(2,1)S(1)}, u32[]{:S(2)}, u32[]{:S(2)}) collective-permute-start(bf16[128,512]{1,0:T(8,128)(2,1)S(1)} %shard_map.70.refs_1_), channel_id=1, source_target_pairs={{0,4},{4,0},{8,12},{12,8},{1,5},{5,1},{9,13},{13,9},{2,6},{6,2},{1... | collective-permute-start | bytes 393224 | tf_op jit(solution)/shard_map/ppermute | solution.py:214
  12.5 0.7 %collective-permute-done.2.refs_5_ = bf16[2,64,384]{2,1,0:T(8,128)(2,1)S(1)} collective-permute-done((bf16[2,64,384]{2,1,0:T(8,128)(2,1)S(1)}, bf16[2,64,384]{2,1,0:T(8,128)(2,1)S(1)}, u32[]{:S(2)}, u32[]{:S(2)}) %collective-permute-start.2) | collective-permute-done | bytes 98336 | tf_op jit(solution)/shard_map/ppermute | solution.py:209
  13.2 0.0 collective-permute-done.1.refs_4_
  13.2 0.0 collective-permute-done.3.refs_6_
  13.2 0.4 %shard_map.68 = (f32[128,128]{1,0:T(8,128)S(1)}, bf16[128,128]{1,0:T(8,128)(2,1)S(1)}) custom-call(s32[1]{0:T(128)S(6)} %copy.7.refs_0_, bf16[2,128,4096]{2,1,0:T(8,128)(2,1)S(1)} %copy-done, f32[128,128]{1,0:T(8,128)S(1)} %get-tuple-element.24.refs_2_, f32[128,128]{1,0:T(8,128)S(1)} %get-tuple-element.25.refs_3_, ...), custom_call_target="tpu_custom_call" | custom-call | flops 1 | bytes 1 | tf_op jit(solution)/shard_map/pallas_call | solution.py:31
  13.6 0.4 %shard_map.69 = bf16[16,512]{1,0:T(8,128)(2,1)S(1)} custom-call(bf16[2,128,4096]{2,1,0:T(8,128)(2,1)S(1)} %copy-done, f32[128,128]{1,0:T(8,128)S(1)} %get-tuple-element.27.refs_1_, bf16[128,128]{1,0:T(8,128)(2,1)S(1)} %get-tuple-element.28.refs_2_, bf16[2,64,384]{2,1,0:T(8,128)(2,1)S(1)} %collective-permute-done.4.refs_3_), custom_call_target="tpu_custom_call" | custom-call | flops 1 | bytes 1 | tf_op jit(solution)/shard_map/pallas_call | solution.py:31
  14.0 1.6 %collective-permute-start.5 = (bf16[1,16,512]{2,1,0:T(8,128)(2,1)S(1)}, bf16[1,16,512]{2,1,0:T(8,128)(2,1)S(1)}, u32[]{:S(2)}, u32[]{:S(2)}) collective-permute-start(bf16[1,16,512]{2,1,0:T(8,128)(2,1)S(1)} %bitcast.16), channel_id=1, source_target_pairs={{0,9},{1,8},{4,13},{5,12},{8,1},{9,0},{12,5},{13,4},{2,11},{3,10},... | collective-permute-start | bytes 49160 | tf_op jit(solution)/shard_map/ppermute | solution.py:220
  15.6 2.6 %collective-permute-done.5 = bf16[1,16,512]{2,1,0:T(8,128)(2,1)S(1)} collective-permute-done((bf16[1,16,512]{2,1,0:T(8,128)(2,1)S(1)}, bf16[1,16,512]{2,1,0:T(8,128)(2,1)S(1)}, u32[]{:S(2)}, u32[]{:S(2)}) %collective-permute-start.5) | collective-permute-done | bytes 16416 | tf_op jit(solution)/shard_map/ppermute | solution.py:220
  18.2 0.0 collective-permute-done.6.refs_3_
  18.2 1.6 %collective-permute-start.7 = (bf16[2,16,512]{2,1,0:T(8,128)(2,1)S(1)}, bf16[2,16,512]{2,1,0:T(8,128)(2,1)S(1)}, u32[]{:S(2)}, u32[]{:S(2)}) collective-permute-start(bf16[2,16,512]{2,1,0:T(8,128)(2,1)S(1)} %pad_maximum_fusion.1), channel_id=1, source_target_pairs={{0,3},{1,2},{2,1},{3,0},{4,7},{5,6},{6,5},{7,4},{8,11},{9,10},{10,... | collective-permute-start | bytes 98312 | tf_op jit(solution)/shard_map/ppermute | solution.py:220
  19.8 0.4 %collective-permute-start.8 = (bf16[128,512]{1,0:T(8,128)(2,1)S(1)}, bf16[128,512]{1,0:T(8,128)(2,1)S(1)}, u32[]{:S(2)}, u32[]{:S(2)}) collective-permute-start(bf16[128,512]{1,0:T(8,128)(2,1)S(1)} %shard_map.70.refs_1_), channel_id=1, source_target_pairs={{0,1},{1,0},{2,3},{3,2},{4,5},{5,4},{6,7},{7,6},{8,9},{9,8},{10,11... | collective-permute-start | bytes 393224 | tf_op jit(solution)/shard_map/ppermute | solution.py:214
  20.2 0.1 collective-permute-start.9
  20.3 1.3 %collective-permute-done.7 = bf16[2,16,512]{2,1,0:T(8,128)(2,1)S(1)} collective-permute-done((bf16[2,16,512]{2,1,0:T(8,128)(2,1)S(1)}, bf16[2,16,512]{2,1,0:T(8,128)(2,1)S(1)}, u32[]{:S(2)}, u32[]{:S(2)}) %collective-permute-start.7) | collective-permute-done | bytes 32800 | tf_op jit(solution)/shard_map/ppermute | solution.py:220
  21.6 0.0 collective-permute-done.9.refs_4_
  21.6 0.4 %shard_map.71 = (f32[4,8]{1,0:T(4,128)S(1)}, f32[4,8]{1,0:T(4,128)S(1)}, s32[2,2,8]{2,1,0:T(2,128)S(1)}) custom-call(bf16[4,16,512]{2,1,0:T(8,128)(2,1)S(1)} %pad_maximum_fusion.refs_0_, bf16[128,512]{1,0:T(8,128)(2,1)S(1)} %shard_map.70.refs_1_, bf16[128,512]{1,0:T(8,128)(2,1)S(1)} %collective-permute-done.8.refs_2_, ...), custom_call_target="tpu_custom_call" | custom-call | flops 1 | bytes 1 | tf_op jit(solution)/shard_map/pallas_call | solution.py:31
  22.1 1.7 %collective-permute-start.10 = (f32[4,8]{1,0:T(4,128)S(1)}, f32[4,8]{1,0:T(4,128)S(1)}, u32[]{:S(2)}, u32[]{:S(2)}) collective-permute-start(f32[4,8]{1,0:T(4,128)S(1)} %get-tuple-element.34), channel_id=1, source_target_pairs={{0,5},{1,4},{4,1},{5,0},{8,13},{9,12},{12,9},{13,8},{2,7},{3,6},{6... | collective-permute-start | bytes 392 | tf_op jit(solution)/shard_map/ppermute | solution.py:220
  23.8 1.4 %collective-permute-done.10 = f32[4,8]{1,0:T(4,128)S(1)} collective-permute-done((f32[4,8]{1,0:T(4,128)S(1)}, f32[4,8]{1,0:T(4,128)S(1)}, u32[]{:S(2)}, u32[]{:S(2)}) %collective-permute-start.10) | collective-permute-done | bytes 160 | tf_op jit(solution)/shard_map/ppermute | solution.py:220
  25.2 0.4 %collective-permute-start.11 = (f32[2,2,8]{2,1,0:T(2,128)S(1)}, f32[2,2,8]{2,1,0:T(2,128)S(1)}, u32[]{:S(2)}, u32[]{:S(2)}) collective-permute-start(f32[2,2,8]{2,1,0:T(2,128)S(1)} %pad_maximum_fusion.2), channel_id=1, source_target_pairs={{0,1},{1,0},{2,3},{3,2},{4,5},{5,4},{6,7},{7,6},{8,9},{9,8},{10,11... | collective-permute-start | bytes 392 | tf_op jit(solution)/shard_map/ppermute | solution.py:214
  25.6 0.8 %collective-permute-done.11 = f32[2,2,8]{2,1,0:T(2,128)S(1)} collective-permute-done((f32[2,2,8]{2,1,0:T(2,128)S(1)}, f32[2,2,8]{2,1,0:T(2,128)S(1)}, u32[]{:S(2)}, u32[]{:S(2)}) %collective-permute-start.11) | collective-permute-done | bytes 160 | tf_op jit(solution)/shard_map/ppermute | solution.py:214
  26.4 0.6 %compare_select_fusion = f32[2,2,8]{2,1,0:T(2,128)} fusion(f32[2,2,8]{2,1,0:T(2,128)S(1)} %maximum_add_fusion, s32[2,2,8]{2,1,0:T(2,128)S(1)} %get-tuple-element.32), kind=kLoop, calls=%fused_computation.2 | loop fusion | flops 64 | bytes 384 | tf_op jit(solution)/shard_map/jit(_where)/select_n | solution.py:332
  (17 shorter events, 0.1 us)
Async XLA Ops:
  1.0 3.0 %copy-start.1 = (bf16[2,256,2048]{2,1,0:T(8,128)(2,1)S(1)}, bf16[2,256,2048]{2,1,0:T(8,128)(2,1)}, u32[]{:S(2)}) copy-start(bf16[2,256,2048]{2,1,0:T(8,128)(2,1)} %refs_2_.3) | copy-start | bytes 6291460
  1.0 3.0 %copy-start.3 = (bf16[2,2048,64]{1,2,0:T(8,128)(2,1)S(1)}, bf16[2,2048,64]{1,2,0:T(8,128)(2,1)}, u32[]{:S(2)}) copy-start(bf16[2,2048,64]{1,2,0:T(8,128)(2,1)} %param.9) | copy-start | bytes 1572868
  1.1 5.8 %collective-permute-start = (bf16[2,64,384]{2,1,0:T(8,128)(2,1)S(1)}, bf16[2,64,384]{2,1,0:T(8,128)(2,1)S(1)}, u32[]{:S(2)}, u32[]{:S(2)}) collective-permute-start(bf16[2,64,384]{2,1,0:T(8,128)(2,1)S(1)} %get-tuple-element.20.refs_0_), channel_id=1, source_target_pairs={{0,2},{2,0},{1,3},{3,1},{4,6},{6,4},{5,7},{7,5},{8,10},{10,8},{9,1... | collective-permute-start | bytes 294920 | tf_op jit(solution)/shard_map/ppermute | solution.py:209
  4.1 6.3 %copy-start = (bf16[2,128,4096]{2,1,0:T(8,128)(2,1)S(1)}, bf16[2,128,4096]{2,1,0:T(8,128)(2,1)}, u32[]{:S(2)}) copy-start(bf16[2,128,4096]{2,1,0:T(8,128)(2,1)} %refs_0_.6) | copy-start | bytes 6291460
  4.1 6.3 %copy-start.2 = (bf16[2,2048,64]{1,2,0:T(8,128)(2,1)S(1)}, bf16[2,2048,64]{1,2,0:T(8,128)(2,1)}, u32[]{:S(2)}) copy-start(bf16[2,2048,64]{1,2,0:T(8,128)(2,1)} %param.10) | copy-start | bytes 1572868
  4.6 8.6 %collective-permute-start.3 = (bf16[2,64,768]{2,1,0:T(8,128)(2,1)S(1)}, bf16[2,64,768]{2,1,0:T(8,128)(2,1)S(1)}, u32[]{:S(2)}, u32[]{:S(2)}) collective-permute-start(bf16[2,64,768]{2,1,0:T(8,128)(2,1)S(1)} %shard_map.66), channel_id=1, source_target_pairs={{0,2},{2,0},{1,3},{3,1},{4,6},{6,4},{5,7},{7,5},{8,10},{10,8},{9,1... | collective-permute-start | bytes 589832 | tf_op jit(solution)/shard_map/ppermute | solution.py:209
  6.2 5.0 %copy-start.4 = (bf16[2,8,4096]{2,1,0:T(8,128)(2,1)S(1)}, bf16[2,8,4096]{2,1,0:T(8,128)(2,1)}, u32[]{:S(2)}) copy-start(bf16[2,8,4096]{2,1,0:T(8,128)(2,1)} %refs_0_.7) | copy-start | bytes 393220
  6.2 7.0 %collective-permute-start.2 = (bf16[2,64,384]{2,1,0:T(8,128)(2,1)S(1)}, bf16[2,64,384]{2,1,0:T(8,128)(2,1)S(1)}, u32[]{:S(2)}, u32[]{:S(2)}) collective-permute-start(bf16[2,64,384]{2,1,0:T(8,128)(2,1)S(1)} %get-tuple-element.26), channel_id=1, source_target_pairs={{0,2},{2,0},{1,3},{3,1},{4,6},{6,4},{5,7},{7,5},{8,10},{10,8},{9,1... | collective-permute-start | bytes 294920 | tf_op jit(solution)/shard_map/ppermute | solution.py:209
  6.9 6.4 %collective-permute-start.1 = (bf16[2,64,384]{2,1,0:T(8,128)(2,1)S(1)}, bf16[2,64,384]{2,1,0:T(8,128)(2,1)S(1)}, u32[]{:S(2)}, u32[]{:S(2)}) collective-permute-start(bf16[2,64,384]{2,1,0:T(8,128)(2,1)S(1)} %collective-permute-done.refs_4_), channel_id=1, source_target_pairs={{0,4},{1,17},{4,0},{5,21},{8,12},{9,25},{12,8},{13,29},{16,20},{17... | collective-permute-start | bytes 294920 | tf_op jit(solution)/shard_map/ppermute | solution.py:227
  8.8 4.8 %collective-permute-start.4 = (bf16[2,64,384]{2,1,0:T(8,128)(2,1)S(1)}, bf16[2,64,384]{2,1,0:T(8,128)(2,1)S(1)}, u32[]{:S(2)}, u32[]{:S(2)}) collective-permute-start(bf16[2,64,384]{2,1,0:T(8,128)(2,1)S(1)} %collective-permute-done.refs_4_), channel_id=1, source_target_pairs={{0,16},{1,5},{4,20},{5,1},{8,24},{9,13},{12,28},{13,9},{16,0},{17,... | collective-permute-start | bytes 294920 | tf_op jit(solution)/shard_map/ppermute | solution.py:227
  11.4 6.8 %collective-permute-start.6 = (bf16[128,512]{1,0:T(8,128)(2,1)S(1)}, bf16[128,512]{1,0:T(8,128)(2,1)S(1)}, u32[]{:S(2)}, u32[]{:S(2)}) collective-permute-start(bf16[128,512]{1,0:T(8,128)(2,1)S(1)} %shard_map.70.refs_1_), channel_id=1, source_target_pairs={{0,4},{4,0},{8,12},{12,8},{1,5},{5,1},{9,13},{13,9},{2,6},{6,2},{1... | collective-permute-start | bytes 393224 | tf_op jit(solution)/shard_map/ppermute | solution.py:214
  14.0 4.1 %collective-permute-start.5 = (bf16[1,16,512]{2,1,0:T(8,128)(2,1)S(1)}, bf16[1,16,512]{2,1,0:T(8,128)(2,1)S(1)}, u32[]{:S(2)}, u32[]{:S(2)}) collective-permute-start(bf16[1,16,512]{2,1,0:T(8,128)(2,1)S(1)} %bitcast.16), channel_id=1, source_target_pairs={{0,9},{1,8},{4,13},{5,12},{8,1},{9,0},{12,5},{13,4},{2,11},{3,10},... | collective-permute-start | bytes 49160 | tf_op jit(solution)/shard_map/ppermute | solution.py:220
  18.2 3.4 %collective-permute-start.7 = (bf16[2,16,512]{2,1,0:T(8,128)(2,1)S(1)}, bf16[2,16,512]{2,1,0:T(8,128)(2,1)S(1)}, u32[]{:S(2)}, u32[]{:S(2)}) collective-permute-start(bf16[2,16,512]{2,1,0:T(8,128)(2,1)S(1)} %pad_maximum_fusion.1), channel_id=1, source_target_pairs={{0,3},{1,2},{2,1},{3,0},{4,7},{5,6},{6,5},{7,4},{8,11},{9,10},{10,... | collective-permute-start | bytes 98312 | tf_op jit(solution)/shard_map/ppermute | solution.py:220
  19.8 1.9 %collective-permute-start.8 = (bf16[128,512]{1,0:T(8,128)(2,1)S(1)}, bf16[128,512]{1,0:T(8,128)(2,1)S(1)}, u32[]{:S(2)}, u32[]{:S(2)}) collective-permute-start(bf16[128,512]{1,0:T(8,128)(2,1)S(1)} %shard_map.70.refs_1_), channel_id=1, source_target_pairs={{0,1},{1,0},{2,3},{3,2},{4,5},{5,4},{6,7},{7,6},{8,9},{9,8},{10,11... | collective-permute-start | bytes 393224 | tf_op jit(solution)/shard_map/ppermute | solution.py:214
  20.2 1.5 %collective-permute-start.9 = (bf16[128,512]{1,0:T(8,128)(2,1)S(1)}, bf16[128,512]{1,0:T(8,128)(2,1)S(1)}, u32[]{:S(2)}, u32[]{:S(2)}) collective-permute-start(bf16[128,512]{1,0:T(8,128)(2,1)S(1)} %collective-permute-done.6.refs_3_), channel_id=1, source_target_pairs={{0,1},{1,0},{2,3},{3,2},{4,5},{5,4},{6,7},{7,6},{8,9},{9,8},{10,11... | collective-permute-start | bytes 393224 | tf_op jit(solution)/shard_map/ppermute | solution.py:214
  22.1 3.1 %collective-permute-start.10 = (f32[4,8]{1,0:T(4,128)S(1)}, f32[4,8]{1,0:T(4,128)S(1)}, u32[]{:S(2)}, u32[]{:S(2)}) collective-permute-start(f32[4,8]{1,0:T(4,128)S(1)} %get-tuple-element.34), channel_id=1, source_target_pairs={{0,5},{1,4},{4,1},{5,0},{8,13},{9,12},{12,9},{13,8},{2,7},{3,6},{6... | collective-permute-start | bytes 392 | tf_op jit(solution)/shard_map/ppermute | solution.py:220
  25.2 1.2 %collective-permute-start.11 = (f32[2,2,8]{2,1,0:T(2,128)S(1)}, f32[2,2,8]{2,1,0:T(2,128)S(1)}, u32[]{:S(2)}, u32[]{:S(2)}) collective-permute-start(f32[2,2,8]{2,1,0:T(2,128)S(1)} %pad_maximum_fusion.2), channel_id=1, source_target_pairs={{0,1},{1,0},{2,3},{3,2},{4,5},{5,4},{6,7},{7,6},{8,9},{9,8},{10,11... | collective-permute-start | bytes 392 | tf_op jit(solution)/shard_map/ppermute | solution.py:214

commit v11 on v9

--- a/solution.py
+++ b/solution.py
@@ -273,7 +273,6 @@
         *firsts,
     )
     asked, outputs = lax.optimization_barrier((query_grads, outputs))
-    near = flipped(asked, "dp", 1)
     fold = functools.partial(
         call,
         functools.partial(fold_queries, width),
@@ -282,7 +281,7 @@
     )
     own = fold(asked)
     own_other = flipped(own, "query", 1)
-    near = fold(near)
+    near = flipped(own, "dp", 1)
     near_other = flipped(near, "query", 1)
     outputs, inputs = call(
         functools.partial(middle, n, depth),

time: 27.1 us -> 26.9 us (level)
    ppermute x3, waiting for transfers between devices: 6.3 us -> 6.62 us  [crossed(): lax.ppermute(x, (axis, 'query'), [(i, i ^ bit * cores + 1) for i in range...]
    pallas_call x9 -> x8, Pallas kernels: 3.91 us -> 3.75 us  [call(): pl.pallas_call(body, out_shape=out_shape, in_specs=specs + [ANY] * len(af...]
  transfers between devices with their start and end apart: 12 -> 12, of which waited for: 7 -> 6; matrix products, arithmetic and copies ran while one was open for 0% -> 0% of each run, Pallas kernels for 8% -> 8%
where the time goes in v11:
time: 26.9 us; the launch traced here: 26.8 us
  starting transfers between devices  13.3 us (49%)
  waiting for transfers between devices  8.34 us (31%)
  Pallas kernels  3.75 us (14%)
  between operations  0.78 us (3%)
  other arithmetic  0.61 us (2%)
    ppermute x3, waiting for transfers between devices, crossed(): lax.ppermute(x, (axis, 'query'), [(i, i ^ bit * cores + 1) for i in range...  6.62 us
    ppermute x3, starting transfers between devices, shifted(): return lax.ppermute(x, axis, [(i, (i + shift) % n) for i in range(n)])  5.09 us
    pallas_call x8, Pallas kernels, call(): pl.pallas_call(body, out_shape=out_shape, in_specs=specs + [ANY] * len(af...  3.75 us
    ppermute x3, starting transfers between devices, crossed(): lax.ppermute(x, (axis, 'query'), [(i, i ^ bit * cores + 1) for i in range...  3.53 us
    ppermute x2, starting transfers between devices, forwarded(): return lax.ppermute(x, ('parts', 'dp', 'query'), pairs)  3.49 us
    ppermute x4, starting transfers between devices, flipped(): return lax.ppermute(x, axis, [(i, i ^ bit) for i in range(n)])  1.19 us
    ppermute x4, waiting for transfers between devices, flipped(): return lax.ppermute(x, axis, [(i, i ^ bit) for i in range(n)])  1.05 us
    select_n x1, other arithmetic, local(): kept = jnp.where(odd_place == 0, kept, kept[::-1]).reshape(2, -1, n, nq)  0.58 us
  transfers between devices with their start and end apart: 12, of which 6 were waited for; matrix products, arithmetic and copies ran while one was open for 0% of the time, Pallas kernels for 8%

profile of v11, /device:TPU:0, one launch (start us, length us, event | category | flops | bytes accessed | tf_op | source)
XLA Modules:
  0.0 26.8 jit_solution(6026999584063116580)
XLA Ops:
  0.0 1.0 %shard_map.64 = (bf16[2,64,384]{2,1,0:T(8,128)(2,1)S(1)}, bf16[2,64,384]{2,1,0:T(8,128)(2,1)S(1)}, bf16[2,64,512]{2,1,0:T(8,128)(2,1)S(1)}) custom-call(bf16[2,64,2048]{2,1,0:T(8,128)(2,1)} %bitcast.12), custom_call_target="tpu_custom_call" | custom-call | flops 1 | bytes 1 | tf_op jit(solution)/shard_map/pallas_call | solution.py:31
  1.0 0.0 copy-start.1
  1.0 0.0 copy-start.3
  1.1 3.0 %collective-permute-start = (bf16[2,64,384]{2,1,0:T(8,128)(2,1)S(1)}, bf16[2,64,384]{2,1,0:T(8,128)(2,1)S(1)}, u32[]{:S(2)}, u32[]{:S(2)}) collective-permute-start(bf16[2,64,384]{2,1,0:T(8,128)(2,1)S(1)} %get-tuple-element.20.refs_0_), channel_id=1, source_target_pairs={{0,2},{2,0},{1,3},{3,1},{4,6},{6,4},{5,7},{7,5},{8,10},{10,8},{9,1... | collective-permute-start | bytes 294920 | tf_op jit(solution)/shard_map/ppermute | solution.py:203
  4.1 0.5 %shard_map.66 = bf16[2,64,640]{2,1,0:T(8,128)(2,1)S(1)} custom-call(bf16[2,256,2048]{2,1,0:T(8,128)(2,1)S(1)} %copy-done.1, bf16[2,64,2048]{2,1,0:T(8,128)(2,1)S(1)} %bitcast.14, bf16[2,64,512]{2,1,0:T(8,128)(2,1)S(1)} %get-tuple-element.21.refs_2_, f32[8,128]{1,0:T(8,128)S(1)} %shard_map.65.refs_3_), custom_call_target="tpu_custom_call" | custom-call | flops 1 | bytes 1 | tf_op jit(solution)/shard_map/pallas_call | solution.py:31
  4.6 1.6 %collective-permute-start.3 = (bf16[2,64,640]{2,1,0:T(8,128)(2,1)S(1)}, bf16[2,64,640]{2,1,0:T(8,128)(2,1)S(1)}, u32[]{:S(2)}, u32[]{:S(2)}) collective-permute-start(bf16[2,64,640]{2,1,0:T(8,128)(2,1)S(1)} %shard_map.66), channel_id=1, source_target_pairs={{0,2},{2,0},{1,3},{3,1},{4,6},{6,4},{5,7},{7,5},{8,10},{10,8},{9,1... | collective-permute-start | bytes 491528 | tf_op jit(solution)/shard_map/ppermute | solution.py:203
  6.2 0.5 %collective-permute-start.2 = (bf16[2,64,384]{2,1,0:T(8,128)(2,1)S(1)}, bf16[2,64,384]{2,1,0:T(8,128)(2,1)S(1)}, u32[]{:S(2)}, u32[]{:S(2)}) collective-permute-start(bf16[2,64,384]{2,1,0:T(8,128)(2,1)S(1)} %get-tuple-element.26), channel_id=1, source_target_pairs={{0,2},{2,0},{1,3},{3,1},{4,6},{6,4},{5,7},{7,5},{8,10},{10,8},{9,1... | collective-permute-start | bytes 294920 | tf_op jit(solution)/shard_map/ppermute | solution.py:203
  6.7 0.2 collective-permute-done.refs_4_
  6.9 2.0 %collective-permute-start.1 = (bf16[2,64,384]{2,1,0:T(8,128)(2,1)S(1)}, bf16[2,64,384]{2,1,0:T(8,128)(2,1)S(1)}, u32[]{:S(2)}, u32[]{:S(2)}) collective-permute-start(bf16[2,64,384]{2,1,0:T(8,128)(2,1)S(1)} %collective-permute-done.refs_4_), channel_id=1, source_target_pairs={{0,4},{1,17},{4,0},{5,21},{8,12},{9,25},{12,8},{13,29},{16,20},{17... | collective-permute-start | bytes 294920 | tf_op jit(solution)/shard_map/ppermute | solution.py:221
  8.8 1.5 %collective-permute-start.4 = (bf16[2,64,384]{2,1,0:T(8,128)(2,1)S(1)}, bf16[2,64,384]{2,1,0:T(8,128)(2,1)S(1)}, u32[]{:S(2)}, u32[]{:S(2)}) collective-permute-start(bf16[2,64,384]{2,1,0:T(8,128)(2,1)S(1)} %collective-permute-done.refs_4_), channel_id=1, source_target_pairs={{0,16},{1,5},{4,20},{5,1},{8,24},{9,13},{12,28},{13,9},{16,0},{17,... | collective-permute-start | bytes 294920 | tf_op jit(solution)/shard_map/ppermute | solution.py:221
  10.3 0.8 %shard_map.67 = (f32[128,128]{1,0:T(8,128)S(1)}, f32[128,128]{1,0:T(8,128)S(1)}) custom-call(bf16[2,128,4096]{2,1,0:T(8,128)(2,1)S(1)} %copy-done, bf16[2,64,2048]{2,1,0:T(8,128)(2,1)S(1)} %bitcast.13, bf16[2,256,2048]{2,1,0:T(8,128)(2,1)S(1)} %copy-done.1, bf16[2,64,2048]{2,1,0:T(8,128)(2,1)S(1)} %bitcast.15, ...), custom_call_target="tpu_custom_call" | custom-call | flops 1 | bytes 1 | tf_op jit(solution)/shard_map/pallas_call | solution.py:31
  11.2 0.2 shard_map.70.refs_1_
  11.4 0.5 %collective-permute-start.6 = (bf16[128,512]{1,0:T(8,128)(2,1)S(1)}, bf16[128,512]{1,0:T(8,128)(2,1)S(1)}, u32[]{:S(2)}, u32[]{:S(2)}) collective-permute-start(bf16[128,512]{1,0:T(8,128)(2,1)S(1)} %shard_map.70.refs_1_), channel_id=1, source_target_pairs={{0,4},{4,0},{8,12},{12,8},{1,5},{5,1},{9,13},{13,9},{2,6},{6,2},{1... | collective-permute-start | bytes 393224 | tf_op jit(solution)/shard_map/ppermute | solution.py:208
  12.5 0.0 collective-permute-done.2.refs_5_
  12.5 0.0 collective-permute-done.1.refs_4_
  12.5 0.4 %shard_map.68 = (f32[128,128]{1,0:T(8,128)S(1)}, bf16[128,128]{1,0:T(8,128)(2,1)S(1)}) custom-call(s32[1]{0:T(128)S(6)} %copy.7.refs_0_, bf16[2,128,4096]{2,1,0:T(8,128)(2,1)S(1)} %copy-done, f32[128,128]{1,0:T(8,128)S(1)} %get-tuple-element.24.refs_2_, f32[128,128]{1,0:T(8,128)S(1)} %get-tuple-element.25.refs_3_, ...), custom_call_target="tpu_custom_call" | custom-call | flops 1 | bytes 1 | tf_op jit(solution)/shard_map/pallas_call | solution.py:31
  12.9 0.5 %collective-permute-done.4.refs_3_ = bf16[2,64,384]{2,1,0:T(8,128)(2,1)S(1)} collective-permute-done((bf16[2,64,384]{2,1,0:T(8,128)(2,1)S(1)}, bf16[2,64,384]{2,1,0:T(8,128)(2,1)S(1)}, u32[]{:S(2)}, u32[]{:S(2)}) %collective-permute-start.4) | collective-permute-done | bytes 98336 | tf_op jit(solution)/shard_map/ppermute | solution.py:221
  13.4 0.4 %shard_map.69 = bf16[16,512]{1,0:T(8,128)(2,1)S(1)} custom-call(bf16[2,128,4096]{2,1,0:T(8,128)(2,1)S(1)} %copy-done, f32[128,128]{1,0:T(8,128)S(1)} %get-tuple-element.27.refs_1_, bf16[128,128]{1,0:T(8,128)(2,1)S(1)} %get-tuple-element.28.refs_2_, bf16[2,64,384]{2,1,0:T(8,128)(2,1)S(1)} %collective-permute-done.4.refs_3_), custom_call_target="tpu_custom_call" | custom-call | flops 1 | bytes 1 | tf_op jit(solution)/shard_map/pallas_call | solution.py:31
  13.8 1.1 %collective-permute-start.5 = (bf16[1,16,512]{2,1,0:T(8,128)(2,1)S(1)}, bf16[1,16,512]{2,1,0:T(8,128)(2,1)S(1)}, u32[]{:S(2)}, u32[]{:S(2)}) collective-permute-start(bf16[1,16,512]{2,1,0:T(8,128)(2,1)S(1)} %bitcast.16), channel_id=1, source_target_pairs={{0,9},{1,8},{4,13},{5,12},{8,1},{9,0},{12,5},{13,4},{2,11},{3,10},... | collective-permute-start | bytes 49160 | tf_op jit(solution)/shard_map/ppermute | solution.py:214
  14.9 3.0 %collective-permute-done.5 = bf16[1,16,512]{2,1,0:T(8,128)(2,1)S(1)} collective-permute-done((bf16[1,16,512]{2,1,0:T(8,128)(2,1)S(1)}, bf16[1,16,512]{2,1,0:T(8,128)(2,1)S(1)}, u32[]{:S(2)}, u32[]{:S(2)}) %collective-permute-start.5) | collective-permute-done | bytes 16416 | tf_op jit(solution)/shard_map/ppermute | solution.py:214
  18.0 0.0 collective-permute-done.6.refs_3_
  18.0 1.3 %collective-permute-start.7 = (bf16[2,16,512]{2,1,0:T(8,128)(2,1)S(1)}, bf16[2,16,512]{2,1,0:T(8,128)(2,1)S(1)}, u32[]{:S(2)}, u32[]{:S(2)}) collective-permute-start(bf16[2,16,512]{2,1,0:T(8,128)(2,1)S(1)} %pad_maximum_fusion.1), channel_id=1, source_target_pairs={{0,3},{1,2},{2,1},{3,0},{4,7},{5,6},{6,5},{7,4},{8,11},{9,10},{10,... | collective-permute-start | bytes 98312 | tf_op jit(solution)/shard_map/ppermute | solution.py:214
  19.2 0.4 %collective-permute-start.8 = (bf16[128,512]{1,0:T(8,128)(2,1)S(1)}, bf16[128,512]{1,0:T(8,128)(2,1)S(1)}, u32[]{:S(2)}, u32[]{:S(2)}) collective-permute-start(bf16[128,512]{1,0:T(8,128)(2,1)S(1)} %shard_map.70.refs_1_), channel_id=1, source_target_pairs={{0,1},{1,0},{2,3},{3,2},{4,5},{5,4},{6,7},{7,6},{8,9},{9,8},{10,11... | collective-permute-start | bytes 393224 | tf_op jit(solution)/shard_map/ppermute | solution.py:208
  19.6 0.1 collective-permute-start.9
  19.8 1.7 %collective-permute-done.7 = bf16[2,16,512]{2,1,0:T(8,128)(2,1)S(1)} collective-permute-done((bf16[2,16,512]{2,1,0:T(8,128)(2,1)S(1)}, bf16[2,16,512]{2,1,0:T(8,128)(2,1)S(1)}, u32[]{:S(2)}, u32[]{:S(2)}) %collective-permute-start.7) | collective-permute-done | bytes 32800 | tf_op jit(solution)/shard_map/ppermute | solution.py:214
  21.4 0.0 collective-permute-done.9.refs_4_
  21.5 0.4 %shard_map.71 = (f32[4,8]{1,0:T(4,128)S(1)}, f32[4,8]{1,0:T(4,128)S(1)}, s32[2,2,8]{2,1,0:T(2,128)S(1)}) custom-call(bf16[4,16,512]{2,1,0:T(8,128)(2,1)S(1)} %pad_maximum_fusion.refs_0_, bf16[128,512]{1,0:T(8,128)(2,1)S(1)} %shard_map.70.refs_1_, bf16[128,512]{1,0:T(8,128)(2,1)S(1)} %collective-permute-done.8.refs_2_, ...), custom_call_target="tpu_custom_call" | custom-call | flops 1 | bytes 1 | tf_op jit(solution)/shard_map/pallas_call | solution.py:31
  21.9 1.2 %collective-permute-start.10 = (f32[4,8]{1,0:T(4,128)S(1)}, f32[4,8]{1,0:T(4,128)S(1)}, u32[]{:S(2)}, u32[]{:S(2)}) collective-permute-start(f32[4,8]{1,0:T(4,128)S(1)} %get-tuple-element.34), channel_id=1, source_target_pairs={{0,5},{1,4},{4,1},{5,0},{8,13},{9,12},{12,9},{13,8},{2,7},{3,6},{6... | collective-permute-start | bytes 392 | tf_op jit(solution)/shard_map/ppermute | solution.py:214
  23.1 1.9 %collective-permute-done.10 = f32[4,8]{1,0:T(4,128)S(1)} collective-permute-done((f32[4,8]{1,0:T(4,128)S(1)}, f32[4,8]{1,0:T(4,128)S(1)}, u32[]{:S(2)}, u32[]{:S(2)}) %collective-permute-start.10) | collective-permute-done | bytes 160 | tf_op jit(solution)/shard_map/ppermute | solution.py:214
  25.0 0.2 collective-permute-start.11
  25.2 1.0 %collective-permute-done.11 = f32[2,2,8]{2,1,0:T(2,128)S(1)} collective-permute-done((f32[2,2,8]{2,1,0:T(2,128)S(1)}, f32[2,2,8]{2,1,0:T(2,128)S(1)}, u32[]{:S(2)}, u32[]{:S(2)}) %collective-permute-start.11) | collective-permute-done | bytes 160 | tf_op jit(solution)/shard_map/ppermute | solution.py:208
  26.2 0.6 %compare_select_fusion = f32[2,2,8]{2,1,0:T(2,128)} fusion(f32[2,2,8]{2,1,0:T(2,128)S(1)} %maximum_add_fusion, s32[2,2,8]{2,1,0:T(2,128)S(1)} %get-tuple-element.32), kind=kLoop, calls=%fused_computation.2 | loop fusion | flops 64 | bytes 384 | tf_op jit(solution)/shard_map/jit(_where)/select_n | solution.py:326
  (17 shorter events, 0.1 us)
Async XLA Ops:
  1.0 3.0 %copy-start.1 = (bf16[2,256,2048]{2,1,0:T(8,128)(2,1)S(1)}, bf16[2,256,2048]{2,1,0:T(8,128)(2,1)}, u32[]{:S(2)}) copy-start(bf16[2,256,2048]{2,1,0:T(8,128)(2,1)} %refs_2_.3) | copy-start | bytes 6291460
  1.0 3.0 %copy-start.3 = (bf16[2,2048,64]{1,2,0:T(8,128)(2,1)S(1)}, bf16[2,2048,64]{1,2,0:T(8,128)(2,1)}, u32[]{:S(2)}) copy-start(bf16[2,2048,64]{1,2,0:T(8,128)(2,1)} %param.9) | copy-start | bytes 1572868
  1.1 5.8 %collective-permute-start = (bf16[2,64,384]{2,1,0:T(8,128)(2,1)S(1)}, bf16[2,64,384]{2,1,0:T(8,128)(2,1)S(1)}, u32[]{:S(2)}, u32[]{:S(2)}) collective-permute-start(bf16[2,64,384]{2,1,0:T(8,128)(2,1)S(1)} %get-tuple-element.20.refs_0_), channel_id=1, source_target_pairs={{0,2},{2,0},{1,3},{3,1},{4,6},{6,4},{5,7},{7,5},{8,10},{10,8},{9,1... | collective-permute-start | bytes 294920 | tf_op jit(solution)/shard_map/ppermute | solution.py:203
  4.1 6.3 %copy-start = (bf16[2,128,4096]{2,1,0:T(8,128)(2,1)S(1)}, bf16[2,128,4096]{2,1,0:T(8,128)(2,1)}, u32[]{:S(2)}) copy-start(bf16[2,128,4096]{2,1,0:T(8,128)(2,1)} %refs_0_.6) | copy-start | bytes 6291460
  4.1 6.3 %copy-start.2 = (bf16[2,2048,64]{1,2,0:T(8,128)(2,1)S(1)}, bf16[2,2048,64]{1,2,0:T(8,128)(2,1)}, u32[]{:S(2)}) copy-start(bf16[2,2048,64]{1,2,0:T(8,128)(2,1)} %param.10) | copy-start | bytes 1572868
  4.6 7.9 %collective-permute-start.3 = (bf16[2,64,640]{2,1,0:T(8,128)(2,1)S(1)}, bf16[2,64,640]{2,1,0:T(8,128)(2,1)S(1)}, u32[]{:S(2)}, u32[]{:S(2)}) collective-permute-start(bf16[2,64,640]{2,1,0:T(8,128)(2,1)S(1)} %shard_map.66), channel_id=1, source_target_pairs={{0,2},{2,0},{1,3},{3,1},{4,6},{6,4},{5,7},{7,5},{8,10},{10,8},{9,1... | collective-permute-start | bytes 491528 | tf_op jit(solution)/shard_map/ppermute | solution.py:203
  6.2 5.0 %copy-start.4 = (bf16[2,8,4096]{2,1,0:T(8,128)(2,1)S(1)}, bf16[2,8,4096]{2,1,0:T(8,128)(2,1)}, u32[]{:S(2)}) copy-start(bf16[2,8,4096]{2,1,0:T(8,128)(2,1)} %refs_0_.7) | copy-start | bytes 393220
  6.2 6.3 %collective-permute-start.2 = (bf16[2,64,384]{2,1,0:T(8,128)(2,1)S(1)}, bf16[2,64,384]{2,1,0:T(8,128)(2,1)S(1)}, u32[]{:S(2)}, u32[]{:S(2)}) collective-permute-start(bf16[2,64,384]{2,1,0:T(8,128)(2,1)S(1)} %get-tuple-element.26), channel_id=1, source_target_pairs={{0,2},{2,0},{1,3},{3,1},{4,6},{6,4},{5,7},{7,5},{8,10},{10,8},{9,1... | collective-permute-start | bytes 294920 | tf_op jit(solution)/shard_map/ppermute | solution.py:203
  6.9 5.7 %collective-permute-start.1 = (bf16[2,64,384]{2,1,0:T(8,128)(2,1)S(1)}, bf16[2,64,384]{2,1,0:T(8,128)(2,1)S(1)}, u32[]{:S(2)}, u32[]{:S(2)}) collective-permute-start(bf16[2,64,384]{2,1,0:T(8,128)(2,1)S(1)} %collective-permute-done.refs_4_), channel_id=1, source_target_pairs={{0,4},{1,17},{4,0},{5,21},{8,12},{9,25},{12,8},{13,29},{16,20},{17... | collective-permute-start | bytes 294920 | tf_op jit(solution)/shard_map/ppermute | solution.py:221
  8.8 4.6 %collective-permute-start.4 = (bf16[2,64,384]{2,1,0:T(8,128)(2,1)S(1)}, bf16[2,64,384]{2,1,0:T(8,128)(2,1)S(1)}, u32[]{:S(2)}, u32[]{:S(2)}) collective-permute-start(bf16[2,64,384]{2,1,0:T(8,128)(2,1)S(1)} %collective-permute-done.refs_4_), channel_id=1, source_target_pairs={{0,16},{1,5},{4,20},{5,1},{8,24},{9,13},{12,28},{13,9},{16,0},{17,... | collective-permute-start | bytes 294920 | tf_op jit(solution)/shard_map/ppermute | solution.py:221
  11.4 6.6 %collective-permute-start.6 = (bf16[128,512]{1,0:T(8,128)(2,1)S(1)}, bf16[128,512]{1,0:T(8,128)(2,1)S(1)}, u32[]{:S(2)}, u32[]{:S(2)}) collective-permute-start(bf16[128,512]{1,0:T(8,128)(2,1)S(1)} %shard_map.70.refs_1_), channel_id=1, source_target_pairs={{0,4},{4,0},{8,12},{12,8},{1,5},{5,1},{9,13},{13,9},{2,6},{6,2},{1... | collective-permute-start | bytes 393224 | tf_op jit(solution)/shard_map/ppermute | solution.py:208
  13.8 4.1 %collective-permute-start.5 = (bf16[1,16,512]{2,1,0:T(8,128)(2,1)S(1)}, bf16[1,16,512]{2,1,0:T(8,128)(2,1)S(1)}, u32[]{:S(2)}, u32[]{:S(2)}) collective-permute-start(bf16[1,16,512]{2,1,0:T(8,128)(2,1)S(1)} %bitcast.16), channel_id=1, source_target_pairs={{0,9},{1,8},{4,13},{5,12},{8,1},{9,0},{12,5},{13,4},{2,11},{3,10},... | collective-permute-start | bytes 49160 | tf_op jit(solution)/shard_map/ppermute | solution.py:214
  18.0 3.5 %collective-permute-start.7 = (bf16[2,16,512]{2,1,0:T(8,128)(2,1)S(1)}, bf16[2,16,512]{2,1,0:T(8,128)(2,1)S(1)}, u32[]{:S(2)}, u32[]{:S(2)}) collective-permute-start(bf16[2,16,512]{2,1,0:T(8,128)(2,1)S(1)} %pad_maximum_fusion.1), channel_id=1, source_target_pairs={{0,3},{1,2},{2,1},{3,0},{4,7},{5,6},{6,5},{7,4},{8,11},{9,10},{10,... | collective-permute-start | bytes 98312 | tf_op jit(solution)/shard_map/ppermute | solution.py:214
  19.2 2.2 %collective-permute-start.8 = (bf16[128,512]{1,0:T(8,128)(2,1)S(1)}, bf16[128,512]{1,0:T(8,128)(2,1)S(1)}, u32[]{:S(2)}, u32[]{:S(2)}) collective-permute-start(bf16[128,512]{1,0:T(8,128)(2,1)S(1)} %shard_map.70.refs_1_), channel_id=1, source_target_pairs={{0,1},{1,0},{2,3},{3,2},{4,5},{5,4},{6,7},{7,6},{8,9},{9,8},{10,11... | collective-permute-start | bytes 393224 | tf_op jit(solution)/shard_map/ppermute | solution.py:208
  19.6 1.8 %collective-permute-start.9 = (bf16[128,512]{1,0:T(8,128)(2,1)S(1)}, bf16[128,512]{1,0:T(8,128)(2,1)S(1)}, u32[]{:S(2)}, u32[]{:S(2)}) collective-permute-start(bf16[128,512]{1,0:T(8,128)(2,1)S(1)} %collective-permute-done.6.refs_3_), channel_id=1, source_target_pairs={{0,1},{1,0},{2,3},{3,2},{4,5},{5,4},{6,7},{7,6},{8,9},{9,8},{10,11... | collective-permute-start | bytes 393224 | tf_op jit(solution)/shard_map/ppermute | solution.py:208
  21.9 3.1 %collective-permute-start.10 = (f32[4,8]{1,0:T(4,128)S(1)}, f32[4,8]{1,0:T(4,128)S(1)}, u32[]{:S(2)}, u32[]{:S(2)}) collective-permute-start(f32[4,8]{1,0:T(4,128)S(1)} %get-tuple-element.34), channel_id=1, source_target_pairs={{0,5},{1,4},{4,1},{5,0},{8,13},{9,12},{12,9},{13,8},{2,7},{3,6},{6... | collective-permute-start | bytes 392 | tf_op jit(solution)/shard_map/ppermute | solution.py:214
  25.0 1.2 %collective-permute-start.11 = (f32[2,2,8]{2,1,0:T(2,128)S(1)}, f32[2,2,8]{2,1,0:T(2,128)S(1)}, u32[]{:S(2)}, u32[]{:S(2)}) collective-permute-start(f32[2,2,8]{2,1,0:T(2,128)S(1)} %pad_maximum_fusion.2), channel_id=1, source_target_pairs={{0,1},{1,0},{2,3},{3,2},{4,5},{5,4},{6,7},{7,6},{8,9},{9,8},{10,11... | collective-permute-start | bytes 392 | tf_op jit(solution)/shard_map/ppermute | solution.py:208

commit v12 on v11

--- a/solution.py
+++ b/solution.py
@@ -13,7 +13,7 @@
 SMEM = pl.BlockSpec(memory_space=pltpu.SMEM)
 ANY = pl.BlockSpec(memory_space=pl.ANY)
 NT = (((1,), (1,)), ((), ()))
-TN = (((0,), (0,)), ((), ()))
+NN = (((1,), (0,)), ((), ()))
 FOLD = 16
 EARLY = 1
 
@@ -104,7 +104,7 @@
             rows[g, pl.ds(r, nq, stride=FOLD), :] = jnp.concatenate(
                 [w[:, start : start + width] for w in wide], axis=1
             )
-        out[:, g * lanes : (g + 1) * lanes] = rows[g].astype(BF16)
+        out[g * lanes : (g + 1) * lanes, :] = rows[g].T.astype(BF16)
 
 
 def product(grads, start, factor):
@@ -115,7 +115,7 @@
 
 
 def early(n, grads, factor, acts, factor_in, *rest):
-    pieces, out, inputs = rest[:-2], rest[-2], rest[-1]
+    pieces, out, inputs, turned = rest[:-3], *rest[-3:]
     depth = factor.shape[2]
     t = lax.axis_index("tensor")
     total = product(grads, t * depth, factor)
@@ -124,6 +124,12 @@
         total = total + product(grads, start, piece)
     out[...] = total
     inputs[...] = project(acts, t, inputs.shape[0], factor_in)
+    step = turned.shape[2]
+    for s in range(1, n):
+        start = block_of(t, s, n) * depth + swapped(False) * step
+        columns = pl.ds(pl.multiple_of(start, 128), step)
+        for l in range(grads.shape[0]):
+            turned[s - 1, l] = grads[l, :, columns].T
 
 
 def middle(n, depth, length, grads, outputs, inputs, *rest):
@@ -141,20 +147,20 @@
         total = total + product(grads, start + 4 * step, parcel.at[:, :, :size])
         total = total + product(grads, start + swapped(True) * step, second)
         ins = ins + parcel[:, :, size:].reshape(slots, lanes).astype(F32)
-    total_out[...] = total
+    total_out[...] = total.T
     live = lax.broadcasted_iota(jnp.int32, ins.shape, 0) < length[0]
-    ins_out[...] = jnp.where(live, ins, 0.0).astype(BF16)
-
-
-def example_gradient(n, depth, grads, outputs, inputs, *rest):
+    ins_out[...] = jnp.where(live, ins, 0.0).T.astype(BF16)
+
+
+def example_gradient(n, turned, outputs, inputs, *rest):
     thirds, out = rest[:-1], rest[-1]
-    t = lax.axis_index("tensor")
+    layers = turned.shape[1]
     total = outputs[...]
-    for s, third in enumerate(thirds, 1):
-        start = block_of(t, s, n) * depth + swapped(False) * third.shape[2]
-        total = total + product(grads, start, third)
-    both = dot(inputs[...], total.astype(BF16), TN)
-    layers = grads.shape[0]
+    for s, third in enumerate(thirds):
+        total = total + jnp.concatenate(
+            [dot(third[l], turned[s, l], NN) for l in range(layers)], axis=0
+        )
+    both = dot(inputs[...], total.astype(BF16), NT)
     width = both.shape[1] // layers
     lane = lax.broadcasted_iota(jnp.int32, (width, both.shape[1]), 1)
     grad = both[:width]
@@ -173,7 +179,7 @@
     products = []
     for asked, chosen in ((own, even), (own_other, odd), (near, even), (near_other, odd)):
         lhs = jnp.concatenate([grads[s] for s in chosen], axis=0)
-        products.append(dot(lhs, asked[...], NT))
+        products.append(dot(lhs, asked[...], NN))
     products = jnp.concatenate(products, axis=0)
     row = lax.broadcasted_iota(jnp.int32, products.shape, 0)
     column = lax.broadcasted_iota(jnp.int32, products.shape, 1)
@@ -263,9 +269,12 @@
     parcels = [shifted(parcel, "tensor", s) for s, parcel in enumerate(parcels, 1)]
     seconds = [forwarded(first, True) for first in firsts]
     thirds = [forwarded(first, False) for first in firsts]
-    outputs, mine = call(
+    outputs, mine, turned = call(
         functools.partial(early, n),
-        (jax.ShapeDtypeStruct((slots, lanes), F32),) * 2,
+        (
+            *[jax.ShapeDtypeStruct((slots, lanes), F32)] * 2,
+            jax.ShapeDtypeStruct((n - 1, layers, step, slots), BF16),
+        ),
         out_grads,
         factor,
         acts,
@@ -276,7 +285,7 @@
     fold = functools.partial(
         call,
         functools.partial(fold_queries, width),
-        jax.ShapeDtypeStruct((nq * FOLD, width // FOLD * lanes), BF16),
+        jax.ShapeDtypeStruct((width // FOLD * lanes, nq * FOLD), BF16),
         scratch=[pltpu.VMEM((width // FOLD, nq * FOLD, lanes), F32)],
     )
     own = fold(asked)
@@ -286,8 +295,8 @@
     outputs, inputs = call(
         functools.partial(middle, n, depth),
         (
-            jax.ShapeDtypeStruct((slots, lanes), F32),
-            jax.ShapeDtypeStruct((slots, lanes), BF16),
+            jax.ShapeDtypeStruct((lanes, slots), F32),
+            jax.ShapeDtypeStruct((lanes, slots), BF16),
         ),
         lengths,
         out_grads,
@@ -298,9 +307,9 @@
         *[in_vmem(x) for x in parcels],
     )
     grad = call(
-        functools.partial(example_gradient, n, depth),
+        functools.partial(example_gradient, n),
         jax.ShapeDtypeStruct((FOLD, width // FOLD * lanes), BF16),
-        out_grads,
+        turned,
         outputs,
         inputs,
         *[in_vmem(x) for x in thirds],

time: 26.9 us -> 26.8 us (level)
  waiting for transfers between devices: 8.34 us -> 7.91 us
    ppermute x2, waiting for transfers between devices: 0.48 us -> 0.2 us  [forwarded(): return lax.ppermute(x, ('parts', 'dp', 'query'), pairs)]
  transfers between devices with their start and end apart: 12 -> 12, of which waited for: 6 -> 6; matrix products, arithmetic and copies ran while one was open for 0% -> 0% of each run, Pallas kernels for 8% -> 9%
where the time goes in v12:
time: 26.8 us; the launch traced here: 26.6 us
  starting transfers between devices  13.4 us (50%)
  waiting for transfers between devices  7.91 us (30%)
  Pallas kernels  3.86 us (14%)
  between operations  0.79 us (3%)
  other arithmetic  0.61 us (2%)
    ppermute x3, waiting for transfers between devices, crossed(): lax.ppermute(x, (axis, 'query'), [(i, i ^ bit * cores + 1) for i in range...  6.47 us
    ppermute x3, starting transfers between devices, shifted(): return lax.ppermute(x, axis, [(i, (i + shift) % n) for i in range(n)])  5.09 us
    pallas_call x8, Pallas kernels, call(): pl.pallas_call(body, out_shape=out_shape, in_specs=specs + [ANY] * len(af...  3.86 us
    ppermute x3, starting transfers between devices, crossed(): lax.ppermute(x, (axis, 'query'), [(i, i ^ bit * cores + 1) for i in range...  3.67 us
    ppermute x2, starting transfers between devices, forwarded(): return lax.ppermute(x, ('parts', 'dp', 'query'), pairs)  3.47 us
    ppermute x4, starting transfers between devices, flipped(): return lax.ppermute(x, axis, [(i, i ^ bit) for i in range(n)])  1.21 us
    ppermute x4, waiting for transfers between devices, flipped(): return lax.ppermute(x, axis, [(i, i ^ bit) for i in range(n)])  1.05 us
    select_n x1, other arithmetic, local(): kept = jnp.where(odd_place == 0, kept, kept[::-1]).reshape(2, -1, n, nq)  0.58 us
  transfers between devices with their start and end apart: 12, of which 6 were waited for; matrix products, arithmetic and copies ran while one was open for 0% of the time, Pallas kernels for 9%

profile of v12, /device:TPU:0, one launch (start us, length us, event | category | flops | bytes accessed | tf_op | source)
XLA Modules:
  0.0 26.6 jit_solution(17719058588326909357)
XLA Ops:
  0.0 1.0 %shard_map.64 = (bf16[2,64,384]{2,1,0:T(8,128)(2,1)S(1)}, bf16[2,64,384]{2,1,0:T(8,128)(2,1)S(1)}, bf16[2,64,512]{2,1,0:T(8,128)(2,1)S(1)}) custom-call(bf16[2,64,2048]{2,1,0:T(8,128)(2,1)} %bitcast.12), custom_call_target="tpu_custom_call" | custom-call | flops 1 | bytes 1 | tf_op jit(solution)/shard_map/pallas_call | solution.py:31
  1.0 0.0 copy-start
  1.0 0.0 copy-start.3
  1.1 3.0 %collective-permute-start = (bf16[2,64,384]{2,1,0:T(8,128)(2,1)S(1)}, bf16[2,64,384]{2,1,0:T(8,128)(2,1)S(1)}, u32[]{:S(2)}, u32[]{:S(2)}) collective-permute-start(bf16[2,64,384]{2,1,0:T(8,128)(2,1)S(1)} %get-tuple-element.21.refs_0_), channel_id=1, source_target_pairs={{0,2},{2,0},{1,3},{3,1},{4,6},{6,4},{5,7},{7,5},{8,10},{10,8},{9,1... | collective-permute-start | bytes 294920 | tf_op jit(solution)/shard_map/ppermute | solution.py:209
  4.1 0.5 %shard_map.66 = bf16[2,64,640]{2,1,0:T(8,128)(2,1)S(1)} custom-call(bf16[2,256,2048]{2,1,0:T(8,128)(2,1)S(1)} %copy-done, bf16[2,64,2048]{2,1,0:T(8,128)(2,1)S(1)} %bitcast.14, bf16[2,64,512]{2,1,0:T(8,128)(2,1)S(1)} %get-tuple-element.22.refs_2_, f32[8,128]{1,0:T(8,128)S(1)} %shard_map.65.refs_3_), custom_call_target="tpu_custom_call" | custom-call | flops 1 | bytes 1 | tf_op jit(solution)/shard_map/pallas_call | solution.py:31
  4.6 1.6 %collective-permute-start.3 = (bf16[2,64,640]{2,1,0:T(8,128)(2,1)S(1)}, bf16[2,64,640]{2,1,0:T(8,128)(2,1)S(1)}, u32[]{:S(2)}, u32[]{:S(2)}) collective-permute-start(bf16[2,64,640]{2,1,0:T(8,128)(2,1)S(1)} %shard_map.66), channel_id=1, source_target_pairs={{0,2},{2,0},{1,3},{3,1},{4,6},{6,4},{5,7},{7,5},{8,10},{10,8},{9,1... | collective-permute-start | bytes 491528 | tf_op jit(solution)/shard_map/ppermute | solution.py:209
  6.2 0.5 %collective-permute-start.2 = (bf16[2,64,384]{2,1,0:T(8,128)(2,1)S(1)}, bf16[2,64,384]{2,1,0:T(8,128)(2,1)S(1)}, u32[]{:S(2)}, u32[]{:S(2)}) collective-permute-start(bf16[2,64,384]{2,1,0:T(8,128)(2,1)S(1)} %get-tuple-element.28), channel_id=1, source_target_pairs={{0,2},{2,0},{1,3},{3,1},{4,6},{6,4},{5,7},{7,5},{8,10},{10,8},{9,1... | collective-permute-start | bytes 294920 | tf_op jit(solution)/shard_map/ppermute | solution.py:209
  6.7 0.2 collective-permute-done.refs_4_
  6.9 2.0 %collective-permute-start.1 = (bf16[2,64,384]{2,1,0:T(8,128)(2,1)S(1)}, bf16[2,64,384]{2,1,0:T(8,128)(2,1)S(1)}, u32[]{:S(2)}, u32[]{:S(2)}) collective-permute-start(bf16[2,64,384]{2,1,0:T(8,128)(2,1)S(1)} %collective-permute-done.refs_4_), channel_id=1, source_target_pairs={{0,4},{1,17},{4,0},{5,21},{8,12},{9,25},{12,8},{13,29},{16,20},{17... | collective-permute-start | bytes 294920 | tf_op jit(solution)/shard_map/ppermute | solution.py:227
  8.8 1.5 %collective-permute-start.4 = (bf16[2,64,384]{2,1,0:T(8,128)(2,1)S(1)}, bf16[2,64,384]{2,1,0:T(8,128)(2,1)S(1)}, u32[]{:S(2)}, u32[]{:S(2)}) collective-permute-start(bf16[2,64,384]{2,1,0:T(8,128)(2,1)S(1)} %collective-permute-done.refs_4_), channel_id=1, source_target_pairs={{0,16},{1,5},{4,20},{5,1},{8,24},{9,13},{12,28},{13,9},{16,0},{17,... | collective-permute-start | bytes 294920 | tf_op jit(solution)/shard_map/ppermute | solution.py:227
  10.3 0.8 %shard_map.67 = (f32[128,128]{1,0:T(8,128)S(1)}, f32[128,128]{1,0:T(8,128)S(1)}, bf16[1,2,384,128]{3,2,1,0:T(8,128)(2,1)S(1)}) custom-call(bf16[2,128,4096]{2,1,0:T(8,128)(2,1)S(1)} %copy-done.1, bf16[2,64,2048]{2,1,0:T(8,128)(2,1)S(1)} %bitcast.13, bf16[2,256,2048]{2,1,0:T(8,128)(2,1)S(1)} %copy-done, bf16[2,64,2048]{2,1,0:T(8,128)(2,1)S(1)} %bitcast.15, ...), custom_call_target="tpu_custom_call" | custom-call | flops 1 | bytes 1 | tf_op jit(solution)/shard_map/pallas_call | solution.py:31
  11.2 0.3 %shard_map.70.refs_1_ = bf16[512,128]{1,0:T(8,128)(2,1)S(1)} custom-call(bf16[2,8,4096]{2,1,0:T(8,128)(2,1)S(1)} %copy-done.4), custom_call_target="tpu_custom_call" | custom-call | flops 1 | bytes 1 | tf_op jit(solution)/shard_map/pallas_call | solution.py:31
  11.5 0.5 %collective-permute-start.6 = (bf16[512,128]{1,0:T(8,128)(2,1)S(1)}, bf16[512,128]{1,0:T(8,128)(2,1)S(1)}, u32[]{:S(2)}, u32[]{:S(2)}) collective-permute-start(bf16[512,128]{1,0:T(8,128)(2,1)S(1)} %shard_map.70.refs_1_), channel_id=1, source_target_pairs={{0,4},{4,0},{8,12},{12,8},{1,5},{5,1},{9,13},{13,9},{2,6},{6,2},{1... | collective-permute-start | bytes 393224 | tf_op jit(solution)/shard_map/ppermute | solution.py:214
  12.7 0.0 collective-permute-done.2.refs_5_
  12.7 0.0 collective-permute-done.3.refs_6_
  12.7 0.5 %shard_map.68 = (f32[128,128]{1,0:T(8,128)S(1)}, bf16[128,128]{1,0:T(8,128)(2,1)S(1)}) custom-call(s32[1]{0:T(128)S(6)} %copy.7.refs_0_, bf16[2,128,4096]{2,1,0:T(8,128)(2,1)S(1)} %copy-done.1, f32[128,128]{1,0:T(8,128)S(1)} %get-tuple-element.26.refs_2_, f32[128,128]{1,0:T(8,128)S(1)} %get-tuple-element.27.refs_3_, ...), custom_call_target="tpu_custom_call" | custom-call | flops 1 | bytes 1 | tf_op jit(solution)/shard_map/pallas_call | solution.py:31
  13.2 0.2 collective-permute-done.4.refs_3_
  13.4 0.3 %shard_map.69 = bf16[16,512]{1,0:T(8,128)(2,1)S(1)} custom-call(bf16[1,2,384,128]{3,2,1,0:T(8,128)(2,1)S(1)} %get-tuple-element.24.refs_0_, f32[128,128]{1,0:T(8,128)S(1)} %get-tuple-element.29.refs_1_, bf16[128,128]{1,0:T(8,128)(2,1)S(1)} %get-tuple-element.30.refs_2_, bf16[2,64,384]{2,1,0:T(8,128)(2,1)S(1)} %collective-permute-done.4.refs_3_), custom_call_target="tpu_custom_call" | custom-call | flops 1 | bytes 1 | tf_op jit(solution)/shard_map/pallas_call | solution.py:31
  13.8 1.2 %collective-permute-start.5 = (bf16[1,16,512]{2,1,0:T(8,128)(2,1)S(1)}, bf16[1,16,512]{2,1,0:T(8,128)(2,1)S(1)}, u32[]{:S(2)}, u32[]{:S(2)}) collective-permute-start(bf16[1,16,512]{2,1,0:T(8,128)(2,1)S(1)} %bitcast.16), channel_id=1, source_target_pairs={{0,9},{1,8},{4,13},{5,12},{8,1},{9,0},{12,5},{13,4},{2,11},{3,10},... | collective-permute-start | bytes 49160 | tf_op jit(solution)/shard_map/ppermute | solution.py:220
  14.9 3.0 %collective-permute-done.5 = bf16[1,16,512]{2,1,0:T(8,128)(2,1)S(1)} collective-permute-done((bf16[1,16,512]{2,1,0:T(8,128)(2,1)S(1)}, bf16[1,16,512]{2,1,0:T(8,128)(2,1)S(1)}, u32[]{:S(2)}, u32[]{:S(2)}) %collective-permute-start.5) | collective-permute-done | bytes 16416 | tf_op jit(solution)/shard_map/ppermute | solution.py:220
  17.9 1.3 %collective-permute-start.7 = (bf16[2,16,512]{2,1,0:T(8,128)(2,1)S(1)}, bf16[2,16,512]{2,1,0:T(8,128)(2,1)S(1)}, u32[]{:S(2)}, u32[]{:S(2)}) collective-permute-start(bf16[2,16,512]{2,1,0:T(8,128)(2,1)S(1)} %pad_maximum_fusion.1), channel_id=1, source_target_pairs={{0,3},{1,2},{2,1},{3,0},{4,7},{5,6},{6,5},{7,4},{8,11},{9,10},{10,... | collective-permute-start | bytes 98312 | tf_op jit(solution)/shard_map/ppermute | solution.py:220
  19.2 0.4 %collective-permute-start.8 = (bf16[512,128]{1,0:T(8,128)(2,1)S(1)}, bf16[512,128]{1,0:T(8,128)(2,1)S(1)}, u32[]{:S(2)}, u32[]{:S(2)}) collective-permute-start(bf16[512,128]{1,0:T(8,128)(2,1)S(1)} %shard_map.70.refs_1_), channel_id=1, source_target_pairs={{0,1},{1,0},{2,3},{3,2},{4,5},{5,4},{6,7},{7,6},{8,9},{9,8},{10,11... | collective-permute-start | bytes 393224 | tf_op jit(solution)/shard_map/ppermute | solution.py:214
  19.6 0.1 collective-permute-start.9
  19.7 1.7 %collective-permute-done.7 = bf16[2,16,512]{2,1,0:T(8,128)(2,1)S(1)} collective-permute-done((bf16[2,16,512]{2,1,0:T(8,128)(2,1)S(1)}, bf16[2,16,512]{2,1,0:T(8,128)(2,1)S(1)}, u32[]{:S(2)}, u32[]{:S(2)}) %collective-permute-start.7) | collective-permute-done | bytes 32800 | tf_op jit(solution)/shard_map/ppermute | solution.py:220
  21.4 0.0 collective-permute-done.8.refs_2_
  21.4 0.0 collective-permute-done.9.refs_4_
  21.4 0.4 %shard_map.71 = (f32[4,8]{1,0:T(4,128)S(1)}, f32[4,8]{1,0:T(4,128)S(1)}, s32[2,2,8]{2,1,0:T(2,128)S(1)}) custom-call(bf16[4,16,512]{2,1,0:T(8,128)(2,1)S(1)} %pad_maximum_fusion.refs_0_, bf16[512,128]{1,0:T(8,128)(2,1)S(1)} %shard_map.70.refs_1_, bf16[512,128]{1,0:T(8,128)(2,1)S(1)} %collective-permute-done.8.refs_2_, ...), custom_call_target="tpu_custom_call" | custom-call | flops 1 | bytes 1 | tf_op jit(solution)/shard_map/pallas_call | solution.py:31
  21.7 1.2 %collective-permute-start.10 = (f32[4,8]{1,0:T(4,128)S(1)}, f32[4,8]{1,0:T(4,128)S(1)}, u32[]{:S(2)}, u32[]{:S(2)}) collective-permute-start(f32[4,8]{1,0:T(4,128)S(1)} %get-tuple-element.36), channel_id=1, source_target_pairs={{0,5},{1,4},{4,1},{5,0},{8,13},{9,12},{12,9},{13,8},{2,7},{3,6},{6... | collective-permute-start | bytes 392 | tf_op jit(solution)/shard_map/ppermute | solution.py:220
  23.0 1.8 %collective-permute-done.10 = f32[4,8]{1,0:T(4,128)S(1)} collective-permute-done((f32[4,8]{1,0:T(4,128)S(1)}, f32[4,8]{1,0:T(4,128)S(1)}, u32[]{:S(2)}, u32[]{:S(2)}) %collective-permute-start.10) | collective-permute-done | bytes 160 | tf_op jit(solution)/shard_map/ppermute | solution.py:220
  24.8 0.2 collective-permute-start.11
  25.0 1.0 %collective-permute-done.11 = f32[2,2,8]{2,1,0:T(2,128)S(1)} collective-permute-done((f32[2,2,8]{2,1,0:T(2,128)S(1)}, f32[2,2,8]{2,1,0:T(2,128)S(1)}, u32[]{:S(2)}, u32[]{:S(2)}) %collective-permute-start.11) | collective-permute-done | bytes 160 | tf_op jit(solution)/shard_map/ppermute | solution.py:214
  26.1 0.6 %compare_select_fusion = f32[2,2,8]{2,1,0:T(2,128)} fusion(f32[2,2,8]{2,1,0:T(2,128)S(1)} %maximum_add_fusion, s32[2,2,8]{2,1,0:T(2,128)S(1)} %get-tuple-element.34), kind=kLoop, calls=%fused_computation.2 | loop fusion | flops 64 | bytes 384 | tf_op jit(solution)/shard_map/jit(_where)/select_n | solution.py:335
  (17 shorter events, 0.1 us)
Async XLA Ops:
  1.0 3.0 %copy-start = (bf16[2,256,2048]{2,1,0:T(8,128)(2,1)S(1)}, bf16[2,256,2048]{2,1,0:T(8,128)(2,1)}, u32[]{:S(2)}) copy-start(bf16[2,256,2048]{2,1,0:T(8,128)(2,1)} %refs_2_.3) | copy-start | bytes 6291460
  1.0 3.0 %copy-start.3 = (bf16[2,2048,64]{1,2,0:T(8,128)(2,1)S(1)}, bf16[2,2048,64]{1,2,0:T(8,128)(2,1)}, u32[]{:S(2)}) copy-start(bf16[2,2048,64]{1,2,0:T(8,128)(2,1)} %param.9) | copy-start | bytes 1572868
  1.1 5.8 %collective-permute-start = (bf16[2,64,384]{2,1,0:T(8,128)(2,1)S(1)}, bf16[2,64,384]{2,1,0:T(8,128)(2,1)S(1)}, u32[]{:S(2)}, u32[]{:S(2)}) collective-permute-start(bf16[2,64,384]{2,1,0:T(8,128)(2,1)S(1)} %get-tuple-element.21.refs_0_), channel_id=1, source_target_pairs={{0,2},{2,0},{1,3},{3,1},{4,6},{6,4},{5,7},{7,5},{8,10},{10,8},{9,1... | collective-permute-start | bytes 294920 | tf_op jit(solution)/shard_map/ppermute | solution.py:209
  4.1 6.3 %copy-start.1 = (bf16[2,128,4096]{2,1,0:T(8,128)(2,1)S(1)}, bf16[2,128,4096]{2,1,0:T(8,128)(2,1)}, u32[]{:S(2)}) copy-start(bf16[2,128,4096]{2,1,0:T(8,128)(2,1)} %refs_1_.3) | copy-start | bytes 6291460
  4.1 6.3 %copy-start.2 = (bf16[2,2048,64]{1,2,0:T(8,128)(2,1)S(1)}, bf16[2,2048,64]{1,2,0:T(8,128)(2,1)}, u32[]{:S(2)}) copy-start(bf16[2,2048,64]{1,2,0:T(8,128)(2,1)} %param.10) | copy-start | bytes 1572868
  4.6 8.1 %collective-permute-start.3 = (bf16[2,64,640]{2,1,0:T(8,128)(2,1)S(1)}, bf16[2,64,640]{2,1,0:T(8,128)(2,1)S(1)}, u32[]{:S(2)}, u32[]{:S(2)}) collective-permute-start(bf16[2,64,640]{2,1,0:T(8,128)(2,1)S(1)} %shard_map.66), channel_id=1, source_target_pairs={{0,2},{2,0},{1,3},{3,1},{4,6},{6,4},{5,7},{7,5},{8,10},{10,8},{9,1... | collective-permute-start | bytes 491528 | tf_op jit(solution)/shard_map/ppermute | solution.py:209
  6.2 5.0 %copy-start.4 = (bf16[2,8,4096]{2,1,0:T(8,128)(2,1)S(1)}, bf16[2,8,4096]{2,1,0:T(8,128)(2,1)}, u32[]{:S(2)}) copy-start(bf16[2,8,4096]{2,1,0:T(8,128)(2,1)} %refs_0_.5) | copy-start | bytes 393220
  6.2 6.5 %collective-permute-start.2 = (bf16[2,64,384]{2,1,0:T(8,128)(2,1)S(1)}, bf16[2,64,384]{2,1,0:T(8,128)(2,1)S(1)}, u32[]{:S(2)}, u32[]{:S(2)}) collective-permute-start(bf16[2,64,384]{2,1,0:T(8,128)(2,1)S(1)} %get-tuple-element.28), channel_id=1, source_target_pairs={{0,2},{2,0},{1,3},{3,1},{4,6},{6,4},{5,7},{7,5},{8,10},{10,8},{9,1... | collective-permute-start | bytes 294920 | tf_op jit(solution)/shard_map/ppermute | solution.py:209
  6.9 5.9 %collective-permute-start.1 = (bf16[2,64,384]{2,1,0:T(8,128)(2,1)S(1)}, bf16[2,64,384]{2,1,0:T(8,128)(2,1)S(1)}, u32[]{:S(2)}, u32[]{:S(2)}) collective-permute-start(bf16[2,64,384]{2,1,0:T(8,128)(2,1)S(1)} %collective-permute-done.refs_4_), channel_id=1, source_target_pairs={{0,4},{1,17},{4,0},{5,21},{8,12},{9,25},{12,8},{13,29},{16,20},{17... | collective-permute-start | bytes 294920 | tf_op jit(solution)/shard_map/ppermute | solution.py:227
  8.8 4.6 %collective-permute-start.4 = (bf16[2,64,384]{2,1,0:T(8,128)(2,1)S(1)}, bf16[2,64,384]{2,1,0:T(8,128)(2,1)S(1)}, u32[]{:S(2)}, u32[]{:S(2)}) collective-permute-start(bf16[2,64,384]{2,1,0:T(8,128)(2,1)S(1)} %collective-permute-done.refs_4_), channel_id=1, source_target_pairs={{0,16},{1,5},{4,20},{5,1},{8,24},{9,13},{12,28},{13,9},{16,0},{17,... | collective-permute-start | bytes 294920 | tf_op jit(solution)/shard_map/ppermute | solution.py:227
  11.5 6.4 %collective-permute-start.6 = (bf16[512,128]{1,0:T(8,128)(2,1)S(1)}, bf16[512,128]{1,0:T(8,128)(2,1)S(1)}, u32[]{:S(2)}, u32[]{:S(2)}) collective-permute-start(bf16[512,128]{1,0:T(8,128)(2,1)S(1)} %shard_map.70.refs_1_), channel_id=1, source_target_pairs={{0,4},{4,0},{8,12},{12,8},{1,5},{5,1},{9,13},{13,9},{2,6},{6,2},{1... | collective-permute-start | bytes 393224 | tf_op jit(solution)/shard_map/ppermute | solution.py:214
  13.8 4.1 %collective-permute-start.5 = (bf16[1,16,512]{2,1,0:T(8,128)(2,1)S(1)}, bf16[1,16,512]{2,1,0:T(8,128)(2,1)S(1)}, u32[]{:S(2)}, u32[]{:S(2)}) collective-permute-start(bf16[1,16,512]{2,1,0:T(8,128)(2,1)S(1)} %bitcast.16), channel_id=1, source_target_pairs={{0,9},{1,8},{4,13},{5,12},{8,1},{9,0},{12,5},{13,4},{2,11},{3,10},... | collective-permute-start | bytes 49160 | tf_op jit(solution)/shard_map/ppermute | solution.py:220
  17.9 3.5 %collective-permute-start.7 = (bf16[2,16,512]{2,1,0:T(8,128)(2,1)S(1)}, bf16[2,16,512]{2,1,0:T(8,128)(2,1)S(1)}, u32[]{:S(2)}, u32[]{:S(2)}) collective-permute-start(bf16[2,16,512]{2,1,0:T(8,128)(2,1)S(1)} %pad_maximum_fusion.1), channel_id=1, source_target_pairs={{0,3},{1,2},{2,1},{3,0},{4,7},{5,6},{6,5},{7,4},{8,11},{9,10},{10,... | collective-permute-start | bytes 98312 | tf_op jit(solution)/shard_map/ppermute | solution.py:220
  19.2 2.2 %collective-permute-start.8 = (bf16[512,128]{1,0:T(8,128)(2,1)S(1)}, bf16[512,128]{1,0:T(8,128)(2,1)S(1)}, u32[]{:S(2)}, u32[]{:S(2)}) collective-permute-start(bf16[512,128]{1,0:T(8,128)(2,1)S(1)} %shard_map.70.refs_1_), channel_id=1, source_target_pairs={{0,1},{1,0},{2,3},{3,2},{4,5},{5,4},{6,7},{7,6},{8,9},{9,8},{10,11... | collective-permute-start | bytes 393224 | tf_op jit(solution)/shard_map/ppermute | solution.py:214
  19.6 1.8 %collective-permute-start.9 = (bf16[512,128]{1,0:T(8,128)(2,1)S(1)}, bf16[512,128]{1,0:T(8,128)(2,1)S(1)}, u32[]{:S(2)}, u32[]{:S(2)}) collective-permute-start(bf16[512,128]{1,0:T(8,128)(2,1)S(1)} %collective-permute-done.6.refs_3_), channel_id=1, source_target_pairs={{0,1},{1,0},{2,3},{3,2},{4,5},{5,4},{6,7},{7,6},{8,9},{9,8},{10,11... | collective-permute-start | bytes 393224 | tf_op jit(solution)/shard_map/ppermute | solution.py:214
  21.7 3.1 %collective-permute-start.10 = (f32[4,8]{1,0:T(4,128)S(1)}, f32[4,8]{1,0:T(4,128)S(1)}, u32[]{:S(2)}, u32[]{:S(2)}) collective-permute-start(f32[4,8]{1,0:T(4,128)S(1)} %get-tuple-element.36), channel_id=1, source_target_pairs={{0,5},{1,4},{4,1},{5,0},{8,13},{9,12},{12,9},{13,8},{2,7},{3,6},{6... | collective-permute-start | bytes 392 | tf_op jit(solution)/shard_map/ppermute | solution.py:220
  24.8 1.2 %collective-permute-start.11 = (f32[2,2,8]{2,1,0:T(2,128)S(1)}, f32[2,2,8]{2,1,0:T(2,128)S(1)}, u32[]{:S(2)}, u32[]{:S(2)}) collective-permute-start(f32[2,2,8]{2,1,0:T(2,128)S(1)} %pad_maximum_fusion.2), channel_id=1, source_target_pairs={{0,1},{1,0},{2,3},{3,2},{4,5},{5,4},{6,7},{7,6},{8,9},{9,8},{10,11... | collective-permute-start | bytes 392 | tf_op jit(solution)/shard_map/ppermute | solution.py:214

commit v13 on v12

--- a/solution.py
+++ b/solution.py
@@ -91,7 +91,11 @@
     for s, out in enumerate(parcels, 1):
         out[:, :, :size] = tail[...]
         block = project(acts, lax.rem(lax.axis_index("tensor") + s, n), slots, factor)
-        out[:, :, size:] = block.astype(BF16).reshape(layers, width, layers * width)
+        high = block.astype(BF16)
+        low = (block - high.astype(F32)).astype(BF16)
+        lanes = layers * width
+        out[:, :, size : size + lanes] = high.reshape(layers, width, lanes)
+        out[:, :, size + lanes :] = low.reshape(layers, width, lanes)
 
 
 def fold_queries(width, queries, out, rows):
@@ -142,11 +146,13 @@
     for s in range(1, n):
         second, fourth, parcel = (x[s - 1] for x in (seconds, fourths, parcels))
         start = block_of(t, s, n) * depth
-        step, size = second.shape[2], parcel.shape[2] - lanes
+        step, size = second.shape[2], parcel.shape[2] - 2 * lanes
         total = total + product(grads, start + side(1, 1) * step, fourth)
         total = total + product(grads, start + 4 * step, parcel.at[:, :, :size])
         total = total + product(grads, start + swapped(True) * step, second)
-        ins = ins + parcel[:, :, size:].reshape(slots, lanes).astype(F32)
+        high, low = parcel[:, :, size : size + lanes], parcel[:, :, size + lanes :]
+        ins = ins + high.reshape(slots, lanes).astype(F32)
+        ins = ins + low.reshape(slots, lanes).astype(F32)
     total_out[...] = total.T
     live = lax.broadcasted_iota(jnp.int32, ins.shape, 0) < length[0]
     ins_out[...] = jnp.where(live, ins, 0.0).T.astype(BF16)
@@ -188,13 +194,13 @@
     fold = lax.broadcasted_iota(jnp.int32, (nq * FOLD, nq), 0)
     fold = fold - FOLD * lax.broadcasted_iota(jnp.int32, (nq * FOLD, nq), 1)
     fold = ((fold >= 0) & (fold < FOLD)).astype(F32)
-    table = lax.dot_general(
-        sums,
-        fold,
-        (((1,), (0,)), ((), ())),
-        precision=lax.Precision.HIGHEST,
-        preferred_element_type=F32,
-    )
+    high = sums.astype(BF16)
+    rest = sums - high.astype(F32)
+    low = rest.astype(BF16)
+    least = (rest - low.astype(F32)).astype(BF16)
+    parts = dot(jnp.concatenate([high, low, least], axis=0), fold.astype(BF16), NN)
+    rows = 2 * slots
+    table = parts[:rows] + (parts[rows : 2 * rows] + parts[2 * rows :])
     odd_place[...] = jnp.full(odd_place.shape, lax.axis_index("dp") & 1, jnp.int32)
     core = lax.axis_index("query")
     place = lax.axis_index("dp") // 2 * n + lax.axis_index("tensor")
@@ -259,7 +265,7 @@
     factor_in = proj_in.transpose(0, 2, 1)
     parcels = call(
         functools.partial(project_inputs, n),
-        [jax.ShapeDtypeStruct((layers, width, depth - 4 * step + lanes), BF16)] * (n - 1),
+        [jax.ShapeDtypeStruct((layers, width, depth - 4 * step + 2 * lanes), BF16)] * (n - 1),
         acts,
         factor_in,
         tail,

time: 26.8 us -> 27 us (level)
  starting transfers between devices: 13.4 us -> 14.7 us
  waiting for transfers between devices: 7.91 us -> 6.84 us
    ppermute x3, waiting for transfers between devices: 6.47 us -> 5.3 us  [crossed(): lax.ppermute(x, (axis, 'query'), [(i, i ^ bit * cores + 1) for i in range...]
    ppermute x3, starting transfers between devices: 3.67 us -> 4.75 us  [crossed(): lax.ppermute(x, (axis, 'query'), [(i, i ^ bit * cores + 1) for i in range...]
    ppermute x3, waiting for transfers between devices: 0.19 us -> 0.7 us  [shifted(): return lax.ppermute(x, axis, [(i, (i + shift) % n) for i in range(n)])]
where the time goes in v13:
time: 27 us; the launch traced here: 26.8 us
  starting transfers between devices  14.7 us (54%)
  waiting for transfers between devices  6.84 us (25%)
  Pallas kernels  3.84 us (14%)
  between operations  0.78 us (3%)
  other arithmetic  0.61 us (2%)
    ppermute x3, waiting for transfers between devices, crossed(): lax.ppermute(x, (axis, 'query'), [(i, i ^ bit * cores + 1) for i in range...  5.3 us
    ppermute x3, starting transfers between devices, shifted(): return lax.ppermute(x, axis, [(i, (i + shift) % n) for i in range(n)])  5.09 us
    ppermute x3, starting transfers between devices, crossed(): lax.ppermute(x, (axis, 'query'), [(i, i ^ bit * cores + 1) for i in range...  4.75 us
    pallas_call x8, Pallas kernels, call(): pl.pallas_call(body, out_shape=out_shape, in_specs=specs + [ANY] * len(af...  3.84 us
    ppermute x2, starting transfers between devices, forwarded(): return lax.ppermute(x, ('parts', 'dp', 'query'), pairs)  3.47 us
    ppermute x4, starting transfers between devices, flipped(): return lax.ppermute(x, axis, [(i, i ^ bit) for i in range(n)])  1.43 us
    ppermute x4, waiting for transfers between devices, flipped(): return lax.ppermute(x, axis, [(i, i ^ bit) for i in range(n)])  0.83 us
    ppermute x3, waiting for transfers between devices, shifted(): return lax.ppermute(x, axis, [(i, (i + shift) % n) for i in range(n)])  0.7 us
  transfers between devices with their start and end apart: 12, of which 6 were waited for; matrix products, arithmetic and copies ran while one was open for 0% of the time, Pallas kernels for 9%

profile of v13, /device:TPU:0, one launch (start us, length us, event | category | flops | bytes accessed | tf_op | source)
XLA Modules:
  0.0 26.8 jit_solution(2452573632373713885)
XLA Ops:
  0.0 1.0 %shard_map.64 = (bf16[2,64,384]{2,1,0:T(8,128)(2,1)S(1)}, bf16[2,64,384]{2,1,0:T(8,128)(2,1)S(1)}, bf16[2,64,512]{2,1,0:T(8,128)(2,1)S(1)}) custom-call(bf16[2,64,2048]{2,1,0:T(8,128)(2,1)} %bitcast.12), custom_call_target="tpu_custom_call" | custom-call | flops 1 | bytes 1 | tf_op jit(solution)/shard_map/pallas_call | solution.py:31
  1.0 0.0 copy-start
  1.0 0.0 copy-start.3
  1.1 3.0 %collective-permute-start = (bf16[2,64,384]{2,1,0:T(8,128)(2,1)S(1)}, bf16[2,64,384]{2,1,0:T(8,128)(2,1)S(1)}, u32[]{:S(2)}, u32[]{:S(2)}) collective-permute-start(bf16[2,64,384]{2,1,0:T(8,128)(2,1)S(1)} %get-tuple-element.21.refs_0_), channel_id=1, source_target_pairs={{0,2},{2,0},{1,3},{3,1},{4,6},{6,4},{5,7},{7,5},{8,10},{10,8},{9,1... | collective-permute-start | bytes 294920 | tf_op jit(solution)/shard_map/ppermute | solution.py:215
  4.1 0.5 %shard_map.66 = bf16[2,64,768]{2,1,0:T(8,128)(2,1)S(1)} custom-call(bf16[2,256,2048]{2,1,0:T(8,128)(2,1)S(1)} %copy-done, bf16[2,64,2048]{2,1,0:T(8,128)(2,1)S(1)} %bitcast.14, bf16[2,64,512]{2,1,0:T(8,128)(2,1)S(1)} %get-tuple-element.22.refs_2_, f32[8,128]{1,0:T(8,128)S(1)} %shard_map.65.refs_3_), custom_call_target="tpu_custom_call" | custom-call | flops 1 | bytes 1 | tf_op jit(solution)/shard_map/pallas_call | solution.py:31
  4.6 1.6 %collective-permute-start.3 = (bf16[2,64,768]{2,1,0:T(8,128)(2,1)S(1)}, bf16[2,64,768]{2,1,0:T(8,128)(2,1)S(1)}, u32[]{:S(2)}, u32[]{:S(2)}) collective-permute-start(bf16[2,64,768]{2,1,0:T(8,128)(2,1)S(1)} %shard_map.66), channel_id=1, source_target_pairs={{0,2},{2,0},{1,3},{3,1},{4,6},{6,4},{5,7},{7,5},{8,10},{10,8},{9,1... | collective-permute-start | bytes 589832 | tf_op jit(solution)/shard_map/ppermute | solution.py:215
  6.2 0.5 %collective-permute-start.2 = (bf16[2,64,384]{2,1,0:T(8,128)(2,1)S(1)}, bf16[2,64,384]{2,1,0:T(8,128)(2,1)S(1)}, u32[]{:S(2)}, u32[]{:S(2)}) collective-permute-start(bf16[2,64,384]{2,1,0:T(8,128)(2,1)S(1)} %get-tuple-element.28), channel_id=1, source_target_pairs={{0,2},{2,0},{1,3},{3,1},{4,6},{6,4},{5,7},{7,5},{8,10},{10,8},{9,1... | collective-permute-start | bytes 294920 | tf_op jit(solution)/shard_map/ppermute | solution.py:215
  6.7 0.2 collective-permute-done.refs_4_
  6.9 1.9 %collective-permute-start.1 = (bf16[2,64,384]{2,1,0:T(8,128)(2,1)S(1)}, bf16[2,64,384]{2,1,0:T(8,128)(2,1)S(1)}, u32[]{:S(2)}, u32[]{:S(2)}) collective-permute-start(bf16[2,64,384]{2,1,0:T(8,128)(2,1)S(1)} %collective-permute-done.refs_4_), channel_id=1, source_target_pairs={{0,4},{1,17},{4,0},{5,21},{8,12},{9,25},{12,8},{13,29},{16,20},{17... | collective-permute-start | bytes 294920 | tf_op jit(solution)/shard_map/ppermute | solution.py:233
  8.8 1.5 %collective-permute-start.4 = (bf16[2,64,384]{2,1,0:T(8,128)(2,1)S(1)}, bf16[2,64,384]{2,1,0:T(8,128)(2,1)S(1)}, u32[]{:S(2)}, u32[]{:S(2)}) collective-permute-start(bf16[2,64,384]{2,1,0:T(8,128)(2,1)S(1)} %collective-permute-done.refs_4_), channel_id=1, source_target_pairs={{0,16},{1,5},{4,20},{5,1},{8,24},{9,13},{12,28},{13,9},{16,0},{17,... | collective-permute-start | bytes 294920 | tf_op jit(solution)/shard_map/ppermute | solution.py:233
  10.3 0.8 %shard_map.67 = (f32[128,128]{1,0:T(8,128)S(1)}, f32[128,128]{1,0:T(8,128)S(1)}, bf16[1,2,384,128]{3,2,1,0:T(8,128)(2,1)S(1)}) custom-call(bf16[2,128,4096]{2,1,0:T(8,128)(2,1)S(1)} %copy-done.1, bf16[2,64,2048]{2,1,0:T(8,128)(2,1)S(1)} %bitcast.13, bf16[2,256,2048]{2,1,0:T(8,128)(2,1)S(1)} %copy-done, bf16[2,64,2048]{2,1,0:T(8,128)(2,1)S(1)} %bitcast.15, ...), custom_call_target="tpu_custom_call" | custom-call | flops 1 | bytes 1 | tf_op jit(solution)/shard_map/pallas_call | solution.py:31
  11.2 0.3 %shard_map.70.refs_1_ = bf16[512,128]{1,0:T(8,128)(2,1)S(1)} custom-call(bf16[2,8,4096]{2,1,0:T(8,128)(2,1)S(1)} %copy-done.4), custom_call_target="tpu_custom_call" | custom-call | flops 1 | bytes 1 | tf_op jit(solution)/shard_map/pallas_call | solution.py:31
  11.5 0.5 %collective-permute-start.6 = (bf16[512,128]{1,0:T(8,128)(2,1)S(1)}, bf16[512,128]{1,0:T(8,128)(2,1)S(1)}, u32[]{:S(2)}, u32[]{:S(2)}) collective-permute-start(bf16[512,128]{1,0:T(8,128)(2,1)S(1)} %shard_map.70.refs_1_), channel_id=1, source_target_pairs={{0,4},{4,0},{8,12},{12,8},{1,5},{5,1},{9,13},{13,9},{2,6},{6,2},{1... | collective-permute-start | bytes 393224 | tf_op jit(solution)/shard_map/ppermute | solution.py:220
  12.7 0.5 %collective-permute-done.2.refs_5_ = bf16[2,64,384]{2,1,0:T(8,128)(2,1)S(1)} collective-permute-done((bf16[2,64,384]{2,1,0:T(8,128)(2,1)S(1)}, bf16[2,64,384]{2,1,0:T(8,128)(2,1)S(1)}, u32[]{:S(2)}, u32[]{:S(2)}) %collective-permute-start.2) | collective-permute-done | bytes 98336 | tf_op jit(solution)/shard_map/ppermute | solution.py:215
  13.2 0.0 collective-permute-done.1.refs_4_
  13.2 0.0 collective-permute-done.3.refs_6_
  13.2 0.5 %shard_map.68 = (f32[128,128]{1,0:T(8,128)S(1)}, bf16[128,128]{1,0:T(8,128)(2,1)S(1)}) custom-call(s32[1]{0:T(128)S(6)} %copy.7.refs_0_, bf16[2,128,4096]{2,1,0:T(8,128)(2,1)S(1)} %copy-done.1, f32[128,128]{1,0:T(8,128)S(1)} %get-tuple-element.26.refs_2_, f32[128,128]{1,0:T(8,128)S(1)} %get-tuple-element.27.refs_3_, ...), custom_call_target="tpu_custom_call" | custom-call | flops 1 | bytes 1 | tf_op jit(solution)/shard_map/pallas_call | solution.py:31
  13.7 0.0 collective-permute-done.4.refs_3_
  13.7 0.3 %shard_map.69 = bf16[16,512]{1,0:T(8,128)(2,1)S(1)} custom-call(bf16[1,2,384,128]{3,2,1,0:T(8,128)(2,1)S(1)} %get-tuple-element.24.refs_0_, f32[128,128]{1,0:T(8,128)S(1)} %get-tuple-element.29.refs_1_, bf16[128,128]{1,0:T(8,128)(2,1)S(1)} %get-tuple-element.30.refs_2_, bf16[2,64,384]{2,1,0:T(8,128)(2,1)S(1)} %collective-permute-done.4.refs_3_), custom_call_target="tpu_custom_call" | custom-call | flops 1 | bytes 1 | tf_op jit(solution)/shard_map/pallas_call | solution.py:31
  14.0 1.6 %collective-permute-start.5 = (bf16[1,16,512]{2,1,0:T(8,128)(2,1)S(1)}, bf16[1,16,512]{2,1,0:T(8,128)(2,1)S(1)}, u32[]{:S(2)}, u32[]{:S(2)}) collective-permute-start(bf16[1,16,512]{2,1,0:T(8,128)(2,1)S(1)} %bitcast.16), channel_id=1, source_target_pairs={{0,9},{1,8},{4,13},{5,12},{8,1},{9,0},{12,5},{13,4},{2,11},{3,10},... | collective-permute-start | bytes 49160 | tf_op jit(solution)/shard_map/ppermute | solution.py:226
  15.6 2.6 %collective-permute-done.5 = bf16[1,16,512]{2,1,0:T(8,128)(2,1)S(1)} collective-permute-done((bf16[1,16,512]{2,1,0:T(8,128)(2,1)S(1)}, bf16[1,16,512]{2,1,0:T(8,128)(2,1)S(1)}, u32[]{:S(2)}, u32[]{:S(2)}) %collective-permute-start.5) | collective-permute-done | bytes 16416 | tf_op jit(solution)/shard_map/ppermute | solution.py:226
  18.2 0.0 collective-permute-done.6.refs_3_
  18.2 1.6 %collective-permute-start.7 = (bf16[2,16,512]{2,1,0:T(8,128)(2,1)S(1)}, bf16[2,16,512]{2,1,0:T(8,128)(2,1)S(1)}, u32[]{:S(2)}, u32[]{:S(2)}) collective-permute-start(bf16[2,16,512]{2,1,0:T(8,128)(2,1)S(1)} %pad_maximum_fusion.1), channel_id=1, source_target_pairs={{0,3},{1,2},{2,1},{3,0},{4,7},{5,6},{6,5},{7,4},{8,11},{9,10},{10,... | collective-permute-start | bytes 98312 | tf_op jit(solution)/shard_map/ppermute | solution.py:226
  19.7 0.4 %collective-permute-start.8 = (bf16[512,128]{1,0:T(8,128)(2,1)S(1)}, bf16[512,128]{1,0:T(8,128)(2,1)S(1)}, u32[]{:S(2)}, u32[]{:S(2)}) collective-permute-start(bf16[512,128]{1,0:T(8,128)(2,1)S(1)} %shard_map.70.refs_1_), channel_id=1, source_target_pairs={{0,1},{1,0},{2,3},{3,2},{4,5},{5,4},{6,7},{7,6},{8,9},{9,8},{10,11... | collective-permute-start | bytes 393224 | tf_op jit(solution)/shard_map/ppermute | solution.py:220
  20.1 0.1 collective-permute-start.9
  20.3 1.3 %collective-permute-done.7 = bf16[2,16,512]{2,1,0:T(8,128)(2,1)S(1)} collective-permute-done((bf16[2,16,512]{2,1,0:T(8,128)(2,1)S(1)}, bf16[2,16,512]{2,1,0:T(8,128)(2,1)S(1)}, u32[]{:S(2)}, u32[]{:S(2)}) %collective-permute-start.7) | collective-permute-done | bytes 32800 | tf_op jit(solution)/shard_map/ppermute | solution.py:226
  21.6 0.3 %shard_map.71 = (f32[4,8]{1,0:T(4,128)S(1)}, f32[4,8]{1,0:T(4,128)S(1)}, s32[2,2,8]{2,1,0:T(2,128)S(1)}) custom-call(bf16[4,16,512]{2,1,0:T(8,128)(2,1)S(1)} %pad_maximum_fusion.refs_0_, bf16[512,128]{1,0:T(8,128)(2,1)S(1)} %shard_map.70.refs_1_, bf16[512,128]{1,0:T(8,128)(2,1)S(1)} %collective-permute-done.8.refs_2_, ...), custom_call_target="tpu_custom_call" | custom-call | flops 1 | bytes 1 | tf_op jit(solution)/shard_map/pallas_call | solution.py:31
  22.0 1.6 %collective-permute-start.10 = (f32[4,8]{1,0:T(4,128)S(1)}, f32[4,8]{1,0:T(4,128)S(1)}, u32[]{:S(2)}, u32[]{:S(2)}) collective-permute-start(f32[4,8]{1,0:T(4,128)S(1)} %get-tuple-element.36), channel_id=1, source_target_pairs={{0,5},{1,4},{4,1},{5,0},{8,13},{9,12},{12,9},{13,8},{2,7},{3,6},{6... | collective-permute-start | bytes 392 | tf_op jit(solution)/shard_map/ppermute | solution.py:226
  23.6 1.4 %collective-permute-done.10 = f32[4,8]{1,0:T(4,128)S(1)} collective-permute-done((f32[4,8]{1,0:T(4,128)S(1)}, f32[4,8]{1,0:T(4,128)S(1)}, u32[]{:S(2)}, u32[]{:S(2)}) %collective-permute-start.10) | collective-permute-done | bytes 160 | tf_op jit(solution)/shard_map/ppermute | solution.py:226
  25.0 0.4 %collective-permute-start.11 = (f32[2,2,8]{2,1,0:T(2,128)S(1)}, f32[2,2,8]{2,1,0:T(2,128)S(1)}, u32[]{:S(2)}, u32[]{:S(2)}) collective-permute-start(f32[2,2,8]{2,1,0:T(2,128)S(1)} %pad_maximum_fusion.2), channel_id=1, source_target_pairs={{0,1},{1,0},{2,3},{3,2},{4,5},{5,4},{6,7},{7,6},{8,9},{9,8},{10,11... | collective-permute-start | bytes 392 | tf_op jit(solution)/shard_map/ppermute | solution.py:220
  25.4 0.8 %collective-permute-done.11 = f32[2,2,8]{2,1,0:T(2,128)S(1)} collective-permute-done((f32[2,2,8]{2,1,0:T(2,128)S(1)}, f32[2,2,8]{2,1,0:T(2,128)S(1)}, u32[]{:S(2)}, u32[]{:S(2)}) %collective-permute-start.11) | collective-permute-done | bytes 160 | tf_op jit(solution)/shard_map/ppermute | solution.py:220
  26.2 0.6 %compare_select_fusion = f32[2,2,8]{2,1,0:T(2,128)} fusion(f32[2,2,8]{2,1,0:T(2,128)S(1)} %maximum_add_fusion, s32[2,2,8]{2,1,0:T(2,128)S(1)} %get-tuple-element.34), kind=kLoop, calls=%fused_computation.2 | loop fusion | flops 64 | bytes 384 | tf_op jit(solution)/shard_map/jit(_where)/select_n | solution.py:341
  (17 shorter events, 0.1 us)
Async XLA Ops:
  1.0 3.0 %copy-start = (bf16[2,256,2048]{2,1,0:T(8,128)(2,1)S(1)}, bf16[2,256,2048]{2,1,0:T(8,128)(2,1)}, u32[]{:S(2)}) copy-start(bf16[2,256,2048]{2,1,0:T(8,128)(2,1)} %refs_2_.3) | copy-start | bytes 6291460
  1.0 3.0 %copy-start.3 = (bf16[2,2048,64]{1,2,0:T(8,128)(2,1)S(1)}, bf16[2,2048,64]{1,2,0:T(8,128)(2,1)}, u32[]{:S(2)}) copy-start(bf16[2,2048,64]{1,2,0:T(8,128)(2,1)} %param.9) | copy-start | bytes 1572868
  1.1 5.8 %collective-permute-start = (bf16[2,64,384]{2,1,0:T(8,128)(2,1)S(1)}, bf16[2,64,384]{2,1,0:T(8,128)(2,1)S(1)}, u32[]{:S(2)}, u32[]{:S(2)}) collective-permute-start(bf16[2,64,384]{2,1,0:T(8,128)(2,1)S(1)} %get-tuple-element.21.refs_0_), channel_id=1, source_target_pairs={{0,2},{2,0},{1,3},{3,1},{4,6},{6,4},{5,7},{7,5},{8,10},{10,8},{9,1... | collective-permute-start | bytes 294920 | tf_op jit(solution)/shard_map/ppermute | solution.py:215
  4.1 6.3 %copy-start.1 = (bf16[2,128,4096]{2,1,0:T(8,128)(2,1)S(1)}, bf16[2,128,4096]{2,1,0:T(8,128)(2,1)}, u32[]{:S(2)}) copy-start(bf16[2,128,4096]{2,1,0:T(8,128)(2,1)} %refs_1_.3) | copy-start | bytes 6291460
  4.1 6.3 %copy-start.2 = (bf16[2,2048,64]{1,2,0:T(8,128)(2,1)S(1)}, bf16[2,2048,64]{1,2,0:T(8,128)(2,1)}, u32[]{:S(2)}) copy-start(bf16[2,2048,64]{1,2,0:T(8,128)(2,1)} %param.10) | copy-start | bytes 1572868
  4.6 8.6 %collective-permute-start.3 = (bf16[2,64,768]{2,1,0:T(8,128)(2,1)S(1)}, bf16[2,64,768]{2,1,0:T(8,128)(2,1)S(1)}, u32[]{:S(2)}, u32[]{:S(2)}) collective-permute-start(bf16[2,64,768]{2,1,0:T(8,128)(2,1)S(1)} %shard_map.66), channel_id=1, source_target_pairs={{0,2},{2,0},{1,3},{3,1},{4,6},{6,4},{5,7},{7,5},{8,10},{10,8},{9,1... | collective-permute-start | bytes 589832 | tf_op jit(solution)/shard_map/ppermute | solution.py:215
  6.2 5.0 %copy-start.4 = (bf16[2,8,4096]{2,1,0:T(8,128)(2,1)S(1)}, bf16[2,8,4096]{2,1,0:T(8,128)(2,1)}, u32[]{:S(2)}) copy-start(bf16[2,8,4096]{2,1,0:T(8,128)(2,1)} %refs_0_.5) | copy-start | bytes 393220
  6.2 7.0 %collective-permute-start.2 = (bf16[2,64,384]{2,1,0:T(8,128)(2,1)S(1)}, bf16[2,64,384]{2,1,0:T(8,128)(2,1)S(1)}, u32[]{:S(2)}, u32[]{:S(2)}) collective-permute-start(bf16[2,64,384]{2,1,0:T(8,128)(2,1)S(1)} %get-tuple-element.28), channel_id=1, source_target_pairs={{0,2},{2,0},{1,3},{3,1},{4,6},{6,4},{5,7},{7,5},{8,10},{10,8},{9,1... | collective-permute-start | bytes 294920 | tf_op jit(solution)/shard_map/ppermute | solution.py:215
  6.9 6.4 %collective-permute-start.1 = (bf16[2,64,384]{2,1,0:T(8,128)(2,1)S(1)}, bf16[2,64,384]{2,1,0:T(8,128)(2,1)S(1)}, u32[]{:S(2)}, u32[]{:S(2)}) collective-permute-start(bf16[2,64,384]{2,1,0:T(8,128)(2,1)S(1)} %collective-permute-done.refs_4_), channel_id=1, source_target_pairs={{0,4},{1,17},{4,0},{5,21},{8,12},{9,25},{12,8},{13,29},{16,20},{17... | collective-permute-start | bytes 294920 | tf_op jit(solution)/shard_map/ppermute | solution.py:233
  8.8 4.9 %collective-permute-start.4 = (bf16[2,64,384]{2,1,0:T(8,128)(2,1)S(1)}, bf16[2,64,384]{2,1,0:T(8,128)(2,1)S(1)}, u32[]{:S(2)}, u32[]{:S(2)}) collective-permute-start(bf16[2,64,384]{2,1,0:T(8,128)(2,1)S(1)} %collective-permute-done.refs_4_), channel_id=1, source_target_pairs={{0,16},{1,5},{4,20},{5,1},{8,24},{9,13},{12,28},{13,9},{16,0},{17,... | collective-permute-start | bytes 294920 | tf_op jit(solution)/shard_map/ppermute | solution.py:233
  11.5 6.7 %collective-permute-start.6 = (bf16[512,128]{1,0:T(8,128)(2,1)S(1)}, bf16[512,128]{1,0:T(8,128)(2,1)S(1)}, u32[]{:S(2)}, u32[]{:S(2)}) collective-permute-start(bf16[512,128]{1,0:T(8,128)(2,1)S(1)} %shard_map.70.refs_1_), channel_id=1, source_target_pairs={{0,4},{4,0},{8,12},{12,8},{1,5},{5,1},{9,13},{13,9},{2,6},{6,2},{1... | collective-permute-start | bytes 393224 | tf_op jit(solution)/shard_map/ppermute | solution.py:220
  14.0 4.1 %collective-permute-start.5 = (bf16[1,16,512]{2,1,0:T(8,128)(2,1)S(1)}, bf16[1,16,512]{2,1,0:T(8,128)(2,1)S(1)}, u32[]{:S(2)}, u32[]{:S(2)}) collective-permute-start(bf16[1,16,512]{2,1,0:T(8,128)(2,1)S(1)} %bitcast.16), channel_id=1, source_target_pairs={{0,9},{1,8},{4,13},{5,12},{8,1},{9,0},{12,5},{13,4},{2,11},{3,10},... | collective-permute-start | bytes 49160 | tf_op jit(solution)/shard_map/ppermute | solution.py:226
  18.2 3.4 %collective-permute-start.7 = (bf16[2,16,512]{2,1,0:T(8,128)(2,1)S(1)}, bf16[2,16,512]{2,1,0:T(8,128)(2,1)S(1)}, u32[]{:S(2)}, u32[]{:S(2)}) collective-permute-start(bf16[2,16,512]{2,1,0:T(8,128)(2,1)S(1)} %pad_maximum_fusion.1), channel_id=1, source_target_pairs={{0,3},{1,2},{2,1},{3,0},{4,7},{5,6},{6,5},{7,4},{8,11},{9,10},{10,... | collective-permute-start | bytes 98312 | tf_op jit(solution)/shard_map/ppermute | solution.py:226
  19.7 1.9 %collective-permute-start.8 = (bf16[512,128]{1,0:T(8,128)(2,1)S(1)}, bf16[512,128]{1,0:T(8,128)(2,1)S(1)}, u32[]{:S(2)}, u32[]{:S(2)}) collective-permute-start(bf16[512,128]{1,0:T(8,128)(2,1)S(1)} %shard_map.70.refs_1_), channel_id=1, source_target_pairs={{0,1},{1,0},{2,3},{3,2},{4,5},{5,4},{6,7},{7,6},{8,9},{9,8},{10,11... | collective-permute-start | bytes 393224 | tf_op jit(solution)/shard_map/ppermute | solution.py:220
  20.1 1.5 %collective-permute-start.9 = (bf16[512,128]{1,0:T(8,128)(2,1)S(1)}, bf16[512,128]{1,0:T(8,128)(2,1)S(1)}, u32[]{:S(2)}, u32[]{:S(2)}) collective-permute-start(bf16[512,128]{1,0:T(8,128)(2,1)S(1)} %collective-permute-done.6.refs_3_), channel_id=1, source_target_pairs={{0,1},{1,0},{2,3},{3,2},{4,5},{5,4},{6,7},{7,6},{8,9},{9,8},{10,11... | collective-permute-start | bytes 393224 | tf_op jit(solution)/shard_map/ppermute | solution.py:220
  22.0 3.0 %collective-permute-start.10 = (f32[4,8]{1,0:T(4,128)S(1)}, f32[4,8]{1,0:T(4,128)S(1)}, u32[]{:S(2)}, u32[]{:S(2)}) collective-permute-start(f32[4,8]{1,0:T(4,128)S(1)} %get-tuple-element.36), channel_id=1, source_target_pairs={{0,5},{1,4},{4,1},{5,0},{8,13},{9,12},{12,9},{13,8},{2,7},{3,6},{6... | collective-permute-start | bytes 392 | tf_op jit(solution)/shard_map/ppermute | solution.py:226
  25.0 1.2 %collective-permute-start.11 = (f32[2,2,8]{2,1,0:T(2,128)S(1)}, f32[2,2,8]{2,1,0:T(2,128)S(1)}, u32[]{:S(2)}, u32[]{:S(2)}) collective-permute-start(f32[2,2,8]{2,1,0:T(2,128)S(1)} %pad_maximum_fusion.2), channel_id=1, source_target_pairs={{0,1},{1,0},{2,3},{3,2},{4,5},{5,4},{6,7},{7,6},{8,9},{9,8},{10,11... | collective-permute-start | bytes 392 | tf_op jit(solution)/shard_map/ppermute | solution.py:220

commit v14 on v13

--- a/solution.py
+++ b/solution.py
@@ -91,11 +91,7 @@
     for s, out in enumerate(parcels, 1):
         out[:, :, :size] = tail[...]
         block = project(acts, lax.rem(lax.axis_index("tensor") + s, n), slots, factor)
-        high = block.astype(BF16)
-        low = (block - high.astype(F32)).astype(BF16)
-        lanes = layers * width
-        out[:, :, size : size + lanes] = high.reshape(layers, width, lanes)
-        out[:, :, size + lanes :] = low.reshape(layers, width, lanes)
+        out[:, :, size:] = block.astype(BF16).reshape(layers, width, layers * width)
 
 
 def fold_queries(width, queries, out, rows):
@@ -146,13 +142,11 @@
     for s in range(1, n):
         second, fourth, parcel = (x[s - 1] for x in (seconds, fourths, parcels))
         start = block_of(t, s, n) * depth
-        step, size = second.shape[2], parcel.shape[2] - 2 * lanes
+        step, size = second.shape[2], parcel.shape[2] - lanes
         total = total + product(grads, start + side(1, 1) * step, fourth)
         total = total + product(grads, start + 4 * step, parcel.at[:, :, :size])
         total = total + product(grads, start + swapped(True) * step, second)
-        high, low = parcel[:, :, size : size + lanes], parcel[:, :, size + lanes :]
-        ins = ins + high.reshape(slots, lanes).astype(F32)
-        ins = ins + low.reshape(slots, lanes).astype(F32)
+        ins = ins + parcel[:, :, size:].reshape(slots, lanes).astype(F32)
     total_out[...] = total.T
     live = lax.broadcasted_iota(jnp.int32, ins.shape, 0) < length[0]
     ins_out[...] = jnp.where(live, ins, 0.0).T.astype(BF16)
@@ -265,7 +259,7 @@
     factor_in = proj_in.transpose(0, 2, 1)
     parcels = call(
         functools.partial(project_inputs, n),
-        [jax.ShapeDtypeStruct((layers, width, depth - 4 * step + 2 * lanes), BF16)] * (n - 1),
+        [jax.ShapeDtypeStruct((layers, width, depth - 4 * step + lanes), BF16)] * (n - 1),
         acts,
         factor_in,
         tail,

time: 27 us -> 26.7 us (0.989)
  starting transfers between devices: 14.7 us -> 13.4 us
  waiting for transfers between devices: 6.84 us -> 7.9 us
    ppermute x3, waiting for transfers between devices: 5.3 us -> 6.47 us  [crossed(): lax.ppermute(x, (axis, 'query'), [(i, i ^ bit * cores + 1) for i in range...]
    ppermute x3, starting transfers between devices: 4.75 us -> 3.62 us  [crossed(): lax.ppermute(x, (axis, 'query'), [(i, i ^ bit * cores + 1) for i in range...]
    ppermute x3, waiting for transfers between devices: 0.7 us -> 0.19 us  [shifted(): return lax.ppermute(x, axis, [(i, (i + shift) % n) for i in range(n)])]
where the time goes in v14:
time: 26.7 us; the launch traced here: 26.6 us
  starting transfers between devices  13.4 us (50%)
  waiting for transfers between devices  7.9 us (30%)
  Pallas kernels  3.84 us (14%)
  between operations  0.79 us (3%)
  other arithmetic  0.61 us (2%)
    ppermute x3, waiting for transfers between devices, crossed(): lax.ppermute(x, (axis, 'query'), [(i, i ^ bit * cores + 1) for i in range...  6.47 us
    ppermute x3, starting transfers between devices, shifted(): return lax.ppermute(x, axis, [(i, (i + shift) % n) for i in range(n)])  5.09 us
    pallas_call x8, Pallas kernels, call(): pl.pallas_call(body, out_shape=out_shape, in_specs=specs + [ANY] * len(af...  3.84 us
    ppermute x3, starting transfers between devices, crossed(): lax.ppermute(x, (axis, 'query'), [(i, i ^ bit * cores + 1) for i in range...  3.62 us
    ppermute x2, starting transfers between devices, forwarded(): return lax.ppermute(x, ('parts', 'dp', 'query'), pairs)  3.47 us
    ppermute x4, starting transfers between devices, flipped(): return lax.ppermute(x, axis, [(i, i ^ bit) for i in range(n)])  1.21 us
    ppermute x4, waiting for transfers between devices, flipped(): return lax.ppermute(x, axis, [(i, i ^ bit) for i in range(n)])  1.04 us
    select_n x1, other arithmetic, local(): kept = jnp.where(odd_place == 0, kept, kept[::-1]).reshape(2, -1, n, nq)  0.58 us
  transfers between devices with their start and end apart: 12, of which 6 were waited for; matrix products, arithmetic and copies ran while one was open for 0% of the time, Pallas kernels for 9%

profile of v14, /device:TPU:0, one launch (start us, length us, event | category | flops | bytes accessed | tf_op | source)
XLA Modules:
  0.0 26.6 jit_solution(1768932729780786852)
XLA Ops:
  0.0 1.0 %shard_map.64 = (bf16[2,64,384]{2,1,0:T(8,128)(2,1)S(1)}, bf16[2,64,384]{2,1,0:T(8,128)(2,1)S(1)}, bf16[2,64,512]{2,1,0:T(8,128)(2,1)S(1)}) custom-call(bf16[2,64,2048]{2,1,0:T(8,128)(2,1)} %bitcast.12), custom_call_target="tpu_custom_call" | custom-call | flops 1 | bytes 1 | tf_op jit(solution)/shard_map/pallas_call | solution.py:31
  1.0 0.0 copy-start
  1.0 0.0 copy-start.3
  1.1 3.0 %collective-permute-start = (bf16[2,64,384]{2,1,0:T(8,128)(2,1)S(1)}, bf16[2,64,384]{2,1,0:T(8,128)(2,1)S(1)}, u32[]{:S(2)}, u32[]{:S(2)}) collective-permute-start(bf16[2,64,384]{2,1,0:T(8,128)(2,1)S(1)} %get-tuple-element.21.refs_0_), channel_id=1, source_target_pairs={{0,2},{2,0},{1,3},{3,1},{4,6},{6,4},{5,7},{7,5},{8,10},{10,8},{9,1... | collective-permute-start | bytes 294920 | tf_op jit(solution)/shard_map/ppermute | solution.py:209
  4.1 0.5 %shard_map.66 = bf16[2,64,640]{2,1,0:T(8,128)(2,1)S(1)} custom-call(bf16[2,256,2048]{2,1,0:T(8,128)(2,1)S(1)} %copy-done, bf16[2,64,2048]{2,1,0:T(8,128)(2,1)S(1)} %bitcast.14, bf16[2,64,512]{2,1,0:T(8,128)(2,1)S(1)} %get-tuple-element.22.refs_2_, f32[8,128]{1,0:T(8,128)S(1)} %shard_map.65.refs_3_), custom_call_target="tpu_custom_call" | custom-call | flops 1 | bytes 1 | tf_op jit(solution)/shard_map/pallas_call | solution.py:31
  4.6 1.6 %collective-permute-start.3 = (bf16[2,64,640]{2,1,0:T(8,128)(2,1)S(1)}, bf16[2,64,640]{2,1,0:T(8,128)(2,1)S(1)}, u32[]{:S(2)}, u32[]{:S(2)}) collective-permute-start(bf16[2,64,640]{2,1,0:T(8,128)(2,1)S(1)} %shard_map.66), channel_id=1, source_target_pairs={{0,2},{2,0},{1,3},{3,1},{4,6},{6,4},{5,7},{7,5},{8,10},{10,8},{9,1... | collective-permute-start | bytes 491528 | tf_op jit(solution)/shard_map/ppermute | solution.py:209
  6.2 0.5 %collective-permute-start.2 = (bf16[2,64,384]{2,1,0:T(8,128)(2,1)S(1)}, bf16[2,64,384]{2,1,0:T(8,128)(2,1)S(1)}, u32[]{:S(2)}, u32[]{:S(2)}) collective-permute-start(bf16[2,64,384]{2,1,0:T(8,128)(2,1)S(1)} %get-tuple-element.28), channel_id=1, source_target_pairs={{0,2},{2,0},{1,3},{3,1},{4,6},{6,4},{5,7},{7,5},{8,10},{10,8},{9,1... | collective-permute-start | bytes 294920 | tf_op jit(solution)/shard_map/ppermute | solution.py:209
  6.7 0.2 collective-permute-done.refs_4_
  6.9 2.0 %collective-permute-start.1 = (bf16[2,64,384]{2,1,0:T(8,128)(2,1)S(1)}, bf16[2,64,384]{2,1,0:T(8,128)(2,1)S(1)}, u32[]{:S(2)}, u32[]{:S(2)}) collective-permute-start(bf16[2,64,384]{2,1,0:T(8,128)(2,1)S(1)} %collective-permute-done.refs_4_), channel_id=1, source_target_pairs={{0,4},{1,17},{4,0},{5,21},{8,12},{9,25},{12,8},{13,29},{16,20},{17... | collective-permute-start | bytes 294920 | tf_op jit(solution)/shard_map/ppermute | solution.py:227
  8.8 1.5 %collective-permute-start.4 = (bf16[2,64,384]{2,1,0:T(8,128)(2,1)S(1)}, bf16[2,64,384]{2,1,0:T(8,128)(2,1)S(1)}, u32[]{:S(2)}, u32[]{:S(2)}) collective-permute-start(bf16[2,64,384]{2,1,0:T(8,128)(2,1)S(1)} %collective-permute-done.refs_4_), channel_id=1, source_target_pairs={{0,16},{1,5},{4,20},{5,1},{8,24},{9,13},{12,28},{13,9},{16,0},{17,... | collective-permute-start | bytes 294920 | tf_op jit(solution)/shard_map/ppermute | solution.py:227
  10.3 0.8 %shard_map.67 = (f32[128,128]{1,0:T(8,128)S(1)}, f32[128,128]{1,0:T(8,128)S(1)}, bf16[1,2,384,128]{3,2,1,0:T(8,128)(2,1)S(1)}) custom-call(bf16[2,128,4096]{2,1,0:T(8,128)(2,1)S(1)} %copy-done.1, bf16[2,64,2048]{2,1,0:T(8,128)(2,1)S(1)} %bitcast.13, bf16[2,256,2048]{2,1,0:T(8,128)(2,1)S(1)} %copy-done, bf16[2,64,2048]{2,1,0:T(8,128)(2,1)S(1)} %bitcast.15, ...), custom_call_target="tpu_custom_call" | custom-call | flops 1 | bytes 1 | tf_op jit(solution)/shard_map/pallas_call | solution.py:31
  11.2 0.3 %shard_map.70.refs_1_ = bf16[512,128]{1,0:T(8,128)(2,1)S(1)} custom-call(bf16[2,8,4096]{2,1,0:T(8,128)(2,1)S(1)} %copy-done.4), custom_call_target="tpu_custom_call" | custom-call | flops 1 | bytes 1 | tf_op jit(solution)/shard_map/pallas_call | solution.py:31
  11.5 0.5 %collective-permute-start.6 = (bf16[512,128]{1,0:T(8,128)(2,1)S(1)}, bf16[512,128]{1,0:T(8,128)(2,1)S(1)}, u32[]{:S(2)}, u32[]{:S(2)}) collective-permute-start(bf16[512,128]{1,0:T(8,128)(2,1)S(1)} %shard_map.70.refs_1_), channel_id=1, source_target_pairs={{0,4},{4,0},{8,12},{12,8},{1,5},{5,1},{9,13},{13,9},{2,6},{6,2},{1... | collective-permute-start | bytes 393224 | tf_op jit(solution)/shard_map/ppermute | solution.py:214
  12.7 0.0 collective-permute-done.2.refs_5_
  12.7 0.0 collective-permute-done.1.refs_4_
  12.7 0.5 %shard_map.68 = (f32[128,128]{1,0:T(8,128)S(1)}, bf16[128,128]{1,0:T(8,128)(2,1)S(1)}) custom-call(s32[1]{0:T(128)S(6)} %copy.7.refs_0_, bf16[2,128,4096]{2,1,0:T(8,128)(2,1)S(1)} %copy-done.1, f32[128,128]{1,0:T(8,128)S(1)} %get-tuple-element.26.refs_2_, f32[128,128]{1,0:T(8,128)S(1)} %get-tuple-element.27.refs_3_, ...), custom_call_target="tpu_custom_call" | custom-call | flops 1 | bytes 1 | tf_op jit(solution)/shard_map/pallas_call | solution.py:31
  13.2 0.2 collective-permute-done.4.refs_3_
  13.4 0.3 %shard_map.69 = bf16[16,512]{1,0:T(8,128)(2,1)S(1)} custom-call(bf16[1,2,384,128]{3,2,1,0:T(8,128)(2,1)S(1)} %get-tuple-element.24.refs_0_, f32[128,128]{1,0:T(8,128)S(1)} %get-tuple-element.29.refs_1_, bf16[128,128]{1,0:T(8,128)(2,1)S(1)} %get-tuple-element.30.refs_2_, bf16[2,64,384]{2,1,0:T(8,128)(2,1)S(1)} %collective-permute-done.4.refs_3_), custom_call_target="tpu_custom_call" | custom-call | flops 1 | bytes 1 | tf_op jit(solution)/shard_map/pallas_call | solution.py:31
  13.8 1.2 %collective-permute-start.5 = (bf16[1,16,512]{2,1,0:T(8,128)(2,1)S(1)}, bf16[1,16,512]{2,1,0:T(8,128)(2,1)S(1)}, u32[]{:S(2)}, u32[]{:S(2)}) collective-permute-start(bf16[1,16,512]{2,1,0:T(8,128)(2,1)S(1)} %bitcast.16), channel_id=1, source_target_pairs={{0,9},{1,8},{4,13},{5,12},{8,1},{9,0},{12,5},{13,4},{2,11},{3,10},... | collective-permute-start | bytes 49160 | tf_op jit(solution)/shard_map/ppermute | solution.py:220
  14.9 3.0 %collective-permute-done.5 = bf16[1,16,512]{2,1,0:T(8,128)(2,1)S(1)} collective-permute-done((bf16[1,16,512]{2,1,0:T(8,128)(2,1)S(1)}, bf16[1,16,512]{2,1,0:T(8,128)(2,1)S(1)}, u32[]{:S(2)}, u32[]{:S(2)}) %collective-permute-start.5) | collective-permute-done | bytes 16416 | tf_op jit(solution)/shard_map/ppermute | solution.py:220
  17.9 0.0 collective-permute-done.6.refs_3_
  17.9 1.3 %collective-permute-start.7 = (bf16[2,16,512]{2,1,0:T(8,128)(2,1)S(1)}, bf16[2,16,512]{2,1,0:T(8,128)(2,1)S(1)}, u32[]{:S(2)}, u32[]{:S(2)}) collective-permute-start(bf16[2,16,512]{2,1,0:T(8,128)(2,1)S(1)} %pad_maximum_fusion.1), channel_id=1, source_target_pairs={{0,3},{1,2},{2,1},{3,0},{4,7},{5,6},{6,5},{7,4},{8,11},{9,10},{10,... | collective-permute-start | bytes 98312 | tf_op jit(solution)/shard_map/ppermute | solution.py:220
  19.2 0.4 %collective-permute-start.8 = (bf16[512,128]{1,0:T(8,128)(2,1)S(1)}, bf16[512,128]{1,0:T(8,128)(2,1)S(1)}, u32[]{:S(2)}, u32[]{:S(2)}) collective-permute-start(bf16[512,128]{1,0:T(8,128)(2,1)S(1)} %shard_map.70.refs_1_), channel_id=1, source_target_pairs={{0,1},{1,0},{2,3},{3,2},{4,5},{5,4},{6,7},{7,6},{8,9},{9,8},{10,11... | collective-permute-start | bytes 393224 | tf_op jit(solution)/shard_map/ppermute | solution.py:214
  19.6 0.1 collective-permute-start.9
  19.7 1.7 %collective-permute-done.7 = bf16[2,16,512]{2,1,0:T(8,128)(2,1)S(1)} collective-permute-done((bf16[2,16,512]{2,1,0:T(8,128)(2,1)S(1)}, bf16[2,16,512]{2,1,0:T(8,128)(2,1)S(1)}, u32[]{:S(2)}, u32[]{:S(2)}) %collective-permute-start.7) | collective-permute-done | bytes 32800 | tf_op jit(solution)/shard_map/ppermute | solution.py:220
  21.4 0.0 collective-permute-done.8.refs_2_
  21.4 0.3 %shard_map.71 = (f32[4,8]{1,0:T(4,128)S(1)}, f32[4,8]{1,0:T(4,128)S(1)}, s32[2,2,8]{2,1,0:T(2,128)S(1)}) custom-call(bf16[4,16,512]{2,1,0:T(8,128)(2,1)S(1)} %pad_maximum_fusion.refs_0_, bf16[512,128]{1,0:T(8,128)(2,1)S(1)} %shard_map.70.refs_1_, bf16[512,128]{1,0:T(8,128)(2,1)S(1)} %collective-permute-done.8.refs_2_, ...), custom_call_target="tpu_custom_call" | custom-call | flops 1 | bytes 1 | tf_op jit(solution)/shard_map/pallas_call | solution.py:31
  21.7 1.2 %collective-permute-start.10 = (f32[4,8]{1,0:T(4,128)S(1)}, f32[4,8]{1,0:T(4,128)S(1)}, u32[]{:S(2)}, u32[]{:S(2)}) collective-permute-start(f32[4,8]{1,0:T(4,128)S(1)} %get-tuple-element.36), channel_id=1, source_target_pairs={{0,5},{1,4},{4,1},{5,0},{8,13},{9,12},{12,9},{13,8},{2,7},{3,6},{6... | collective-permute-start | bytes 392 | tf_op jit(solution)/shard_map/ppermute | solution.py:220
  22.9 1.8 %collective-permute-done.10 = f32[4,8]{1,0:T(4,128)S(1)} collective-permute-done((f32[4,8]{1,0:T(4,128)S(1)}, f32[4,8]{1,0:T(4,128)S(1)}, u32[]{:S(2)}, u32[]{:S(2)}) %collective-permute-start.10) | collective-permute-done | bytes 160 | tf_op jit(solution)/shard_map/ppermute | solution.py:220
  24.8 0.2 collective-permute-start.11
  24.9 1.0 %collective-permute-done.11 = f32[2,2,8]{2,1,0:T(2,128)S(1)} collective-permute-done((f32[2,2,8]{2,1,0:T(2,128)S(1)}, f32[2,2,8]{2,1,0:T(2,128)S(1)}, u32[]{:S(2)}, u32[]{:S(2)}) %collective-permute-start.11) | collective-permute-done | bytes 160 | tf_op jit(solution)/shard_map/ppermute | solution.py:214
  26.0 0.6 %compare_select_fusion = f32[2,2,8]{2,1,0:T(2,128)} fusion(f32[2,2,8]{2,1,0:T(2,128)S(1)} %maximum_add_fusion, s32[2,2,8]{2,1,0:T(2,128)S(1)} %get-tuple-element.34), kind=kLoop, calls=%fused_computation.2 | loop fusion | flops 64 | bytes 384 | tf_op jit(solution)/shard_map/jit(_where)/select_n | solution.py:335
  (17 shorter events, 0.1 us)
Async XLA Ops:
  1.0 3.0 %copy-start = (bf16[2,256,2048]{2,1,0:T(8,128)(2,1)S(1)}, bf16[2,256,2048]{2,1,0:T(8,128)(2,1)}, u32[]{:S(2)}) copy-start(bf16[2,256,2048]{2,1,0:T(8,128)(2,1)} %refs_2_.3) | copy-start | bytes 6291460
  1.0 3.0 %copy-start.3 = (bf16[2,2048,64]{1,2,0:T(8,128)(2,1)S(1)}, bf16[2,2048,64]{1,2,0:T(8,128)(2,1)}, u32[]{:S(2)}) copy-start(bf16[2,2048,64]{1,2,0:T(8,128)(2,1)} %param.9) | copy-start | bytes 1572868
  1.1 5.8 %collective-permute-start = (bf16[2,64,384]{2,1,0:T(8,128)(2,1)S(1)}, bf16[2,64,384]{2,1,0:T(8,128)(2,1)S(1)}, u32[]{:S(2)}, u32[]{:S(2)}) collective-permute-start(bf16[2,64,384]{2,1,0:T(8,128)(2,1)S(1)} %get-tuple-element.21.refs_0_), channel_id=1, source_target_pairs={{0,2},{2,0},{1,3},{3,1},{4,6},{6,4},{5,7},{7,5},{8,10},{10,8},{9,1... | collective-permute-start | bytes 294920 | tf_op jit(solution)/shard_map/ppermute | solution.py:209
  4.1 6.3 %copy-start.1 = (bf16[2,128,4096]{2,1,0:T(8,128)(2,1)S(1)}, bf16[2,128,4096]{2,1,0:T(8,128)(2,1)}, u32[]{:S(2)}) copy-start(bf16[2,128,4096]{2,1,0:T(8,128)(2,1)} %refs_1_.3) | copy-start | bytes 6291460
  4.1 6.3 %copy-start.2 = (bf16[2,2048,64]{1,2,0:T(8,128)(2,1)S(1)}, bf16[2,2048,64]{1,2,0:T(8,128)(2,1)}, u32[]{:S(2)}) copy-start(bf16[2,2048,64]{1,2,0:T(8,128)(2,1)} %param.10) | copy-start | bytes 1572868
  4.6 8.1 %collective-permute-start.3 = (bf16[2,64,640]{2,1,0:T(8,128)(2,1)S(1)}, bf16[2,64,640]{2,1,0:T(8,128)(2,1)S(1)}, u32[]{:S(2)}, u32[]{:S(2)}) collective-permute-start(bf16[2,64,640]{2,1,0:T(8,128)(2,1)S(1)} %shard_map.66), channel_id=1, source_target_pairs={{0,2},{2,0},{1,3},{3,1},{4,6},{6,4},{5,7},{7,5},{8,10},{10,8},{9,1... | collective-permute-start | bytes 491528 | tf_op jit(solution)/shard_map/ppermute | solution.py:209
  6.2 5.0 %copy-start.4 = (bf16[2,8,4096]{2,1,0:T(8,128)(2,1)S(1)}, bf16[2,8,4096]{2,1,0:T(8,128)(2,1)}, u32[]{:S(2)}) copy-start(bf16[2,8,4096]{2,1,0:T(8,128)(2,1)} %refs_0_.5) | copy-start | bytes 393220
  6.2 6.5 %collective-permute-start.2 = (bf16[2,64,384]{2,1,0:T(8,128)(2,1)S(1)}, bf16[2,64,384]{2,1,0:T(8,128)(2,1)S(1)}, u32[]{:S(2)}, u32[]{:S(2)}) collective-permute-start(bf16[2,64,384]{2,1,0:T(8,128)(2,1)S(1)} %get-tuple-element.28), channel_id=1, source_target_pairs={{0,2},{2,0},{1,3},{3,1},{4,6},{6,4},{5,7},{7,5},{8,10},{10,8},{9,1... | collective-permute-start | bytes 294920 | tf_op jit(solution)/shard_map/ppermute | solution.py:209
  6.9 5.9 %collective-permute-start.1 = (bf16[2,64,384]{2,1,0:T(8,128)(2,1)S(1)}, bf16[2,64,384]{2,1,0:T(8,128)(2,1)S(1)}, u32[]{:S(2)}, u32[]{:S(2)}) collective-permute-start(bf16[2,64,384]{2,1,0:T(8,128)(2,1)S(1)} %collective-permute-done.refs_4_), channel_id=1, source_target_pairs={{0,4},{1,17},{4,0},{5,21},{8,12},{9,25},{12,8},{13,29},{16,20},{17... | collective-permute-start | bytes 294920 | tf_op jit(solution)/shard_map/ppermute | solution.py:227
  8.8 4.6 %collective-permute-start.4 = (bf16[2,64,384]{2,1,0:T(8,128)(2,1)S(1)}, bf16[2,64,384]{2,1,0:T(8,128)(2,1)S(1)}, u32[]{:S(2)}, u32[]{:S(2)}) collective-permute-start(bf16[2,64,384]{2,1,0:T(8,128)(2,1)S(1)} %collective-permute-done.refs_4_), channel_id=1, source_target_pairs={{0,16},{1,5},{4,20},{5,1},{8,24},{9,13},{12,28},{13,9},{16,0},{17,... | collective-permute-start | bytes 294920 | tf_op jit(solution)/shard_map/ppermute | solution.py:227
  11.5 6.4 %collective-permute-start.6 = (bf16[512,128]{1,0:T(8,128)(2,1)S(1)}, bf16[512,128]{1,0:T(8,128)(2,1)S(1)}, u32[]{:S(2)}, u32[]{:S(2)}) collective-permute-start(bf16[512,128]{1,0:T(8,128)(2,1)S(1)} %shard_map.70.refs_1_), channel_id=1, source_target_pairs={{0,4},{4,0},{8,12},{12,8},{1,5},{5,1},{9,13},{13,9},{2,6},{6,2},{1... | collective-permute-start | bytes 393224 | tf_op jit(solution)/shard_map/ppermute | solution.py:214
  13.8 4.1 %collective-permute-start.5 = (bf16[1,16,512]{2,1,0:T(8,128)(2,1)S(1)}, bf16[1,16,512]{2,1,0:T(8,128)(2,1)S(1)}, u32[]{:S(2)}, u32[]{:S(2)}) collective-permute-start(bf16[1,16,512]{2,1,0:T(8,128)(2,1)S(1)} %bitcast.16), channel_id=1, source_target_pairs={{0,9},{1,8},{4,13},{5,12},{8,1},{9,0},{12,5},{13,4},{2,11},{3,10},... | collective-permute-start | bytes 49160 | tf_op jit(solution)/shard_map/ppermute | solution.py:220
  17.9 3.5 %collective-permute-start.7 = (bf16[2,16,512]{2,1,0:T(8,128)(2,1)S(1)}, bf16[2,16,512]{2,1,0:T(8,128)(2,1)S(1)}, u32[]{:S(2)}, u32[]{:S(2)}) collective-permute-start(bf16[2,16,512]{2,1,0:T(8,128)(2,1)S(1)} %pad_maximum_fusion.1), channel_id=1, source_target_pairs={{0,3},{1,2},{2,1},{3,0},{4,7},{5,6},{6,5},{7,4},{8,11},{9,10},{10,... | collective-permute-start | bytes 98312 | tf_op jit(solution)/shard_map/ppermute | solution.py:220
  19.2 2.2 %collective-permute-start.8 = (bf16[512,128]{1,0:T(8,128)(2,1)S(1)}, bf16[512,128]{1,0:T(8,128)(2,1)S(1)}, u32[]{:S(2)}, u32[]{:S(2)}) collective-permute-start(bf16[512,128]{1,0:T(8,128)(2,1)S(1)} %shard_map.70.refs_1_), channel_id=1, source_target_pairs={{0,1},{1,0},{2,3},{3,2},{4,5},{5,4},{6,7},{7,6},{8,9},{9,8},{10,11... | collective-permute-start | bytes 393224 | tf_op jit(solution)/shard_map/ppermute | solution.py:214
  19.6 1.8 %collective-permute-start.9 = (bf16[512,128]{1,0:T(8,128)(2,1)S(1)}, bf16[512,128]{1,0:T(8,128)(2,1)S(1)}, u32[]{:S(2)}, u32[]{:S(2)}) collective-permute-start(bf16[512,128]{1,0:T(8,128)(2,1)S(1)} %collective-permute-done.6.refs_3_), channel_id=1, source_target_pairs={{0,1},{1,0},{2,3},{3,2},{4,5},{5,4},{6,7},{7,6},{8,9},{9,8},{10,11... | collective-permute-start | bytes 393224 | tf_op jit(solution)/shard_map/ppermute | solution.py:214
  21.7 3.0 %collective-permute-start.10 = (f32[4,8]{1,0:T(4,128)S(1)}, f32[4,8]{1,0:T(4,128)S(1)}, u32[]{:S(2)}, u32[]{:S(2)}) collective-permute-start(f32[4,8]{1,0:T(4,128)S(1)} %get-tuple-element.36), channel_id=1, source_target_pairs={{0,5},{1,4},{4,1},{5,0},{8,13},{9,12},{12,9},{13,8},{2,7},{3,6},{6... | collective-permute-start | bytes 392 | tf_op jit(solution)/shard_map/ppermute | solution.py:220
  24.8 1.2 %collective-permute-start.11 = (f32[2,2,8]{2,1,0:T(2,128)S(1)}, f32[2,2,8]{2,1,0:T(2,128)S(1)}, u32[]{:S(2)}, u32[]{:S(2)}) collective-permute-start(f32[2,2,8]{2,1,0:T(2,128)S(1)} %pad_maximum_fusion.2), channel_id=1, source_target_pairs={{0,1},{1,0},{2,3},{3,2},{4,5},{5,4},{6,7},{7,6},{8,9},{9,8},{10,11... | collective-permute-start | bytes 392 | tf_op jit(solution)/shard_map/ppermute | solution.py:214

commit v15 on v14

--- a/solution.py
+++ b/solution.py
@@ -71,7 +71,10 @@
     copies = []
     for i, (out, start) in enumerate(((piece, side() * step), (other, side(1, 1) * step), (tail, 4 * step))):
         columns = pl.ds(pl.multiple_of(start, 128), out.shape[2])
-        copies.append(pltpu.make_async_copy(factor.at[:, :, columns], out, sems.at[i]))
+        for l in range(out.shape[0]):
+            copies.append(
+                pltpu.make_async_copy(factor.at[l, :, columns], out.at[l], sems.at[i, l])
+            )
     for copy in copies:
         copy.start()
     for copy in copies:
@@ -246,7 +249,7 @@
         ),
         in_hbm(factor),
         specs=[ANY],
-        scratch=[pltpu.SemaphoreType.DMA((3,))],
+        scratch=[pltpu.SemaphoreType.DMA((3, layers))],
     )
     firsts = [shifted(piece, "tensor", s) for s in range(1, n)]
     fourths = [shifted(other, "tensor", s) for s in range(1, n)]

time: 26.7 us -> 26.7 us (level)
  no operation moved by 1% of the time
where the time goes in v15:
time: 26.7 us; the launch traced here: 26.6 us
  starting transfers between devices  13.4 us (50%)
  waiting for transfers between devices  7.92 us (30%)
  Pallas kernels  3.84 us (14%)
  between operations  0.79 us (3%)
  other arithmetic  0.61 us (2%)
    ppermute x3, waiting for transfers between devices, crossed(): lax.ppermute(x, (axis, 'query'), [(i, i ^ bit * cores + 1) for i in range...  6.49 us
    ppermute x3, starting transfers between devices, shifted(): return lax.ppermute(x, axis, [(i, (i + shift) % n) for i in range(n)])  5.09 us
    pallas_call x8, Pallas kernels, call(): pl.pallas_call(body, out_shape=out_shape, in_specs=specs + [ANY] * len(af...  3.84 us
    ppermute x3, starting transfers between devices, crossed(): lax.ppermute(x, (axis, 'query'), [(i, i ^ bit * cores + 1) for i in range...  3.6 us
    ppermute x2, starting transfers between devices, forwarded(): return lax.ppermute(x, ('parts', 'dp', 'query'), pairs)  3.47 us
    ppermute x4, starting transfers between devices, flipped(): return lax.ppermute(x, axis, [(i, i ^ bit) for i in range(n)])  1.2 us
    ppermute x4, waiting for transfers between devices, flipped(): return lax.ppermute(x, axis, [(i, i ^ bit) for i in range(n)])  1.04 us
    select_n x1, other arithmetic, local(): kept = jnp.where(odd_place == 0, kept, kept[::-1]).reshape(2, -1, n, nq)  0.58 us
  transfers between devices with their start and end apart: 12, of which 6 were waited for; matrix products, arithmetic and copies ran while one was open for 0% of the time, Pallas kernels for 9%

profile of v15, /device:TPU:0, one launch (start us, length us, event | category | flops | bytes accessed | tf_op | source)
XLA Modules:
  0.0 26.6 jit_solution(6008194198205530176)
XLA Ops:
  0.0 1.0 %shard_map.64 = (bf16[2,64,384]{2,1,0:T(8,128)(2,1)S(1)}, bf16[2,64,384]{2,1,0:T(8,128)(2,1)S(1)}, bf16[2,64,512]{2,1,0:T(8,128)(2,1)S(1)}) custom-call(bf16[2,64,2048]{2,1,0:T(8,128)(2,1)} %bitcast.12), custom_call_target="tpu_custom_call" | custom-call | flops 1 | bytes 1 | tf_op jit(solution)/shard_map/pallas_call | solution.py:31
  1.0 0.0 copy-start
  1.0 0.0 copy-start.3
  1.1 3.0 %collective-permute-start = (bf16[2,64,384]{2,1,0:T(8,128)(2,1)S(1)}, bf16[2,64,384]{2,1,0:T(8,128)(2,1)S(1)}, u32[]{:S(2)}, u32[]{:S(2)}) collective-permute-start(bf16[2,64,384]{2,1,0:T(8,128)(2,1)S(1)} %get-tuple-element.21.refs_0_), channel_id=1, source_target_pairs={{0,2},{2,0},{1,3},{3,1},{4,6},{6,4},{5,7},{7,5},{8,10},{10,8},{9,1... | collective-permute-start | bytes 294920 | tf_op jit(solution)/shard_map/ppermute | solution.py:212
  4.1 0.5 %shard_map.66 = bf16[2,64,640]{2,1,0:T(8,128)(2,1)S(1)} custom-call(bf16[2,256,2048]{2,1,0:T(8,128)(2,1)S(1)} %copy-done, bf16[2,64,2048]{2,1,0:T(8,128)(2,1)S(1)} %bitcast.14, bf16[2,64,512]{2,1,0:T(8,128)(2,1)S(1)} %get-tuple-element.22.refs_2_, f32[8,128]{1,0:T(8,128)S(1)} %shard_map.65.refs_3_), custom_call_target="tpu_custom_call" | custom-call | flops 1 | bytes 1 | tf_op jit(solution)/shard_map/pallas_call | solution.py:31
  4.6 1.6 %collective-permute-start.3 = (bf16[2,64,640]{2,1,0:T(8,128)(2,1)S(1)}, bf16[2,64,640]{2,1,0:T(8,128)(2,1)S(1)}, u32[]{:S(2)}, u32[]{:S(2)}) collective-permute-start(bf16[2,64,640]{2,1,0:T(8,128)(2,1)S(1)} %shard_map.66), channel_id=1, source_target_pairs={{0,2},{2,0},{1,3},{3,1},{4,6},{6,4},{5,7},{7,5},{8,10},{10,8},{9,1... | collective-permute-start | bytes 491528 | tf_op jit(solution)/shard_map/ppermute | solution.py:212
  6.2 0.5 %collective-permute-start.2 = (bf16[2,64,384]{2,1,0:T(8,128)(2,1)S(1)}, bf16[2,64,384]{2,1,0:T(8,128)(2,1)S(1)}, u32[]{:S(2)}, u32[]{:S(2)}) collective-permute-start(bf16[2,64,384]{2,1,0:T(8,128)(2,1)S(1)} %get-tuple-element.28), channel_id=1, source_target_pairs={{0,2},{2,0},{1,3},{3,1},{4,6},{6,4},{5,7},{7,5},{8,10},{10,8},{9,1... | collective-permute-start | bytes 294920 | tf_op jit(solution)/shard_map/ppermute | solution.py:212
  6.7 0.2 collective-permute-done.refs_4_
  6.9 2.0 %collective-permute-start.1 = (bf16[2,64,384]{2,1,0:T(8,128)(2,1)S(1)}, bf16[2,64,384]{2,1,0:T(8,128)(2,1)S(1)}, u32[]{:S(2)}, u32[]{:S(2)}) collective-permute-start(bf16[2,64,384]{2,1,0:T(8,128)(2,1)S(1)} %collective-permute-done.refs_4_), channel_id=1, source_target_pairs={{0,4},{1,17},{4,0},{5,21},{8,12},{9,25},{12,8},{13,29},{16,20},{17... | collective-permute-start | bytes 294920 | tf_op jit(solution)/shard_map/ppermute | solution.py:230
  8.8 1.5 %collective-permute-start.4 = (bf16[2,64,384]{2,1,0:T(8,128)(2,1)S(1)}, bf16[2,64,384]{2,1,0:T(8,128)(2,1)S(1)}, u32[]{:S(2)}, u32[]{:S(2)}) collective-permute-start(bf16[2,64,384]{2,1,0:T(8,128)(2,1)S(1)} %collective-permute-done.refs_4_), channel_id=1, source_target_pairs={{0,16},{1,5},{4,20},{5,1},{8,24},{9,13},{12,28},{13,9},{16,0},{17,... | collective-permute-start | bytes 294920 | tf_op jit(solution)/shard_map/ppermute | solution.py:230
  10.3 0.8 %shard_map.67 = (f32[128,128]{1,0:T(8,128)S(1)}, f32[128,128]{1,0:T(8,128)S(1)}, bf16[1,2,384,128]{3,2,1,0:T(8,128)(2,1)S(1)}) custom-call(bf16[2,128,4096]{2,1,0:T(8,128)(2,1)S(1)} %copy-done.1, bf16[2,64,2048]{2,1,0:T(8,128)(2,1)S(1)} %bitcast.13, bf16[2,256,2048]{2,1,0:T(8,128)(2,1)S(1)} %copy-done, bf16[2,64,2048]{2,1,0:T(8,128)(2,1)S(1)} %bitcast.15, ...), custom_call_target="tpu_custom_call" | custom-call | flops 1 | bytes 1 | tf_op jit(solution)/shard_map/pallas_call | solution.py:31
  11.2 0.3 %shard_map.70.refs_1_ = bf16[512,128]{1,0:T(8,128)(2,1)S(1)} custom-call(bf16[2,8,4096]{2,1,0:T(8,128)(2,1)S(1)} %copy-done.4), custom_call_target="tpu_custom_call" | custom-call | flops 1 | bytes 1 | tf_op jit(solution)/shard_map/pallas_call | solution.py:31
  11.5 0.5 %collective-permute-start.6 = (bf16[512,128]{1,0:T(8,128)(2,1)S(1)}, bf16[512,128]{1,0:T(8,128)(2,1)S(1)}, u32[]{:S(2)}, u32[]{:S(2)}) collective-permute-start(bf16[512,128]{1,0:T(8,128)(2,1)S(1)} %shard_map.70.refs_1_), channel_id=1, source_target_pairs={{0,4},{4,0},{8,12},{12,8},{1,5},{5,1},{9,13},{13,9},{2,6},{6,2},{1... | collective-permute-start | bytes 393224 | tf_op jit(solution)/shard_map/ppermute | solution.py:217
  12.7 0.0 collective-permute-done.3.refs_6_
  12.7 0.0 collective-permute-done.1.refs_4_
  12.7 0.5 %shard_map.68 = (f32[128,128]{1,0:T(8,128)S(1)}, bf16[128,128]{1,0:T(8,128)(2,1)S(1)}) custom-call(s32[1]{0:T(128)S(6)} %copy.7.refs_0_, bf16[2,128,4096]{2,1,0:T(8,128)(2,1)S(1)} %copy-done.1, f32[128,128]{1,0:T(8,128)S(1)} %get-tuple-element.26.refs_2_, f32[128,128]{1,0:T(8,128)S(1)} %get-tuple-element.27.refs_3_, ...), custom_call_target="tpu_custom_call" | custom-call | flops 1 | bytes 1 | tf_op jit(solution)/shard_map/pallas_call | solution.py:31
  13.2 0.2 collective-permute-done.4.refs_3_
  13.4 0.3 %shard_map.69 = bf16[16,512]{1,0:T(8,128)(2,1)S(1)} custom-call(bf16[1,2,384,128]{3,2,1,0:T(8,128)(2,1)S(1)} %get-tuple-element.24.refs_0_, f32[128,128]{1,0:T(8,128)S(1)} %get-tuple-element.29.refs_1_, bf16[128,128]{1,0:T(8,128)(2,1)S(1)} %get-tuple-element.30.refs_2_, bf16[2,64,384]{2,1,0:T(8,128)(2,1)S(1)} %collective-permute-done.4.refs_3_), custom_call_target="tpu_custom_call" | custom-call | flops 1 | bytes 1 | tf_op jit(solution)/shard_map/pallas_call | solution.py:31
  13.8 1.1 %collective-permute-start.5 = (bf16[1,16,512]{2,1,0:T(8,128)(2,1)S(1)}, bf16[1,16,512]{2,1,0:T(8,128)(2,1)S(1)}, u32[]{:S(2)}, u32[]{:S(2)}) collective-permute-start(bf16[1,16,512]{2,1,0:T(8,128)(2,1)S(1)} %bitcast.16), channel_id=1, source_target_pairs={{0,9},{1,8},{4,13},{5,12},{8,1},{9,0},{12,5},{13,4},{2,11},{3,10},... | collective-permute-start | bytes 49160 | tf_op jit(solution)/shard_map/ppermute | solution.py:223
  14.9 3.0 %collective-permute-done.5 = bf16[1,16,512]{2,1,0:T(8,128)(2,1)S(1)} collective-permute-done((bf16[1,16,512]{2,1,0:T(8,128)(2,1)S(1)}, bf16[1,16,512]{2,1,0:T(8,128)(2,1)S(1)}, u32[]{:S(2)}, u32[]{:S(2)}) %collective-permute-start.5) | collective-permute-done | bytes 16416 | tf_op jit(solution)/shard_map/ppermute | solution.py:223
  17.9 0.0 collective-permute-done.6.refs_3_
  17.9 1.3 %collective-permute-start.7 = (bf16[2,16,512]{2,1,0:T(8,128)(2,1)S(1)}, bf16[2,16,512]{2,1,0:T(8,128)(2,1)S(1)}, u32[]{:S(2)}, u32[]{:S(2)}) collective-permute-start(bf16[2,16,512]{2,1,0:T(8,128)(2,1)S(1)} %pad_maximum_fusion.1), channel_id=1, source_target_pairs={{0,3},{1,2},{2,1},{3,0},{4,7},{5,6},{6,5},{7,4},{8,11},{9,10},{10,... | collective-permute-start | bytes 98312 | tf_op jit(solution)/shard_map/ppermute | solution.py:223
  19.2 0.4 %collective-permute-start.8 = (bf16[512,128]{1,0:T(8,128)(2,1)S(1)}, bf16[512,128]{1,0:T(8,128)(2,1)S(1)}, u32[]{:S(2)}, u32[]{:S(2)}) collective-permute-start(bf16[512,128]{1,0:T(8,128)(2,1)S(1)} %shard_map.70.refs_1_), channel_id=1, source_target_pairs={{0,1},{1,0},{2,3},{3,2},{4,5},{5,4},{6,7},{7,6},{8,9},{9,8},{10,11... | collective-permute-start | bytes 393224 | tf_op jit(solution)/shard_map/ppermute | solution.py:217
  19.6 0.1 collective-permute-start.9
  19.7 1.7 %collective-permute-done.7 = bf16[2,16,512]{2,1,0:T(8,128)(2,1)S(1)} collective-permute-done((bf16[2,16,512]{2,1,0:T(8,128)(2,1)S(1)}, bf16[2,16,512]{2,1,0:T(8,128)(2,1)S(1)}, u32[]{:S(2)}, u32[]{:S(2)}) %collective-permute-start.7) | collective-permute-done | bytes 32800 | tf_op jit(solution)/shard_map/ppermute | solution.py:223
  21.4 0.0 collective-permute-done.8.refs_2_
  21.4 0.3 %shard_map.71 = (f32[4,8]{1,0:T(4,128)S(1)}, f32[4,8]{1,0:T(4,128)S(1)}, s32[2,2,8]{2,1,0:T(2,128)S(1)}) custom-call(bf16[4,16,512]{2,1,0:T(8,128)(2,1)S(1)} %pad_maximum_fusion.refs_0_, bf16[512,128]{1,0:T(8,128)(2,1)S(1)} %shard_map.70.refs_1_, bf16[512,128]{1,0:T(8,128)(2,1)S(1)} %collective-permute-done.8.refs_2_, ...), custom_call_target="tpu_custom_call" | custom-call | flops 1 | bytes 1 | tf_op jit(solution)/shard_map/pallas_call | solution.py:31
  21.7 1.2 %collective-permute-start.10 = (f32[4,8]{1,0:T(4,128)S(1)}, f32[4,8]{1,0:T(4,128)S(1)}, u32[]{:S(2)}, u32[]{:S(2)}) collective-permute-start(f32[4,8]{1,0:T(4,128)S(1)} %get-tuple-element.36), channel_id=1, source_target_pairs={{0,5},{1,4},{4,1},{5,0},{8,13},{9,12},{12,9},{13,8},{2,7},{3,6},{6... | collective-permute-start | bytes 392 | tf_op jit(solution)/shard_map/ppermute | solution.py:223
  22.9 1.8 %collective-permute-done.10 = f32[4,8]{1,0:T(4,128)S(1)} collective-permute-done((f32[4,8]{1,0:T(4,128)S(1)}, f32[4,8]{1,0:T(4,128)S(1)}, u32[]{:S(2)}, u32[]{:S(2)}) %collective-permute-start.10) | collective-permute-done | bytes 160 | tf_op jit(solution)/shard_map/ppermute | solution.py:223
  24.8 0.2 collective-permute-start.11
  24.9 1.0 %collective-permute-done.11 = f32[2,2,8]{2,1,0:T(2,128)S(1)} collective-permute-done((f32[2,2,8]{2,1,0:T(2,128)S(1)}, f32[2,2,8]{2,1,0:T(2,128)S(1)}, u32[]{:S(2)}, u32[]{:S(2)}) %collective-permute-start.11) | collective-permute-done | bytes 160 | tf_op jit(solution)/shard_map/ppermute | solution.py:217
  26.0 0.6 %compare_select_fusion = f32[2,2,8]{2,1,0:T(2,128)} fusion(f32[2,2,8]{2,1,0:T(2,128)S(1)} %maximum_add_fusion, s32[2,2,8]{2,1,0:T(2,128)S(1)} %get-tuple-element.34), kind=kLoop, calls=%fused_computation.2 | loop fusion | flops 64 | bytes 384 | tf_op jit(solution)/shard_map/jit(_where)/select_n | solution.py:338
  (17 shorter events, 0.1 us)
Async XLA Ops:
  1.0 3.0 %copy-start = (bf16[2,256,2048]{2,1,0:T(8,128)(2,1)S(1)}, bf16[2,256,2048]{2,1,0:T(8,128)(2,1)}, u32[]{:S(2)}) copy-start(bf16[2,256,2048]{2,1,0:T(8,128)(2,1)} %refs_2_.3) | copy-start | bytes 6291460
  1.0 3.0 %copy-start.3 = (bf16[2,2048,64]{1,2,0:T(8,128)(2,1)S(1)}, bf16[2,2048,64]{1,2,0:T(8,128)(2,1)}, u32[]{:S(2)}) copy-start(bf16[2,2048,64]{1,2,0:T(8,128)(2,1)} %param.9) | copy-start | bytes 1572868
  1.1 5.8 %collective-permute-start = (bf16[2,64,384]{2,1,0:T(8,128)(2,1)S(1)}, bf16[2,64,384]{2,1,0:T(8,128)(2,1)S(1)}, u32[]{:S(2)}, u32[]{:S(2)}) collective-permute-start(bf16[2,64,384]{2,1,0:T(8,128)(2,1)S(1)} %get-tuple-element.21.refs_0_), channel_id=1, source_target_pairs={{0,2},{2,0},{1,3},{3,1},{4,6},{6,4},{5,7},{7,5},{8,10},{10,8},{9,1... | collective-permute-start | bytes 294920 | tf_op jit(solution)/shard_map/ppermute | solution.py:212
  4.1 6.3 %copy-start.1 = (bf16[2,128,4096]{2,1,0:T(8,128)(2,1)S(1)}, bf16[2,128,4096]{2,1,0:T(8,128)(2,1)}, u32[]{:S(2)}) copy-start(bf16[2,128,4096]{2,1,0:T(8,128)(2,1)} %refs_1_.3) | copy-start | bytes 6291460
  4.1 6.3 %copy-start.2 = (bf16[2,2048,64]{1,2,0:T(8,128)(2,1)S(1)}, bf16[2,2048,64]{1,2,0:T(8,128)(2,1)}, u32[]{:S(2)}) copy-start(bf16[2,2048,64]{1,2,0:T(8,128)(2,1)} %param.10) | copy-start | bytes 1572868
  4.6 8.1 %collective-permute-start.3 = (bf16[2,64,640]{2,1,0:T(8,128)(2,1)S(1)}, bf16[2,64,640]{2,1,0:T(8,128)(2,1)S(1)}, u32[]{:S(2)}, u32[]{:S(2)}) collective-permute-start(bf16[2,64,640]{2,1,0:T(8,128)(2,1)S(1)} %shard_map.66), channel_id=1, source_target_pairs={{0,2},{2,0},{1,3},{3,1},{4,6},{6,4},{5,7},{7,5},{8,10},{10,8},{9,1... | collective-permute-start | bytes 491528 | tf_op jit(solution)/shard_map/ppermute | solution.py:212
  6.2 5.0 %copy-start.4 = (bf16[2,8,4096]{2,1,0:T(8,128)(2,1)S(1)}, bf16[2,8,4096]{2,1,0:T(8,128)(2,1)}, u32[]{:S(2)}) copy-start(bf16[2,8,4096]{2,1,0:T(8,128)(2,1)} %refs_0_.5) | copy-start | bytes 393220
  6.2 6.5 %collective-permute-start.2 = (bf16[2,64,384]{2,1,0:T(8,128)(2,1)S(1)}, bf16[2,64,384]{2,1,0:T(8,128)(2,1)S(1)}, u32[]{:S(2)}, u32[]{:S(2)}) collective-permute-start(bf16[2,64,384]{2,1,0:T(8,128)(2,1)S(1)} %get-tuple-element.28), channel_id=1, source_target_pairs={{0,2},{2,0},{1,3},{3,1},{4,6},{6,4},{5,7},{7,5},{8,10},{10,8},{9,1... | collective-permute-start | bytes 294920 | tf_op jit(solution)/shard_map/ppermute | solution.py:212
  6.9 5.9 %collective-permute-start.1 = (bf16[2,64,384]{2,1,0:T(8,128)(2,1)S(1)}, bf16[2,64,384]{2,1,0:T(8,128)(2,1)S(1)}, u32[]{:S(2)}, u32[]{:S(2)}) collective-permute-start(bf16[2,64,384]{2,1,0:T(8,128)(2,1)S(1)} %collective-permute-done.refs_4_), channel_id=1, source_target_pairs={{0,4},{1,17},{4,0},{5,21},{8,12},{9,25},{12,8},{13,29},{16,20},{17... | collective-permute-start | bytes 294920 | tf_op jit(solution)/shard_map/ppermute | solution.py:230
  8.8 4.6 %collective-permute-start.4 = (bf16[2,64,384]{2,1,0:T(8,128)(2,1)S(1)}, bf16[2,64,384]{2,1,0:T(8,128)(2,1)S(1)}, u32[]{:S(2)}, u32[]{:S(2)}) collective-permute-start(bf16[2,64,384]{2,1,0:T(8,128)(2,1)S(1)} %collective-permute-done.refs_4_), channel_id=1, source_target_pairs={{0,16},{1,5},{4,20},{5,1},{8,24},{9,13},{12,28},{13,9},{16,0},{17,... | collective-permute-start | bytes 294920 | tf_op jit(solution)/shard_map/ppermute | solution.py:230
  11.5 6.3 %collective-permute-start.6 = (bf16[512,128]{1,0:T(8,128)(2,1)S(1)}, bf16[512,128]{1,0:T(8,128)(2,1)S(1)}, u32[]{:S(2)}, u32[]{:S(2)}) collective-permute-start(bf16[512,128]{1,0:T(8,128)(2,1)S(1)} %shard_map.70.refs_1_), channel_id=1, source_target_pairs={{0,4},{4,0},{8,12},{12,8},{1,5},{5,1},{9,13},{13,9},{2,6},{6,2},{1... | collective-permute-start | bytes 393224 | tf_op jit(solution)/shard_map/ppermute | solution.py:217
  13.8 4.1 %collective-permute-start.5 = (bf16[1,16,512]{2,1,0:T(8,128)(2,1)S(1)}, bf16[1,16,512]{2,1,0:T(8,128)(2,1)S(1)}, u32[]{:S(2)}, u32[]{:S(2)}) collective-permute-start(bf16[1,16,512]{2,1,0:T(8,128)(2,1)S(1)} %bitcast.16), channel_id=1, source_target_pairs={{0,9},{1,8},{4,13},{5,12},{8,1},{9,0},{12,5},{13,4},{2,11},{3,10},... | collective-permute-start | bytes 49160 | tf_op jit(solution)/shard_map/ppermute | solution.py:223
  17.9 3.5 %collective-permute-start.7 = (bf16[2,16,512]{2,1,0:T(8,128)(2,1)S(1)}, bf16[2,16,512]{2,1,0:T(8,128)(2,1)S(1)}, u32[]{:S(2)}, u32[]{:S(2)}) collective-permute-start(bf16[2,16,512]{2,1,0:T(8,128)(2,1)S(1)} %pad_maximum_fusion.1), channel_id=1, source_target_pairs={{0,3},{1,2},{2,1},{3,0},{4,7},{5,6},{6,5},{7,4},{8,11},{9,10},{10,... | collective-permute-start | bytes 98312 | tf_op jit(solution)/shard_map/ppermute | solution.py:223
  19.2 2.2 %collective-permute-start.8 = (bf16[512,128]{1,0:T(8,128)(2,1)S(1)}, bf16[512,128]{1,0:T(8,128)(2,1)S(1)}, u32[]{:S(2)}, u32[]{:S(2)}) collective-permute-start(bf16[512,128]{1,0:T(8,128)(2,1)S(1)} %shard_map.70.refs_1_), channel_id=1, source_target_pairs={{0,1},{1,0},{2,3},{3,2},{4,5},{5,4},{6,7},{7,6},{8,9},{9,8},{10,11... | collective-permute-start | bytes 393224 | tf_op jit(solution)/shard_map/ppermute | solution.py:217
  19.6 1.8 %collective-permute-start.9 = (bf16[512,128]{1,0:T(8,128)(2,1)S(1)}, bf16[512,128]{1,0:T(8,128)(2,1)S(1)}, u32[]{:S(2)}, u32[]{:S(2)}) collective-permute-start(bf16[512,128]{1,0:T(8,128)(2,1)S(1)} %collective-permute-done.6.refs_3_), channel_id=1, source_target_pairs={{0,1},{1,0},{2,3},{3,2},{4,5},{5,4},{6,7},{7,6},{8,9},{9,8},{10,11... | collective-permute-start | bytes 393224 | tf_op jit(solution)/shard_map/ppermute | solution.py:217
  21.7 3.0 %collective-permute-start.10 = (f32[4,8]{1,0:T(4,128)S(1)}, f32[4,8]{1,0:T(4,128)S(1)}, u32[]{:S(2)}, u32[]{:S(2)}) collective-permute-start(f32[4,8]{1,0:T(4,128)S(1)} %get-tuple-element.36), channel_id=1, source_target_pairs={{0,5},{1,4},{4,1},{5,0},{8,13},{9,12},{12,9},{13,8},{2,7},{3,6},{6... | collective-permute-start | bytes 392 | tf_op jit(solution)/shard_map/ppermute | solution.py:223
  24.8 1.2 %collective-permute-start.11 = (f32[2,2,8]{2,1,0:T(2,128)S(1)}, f32[2,2,8]{2,1,0:T(2,128)S(1)}, u32[]{:S(2)}, u32[]{:S(2)}) collective-permute-start(f32[2,2,8]{2,1,0:T(2,128)S(1)} %pad_maximum_fusion.2), channel_id=1, source_target_pairs={{0,1},{1,0},{2,3},{3,2},{4,5},{5,4},{6,7},{7,6},{8,9},{9,8},{10,11... | collective-permute-start | bytes 392 | tf_op jit(solution)/shard_map/ppermute | solution.py:217

commit v16 on v14

--- a/solution.py
+++ b/solution.py
@@ -85,13 +85,17 @@
     )
 
 
-def project_inputs(n, acts, factor, tail, *parcels):
+def project_inputs(n, acts, factor, tail, mine, *parcels):
     layers, width, size = tail.shape
     slots = acts.shape[1] // n
     for s, out in enumerate(parcels, 1):
         out[:, :, :size] = tail[...]
         block = project(acts, lax.rem(lax.axis_index("tensor") + s, n), slots, factor)
         out[:, :, size:] = block.astype(BF16).reshape(layers, width, layers * width)
+
+    @pl.when(lax.axis_index("query") == 1)
+    def _():
+        mine[...] = project(acts, lax.axis_index("tensor"), slots, factor)
 
 
 def fold_queries(width, queries, out, rows):
@@ -114,7 +118,7 @@
     )
 
 
-def early(n, grads, factor, acts, factor_in, *rest):
+def early(n, grads, factor, acts, factor_in, mine, *rest):
     pieces, out, inputs, turned = rest[:-3], *rest[-3:]
     depth = factor.shape[2]
     t = lax.axis_index("tensor")
@@ -123,7 +127,16 @@
         start = block_of(t, s, n) * depth + side() * piece.shape[2]
         total = total + product(grads, start, piece)
     out[...] = total
-    inputs[...] = project(acts, t, inputs.shape[0], factor_in)
+    core = lax.axis_index("query")
+
+    @pl.when(core != 1)
+    def _():
+        inputs[...] = project(acts, t, inputs.shape[0], factor_in)
+
+    @pl.when(core == 1)
+    def _():
+        inputs[...] = mine[...]
+
     step = turned.shape[2]
     for s in range(1, n):
         start = block_of(t, s, n) * depth + swapped(False) * step
@@ -257,9 +270,12 @@
     firsts = [shifted(piece, "tensor", s) for s in range(1, n)]
 
     factor_in = proj_in.transpose(0, 2, 1)
-    parcels = call(
+    mine, *parcels = call(
         functools.partial(project_inputs, n),
-        [jax.ShapeDtypeStruct((layers, width, depth - 4 * step + lanes), BF16)] * (n - 1),
+        [
+            jax.ShapeDtypeStruct((slots, lanes), F32),
+            *[jax.ShapeDtypeStruct((layers, width, depth - 4 * step + lanes), BF16)] * (n - 1),
+        ],
         acts,
         factor_in,
         tail,
@@ -279,6 +295,7 @@
         factor,
         acts,
         factor_in,
+        mine,
         *firsts,
     )
     asked, outputs = lax.optimization_barrier((query_grads, outputs))

time: 26.7 us -> 26.7 us (level)
  waiting for transfers between devices: 7.9 us -> 6.03 us
  starting transfers between devices: 13.4 us -> 15 us
  Pallas kernels: 3.84 us -> 4.12 us
    ppermute x3, waiting for transfers between devices: 6.47 us -> 4.96 us  [crossed(): lax.ppermute(x, (axis, 'query'), [(i, i ^ bit * cores + 1) for i in range...]
    ppermute x3, starting transfers between devices: 3.62 us -> 5.08 us  [crossed(): lax.ppermute(x, (axis, 'query'), [(i, i ^ bit * cores + 1) for i in range...]
    pallas_call x8, Pallas kernels: 3.84 us -> 4.12 us  [call(): pl.pallas_call(body, out_shape=out_shape, in_specs=specs + [ANY] * len(af...]
  transfers between devices with their start and end apart: 12 -> 12, of which waited for: 6 -> 5; matrix products, arithmetic and copies ran while one was open for 0% -> 0% of each run, Pallas kernels for 9% -> 10%
where the time goes in v16:
time: 26.7 us; the launch traced here: 26.6 us
  starting transfers between devices  15 us (56%)
  waiting for transfers between devices  6.03 us (23%)
  Pallas kernels  4.12 us (15%)
  between operations  0.79 us (3%)
  other arithmetic  0.61 us (2%)
    ppermute x3, starting transfers between devices, shifted(): return lax.ppermute(x, axis, [(i, (i + shift) % n) for i in range(n)])  5.09 us
    ppermute x3, starting transfers between devices, crossed(): lax.ppermute(x, (axis, 'query'), [(i, i ^ bit * cores + 1) for i in range...  5.08 us
    ppermute x3, waiting for transfers between devices, crossed(): lax.ppermute(x, (axis, 'query'), [(i, i ^ bit * cores + 1) for i in range...  4.96 us
    pallas_call x8, Pallas kernels, call(): pl.pallas_call(body, out_shape=out_shape, in_specs=specs + [ANY] * len(af...  4.12 us
    ppermute x2, starting transfers between devices, forwarded(): return lax.ppermute(x, ('parts', 'dp', 'query'), pairs)  3.43 us
    ppermute x4, starting transfers between devices, flipped(): return lax.ppermute(x, axis, [(i, i ^ bit) for i in range(n)])  1.39 us
    ppermute x4, waiting for transfers between devices, flipped(): return lax.ppermute(x, axis, [(i, i ^ bit) for i in range(n)])  0.86 us
    select_n x1, other arithmetic, local(): kept = jnp.where(odd_place == 0, kept, kept[::-1]).reshape(2, -1, n, nq)  0.58 us
  transfers between devices with their start and end apart: 12, of which 5 were waited for; matrix products, arithmetic and copies ran while one was open for 0% of the time, Pallas kernels for 10%

profile of v16, /device:TPU:0, one launch (start us, length us, event | category | flops | bytes accessed | tf_op | source)
XLA Modules:
  0.0 26.6 jit_solution(7165228431514502774)
XLA Ops:
  0.0 1.0 %shard_map.64 = (bf16[2,64,384]{2,1,0:T(8,128)(2,1)S(1)}, bf16[2,64,384]{2,1,0:T(8,128)(2,1)S(1)}, bf16[2,64,512]{2,1,0:T(8,128)(2,1)S(1)}) custom-call(bf16[2,64,2048]{2,1,0:T(8,128)(2,1)} %bitcast.12), custom_call_target="tpu_custom_call" | custom-call | flops 1 | bytes 1 | tf_op jit(solution)/shard_map/pallas_call | solution.py:31
  1.0 0.0 copy-start
  1.0 0.0 copy-start.3
  1.1 3.0 %collective-permute-start = (bf16[2,64,384]{2,1,0:T(8,128)(2,1)S(1)}, bf16[2,64,384]{2,1,0:T(8,128)(2,1)S(1)}, u32[]{:S(2)}, u32[]{:S(2)}) collective-permute-start(bf16[2,64,384]{2,1,0:T(8,128)(2,1)S(1)} %get-tuple-element.24.refs_0_), channel_id=1, source_target_pairs={{0,2},{2,0},{1,3},{3,1},{4,6},{6,4},{5,7},{7,5},{8,10},{10,8},{9,1... | collective-permute-start | bytes 294920 | tf_op jit(solution)/shard_map/ppermute | solution.py:222
  4.1 0.5 %shard_map.66 = (f32[128,128]{1,0:T(8,128)S(1)}, bf16[2,64,640]{2,1,0:T(8,128)(2,1)S(1)}) custom-call(bf16[2,256,2048]{2,1,0:T(8,128)(2,1)S(1)} %copy-done, bf16[2,64,2048]{2,1,0:T(8,128)(2,1)S(1)} %bitcast.14, bf16[2,64,512]{2,1,0:T(8,128)(2,1)S(1)} %get-tuple-element.23.refs_2_, f32[8,128]{1,0:T(8,128)S(1)} %shard_map.65.refs_3_), custom_call_target="tpu_custom_call" | custom-call | flops 1 | bytes 1 | tf_op jit(solution)/shard_map/pallas_call | solution.py:31
  4.6 1.6 %collective-permute-start.3 = (bf16[2,64,640]{2,1,0:T(8,128)(2,1)S(1)}, bf16[2,64,640]{2,1,0:T(8,128)(2,1)S(1)}, u32[]{:S(2)}, u32[]{:S(2)}) collective-permute-start(bf16[2,64,640]{2,1,0:T(8,128)(2,1)S(1)} %get-tuple-element.26), channel_id=1, source_target_pairs={{0,2},{2,0},{1,3},{3,1},{4,6},{6,4},{5,7},{7,5},{8,10},{10,8},{9,1... | collective-permute-start | bytes 491528 | tf_op jit(solution)/shard_map/ppermute | solution.py:222
  6.2 0.4 %collective-permute-start.2 = (bf16[2,64,384]{2,1,0:T(8,128)(2,1)S(1)}, bf16[2,64,384]{2,1,0:T(8,128)(2,1)S(1)}, u32[]{:S(2)}, u32[]{:S(2)}) collective-permute-start(bf16[2,64,384]{2,1,0:T(8,128)(2,1)S(1)} %get-tuple-element.32), channel_id=1, source_target_pairs={{0,2},{2,0},{1,3},{3,1},{4,6},{6,4},{5,7},{7,5},{8,10},{10,8},{9,1... | collective-permute-start | bytes 294920 | tf_op jit(solution)/shard_map/ppermute | solution.py:222
  6.7 0.2 collective-permute-done.refs_5_
  6.9 1.9 %collective-permute-start.1 = (bf16[2,64,384]{2,1,0:T(8,128)(2,1)S(1)}, bf16[2,64,384]{2,1,0:T(8,128)(2,1)S(1)}, u32[]{:S(2)}, u32[]{:S(2)}) collective-permute-start(bf16[2,64,384]{2,1,0:T(8,128)(2,1)S(1)} %collective-permute-done.refs_5_), channel_id=1, source_target_pairs={{0,4},{1,17},{4,0},{5,21},{8,12},{9,25},{12,8},{13,29},{16,20},{17... | collective-permute-start | bytes 294920 | tf_op jit(solution)/shard_map/ppermute | solution.py:240
  8.8 1.5 %collective-permute-start.4 = (bf16[2,64,384]{2,1,0:T(8,128)(2,1)S(1)}, bf16[2,64,384]{2,1,0:T(8,128)(2,1)S(1)}, u32[]{:S(2)}, u32[]{:S(2)}) collective-permute-start(bf16[2,64,384]{2,1,0:T(8,128)(2,1)S(1)} %collective-permute-done.refs_5_), channel_id=1, source_target_pairs={{0,16},{1,5},{4,20},{5,1},{8,24},{9,13},{12,28},{13,9},{16,0},{17,... | collective-permute-start | bytes 294920 | tf_op jit(solution)/shard_map/ppermute | solution.py:240
  10.3 1.1 %shard_map.67 = (f32[128,128]{1,0:T(8,128)S(1)}, f32[128,128]{1,0:T(8,128)S(1)}, bf16[1,2,384,128]{3,2,1,0:T(8,128)(2,1)S(1)}) custom-call(bf16[2,128,4096]{2,1,0:T(8,128)(2,1)S(1)} %copy-done.1, bf16[2,64,2048]{2,1,0:T(8,128)(2,1)S(1)} %bitcast.13, bf16[2,256,2048]{2,1,0:T(8,128)(2,1)S(1)} %copy-done, bf16[2,64,2048]{2,1,0:T(8,128)(2,1)S(1)} %bitcast.15, ...), custom_call_target="tpu_custom_call" | custom-call | flops 1 | bytes 1 | tf_op jit(solution)/shard_map/pallas_call | solution.py:31
  11.4 0.3 %shard_map.70.refs_1_ = bf16[512,128]{1,0:T(8,128)(2,1)S(1)} custom-call(bf16[2,8,4096]{2,1,0:T(8,128)(2,1)S(1)} %copy-done.4), custom_call_target="tpu_custom_call" | custom-call | flops 1 | bytes 1 | tf_op jit(solution)/shard_map/pallas_call | solution.py:31
  11.8 0.5 %collective-permute-start.6 = (bf16[512,128]{1,0:T(8,128)(2,1)S(1)}, bf16[512,128]{1,0:T(8,128)(2,1)S(1)}, u32[]{:S(2)}, u32[]{:S(2)}) collective-permute-start(bf16[512,128]{1,0:T(8,128)(2,1)S(1)} %shard_map.70.refs_1_), channel_id=1, source_target_pairs={{0,4},{4,0},{8,12},{12,8},{1,5},{5,1},{9,13},{13,9},{2,6},{6,2},{1... | collective-permute-start | bytes 393224 | tf_op jit(solution)/shard_map/ppermute | solution.py:227
  12.9 0.0 collective-permute-done.2.refs_5_
  13.0 0.0 collective-permute-done.1.refs_4_
  13.0 0.5 %shard_map.68 = (f32[128,128]{1,0:T(8,128)S(1)}, bf16[128,128]{1,0:T(8,128)(2,1)S(1)}) custom-call(s32[1]{0:T(128)S(6)} %copy.7.refs_0_, bf16[2,128,4096]{2,1,0:T(8,128)(2,1)S(1)} %copy-done.1, f32[128,128]{1,0:T(8,128)S(1)} %get-tuple-element.30.refs_2_, f32[128,128]{1,0:T(8,128)S(1)} %get-tuple-element.31.refs_3_, ...), custom_call_target="tpu_custom_call" | custom-call | flops 1 | bytes 1 | tf_op jit(solution)/shard_map/pallas_call | solution.py:31
  13.5 0.0 collective-permute-done.4.refs_3_
  13.5 0.3 %shard_map.69 = bf16[16,512]{1,0:T(8,128)(2,1)S(1)} custom-call(bf16[1,2,384,128]{3,2,1,0:T(8,128)(2,1)S(1)} %get-tuple-element.28.refs_0_, f32[128,128]{1,0:T(8,128)S(1)} %get-tuple-element.33.refs_1_, bf16[128,128]{1,0:T(8,128)(2,1)S(1)} %get-tuple-element.34.refs_2_, bf16[2,64,384]{2,1,0:T(8,128)(2,1)S(1)} %collective-permute-done.4.refs_3_), custom_call_target="tpu_custom_call" | custom-call | flops 1 | bytes 1 | tf_op jit(solution)/shard_map/pallas_call | solution.py:31
  13.8 2.0 %collective-permute-start.5 = (bf16[1,16,512]{2,1,0:T(8,128)(2,1)S(1)}, bf16[1,16,512]{2,1,0:T(8,128)(2,1)S(1)}, u32[]{:S(2)}, u32[]{:S(2)}) collective-permute-start(bf16[1,16,512]{2,1,0:T(8,128)(2,1)S(1)} %bitcast.16), channel_id=1, source_target_pairs={{0,9},{1,8},{4,13},{5,12},{8,1},{9,0},{12,5},{13,4},{2,11},{3,10},... | collective-permute-start | bytes 49160 | tf_op jit(solution)/shard_map/ppermute | solution.py:233
  15.8 2.2 %collective-permute-done.5 = bf16[1,16,512]{2,1,0:T(8,128)(2,1)S(1)} collective-permute-done((bf16[1,16,512]{2,1,0:T(8,128)(2,1)S(1)}, bf16[1,16,512]{2,1,0:T(8,128)(2,1)S(1)}, u32[]{:S(2)}, u32[]{:S(2)}) %collective-permute-start.5) | collective-permute-done | bytes 16416 | tf_op jit(solution)/shard_map/ppermute | solution.py:233
  17.9 0.0 collective-permute-done.6.refs_3_
  17.9 1.5 %collective-permute-start.7 = (bf16[2,16,512]{2,1,0:T(8,128)(2,1)S(1)}, bf16[2,16,512]{2,1,0:T(8,128)(2,1)S(1)}, u32[]{:S(2)}, u32[]{:S(2)}) collective-permute-start(bf16[2,16,512]{2,1,0:T(8,128)(2,1)S(1)} %pad_maximum_fusion.1), channel_id=1, source_target_pairs={{0,3},{1,2},{2,1},{3,0},{4,7},{5,6},{6,5},{7,4},{8,11},{9,10},{10,... | collective-permute-start | bytes 98312 | tf_op jit(solution)/shard_map/ppermute | solution.py:233
  19.5 0.4 %collective-permute-start.8 = (bf16[512,128]{1,0:T(8,128)(2,1)S(1)}, bf16[512,128]{1,0:T(8,128)(2,1)S(1)}, u32[]{:S(2)}, u32[]{:S(2)}) collective-permute-start(bf16[512,128]{1,0:T(8,128)(2,1)S(1)} %shard_map.70.refs_1_), channel_id=1, source_target_pairs={{0,1},{1,0},{2,3},{3,2},{4,5},{5,4},{6,7},{7,6},{8,9},{9,8},{10,11... | collective-permute-start | bytes 393224 | tf_op jit(solution)/shard_map/ppermute | solution.py:227
  19.8 0.1 collective-permute-start.9
  20.0 1.4 %collective-permute-done.7 = bf16[2,16,512]{2,1,0:T(8,128)(2,1)S(1)} collective-permute-done((bf16[2,16,512]{2,1,0:T(8,128)(2,1)S(1)}, bf16[2,16,512]{2,1,0:T(8,128)(2,1)S(1)}, u32[]{:S(2)}, u32[]{:S(2)}) %collective-permute-start.7) | collective-permute-done | bytes 32800 | tf_op jit(solution)/shard_map/ppermute | solution.py:233
  21.4 0.0 collective-permute-done.9.refs_4_
  21.4 0.3 %shard_map.71 = (f32[4,8]{1,0:T(4,128)S(1)}, f32[4,8]{1,0:T(4,128)S(1)}, s32[2,2,8]{2,1,0:T(2,128)S(1)}) custom-call(bf16[4,16,512]{2,1,0:T(8,128)(2,1)S(1)} %pad_maximum_fusion.refs_0_, bf16[512,128]{1,0:T(8,128)(2,1)S(1)} %shard_map.70.refs_1_, bf16[512,128]{1,0:T(8,128)(2,1)S(1)} %collective-permute-done.8.refs_2_, ...), custom_call_target="tpu_custom_call" | custom-call | flops 1 | bytes 1 | tf_op jit(solution)/shard_map/pallas_call | solution.py:31
  21.7 1.6 %collective-permute-start.10 = (f32[4,8]{1,0:T(4,128)S(1)}, f32[4,8]{1,0:T(4,128)S(1)}, u32[]{:S(2)}, u32[]{:S(2)}) collective-permute-start(f32[4,8]{1,0:T(4,128)S(1)} %get-tuple-element.40), channel_id=1, source_target_pairs={{0,5},{1,4},{4,1},{5,0},{8,13},{9,12},{12,9},{13,8},{2,7},{3,6},{6... | collective-permute-start | bytes 392 | tf_op jit(solution)/shard_map/ppermute | solution.py:233
  23.3 1.4 %collective-permute-done.10 = f32[4,8]{1,0:T(4,128)S(1)} collective-permute-done((f32[4,8]{1,0:T(4,128)S(1)}, f32[4,8]{1,0:T(4,128)S(1)}, u32[]{:S(2)}, u32[]{:S(2)}) %collective-permute-start.10) | collective-permute-done | bytes 160 | tf_op jit(solution)/shard_map/ppermute | solution.py:233
  24.8 0.4 %collective-permute-start.11 = (f32[2,2,8]{2,1,0:T(2,128)S(1)}, f32[2,2,8]{2,1,0:T(2,128)S(1)}, u32[]{:S(2)}, u32[]{:S(2)}) collective-permute-start(f32[2,2,8]{2,1,0:T(2,128)S(1)} %pad_maximum_fusion.2), channel_id=1, source_target_pairs={{0,1},{1,0},{2,3},{3,2},{4,5},{5,4},{6,7},{7,6},{8,9},{9,8},{10,11... | collective-permute-start | bytes 392 | tf_op jit(solution)/shard_map/ppermute | solution.py:227
  25.1 0.9 %collective-permute-done.11 = f32[2,2,8]{2,1,0:T(2,128)S(1)} collective-permute-done((f32[2,2,8]{2,1,0:T(2,128)S(1)}, f32[2,2,8]{2,1,0:T(2,128)S(1)}, u32[]{:S(2)}, u32[]{:S(2)}) %collective-permute-start.11) | collective-permute-done | bytes 160 | tf_op jit(solution)/shard_map/ppermute | solution.py:227
  26.0 0.6 %compare_select_fusion = f32[2,2,8]{2,1,0:T(2,128)} fusion(f32[2,2,8]{2,1,0:T(2,128)S(1)} %maximum_add_fusion, s32[2,2,8]{2,1,0:T(2,128)S(1)} %get-tuple-element.38), kind=kLoop, calls=%fused_computation.2 | loop fusion | flops 64 | bytes 384 | tf_op jit(solution)/shard_map/jit(_where)/select_n | solution.py:352
  (17 shorter events, 0.1 us)
Async XLA Ops:
  1.0 3.0 %copy-start = (bf16[2,256,2048]{2,1,0:T(8,128)(2,1)S(1)}, bf16[2,256,2048]{2,1,0:T(8,128)(2,1)}, u32[]{:S(2)}) copy-start(bf16[2,256,2048]{2,1,0:T(8,128)(2,1)} %refs_2_.3) | copy-start | bytes 6291460
  1.0 3.0 %copy-start.3 = (bf16[2,2048,64]{1,2,0:T(8,128)(2,1)S(1)}, bf16[2,2048,64]{1,2,0:T(8,128)(2,1)}, u32[]{:S(2)}) copy-start(bf16[2,2048,64]{1,2,0:T(8,128)(2,1)} %param.9) | copy-start | bytes 1572868
  1.1 5.8 %collective-permute-start = (bf16[2,64,384]{2,1,0:T(8,128)(2,1)S(1)}, bf16[2,64,384]{2,1,0:T(8,128)(2,1)S(1)}, u32[]{:S(2)}, u32[]{:S(2)}) collective-permute-start(bf16[2,64,384]{2,1,0:T(8,128)(2,1)S(1)} %get-tuple-element.24.refs_0_), channel_id=1, source_target_pairs={{0,2},{2,0},{1,3},{3,1},{4,6},{6,4},{5,7},{7,5},{8,10},{10,8},{9,1... | collective-permute-start | bytes 294920 | tf_op jit(solution)/shard_map/ppermute | solution.py:222
  4.1 6.2 %copy-start.1 = (bf16[2,128,4096]{2,1,0:T(8,128)(2,1)S(1)}, bf16[2,128,4096]{2,1,0:T(8,128)(2,1)}, u32[]{:S(2)}) copy-start(bf16[2,128,4096]{2,1,0:T(8,128)(2,1)} %refs_1_.3) | copy-start | bytes 6291460
  4.1 6.2 %copy-start.2 = (bf16[2,2048,64]{1,2,0:T(8,128)(2,1)S(1)}, bf16[2,2048,64]{1,2,0:T(8,128)(2,1)}, u32[]{:S(2)}) copy-start(bf16[2,2048,64]{1,2,0:T(8,128)(2,1)} %param.10) | copy-start | bytes 1572868
  4.6 8.4 %collective-permute-start.3 = (bf16[2,64,640]{2,1,0:T(8,128)(2,1)S(1)}, bf16[2,64,640]{2,1,0:T(8,128)(2,1)S(1)}, u32[]{:S(2)}, u32[]{:S(2)}) collective-permute-start(bf16[2,64,640]{2,1,0:T(8,128)(2,1)S(1)} %get-tuple-element.26), channel_id=1, source_target_pairs={{0,2},{2,0},{1,3},{3,1},{4,6},{6,4},{5,7},{7,5},{8,10},{10,8},{9,1... | collective-permute-start | bytes 491528 | tf_op jit(solution)/shard_map/ppermute | solution.py:222
  6.2 6.7 %collective-permute-start.2 = (bf16[2,64,384]{2,1,0:T(8,128)(2,1)S(1)}, bf16[2,64,384]{2,1,0:T(8,128)(2,1)S(1)}, u32[]{:S(2)}, u32[]{:S(2)}) collective-permute-start(bf16[2,64,384]{2,1,0:T(8,128)(2,1)S(1)} %get-tuple-element.32), channel_id=1, source_target_pairs={{0,2},{2,0},{1,3},{3,1},{4,6},{6,4},{5,7},{7,5},{8,10},{10,8},{9,1... | collective-permute-start | bytes 294920 | tf_op jit(solution)/shard_map/ppermute | solution.py:222
  6.9 6.1 %collective-permute-start.1 = (bf16[2,64,384]{2,1,0:T(8,128)(2,1)S(1)}, bf16[2,64,384]{2,1,0:T(8,128)(2,1)S(1)}, u32[]{:S(2)}, u32[]{:S(2)}) collective-permute-start(bf16[2,64,384]{2,1,0:T(8,128)(2,1)S(1)} %collective-permute-done.refs_5_), channel_id=1, source_target_pairs={{0,4},{1,17},{4,0},{5,21},{8,12},{9,25},{12,8},{13,29},{16,20},{17... | collective-permute-start | bytes 294920 | tf_op jit(solution)/shard_map/ppermute | solution.py:240
  8.8 4.7 %collective-permute-start.4 = (bf16[2,64,384]{2,1,0:T(8,128)(2,1)S(1)}, bf16[2,64,384]{2,1,0:T(8,128)(2,1)S(1)}, u32[]{:S(2)}, u32[]{:S(2)}) collective-permute-start(bf16[2,64,384]{2,1,0:T(8,128)(2,1)S(1)} %collective-permute-done.refs_5_), channel_id=1, source_target_pairs={{0,16},{1,5},{4,20},{5,1},{8,24},{9,13},{12,28},{13,9},{16,0},{17,... | collective-permute-start | bytes 294920 | tf_op jit(solution)/shard_map/ppermute | solution.py:240
  10.3 1.1 %copy-start.4 = (bf16[2,8,4096]{2,1,0:T(8,128)(2,1)S(1)}, bf16[2,8,4096]{2,1,0:T(8,128)(2,1)}, u32[]{:S(2)}) copy-start(bf16[2,8,4096]{2,1,0:T(8,128)(2,1)} %refs_0_.5) | copy-start | bytes 393220
  11.8 6.2 %collective-permute-start.6 = (bf16[512,128]{1,0:T(8,128)(2,1)S(1)}, bf16[512,128]{1,0:T(8,128)(2,1)S(1)}, u32[]{:S(2)}, u32[]{:S(2)}) collective-permute-start(bf16[512,128]{1,0:T(8,128)(2,1)S(1)} %shard_map.70.refs_1_), channel_id=1, source_target_pairs={{0,4},{4,0},{8,12},{12,8},{1,5},{5,1},{9,13},{13,9},{2,6},{6,2},{1... | collective-permute-start | bytes 393224 | tf_op jit(solution)/shard_map/ppermute | solution.py:227
  13.8 4.1 %collective-permute-start.5 = (bf16[1,16,512]{2,1,0:T(8,128)(2,1)S(1)}, bf16[1,16,512]{2,1,0:T(8,128)(2,1)S(1)}, u32[]{:S(2)}, u32[]{:S(2)}) collective-permute-start(bf16[1,16,512]{2,1,0:T(8,128)(2,1)S(1)} %bitcast.16), channel_id=1, source_target_pairs={{0,9},{1,8},{4,13},{5,12},{8,1},{9,0},{12,5},{13,4},{2,11},{3,10},... | collective-permute-start | bytes 49160 | tf_op jit(solution)/shard_map/ppermute | solution.py:233
  17.9 3.4 %collective-permute-start.7 = (bf16[2,16,512]{2,1,0:T(8,128)(2,1)S(1)}, bf16[2,16,512]{2,1,0:T(8,128)(2,1)S(1)}, u32[]{:S(2)}, u32[]{:S(2)}) collective-permute-start(bf16[2,16,512]{2,1,0:T(8,128)(2,1)S(1)} %pad_maximum_fusion.1), channel_id=1, source_target_pairs={{0,3},{1,2},{2,1},{3,0},{4,7},{5,6},{6,5},{7,4},{8,11},{9,10},{10,... | collective-permute-start | bytes 98312 | tf_op jit(solution)/shard_map/ppermute | solution.py:233
  19.5 1.9 %collective-permute-start.8 = (bf16[512,128]{1,0:T(8,128)(2,1)S(1)}, bf16[512,128]{1,0:T(8,128)(2,1)S(1)}, u32[]{:S(2)}, u32[]{:S(2)}) collective-permute-start(bf16[512,128]{1,0:T(8,128)(2,1)S(1)} %shard_map.70.refs_1_), channel_id=1, source_target_pairs={{0,1},{1,0},{2,3},{3,2},{4,5},{5,4},{6,7},{7,6},{8,9},{9,8},{10,11... | collective-permute-start | bytes 393224 | tf_op jit(solution)/shard_map/ppermute | solution.py:227
  19.8 1.5 %collective-permute-start.9 = (bf16[512,128]{1,0:T(8,128)(2,1)S(1)}, bf16[512,128]{1,0:T(8,128)(2,1)S(1)}, u32[]{:S(2)}, u32[]{:S(2)}) collective-permute-start(bf16[512,128]{1,0:T(8,128)(2,1)S(1)} %collective-permute-done.6.refs_3_), channel_id=1, source_target_pairs={{0,1},{1,0},{2,3},{3,2},{4,5},{5,4},{6,7},{7,6},{8,9},{9,8},{10,11... | collective-permute-start | bytes 393224 | tf_op jit(solution)/shard_map/ppermute | solution.py:227
  21.7 3.0 %collective-permute-start.10 = (f32[4,8]{1,0:T(4,128)S(1)}, f32[4,8]{1,0:T(4,128)S(1)}, u32[]{:S(2)}, u32[]{:S(2)}) collective-permute-start(f32[4,8]{1,0:T(4,128)S(1)} %get-tuple-element.40), channel_id=1, source_target_pairs={{0,5},{1,4},{4,1},{5,0},{8,13},{9,12},{12,9},{13,8},{2,7},{3,6},{6... | collective-permute-start | bytes 392 | tf_op jit(solution)/shard_map/ppermute | solution.py:233
  24.8 1.2 %collective-permute-start.11 = (f32[2,2,8]{2,1,0:T(2,128)S(1)}, f32[2,2,8]{2,1,0:T(2,128)S(1)}, u32[]{:S(2)}, u32[]{:S(2)}) collective-permute-start(f32[2,2,8]{2,1,0:T(2,128)S(1)} %pad_maximum_fusion.2), channel_id=1, source_target_pairs={{0,1},{1,0},{2,3},{3,2},{4,5},{5,4},{6,7},{7,6},{8,9},{9,8},{10,11... | collective-permute-start | bytes 392 | tf_op jit(solution)/shard_map/ppermute | solution.py:227

commit v17 on v14

--- a/solution.py
+++ b/solution.py
@@ -265,7 +265,6 @@
         tail,
         after=(token,),
     )
-    firsts, _ = lax.optimization_barrier((firsts, parcels))
     parcels = [shifted(parcel, "tensor", s) for s, parcel in enumerate(parcels, 1)]
     seconds = [forwarded(first, True) for first in firsts]
     thirds = [forwarded(first, False) for first in firsts]

time: 26.7 us -> 26.7 us (level)
  no operation moved by 1% of the time
where the time goes in v17:
time: 26.7 us; the launch traced here: 26.6 us
  starting transfers between devices  13.4 us (50%)
  waiting for transfers between devices  7.9 us (30%)
  Pallas kernels  3.84 us (14%)
  between operations  0.79 us (3%)
  other arithmetic  0.61 us (2%)
    ppermute x3, waiting for transfers between devices, crossed(): lax.ppermute(x, (axis, 'query'), [(i, i ^ bit * cores + 1) for i in range...  6.47 us
    ppermute x3, starting transfers between devices, shifted(): return lax.ppermute(x, axis, [(i, (i + shift) % n) for i in range(n)])  5.09 us
    pallas_call x8, Pallas kernels, call(): pl.pallas_call(body, out_shape=out_shape, in_specs=specs + [ANY] * len(af...  3.84 us
    ppermute x3, starting transfers between devices, crossed(): lax.ppermute(x, (axis, 'query'), [(i, i ^ bit * cores + 1) for i in range...  3.62 us
    ppermute x2, starting transfers between devices, forwarded(): return lax.ppermute(x, ('parts', 'dp', 'query'), pairs)  3.47 us
    ppermute x4, starting transfers between devices, flipped(): return lax.ppermute(x, axis, [(i, i ^ bit) for i in range(n)])  1.21 us
    ppermute x4, waiting for transfers between devices, flipped(): return lax.ppermute(x, axis, [(i, i ^ bit) for i in range(n)])  1.04 us
    select_n x1, other arithmetic, local(): kept = jnp.where(odd_place == 0, kept, kept[::-1]).reshape(2, -1, n, nq)  0.58 us
  transfers between devices with their start and end apart: 12, of which 6 were waited for; matrix products, arithmetic and copies ran while one was open for 0% of the time, Pallas kernels for 9%

profile of v17, /device:TPU:0, one launch (start us, length us, event | category | flops | bytes accessed | tf_op | source)
XLA Modules:
  0.0 26.6 jit_solution(1768932729780786852)
XLA Ops:
  0.0 1.0 %shard_map.64 = (bf16[2,64,384]{2,1,0:T(8,128)(2,1)S(1)}, bf16[2,64,384]{2,1,0:T(8,128)(2,1)S(1)}, bf16[2,64,512]{2,1,0:T(8,128)(2,1)S(1)}) custom-call(bf16[2,64,2048]{2,1,0:T(8,128)(2,1)} %bitcast.12), custom_call_target="tpu_custom_call" | custom-call | flops 1 | bytes 1 | tf_op jit(solution)/shard_map/pallas_call | solution.py:31
  1.0 0.0 copy-start
  1.0 0.0 copy-start.3
  1.1 3.0 %collective-permute-start = (bf16[2,64,384]{2,1,0:T(8,128)(2,1)S(1)}, bf16[2,64,384]{2,1,0:T(8,128)(2,1)S(1)}, u32[]{:S(2)}, u32[]{:S(2)}) collective-permute-start(bf16[2,64,384]{2,1,0:T(8,128)(2,1)S(1)} %get-tuple-element.20.refs_0_), channel_id=1, source_target_pairs={{0,2},{2,0},{1,3},{3,1},{4,6},{6,4},{5,7},{7,5},{8,10},{10,8},{9,1... | collective-permute-start | bytes 294920 | tf_op jit(solution)/shard_map/ppermute | solution.py:209
  4.1 0.5 %shard_map.67 = bf16[2,64,640]{2,1,0:T(8,128)(2,1)S(1)} custom-call(bf16[2,256,2048]{2,1,0:T(8,128)(2,1)S(1)} %copy-done, bf16[2,64,2048]{2,1,0:T(8,128)(2,1)S(1)} %bitcast.14, bf16[2,64,512]{2,1,0:T(8,128)(2,1)S(1)} %get-tuple-element.26.refs_2_, f32[8,128]{1,0:T(8,128)S(1)} %shard_map.66.refs_3_), custom_call_target="tpu_custom_call" | custom-call | flops 1 | bytes 1 | tf_op jit(solution)/shard_map/pallas_call | solution.py:31
  4.6 1.6 %collective-permute-start.3 = (bf16[2,64,640]{2,1,0:T(8,128)(2,1)S(1)}, bf16[2,64,640]{2,1,0:T(8,128)(2,1)S(1)}, u32[]{:S(2)}, u32[]{:S(2)}) collective-permute-start(bf16[2,64,640]{2,1,0:T(8,128)(2,1)S(1)} %shard_map.67), channel_id=1, source_target_pairs={{0,2},{2,0},{1,3},{3,1},{4,6},{6,4},{5,7},{7,5},{8,10},{10,8},{9,1... | collective-permute-start | bytes 491528 | tf_op jit(solution)/shard_map/ppermute | solution.py:209
  6.2 0.5 %collective-permute-start.2 = (bf16[2,64,384]{2,1,0:T(8,128)(2,1)S(1)}, bf16[2,64,384]{2,1,0:T(8,128)(2,1)S(1)}, u32[]{:S(2)}, u32[]{:S(2)}) collective-permute-start(bf16[2,64,384]{2,1,0:T(8,128)(2,1)S(1)} %get-tuple-element.25), channel_id=1, source_target_pairs={{0,2},{2,0},{1,3},{3,1},{4,6},{6,4},{5,7},{7,5},{8,10},{10,8},{9,1... | collective-permute-start | bytes 294920 | tf_op jit(solution)/shard_map/ppermute | solution.py:209
  6.7 0.2 collective-permute-done.refs_4_
  6.9 2.0 %collective-permute-start.1 = (bf16[2,64,384]{2,1,0:T(8,128)(2,1)S(1)}, bf16[2,64,384]{2,1,0:T(8,128)(2,1)S(1)}, u32[]{:S(2)}, u32[]{:S(2)}) collective-permute-start(bf16[2,64,384]{2,1,0:T(8,128)(2,1)S(1)} %collective-permute-done.refs_4_), channel_id=1, source_target_pairs={{0,4},{1,17},{4,0},{5,21},{8,12},{9,25},{12,8},{13,29},{16,20},{17... | collective-permute-start | bytes 294920 | tf_op jit(solution)/shard_map/ppermute | solution.py:227
  8.8 1.5 %collective-permute-start.4 = (bf16[2,64,384]{2,1,0:T(8,128)(2,1)S(1)}, bf16[2,64,384]{2,1,0:T(8,128)(2,1)S(1)}, u32[]{:S(2)}, u32[]{:S(2)}) collective-permute-start(bf16[2,64,384]{2,1,0:T(8,128)(2,1)S(1)} %collective-permute-done.refs_4_), channel_id=1, source_target_pairs={{0,16},{1,5},{4,20},{5,1},{8,24},{9,13},{12,28},{13,9},{16,0},{17,... | collective-permute-start | bytes 294920 | tf_op jit(solution)/shard_map/ppermute | solution.py:227
  10.3 0.8 %shard_map.65 = (f32[128,128]{1,0:T(8,128)S(1)}, f32[128,128]{1,0:T(8,128)S(1)}, bf16[1,2,384,128]{3,2,1,0:T(8,128)(2,1)S(1)}) custom-call(bf16[2,128,4096]{2,1,0:T(8,128)(2,1)S(1)} %copy-done.1, bf16[2,64,2048]{2,1,0:T(8,128)(2,1)S(1)} %bitcast.13, bf16[2,256,2048]{2,1,0:T(8,128)(2,1)S(1)} %copy-done, bf16[2,64,2048]{2,1,0:T(8,128)(2,1)S(1)} %bitcast.15, ...), custom_call_target="tpu_custom_call" | custom-call | flops 1 | bytes 1 | tf_op jit(solution)/shard_map/pallas_call | solution.py:31
  11.2 0.3 %shard_map.70.refs_1_ = bf16[512,128]{1,0:T(8,128)(2,1)S(1)} custom-call(bf16[2,8,4096]{2,1,0:T(8,128)(2,1)S(1)} %copy-done.4), custom_call_target="tpu_custom_call" | custom-call | flops 1 | bytes 1 | tf_op jit(solution)/shard_map/pallas_call | solution.py:31
  11.5 0.5 %collective-permute-start.6 = (bf16[512,128]{1,0:T(8,128)(2,1)S(1)}, bf16[512,128]{1,0:T(8,128)(2,1)S(1)}, u32[]{:S(2)}, u32[]{:S(2)}) collective-permute-start(bf16[512,128]{1,0:T(8,128)(2,1)S(1)} %shard_map.70.refs_1_), channel_id=1, source_target_pairs={{0,4},{4,0},{8,12},{12,8},{1,5},{5,1},{9,13},{13,9},{2,6},{6,2},{1... | collective-permute-start | bytes 393224 | tf_op jit(solution)/shard_map/ppermute | solution.py:214
  12.7 0.0 collective-permute-done.2.refs_5_
  12.7 0.0 collective-permute-done.1.refs_4_
  12.7 0.5 %shard_map.68 = (f32[128,128]{1,0:T(8,128)S(1)}, bf16[128,128]{1,0:T(8,128)(2,1)S(1)}) custom-call(s32[1]{0:T(128)S(6)} %copy.7.refs_0_, bf16[2,128,4096]{2,1,0:T(8,128)(2,1)S(1)} %copy-done.1, f32[128,128]{1,0:T(8,128)S(1)} %get-tuple-element.23.refs_2_, f32[128,128]{1,0:T(8,128)S(1)} %get-tuple-element.24.refs_3_, ...), custom_call_target="tpu_custom_call" | custom-call | flops 1 | bytes 1 | tf_op jit(solution)/shard_map/pallas_call | solution.py:31
  13.2 0.2 collective-permute-done.4.refs_3_
  13.4 0.3 %shard_map.69 = bf16[16,512]{1,0:T(8,128)(2,1)S(1)} custom-call(bf16[1,2,384,128]{3,2,1,0:T(8,128)(2,1)S(1)} %get-tuple-element.21.refs_0_, f32[128,128]{1,0:T(8,128)S(1)} %get-tuple-element.27.refs_1_, bf16[128,128]{1,0:T(8,128)(2,1)S(1)} %get-tuple-element.28.refs_2_, bf16[2,64,384]{2,1,0:T(8,128)(2,1)S(1)} %collective-permute-done.4.refs_3_), custom_call_target="tpu_custom_call" | custom-call | flops 1 | bytes 1 | tf_op jit(solution)/shard_map/pallas_call | solution.py:31
  13.8 1.2 %collective-permute-start.5 = (bf16[1,16,512]{2,1,0:T(8,128)(2,1)S(1)}, bf16[1,16,512]{2,1,0:T(8,128)(2,1)S(1)}, u32[]{:S(2)}, u32[]{:S(2)}) collective-permute-start(bf16[1,16,512]{2,1,0:T(8,128)(2,1)S(1)} %bitcast.16), channel_id=1, source_target_pairs={{0,9},{1,8},{4,13},{5,12},{8,1},{9,0},{12,5},{13,4},{2,11},{3,10},... | collective-permute-start | bytes 49160 | tf_op jit(solution)/shard_map/ppermute | solution.py:220
  14.9 3.0 %collective-permute-done.5 = bf16[1,16,512]{2,1,0:T(8,128)(2,1)S(1)} collective-permute-done((bf16[1,16,512]{2,1,0:T(8,128)(2,1)S(1)}, bf16[1,16,512]{2,1,0:T(8,128)(2,1)S(1)}, u32[]{:S(2)}, u32[]{:S(2)}) %collective-permute-start.5) | collective-permute-done | bytes 16416 | tf_op jit(solution)/shard_map/ppermute | solution.py:220
  17.9 0.0 collective-permute-done.6.refs_3_
  17.9 1.3 %collective-permute-start.7 = (bf16[2,16,512]{2,1,0:T(8,128)(2,1)S(1)}, bf16[2,16,512]{2,1,0:T(8,128)(2,1)S(1)}, u32[]{:S(2)}, u32[]{:S(2)}) collective-permute-start(bf16[2,16,512]{2,1,0:T(8,128)(2,1)S(1)} %pad_maximum_fusion.1), channel_id=1, source_target_pairs={{0,3},{1,2},{2,1},{3,0},{4,7},{5,6},{6,5},{7,4},{8,11},{9,10},{10,... | collective-permute-start | bytes 98312 | tf_op jit(solution)/shard_map/ppermute | solution.py:220
  19.2 0.4 %collective-permute-start.8 = (bf16[512,128]{1,0:T(8,128)(2,1)S(1)}, bf16[512,128]{1,0:T(8,128)(2,1)S(1)}, u32[]{:S(2)}, u32[]{:S(2)}) collective-permute-start(bf16[512,128]{1,0:T(8,128)(2,1)S(1)} %shard_map.70.refs_1_), channel_id=1, source_target_pairs={{0,1},{1,0},{2,3},{3,2},{4,5},{5,4},{6,7},{7,6},{8,9},{9,8},{10,11... | collective-permute-start | bytes 393224 | tf_op jit(solution)/shard_map/ppermute | solution.py:214
  19.6 0.1 collective-permute-start.9
  19.7 1.7 %collective-permute-done.7 = bf16[2,16,512]{2,1,0:T(8,128)(2,1)S(1)} collective-permute-done((bf16[2,16,512]{2,1,0:T(8,128)(2,1)S(1)}, bf16[2,16,512]{2,1,0:T(8,128)(2,1)S(1)}, u32[]{:S(2)}, u32[]{:S(2)}) %collective-permute-start.7) | collective-permute-done | bytes 32800 | tf_op jit(solution)/shard_map/ppermute | solution.py:220
  21.4 0.0 collective-permute-done.8.refs_2_
  21.4 0.3 %shard_map.71 = (f32[4,8]{1,0:T(4,128)S(1)}, f32[4,8]{1,0:T(4,128)S(1)}, s32[2,2,8]{2,1,0:T(2,128)S(1)}) custom-call(bf16[4,16,512]{2,1,0:T(8,128)(2,1)S(1)} %pad_maximum_fusion.refs_0_, bf16[512,128]{1,0:T(8,128)(2,1)S(1)} %shard_map.70.refs_1_, bf16[512,128]{1,0:T(8,128)(2,1)S(1)} %collective-permute-done.8.refs_2_, ...), custom_call_target="tpu_custom_call" | custom-call | flops 1 | bytes 1 | tf_op jit(solution)/shard_map/pallas_call | solution.py:31
  21.7 1.2 %collective-permute-start.10 = (f32[4,8]{1,0:T(4,128)S(1)}, f32[4,8]{1,0:T(4,128)S(1)}, u32[]{:S(2)}, u32[]{:S(2)}) collective-permute-start(f32[4,8]{1,0:T(4,128)S(1)} %get-tuple-element.34), channel_id=1, source_target_pairs={{0,5},{1,4},{4,1},{5,0},{8,13},{9,12},{12,9},{13,8},{2,7},{3,6},{6... | collective-permute-start | bytes 392 | tf_op jit(solution)/shard_map/ppermute | solution.py:220
  22.9 1.8 %collective-permute-done.10 = f32[4,8]{1,0:T(4,128)S(1)} collective-permute-done((f32[4,8]{1,0:T(4,128)S(1)}, f32[4,8]{1,0:T(4,128)S(1)}, u32[]{:S(2)}, u32[]{:S(2)}) %collective-permute-start.10) | collective-permute-done | bytes 160 | tf_op jit(solution)/shard_map/ppermute | solution.py:220
  24.8 0.2 collective-permute-start.11
  24.9 1.0 %collective-permute-done.11 = f32[2,2,8]{2,1,0:T(2,128)S(1)} collective-permute-done((f32[2,2,8]{2,1,0:T(2,128)S(1)}, f32[2,2,8]{2,1,0:T(2,128)S(1)}, u32[]{:S(2)}, u32[]{:S(2)}) %collective-permute-start.11) | collective-permute-done | bytes 160 | tf_op jit(solution)/shard_map/ppermute | solution.py:214
  26.0 0.6 %compare_select_fusion = f32[2,2,8]{2,1,0:T(2,128)} fusion(f32[2,2,8]{2,1,0:T(2,128)S(1)} %maximum_add_fusion, s32[2,2,8]{2,1,0:T(2,128)S(1)} %get-tuple-element.32), kind=kLoop, calls=%fused_computation.2 | loop fusion | flops 64 | bytes 384 | tf_op jit(solution)/shard_map/jit(_where)/select_n | solution.py:334
  (17 shorter events, 0.1 us)
Async XLA Ops:
  1.0 3.0 %copy-start = (bf16[2,256,2048]{2,1,0:T(8,128)(2,1)S(1)}, bf16[2,256,2048]{2,1,0:T(8,128)(2,1)}, u32[]{:S(2)}) copy-start(bf16[2,256,2048]{2,1,0:T(8,128)(2,1)} %refs_0_.4) | copy-start | bytes 6291460
  1.0 3.0 %copy-start.3 = (bf16[2,2048,64]{1,2,0:T(8,128)(2,1)S(1)}, bf16[2,2048,64]{1,2,0:T(8,128)(2,1)}, u32[]{:S(2)}) copy-start(bf16[2,2048,64]{1,2,0:T(8,128)(2,1)} %param.9) | copy-start | bytes 1572868
  1.1 5.8 %collective-permute-start = (bf16[2,64,384]{2,1,0:T(8,128)(2,1)S(1)}, bf16[2,64,384]{2,1,0:T(8,128)(2,1)S(1)}, u32[]{:S(2)}, u32[]{:S(2)}) collective-permute-start(bf16[2,64,384]{2,1,0:T(8,128)(2,1)S(1)} %get-tuple-element.20.refs_0_), channel_id=1, source_target_pairs={{0,2},{2,0},{1,3},{3,1},{4,6},{6,4},{5,7},{7,5},{8,10},{10,8},{9,1... | collective-permute-start | bytes 294920 | tf_op jit(solution)/shard_map/ppermute | solution.py:209
  4.1 6.3 %copy-start.1 = (bf16[2,128,4096]{2,1,0:T(8,128)(2,1)S(1)}, bf16[2,128,4096]{2,1,0:T(8,128)(2,1)}, u32[]{:S(2)}) copy-start(bf16[2,128,4096]{2,1,0:T(8,128)(2,1)} %refs_1_.3) | copy-start | bytes 6291460
  4.1 6.3 %copy-start.2 = (bf16[2,2048,64]{1,2,0:T(8,128)(2,1)S(1)}, bf16[2,2048,64]{1,2,0:T(8,128)(2,1)}, u32[]{:S(2)}) copy-start(bf16[2,2048,64]{1,2,0:T(8,128)(2,1)} %param.10) | copy-start | bytes 1572868
  4.6 8.1 %collective-permute-start.3 = (bf16[2,64,640]{2,1,0:T(8,128)(2,1)S(1)}, bf16[2,64,640]{2,1,0:T(8,128)(2,1)S(1)}, u32[]{:S(2)}, u32[]{:S(2)}) collective-permute-start(bf16[2,64,640]{2,1,0:T(8,128)(2,1)S(1)} %shard_map.67), channel_id=1, source_target_pairs={{0,2},{2,0},{1,3},{3,1},{4,6},{6,4},{5,7},{7,5},{8,10},{10,8},{9,1... | collective-permute-start | bytes 491528 | tf_op jit(solution)/shard_map/ppermute | solution.py:209
  6.2 5.0 %copy-start.4 = (bf16[2,8,4096]{2,1,0:T(8,128)(2,1)S(1)}, bf16[2,8,4096]{2,1,0:T(8,128)(2,1)}, u32[]{:S(2)}) copy-start(bf16[2,8,4096]{2,1,0:T(8,128)(2,1)} %refs_0_.5) | copy-start | bytes 393220
  6.2 6.5 %collective-permute-start.2 = (bf16[2,64,384]{2,1,0:T(8,128)(2,1)S(1)}, bf16[2,64,384]{2,1,0:T(8,128)(2,1)S(1)}, u32[]{:S(2)}, u32[]{:S(2)}) collective-permute-start(bf16[2,64,384]{2,1,0:T(8,128)(2,1)S(1)} %get-tuple-element.25), channel_id=1, source_target_pairs={{0,2},{2,0},{1,3},{3,1},{4,6},{6,4},{5,7},{7,5},{8,10},{10,8},{9,1... | collective-permute-start | bytes 294920 | tf_op jit(solution)/shard_map/ppermute | solution.py:209
  6.9 5.9 %collective-permute-start.1 = (bf16[2,64,384]{2,1,0:T(8,128)(2,1)S(1)}, bf16[2,64,384]{2,1,0:T(8,128)(2,1)S(1)}, u32[]{:S(2)}, u32[]{:S(2)}) collective-permute-start(bf16[2,64,384]{2,1,0:T(8,128)(2,1)S(1)} %collective-permute-done.refs_4_), channel_id=1, source_target_pairs={{0,4},{1,17},{4,0},{5,21},{8,12},{9,25},{12,8},{13,29},{16,20},{17... | collective-permute-start | bytes 294920 | tf_op jit(solution)/shard_map/ppermute | solution.py:227
  8.8 4.6 %collective-permute-start.4 = (bf16[2,64,384]{2,1,0:T(8,128)(2,1)S(1)}, bf16[2,64,384]{2,1,0:T(8,128)(2,1)S(1)}, u32[]{:S(2)}, u32[]{:S(2)}) collective-permute-start(bf16[2,64,384]{2,1,0:T(8,128)(2,1)S(1)} %collective-permute-done.refs_4_), channel_id=1, source_target_pairs={{0,16},{1,5},{4,20},{5,1},{8,24},{9,13},{12,28},{13,9},{16,0},{17,... | collective-permute-start | bytes 294920 | tf_op jit(solution)/shard_map/ppermute | solution.py:227
  11.5 6.4 %collective-permute-start.6 = (bf16[512,128]{1,0:T(8,128)(2,1)S(1)}, bf16[512,128]{1,0:T(8,128)(2,1)S(1)}, u32[]{:S(2)}, u32[]{:S(2)}) collective-permute-start(bf16[512,128]{1,0:T(8,128)(2,1)S(1)} %shard_map.70.refs_1_), channel_id=1, source_target_pairs={{0,4},{4,0},{8,12},{12,8},{1,5},{5,1},{9,13},{13,9},{2,6},{6,2},{1... | collective-permute-start | bytes 393224 | tf_op jit(solution)/shard_map/ppermute | solution.py:214
  13.8 4.1 %collective-permute-start.5 = (bf16[1,16,512]{2,1,0:T(8,128)(2,1)S(1)}, bf16[1,16,512]{2,1,0:T(8,128)(2,1)S(1)}, u32[]{:S(2)}, u32[]{:S(2)}) collective-permute-start(bf16[1,16,512]{2,1,0:T(8,128)(2,1)S(1)} %bitcast.16), channel_id=1, source_target_pairs={{0,9},{1,8},{4,13},{5,12},{8,1},{9,0},{12,5},{13,4},{2,11},{3,10},... | collective-permute-start | bytes 49160 | tf_op jit(solution)/shard_map/ppermute | solution.py:220
  17.9 3.5 %collective-permute-start.7 = (bf16[2,16,512]{2,1,0:T(8,128)(2,1)S(1)}, bf16[2,16,512]{2,1,0:T(8,128)(2,1)S(1)}, u32[]{:S(2)}, u32[]{:S(2)}) collective-permute-start(bf16[2,16,512]{2,1,0:T(8,128)(2,1)S(1)} %pad_maximum_fusion.1), channel_id=1, source_target_pairs={{0,3},{1,2},{2,1},{3,0},{4,7},{5,6},{6,5},{7,4},{8,11},{9,10},{10,... | collective-permute-start | bytes 98312 | tf_op jit(solution)/shard_map/ppermute | solution.py:220
  19.2 2.2 %collective-permute-start.8 = (bf16[512,128]{1,0:T(8,128)(2,1)S(1)}, bf16[512,128]{1,0:T(8,128)(2,1)S(1)}, u32[]{:S(2)}, u32[]{:S(2)}) collective-permute-start(bf16[512,128]{1,0:T(8,128)(2,1)S(1)} %shard_map.70.refs_1_), channel_id=1, source_target_pairs={{0,1},{1,0},{2,3},{3,2},{4,5},{5,4},{6,7},{7,6},{8,9},{9,8},{10,11... | collective-permute-start | bytes 393224 | tf_op jit(solution)/shard_map/ppermute | solution.py:214
  19.6 1.8 %collective-permute-start.9 = (bf16[512,128]{1,0:T(8,128)(2,1)S(1)}, bf16[512,128]{1,0:T(8,128)(2,1)S(1)}, u32[]{:S(2)}, u32[]{:S(2)}) collective-permute-start(bf16[512,128]{1,0:T(8,128)(2,1)S(1)} %collective-permute-done.6.refs_3_), channel_id=1, source_target_pairs={{0,1},{1,0},{2,3},{3,2},{4,5},{5,4},{6,7},{7,6},{8,9},{9,8},{10,11... | collective-permute-start | bytes 393224 | tf_op jit(solution)/shard_map/ppermute | solution.py:214
  21.7 3.0 %collective-permute-start.10 = (f32[4,8]{1,0:T(4,128)S(1)}, f32[4,8]{1,0:T(4,128)S(1)}, u32[]{:S(2)}, u32[]{:S(2)}) collective-permute-start(f32[4,8]{1,0:T(4,128)S(1)} %get-tuple-element.34), channel_id=1, source_target_pairs={{0,5},{1,4},{4,1},{5,0},{8,13},{9,12},{12,9},{13,8},{2,7},{3,6},{6... | collective-permute-start | bytes 392 | tf_op jit(solution)/shard_map/ppermute | solution.py:220
  24.8 1.2 %collective-permute-start.11 = (f32[2,2,8]{2,1,0:T(2,128)S(1)}, f32[2,2,8]{2,1,0:T(2,128)S(1)}, u32[]{:S(2)}, u32[]{:S(2)}) collective-permute-start(f32[2,2,8]{2,1,0:T(2,128)S(1)} %pad_maximum_fusion.2), channel_id=1, source_target_pairs={{0,1},{1,0},{2,3},{3,2},{4,5},{5,4},{6,7},{7,6},{8,9},{9,8},{10,11... | collective-permute-start | bytes 392 | tf_op jit(solution)/shard_map/ppermute | solution.py:214

commit v18 on v14

--- a/solution.py
+++ b/solution.py
@@ -189,12 +189,10 @@
     fold = fold - FOLD * lax.broadcasted_iota(jnp.int32, (nq * FOLD, nq), 1)
     fold = ((fold >= 0) & (fold < FOLD)).astype(F32)
     high = sums.astype(BF16)
-    rest = sums - high.astype(F32)
-    low = rest.astype(BF16)
-    least = (rest - low.astype(F32)).astype(BF16)
-    parts = dot(jnp.concatenate([high, low, least], axis=0), fold.astype(BF16), NN)
+    low = (sums - high.astype(F32)).astype(BF16)
+    parts = dot(jnp.concatenate([high, low], axis=0), fold.astype(BF16), NN)
     rows = 2 * slots
-    table = parts[:rows] + (parts[rows : 2 * rows] + parts[2 * rows :])
+    table = parts[:rows] + parts[rows:]
     odd_place[...] = jnp.full(odd_place.shape, lax.axis_index("dp") & 1, jnp.int32)
     core = lax.axis_index("query")
     place = lax.axis_index("dp") // 2 * n + lax.axis_index("tensor")

time: 26.7 us -> 26.7 us (level)
  no operation moved by 1% of the time
where the time goes in v18:
time: 26.7 us; the launch traced here: 26.6 us
  starting transfers between devices  13.4 us (50%)
  waiting for transfers between devices  7.9 us (30%)
  Pallas kernels  3.84 us (14%)
  between operations  0.79 us (3%)
  other arithmetic  0.61 us (2%)
    ppermute x3, waiting for transfers between devices, crossed(): lax.ppermute(x, (axis, 'query'), [(i, i ^ bit * cores + 1) for i in range...  6.47 us
    ppermute x3, starting transfers between devices, shifted(): return lax.ppermute(x, axis, [(i, (i + shift) % n) for i in range(n)])  5.09 us
    pallas_call x8, Pallas kernels, call(): pl.pallas_call(body, out_shape=out_shape, in_specs=specs + [ANY] * len(af...  3.84 us
    ppermute x3, starting transfers between devices, crossed(): lax.ppermute(x, (axis, 'query'), [(i, i ^ bit * cores + 1) for i in range...  3.62 us
    ppermute x2, starting transfers between devices, forwarded(): return lax.ppermute(x, ('parts', 'dp', 'query'), pairs)  3.47 us
    ppermute x4, starting transfers between devices, flipped(): return lax.ppermute(x, axis, [(i, i ^ bit) for i in range(n)])  1.21 us
    ppermute x4, waiting for transfers between devices, flipped(): return lax.ppermute(x, axis, [(i, i ^ bit) for i in range(n)])  1.04 us
    select_n x1, other arithmetic, local(): kept = jnp.where(odd_place == 0, kept, kept[::-1]).reshape(2, -1, n, nq)  0.58 us
  transfers between devices with their start and end apart: 12, of which 6 were waited for; matrix products, arithmetic and copies ran while one was open for 0% of the time, Pallas kernels for 9%

profile of v18, /device:TPU:0, one launch (start us, length us, event | category | flops | bytes accessed | tf_op | source)
XLA Modules:
  0.0 26.6 jit_solution(12119775395024023524)
XLA Ops:
  0.0 1.0 %shard_map.64 = (bf16[2,64,384]{2,1,0:T(8,128)(2,1)S(1)}, bf16[2,64,384]{2,1,0:T(8,128)(2,1)S(1)}, bf16[2,64,512]{2,1,0:T(8,128)(2,1)S(1)}) custom-call(bf16[2,64,2048]{2,1,0:T(8,128)(2,1)} %bitcast.12), custom_call_target="tpu_custom_call" | custom-call | flops 1 | bytes 1 | tf_op jit(solution)/shard_map/pallas_call | solution.py:31
  1.0 0.0 copy-start
  1.0 0.0 copy-start.3
  1.1 3.0 %collective-permute-start = (bf16[2,64,384]{2,1,0:T(8,128)(2,1)S(1)}, bf16[2,64,384]{2,1,0:T(8,128)(2,1)S(1)}, u32[]{:S(2)}, u32[]{:S(2)}) collective-permute-start(bf16[2,64,384]{2,1,0:T(8,128)(2,1)S(1)} %get-tuple-element.21.refs_0_), channel_id=1, source_target_pairs={{0,2},{2,0},{1,3},{3,1},{4,6},{6,4},{5,7},{7,5},{8,10},{10,8},{9,1... | collective-permute-start | bytes 294920 | tf_op jit(solution)/shard_map/ppermute | solution.py:207
  4.1 0.5 %shard_map.66 = bf16[2,64,640]{2,1,0:T(8,128)(2,1)S(1)} custom-call(bf16[2,256,2048]{2,1,0:T(8,128)(2,1)S(1)} %copy-done, bf16[2,64,2048]{2,1,0:T(8,128)(2,1)S(1)} %bitcast.14, bf16[2,64,512]{2,1,0:T(8,128)(2,1)S(1)} %get-tuple-element.22.refs_2_, f32[8,128]{1,0:T(8,128)S(1)} %shard_map.65.refs_3_), custom_call_target="tpu_custom_call" | custom-call | flops 1 | bytes 1 | tf_op jit(solution)/shard_map/pallas_call | solution.py:31
  4.6 1.6 %collective-permute-start.3 = (bf16[2,64,640]{2,1,0:T(8,128)(2,1)S(1)}, bf16[2,64,640]{2,1,0:T(8,128)(2,1)S(1)}, u32[]{:S(2)}, u32[]{:S(2)}) collective-permute-start(bf16[2,64,640]{2,1,0:T(8,128)(2,1)S(1)} %shard_map.66), channel_id=1, source_target_pairs={{0,2},{2,0},{1,3},{3,1},{4,6},{6,4},{5,7},{7,5},{8,10},{10,8},{9,1... | collective-permute-start | bytes 491528 | tf_op jit(solution)/shard_map/ppermute | solution.py:207
  6.2 0.5 %collective-permute-start.2 = (bf16[2,64,384]{2,1,0:T(8,128)(2,1)S(1)}, bf16[2,64,384]{2,1,0:T(8,128)(2,1)S(1)}, u32[]{:S(2)}, u32[]{:S(2)}) collective-permute-start(bf16[2,64,384]{2,1,0:T(8,128)(2,1)S(1)} %get-tuple-element.28), channel_id=1, source_target_pairs={{0,2},{2,0},{1,3},{3,1},{4,6},{6,4},{5,7},{7,5},{8,10},{10,8},{9,1... | collective-permute-start | bytes 294920 | tf_op jit(solution)/shard_map/ppermute | solution.py:207
  6.7 0.2 collective-permute-done.refs_4_
  6.9 2.0 %collective-permute-start.1 = (bf16[2,64,384]{2,1,0:T(8,128)(2,1)S(1)}, bf16[2,64,384]{2,1,0:T(8,128)(2,1)S(1)}, u32[]{:S(2)}, u32[]{:S(2)}) collective-permute-start(bf16[2,64,384]{2,1,0:T(8,128)(2,1)S(1)} %collective-permute-done.refs_4_), channel_id=1, source_target_pairs={{0,4},{1,17},{4,0},{5,21},{8,12},{9,25},{12,8},{13,29},{16,20},{17... | collective-permute-start | bytes 294920 | tf_op jit(solution)/shard_map/ppermute | solution.py:225
  8.8 1.5 %collective-permute-start.4 = (bf16[2,64,384]{2,1,0:T(8,128)(2,1)S(1)}, bf16[2,64,384]{2,1,0:T(8,128)(2,1)S(1)}, u32[]{:S(2)}, u32[]{:S(2)}) collective-permute-start(bf16[2,64,384]{2,1,0:T(8,128)(2,1)S(1)} %collective-permute-done.refs_4_), channel_id=1, source_target_pairs={{0,16},{1,5},{4,20},{5,1},{8,24},{9,13},{12,28},{13,9},{16,0},{17,... | collective-permute-start | bytes 294920 | tf_op jit(solution)/shard_map/ppermute | solution.py:225
  10.3 0.8 %shard_map.67 = (f32[128,128]{1,0:T(8,128)S(1)}, f32[128,128]{1,0:T(8,128)S(1)}, bf16[1,2,384,128]{3,2,1,0:T(8,128)(2,1)S(1)}) custom-call(bf16[2,128,4096]{2,1,0:T(8,128)(2,1)S(1)} %copy-done.1, bf16[2,64,2048]{2,1,0:T(8,128)(2,1)S(1)} %bitcast.13, bf16[2,256,2048]{2,1,0:T(8,128)(2,1)S(1)} %copy-done, bf16[2,64,2048]{2,1,0:T(8,128)(2,1)S(1)} %bitcast.15, ...), custom_call_target="tpu_custom_call" | custom-call | flops 1 | bytes 1 | tf_op jit(solution)/shard_map/pallas_call | solution.py:31
  11.2 0.3 %shard_map.70.refs_1_ = bf16[512,128]{1,0:T(8,128)(2,1)S(1)} custom-call(bf16[2,8,4096]{2,1,0:T(8,128)(2,1)S(1)} %copy-done.4), custom_call_target="tpu_custom_call" | custom-call | flops 1 | bytes 1 | tf_op jit(solution)/shard_map/pallas_call | solution.py:31
  11.5 0.5 %collective-permute-start.6 = (bf16[512,128]{1,0:T(8,128)(2,1)S(1)}, bf16[512,128]{1,0:T(8,128)(2,1)S(1)}, u32[]{:S(2)}, u32[]{:S(2)}) collective-permute-start(bf16[512,128]{1,0:T(8,128)(2,1)S(1)} %shard_map.70.refs_1_), channel_id=1, source_target_pairs={{0,4},{4,0},{8,12},{12,8},{1,5},{5,1},{9,13},{13,9},{2,6},{6,2},{1... | collective-permute-start | bytes 393224 | tf_op jit(solution)/shard_map/ppermute | solution.py:212
  12.7 0.0 collective-permute-done.2.refs_5_
  12.7 0.0 collective-permute-done.1.refs_4_
  12.7 0.5 %shard_map.68 = (f32[128,128]{1,0:T(8,128)S(1)}, bf16[128,128]{1,0:T(8,128)(2,1)S(1)}) custom-call(s32[1]{0:T(128)S(6)} %copy.7.refs_0_, bf16[2,128,4096]{2,1,0:T(8,128)(2,1)S(1)} %copy-done.1, f32[128,128]{1,0:T(8,128)S(1)} %get-tuple-element.26.refs_2_, f32[128,128]{1,0:T(8,128)S(1)} %get-tuple-element.27.refs_3_, ...), custom_call_target="tpu_custom_call" | custom-call | flops 1 | bytes 1 | tf_op jit(solution)/shard_map/pallas_call | solution.py:31
  13.2 0.2 collective-permute-done.4.refs_3_
  13.4 0.3 %shard_map.69 = bf16[16,512]{1,0:T(8,128)(2,1)S(1)} custom-call(bf16[1,2,384,128]{3,2,1,0:T(8,128)(2,1)S(1)} %get-tuple-element.24.refs_0_, f32[128,128]{1,0:T(8,128)S(1)} %get-tuple-element.29.refs_1_, bf16[128,128]{1,0:T(8,128)(2,1)S(1)} %get-tuple-element.30.refs_2_, bf16[2,64,384]{2,1,0:T(8,128)(2,1)S(1)} %collective-permute-done.4.refs_3_), custom_call_target="tpu_custom_call" | custom-call | flops 1 | bytes 1 | tf_op jit(solution)/shard_map/pallas_call | solution.py:31
  13.8 1.2 %collective-permute-start.5 = (bf16[1,16,512]{2,1,0:T(8,128)(2,1)S(1)}, bf16[1,16,512]{2,1,0:T(8,128)(2,1)S(1)}, u32[]{:S(2)}, u32[]{:S(2)}) collective-permute-start(bf16[1,16,512]{2,1,0:T(8,128)(2,1)S(1)} %bitcast.16), channel_id=1, source_target_pairs={{0,9},{1,8},{4,13},{5,12},{8,1},{9,0},{12,5},{13,4},{2,11},{3,10},... | collective-permute-start | bytes 49160 | tf_op jit(solution)/shard_map/ppermute | solution.py:218
  14.9 3.0 %collective-permute-done.5 = bf16[1,16,512]{2,1,0:T(8,128)(2,1)S(1)} collective-permute-done((bf16[1,16,512]{2,1,0:T(8,128)(2,1)S(1)}, bf16[1,16,512]{2,1,0:T(8,128)(2,1)S(1)}, u32[]{:S(2)}, u32[]{:S(2)}) %collective-permute-start.5) | collective-permute-done | bytes 16416 | tf_op jit(solution)/shard_map/ppermute | solution.py:218
  17.9 0.0 collective-permute-done.6.refs_3_
  17.9 1.3 %collective-permute-start.7 = (bf16[2,16,512]{2,1,0:T(8,128)(2,1)S(1)}, bf16[2,16,512]{2,1,0:T(8,128)(2,1)S(1)}, u32[]{:S(2)}, u32[]{:S(2)}) collective-permute-start(bf16[2,16,512]{2,1,0:T(8,128)(2,1)S(1)} %pad_maximum_fusion.1), channel_id=1, source_target_pairs={{0,3},{1,2},{2,1},{3,0},{4,7},{5,6},{6,5},{7,4},{8,11},{9,10},{10,... | collective-permute-start | bytes 98312 | tf_op jit(solution)/shard_map/ppermute | solution.py:218
  19.2 0.4 %collective-permute-start.8 = (bf16[512,128]{1,0:T(8,128)(2,1)S(1)}, bf16[512,128]{1,0:T(8,128)(2,1)S(1)}, u32[]{:S(2)}, u32[]{:S(2)}) collective-permute-start(bf16[512,128]{1,0:T(8,128)(2,1)S(1)} %shard_map.70.refs_1_), channel_id=1, source_target_pairs={{0,1},{1,0},{2,3},{3,2},{4,5},{5,4},{6,7},{7,6},{8,9},{9,8},{10,11... | collective-permute-start | bytes 393224 | tf_op jit(solution)/shard_map/ppermute | solution.py:212
  19.6 0.1 collective-permute-start.9
  19.7 1.7 %collective-permute-done.7 = bf16[2,16,512]{2,1,0:T(8,128)(2,1)S(1)} collective-permute-done((bf16[2,16,512]{2,1,0:T(8,128)(2,1)S(1)}, bf16[2,16,512]{2,1,0:T(8,128)(2,1)S(1)}, u32[]{:S(2)}, u32[]{:S(2)}) %collective-permute-start.7) | collective-permute-done | bytes 32800 | tf_op jit(solution)/shard_map/ppermute | solution.py:218
  21.4 0.0 collective-permute-done.8.refs_2_
  21.4 0.3 %shard_map.71 = (f32[4,8]{1,0:T(4,128)S(1)}, f32[4,8]{1,0:T(4,128)S(1)}, s32[2,2,8]{2,1,0:T(2,128)S(1)}) custom-call(bf16[4,16,512]{2,1,0:T(8,128)(2,1)S(1)} %pad_maximum_fusion.refs_0_, bf16[512,128]{1,0:T(8,128)(2,1)S(1)} %shard_map.70.refs_1_, bf16[512,128]{1,0:T(8,128)(2,1)S(1)} %collective-permute-done.8.refs_2_, ...), custom_call_target="tpu_custom_call" | custom-call | flops 1 | bytes 1 | tf_op jit(solution)/shard_map/pallas_call | solution.py:31
  21.7 1.2 %collective-permute-start.10 = (f32[4,8]{1,0:T(4,128)S(1)}, f32[4,8]{1,0:T(4,128)S(1)}, u32[]{:S(2)}, u32[]{:S(2)}) collective-permute-start(f32[4,8]{1,0:T(4,128)S(1)} %get-tuple-element.36), channel_id=1, source_target_pairs={{0,5},{1,4},{4,1},{5,0},{8,13},{9,12},{12,9},{13,8},{2,7},{3,6},{6... | collective-permute-start | bytes 392 | tf_op jit(solution)/shard_map/ppermute | solution.py:218
  22.9 1.8 %collective-permute-done.10 = f32[4,8]{1,0:T(4,128)S(1)} collective-permute-done((f32[4,8]{1,0:T(4,128)S(1)}, f32[4,8]{1,0:T(4,128)S(1)}, u32[]{:S(2)}, u32[]{:S(2)}) %collective-permute-start.10) | collective-permute-done | bytes 160 | tf_op jit(solution)/shard_map/ppermute | solution.py:218
  24.8 0.2 collective-permute-start.11
  24.9 1.0 %collective-permute-done.11 = f32[2,2,8]{2,1,0:T(2,128)S(1)} collective-permute-done((f32[2,2,8]{2,1,0:T(2,128)S(1)}, f32[2,2,8]{2,1,0:T(2,128)S(1)}, u32[]{:S(2)}, u32[]{:S(2)}) %collective-permute-start.11) | collective-permute-done | bytes 160 | tf_op jit(solution)/shard_map/ppermute | solution.py:212
  26.0 0.6 %compare_select_fusion = f32[2,2,8]{2,1,0:T(2,128)} fusion(f32[2,2,8]{2,1,0:T(2,128)S(1)} %maximum_add_fusion, s32[2,2,8]{2,1,0:T(2,128)S(1)} %get-tuple-element.34), kind=kLoop, calls=%fused_computation.2 | loop fusion | flops 64 | bytes 384 | tf_op jit(solution)/shard_map/jit(_where)/select_n | solution.py:333
  (17 shorter events, 0.1 us)
Async XLA Ops:
  1.0 3.0 %copy-start = (bf16[2,256,2048]{2,1,0:T(8,128)(2,1)S(1)}, bf16[2,256,2048]{2,1,0:T(8,128)(2,1)}, u32[]{:S(2)}) copy-start(bf16[2,256,2048]{2,1,0:T(8,128)(2,1)} %refs_2_.3) | copy-start | bytes 6291460
  1.0 3.0 %copy-start.3 = (bf16[2,2048,64]{1,2,0:T(8,128)(2,1)S(1)}, bf16[2,2048,64]{1,2,0:T(8,128)(2,1)}, u32[]{:S(2)}) copy-start(bf16[2,2048,64]{1,2,0:T(8,128)(2,1)} %param.9) | copy-start | bytes 1572868
  1.1 5.8 %collective-permute-start = (bf16[2,64,384]{2,1,0:T(8,128)(2,1)S(1)}, bf16[2,64,384]{2,1,0:T(8,128)(2,1)S(1)}, u32[]{:S(2)}, u32[]{:S(2)}) collective-permute-start(bf16[2,64,384]{2,1,0:T(8,128)(2,1)S(1)} %get-tuple-element.21.refs_0_), channel_id=1, source_target_pairs={{0,2},{2,0},{1,3},{3,1},{4,6},{6,4},{5,7},{7,5},{8,10},{10,8},{9,1... | collective-permute-start | bytes 294920 | tf_op jit(solution)/shard_map/ppermute | solution.py:207
  4.1 6.3 %copy-start.1 = (bf16[2,128,4096]{2,1,0:T(8,128)(2,1)S(1)}, bf16[2,128,4096]{2,1,0:T(8,128)(2,1)}, u32[]{:S(2)}) copy-start(bf16[2,128,4096]{2,1,0:T(8,128)(2,1)} %refs_1_.3) | copy-start | bytes 6291460
  4.1 6.3 %copy-start.2 = (bf16[2,2048,64]{1,2,0:T(8,128)(2,1)S(1)}, bf16[2,2048,64]{1,2,0:T(8,128)(2,1)}, u32[]{:S(2)}) copy-start(bf16[2,2048,64]{1,2,0:T(8,128)(2,1)} %param.10) | copy-start | bytes 1572868
  4.6 8.1 %collective-permute-start.3 = (bf16[2,64,640]{2,1,0:T(8,128)(2,1)S(1)}, bf16[2,64,640]{2,1,0:T(8,128)(2,1)S(1)}, u32[]{:S(2)}, u32[]{:S(2)}) collective-permute-start(bf16[2,64,640]{2,1,0:T(8,128)(2,1)S(1)} %shard_map.66), channel_id=1, source_target_pairs={{0,2},{2,0},{1,3},{3,1},{4,6},{6,4},{5,7},{7,5},{8,10},{10,8},{9,1... | collective-permute-start | bytes 491528 | tf_op jit(solution)/shard_map/ppermute | solution.py:207
  6.2 5.0 %copy-start.4 = (bf16[2,8,4096]{2,1,0:T(8,128)(2,1)S(1)}, bf16[2,8,4096]{2,1,0:T(8,128)(2,1)}, u32[]{:S(2)}) copy-start(bf16[2,8,4096]{2,1,0:T(8,128)(2,1)} %refs_0_.5) | copy-start | bytes 393220
  6.2 6.5 %collective-permute-start.2 = (bf16[2,64,384]{2,1,0:T(8,128)(2,1)S(1)}, bf16[2,64,384]{2,1,0:T(8,128)(2,1)S(1)}, u32[]{:S(2)}, u32[]{:S(2)}) collective-permute-start(bf16[2,64,384]{2,1,0:T(8,128)(2,1)S(1)} %get-tuple-element.28), channel_id=1, source_target_pairs={{0,2},{2,0},{1,3},{3,1},{4,6},{6,4},{5,7},{7,5},{8,10},{10,8},{9,1... | collective-permute-start | bytes 294920 | tf_op jit(solution)/shard_map/ppermute | solution.py:207
  6.9 5.9 %collective-permute-start.1 = (bf16[2,64,384]{2,1,0:T(8,128)(2,1)S(1)}, bf16[2,64,384]{2,1,0:T(8,128)(2,1)S(1)}, u32[]{:S(2)}, u32[]{:S(2)}) collective-permute-start(bf16[2,64,384]{2,1,0:T(8,128)(2,1)S(1)} %collective-permute-done.refs_4_), channel_id=1, source_target_pairs={{0,4},{1,17},{4,0},{5,21},{8,12},{9,25},{12,8},{13,29},{16,20},{17... | collective-permute-start | bytes 294920 | tf_op jit(solution)/shard_map/ppermute | solution.py:225
  8.8 4.6 %collective-permute-start.4 = (bf16[2,64,384]{2,1,0:T(8,128)(2,1)S(1)}, bf16[2,64,384]{2,1,0:T(8,128)(2,1)S(1)}, u32[]{:S(2)}, u32[]{:S(2)}) collective-permute-start(bf16[2,64,384]{2,1,0:T(8,128)(2,1)S(1)} %collective-permute-done.refs_4_), channel_id=1, source_target_pairs={{0,16},{1,5},{4,20},{5,1},{8,24},{9,13},{12,28},{13,9},{16,0},{17,... | collective-permute-start | bytes 294920 | tf_op jit(solution)/shard_map/ppermute | solution.py:225
  11.5 6.4 %collective-permute-start.6 = (bf16[512,128]{1,0:T(8,128)(2,1)S(1)}, bf16[512,128]{1,0:T(8,128)(2,1)S(1)}, u32[]{:S(2)}, u32[]{:S(2)}) collective-permute-start(bf16[512,128]{1,0:T(8,128)(2,1)S(1)} %shard_map.70.refs_1_), channel_id=1, source_target_pairs={{0,4},{4,0},{8,12},{12,8},{1,5},{5,1},{9,13},{13,9},{2,6},{6,2},{1... | collective-permute-start | bytes 393224 | tf_op jit(solution)/shard_map/ppermute | solution.py:212
  13.8 4.1 %collective-permute-start.5 = (bf16[1,16,512]{2,1,0:T(8,128)(2,1)S(1)}, bf16[1,16,512]{2,1,0:T(8,128)(2,1)S(1)}, u32[]{:S(2)}, u32[]{:S(2)}) collective-permute-start(bf16[1,16,512]{2,1,0:T(8,128)(2,1)S(1)} %bitcast.16), channel_id=1, source_target_pairs={{0,9},{1,8},{4,13},{5,12},{8,1},{9,0},{12,5},{13,4},{2,11},{3,10},... | collective-permute-start | bytes 49160 | tf_op jit(solution)/shard_map/ppermute | solution.py:218
  17.9 3.5 %collective-permute-start.7 = (bf16[2,16,512]{2,1,0:T(8,128)(2,1)S(1)}, bf16[2,16,512]{2,1,0:T(8,128)(2,1)S(1)}, u32[]{:S(2)}, u32[]{:S(2)}) collective-permute-start(bf16[2,16,512]{2,1,0:T(8,128)(2,1)S(1)} %pad_maximum_fusion.1), channel_id=1, source_target_pairs={{0,3},{1,2},{2,1},{3,0},{4,7},{5,6},{6,5},{7,4},{8,11},{9,10},{10,... | collective-permute-start | bytes 98312 | tf_op jit(solution)/shard_map/ppermute | solution.py:218
  19.2 2.2 %collective-permute-start.8 = (bf16[512,128]{1,0:T(8,128)(2,1)S(1)}, bf16[512,128]{1,0:T(8,128)(2,1)S(1)}, u32[]{:S(2)}, u32[]{:S(2)}) collective-permute-start(bf16[512,128]{1,0:T(8,128)(2,1)S(1)} %shard_map.70.refs_1_), channel_id=1, source_target_pairs={{0,1},{1,0},{2,3},{3,2},{4,5},{5,4},{6,7},{7,6},{8,9},{9,8},{10,11... | collective-permute-start | bytes 393224 | tf_op jit(solution)/shard_map/ppermute | solution.py:212
  19.6 1.8 %collective-permute-start.9 = (bf16[512,128]{1,0:T(8,128)(2,1)S(1)}, bf16[512,128]{1,0:T(8,128)(2,1)S(1)}, u32[]{:S(2)}, u32[]{:S(2)}) collective-permute-start(bf16[512,128]{1,0:T(8,128)(2,1)S(1)} %collective-permute-done.6.refs_3_), channel_id=1, source_target_pairs={{0,1},{1,0},{2,3},{3,2},{4,5},{5,4},{6,7},{7,6},{8,9},{9,8},{10,11... | collective-permute-start | bytes 393224 | tf_op jit(solution)/shard_map/ppermute | solution.py:212
  21.7 3.0 %collective-permute-start.10 = (f32[4,8]{1,0:T(4,128)S(1)}, f32[4,8]{1,0:T(4,128)S(1)}, u32[]{:S(2)}, u32[]{:S(2)}) collective-permute-start(f32[4,8]{1,0:T(4,128)S(1)} %get-tuple-element.36), channel_id=1, source_target_pairs={{0,5},{1,4},{4,1},{5,0},{8,13},{9,12},{12,9},{13,8},{2,7},{3,6},{6... | collective-permute-start | bytes 392 | tf_op jit(solution)/shard_map/ppermute | solution.py:218
  24.8 1.2 %collective-permute-start.11 = (f32[2,2,8]{2,1,0:T(2,128)S(1)}, f32[2,2,8]{2,1,0:T(2,128)S(1)}, u32[]{:S(2)}, u32[]{:S(2)}) collective-permute-start(f32[2,2,8]{2,1,0:T(2,128)S(1)} %pad_maximum_fusion.2), channel_id=1, source_target_pairs={{0,1},{1,0},{2,3},{3,2},{4,5},{5,4},{6,7},{7,6},{8,9},{9,8},{10,11... | collective-permute-start | bytes 392 | tf_op jit(solution)/shard_map/ppermute | solution.py:212
